TPU v7x, 32 devices: a whole 2x2x4 slice. The times are simulated.
32 devices in a mesh: grp: 2 (over x), seq: 16 (over z, y, core).
Axes of the slice: x: 2, y: 2, z: 4, core: 2. Of those that a mesh axis runs over, the one named last changes fastest.
Arguments:
- events: bfloat16 [24576, 1024], P(('grp', 'seq')), parts along dimension 0, may hold values from -6 to 6
- w_query: bfloat16 [1024, 1024], replicated, may hold values from -0.1875 to 0.1875
- w_key: bfloat16 [1024, 1024], replicated, may hold values from -0.1875 to 0.1875
- w_value: bfloat16 [1024, 1024], replicated, may hold values from -0.1875 to 0.1875
- w_output: bfloat16 [1024, 1024], replicated, may hold values from -0.1875 to 0.1875
- expert_in: bfloat16 [1024, 16384], P(None, 'seq'), may hold values from -0.1875 to 0.1875
- expert_out: bfloat16 [16384, 256], P('seq'), may hold values from -0.1875 to 0.1875
- gate_weight: bfloat16 [1024, 32], replicated, may hold values from -0.1875 to 0.1875
- label_rows: int32 [1024], P(('grp', 'seq')), parts along dimension 0, may hold values from 0 to 767
- label_experts: int32 [1024, 2], P(('grp', 'seq')), parts along dimension 0, may hold values from 0 to 15, all different within a row; in each aligned block of 32 rows (0 to 31, 32 to 63, ...) at most 8 rows name the same one
- label_tasks: int32 [1024], P(('grp', 'seq')), parts along dimension 0, may hold values from 0 to 1
Outputs:
- hidden: bfloat16 [24576, 1024], P(('grp', 'seq')), parts along dimension 0
- scores: float32 [1024, 256], P(('grp', 'seq')), parts along dimension 0
There are 2 independent parts, one for each index of `grp`. A program takes and returns all parts, laid end to end along the dimension named above; an argument that names none is the same for every part. Nothing has to cross between parts.
Inputs may be any that keep to these rules, and one draw needn't show every extreme that they name: `label_experts`: each row names two different experts; within the 32 rows of one device (aligned blocks) no expert is named by more than 8 rows, and in every draw some expert is named by exactly 8 rows of some device.
All inputs are finite; a program needn't handle non-finite values.
Results may differ from a plain program's by a relative error of at most 0.012.
Values may be sent and summed in bfloat16 or wider, within the bound.
No kernel may reach another device: no remote copies, remote signals or barrier semaphores. Data moves between devices by JAX's collectives and lax.ppermute only.
A program may use at most 128 MiB of HBM per device.

v0:
```python
import jax
import jax.numpy as jnp
from jax import lax
from jax.sharding import PartitionSpec as P

HEADS = 8
EXPERTS = 16
CAP = 8


def carried_in(shard, axis, combine, identity):
    length, position = (lax.axis_size(axis), lax.axis_index(axis))
    everything = lax.all_gather(shard, axis)
    start = jnp.broadcast_to(jnp.asarray(identity, shard.dtype), shard.shape)

    def step(k, before):
        reached = k < position
        new = combine(before, everything[k])
        return jnp.where(reached, new, before)

    return lax.fori_loop(0, length, step, start)


def slot_places(route):
    flat = route.reshape(-1)
    onehot = (flat[:, None] == jnp.arange(EXPERTS, dtype=jnp.int32)[None, :]).astype(jnp.int32)
    before = jnp.cumsum(onehot, axis=0) - onehot
    slot_index = jnp.sum(before * onehot, axis=1)
    return (flat * CAP + slot_index).reshape(route.shape)


def expert_rows(arrived, weight_in, weight_out):
    count_src = arrived.shape[0]
    count_slot = arrived.shape[1]
    flat = arrived.reshape(count_src * count_slot, arrived.shape[2])
    inner = jax.nn.relu(jnp.dot(flat, weight_in, preferred_element_type=jnp.float32)).astype(
        jnp.bfloat16
    )
    partial_sum = jnp.dot(inner, weight_out, preferred_element_type=jnp.float32)
    return partial_sum.reshape(count_src, count_slot, partial_sum.shape[1])


def add_states(earlier, later):
    return earlier + later


def shards(
    events,
    w_query,
    w_key,
    w_value,
    w_output,
    expert_in,
    expert_out,
    gate_weight,
    label_rows,
    label_experts,
    label_tasks,
):
    tok_rows = events.shape[0]
    width = events.shape[1]
    head_dim = width // HEADS
    query = (
        jnp.dot(events, w_query, preferred_element_type=jnp.float32)
        .astype(jnp.bfloat16)
        .reshape(tok_rows, HEADS, head_dim)
    )
    keys = (
        jnp.dot(events, w_key, preferred_element_type=jnp.float32)
        .astype(jnp.bfloat16)
        .reshape(tok_rows, HEADS, head_dim)
    )
    values = (
        jnp.dot(events, w_value, preferred_element_type=jnp.float32)
        .astype(jnp.bfloat16)
        .reshape(tok_rows, HEADS, head_dim)
    )
    local_state = jnp.einsum("shd,she->hde", keys, values, preferred_element_type=jnp.float32)
    identity = jnp.zeros_like(local_state)
    prefix = carried_in(local_state, "seq", add_states, identity).astype(jnp.bfloat16)
    local_index = jnp.arange(tok_rows, dtype=jnp.int32)
    causal = local_index[None, :] <= local_index[:, None]
    weight = jnp.einsum("thd,shd->hts", query, keys, preferred_element_type=jnp.float32)
    weight = jnp.where(causal[None], weight, 0.0).astype(jnp.bfloat16)
    within = jnp.einsum("hts,shd->thd", weight, values, preferred_element_type=jnp.float32)
    earlier = jnp.einsum("thd,hde->the", query, prefix, preferred_element_type=jnp.float32)
    places_now = lax.axis_index("seq") * tok_rows + local_index
    factor = lax.rsqrt((places_now + 1).astype(jnp.float32) * head_dim)
    attended = (
        ((within + earlier) * factor[:, None, None]).astype(jnp.bfloat16).reshape(tok_rows, width)
    )
    hidden = (
        events.astype(jnp.float32) + jnp.dot(attended, w_output, preferred_element_type=jnp.float32)
    ).astype(jnp.bfloat16)
    picked = jnp.take(hidden, label_rows, axis=0)
    places = slot_places(label_experts)
    copies = lax.axis_size("seq") // EXPERTS
    targets = jnp.arange(EXPERTS * CAP, dtype=jnp.int32)
    selector = jnp.any(targets[:, None, None] == places[None, :, :], axis=2).astype(jnp.bfloat16)
    buffer = jnp.dot(selector, picked, preferred_element_type=jnp.float32).astype(jnp.bfloat16)
    outgoing = jnp.repeat(buffer.reshape(EXPERTS, CAP, width), copies, axis=0)
    partials = expert_rows(
        lax.all_to_all(outgoing, "seq", split_axis=0, concat_axis=0, tiled=True),
        expert_in,
        expert_out,
    )
    back = lax.all_to_all(
        partials.astype(jnp.bfloat16), "seq", split_axis=0, concat_axis=0, tiled=True
    ).astype(partials.dtype)
    out_width = back.shape[2]
    totals = (
        back.reshape(EXPERTS, copies, CAP, out_width).sum(axis=1).reshape(EXPERTS * CAP, out_width)
    )
    chosen = jnp.take(totals, places.reshape(-1), axis=0).reshape(places.shape[0], 2, out_width)
    logits = jnp.dot(picked, gate_weight, preferred_element_type=jnp.float32)
    columns = label_tasks[:, None] * EXPERTS + label_experts
    gates = jax.nn.sigmoid(jnp.take_along_axis(logits, columns, axis=1))
    scores = jnp.sum(gates[:, :, None] * chosen, axis=1)
    return (hidden, scores)


def solution(mesh):
    placed = (
        P(("grp", "seq"), None),
        P(),
        P(),
        P(),
        P(),
        P(None, "seq"),
        P("seq", None),
        P(),
        P(("grp", "seq")),
        P(("grp", "seq"), None),
        P(("grp", "seq")),
    )
    return jax.shard_map(
        shards,
        mesh=mesh,
        in_specs=placed,
        out_specs=(P(("grp", "seq"), None), P(("grp", "seq"), None)),
        check_vma=False,
    )
```

profile of v0, /device:TPU:0, one launch (start us, length us, event | category | flops | bytes accessed | tf_op | source)
XLA Modules:
  0.0 164.9 jit_solution(9241055167782557303)
XLA Ops:
  7.2 1.5 copy-done
  8.8 4.3 %convolution_convert_fusion = bf16[768,1024]{1,0:T(8,128)(2,1)} fusion(bf16[768,1024]{1,0:T(8,128)(2,1)} %param.13, bf16[1024,1024]{1,0:T(8,128)(2,1)S(1)} %copy-done), kind=kOutput, calls=%fused_computation.12 | convolution fusion | flops 1611399168 | bytes 5242880 | tf_op jit(solution)/shard_map/dot_general | solution.py:69
  13.1 2.6 %copy.73 = bf16[768,1024]{0,1:T(8,128)(2,1)} copy(bf16[768,1024]{1,0:T(8,128)(2,1)} %convolution_convert_fusion) | data formatting | bytes 3145728 | tf_op jit(solution)/shard_map/reshape | solution.py:71
  15.7 4.0 %fusion.11 = bf16[96,8,8,128]{3,2,1,0:T(8,128)(2,1)S(1)} fusion(bf16[768,1024]{1,0:T(8,128)(2,1)} %param.13, bf16[1024,1024]{1,0:T(8,128)(2,1)} %param.16), kind=kOutput, calls=%fused_computation.20 | convolution fusion | flops 1611399168 | bytes 5242880 | tf_op jit(solution)/shard_map/dot_general | solution.py:74
  20.9 1.4 fusion.9
  23.9 5.0 %fusion.12 = bf16[96,8,8,128]{3,2,1,0:T(8,128)(2,1)} fusion(bf16[768,1024]{1,0:T(8,128)(2,1)} %param.13, bf16[1024,1024]{1,0:T(8,128)(2,1)} %param.14), kind=kOutput, calls=%fused_computation.21 | convolution fusion | flops 1611399168 | bytes 5242880 | tf_op jit(solution)/shard_map/dot_general | solution.py:64
  28.9 9.8 %fusion = f32[8,128,768]{2,1,0:T(8,128)} fusion(pred[768,768]{1,0:T(8,128)(4,1)S(1)} %iota_compare_fusion, bf16[768,8,128]{0,2,1:T(8,128)(2,1)} %bitcast.59, bf16[96,8,8,128]{3,2,1,0:T(8,128)(2,1)} %fusion.12, bf16[96,8,8,128]{3,2,1,0:T(8,128)(2,1)} %copy-done.9), kind=kOutput, calls=%fused_computation.5 | convolution fusion | flops 2425356288 | bytes 8454144 | tf_op jit(solution)/shard_map/hts,shd->thd/dot_general | solution.py:85
  38.8 61.3 %all-gather.3.cloned.1.call-done = f32[128,128,128]{2,1,0:T(8,128)} async-done(((f32[8,128,128]{2,1,0:T(8,128)}), f32[128,128,128]{2,1,0:T(8,128)}) %all-gather.3.cloned.1.call-update) | async-done | bytes 8388624 | tf_op jit(solution)/shard_map/all_gather | solution.py:13
  100.0 20.0 %while.14 = (s32[]{:T(128)}, f32[8,128,128]{2,1,0:T(8,128)S(1)}, s32[]{:T(128)}, f32[16,8,128,128]{3,2,1,0:T(8,128)}, s32[]{:T(128)}, /*index=5*/s32[]{:T(128)}) while((s32[]{:T(128)}, f32[8,128,128]{2,1,0:T(8,128)S(1)}, s32[]{:T(128)}, f32[16,8,128,128]{3,2,1,0:T(8,128)}, s32[]{:T(128)}, /*index=5*/s32[]{:T(128)}) %tuple.42), condition=%wide.region_1.2_spmd.clone, body=%wide.region_0.1_spmd.clone.sunk | while | flops 393220 | bytes 1572957 | solution.py:21
  101.3 1.2 add_select_fusion.2
  102.5 1.2 add_select_fusion.2
  103.8 1.2 add_select_fusion.2
  105.0 1.2 add_select_fusion.2
  106.3 1.2 add_select_fusion.2
  108.8 1.2 add_select_fusion.2
  110.0 1.2 add_select_fusion.2
  120.1 3.2 %multiply_convert_fusion = bf16[8,128,768]{2,1,0:T(8,128)(2,1)S(1)} fusion(f32[8,128,768]{2,1,0:T(8,128)} %fusion, f32[768]{0:T(1024)S(1)} %multiply_rsqrt_fusion, bf16[96,8,8,128]{3,2,1,0:T(8,128)(2,1)} %fusion.12, f32[8,128,128]{2,1,0:T(8,128)S(1)} %get-tuple-element.81), kind=kOutput, calls=%fused_computation.10 | convolution fusion | flops 203816960 | bytes 6818816 | tf_op jit(solution)/shard_map/thd,hde->the/dot_general | solution.py:86
  123.5 3.0 %add_convert_fusion = bf16[768,1024]{1,0:T(8,128)(2,1)} fusion(bf16[768,1024]{1,0:T(8,128)(2,1)S(1)} %copy-done.5, bf16[768,1024]{0,1:T(8,128)(2,1)S(1)} %bitcast.61, bf16[1024,1024]{1,0:T(8,128)(2,1)S(1)} %copy-done.4), kind=kOutput, calls=%fused_computation.9 | convolution fusion | flops 1612972032 | bytes 6815744 | tf_op jit(solution)/shard_map/dot_general | solution.py:93
  126.5 2.3 %gather_fusion = bf16[32,1024]{1,0:T(8,128)(2,1)S(1)} fusion(bf16[768,1024]{1,0:T(8,128)(2,1)} %add_convert_fusion, s32[1024]{0:T(1024)S(1)} %pad_clamp_fusion.1), kind=kCustom, calls=%fused_computation | custom fusion | bytes 131200 | tf_op jit(solution)/shard_map/jit(_take)/gather | solution.py:95
  129.8 3.5 %all-to-all-start = ((bf16[16,8,1024]{2,1,0:T(8,128)(2,1)}), bf16[16,8,1024]{2,1,0:T(8,128)(2,1)S(1)}, u32[]{:S(2)}, u32[]{:S(2)}) async-start(bf16[16,8,1024]{2,1,0:T(8,128)(2,1)} %fusion.20), calls=%async_computation | async-start | bytes 524288 | tf_op jit(solution)/shard_map/all_to_all | solution.py:103
  134.6 8.8 %all-to-all-done = bf16[16,8,1024]{2,1,0:T(8,128)(2,1)S(1)} async-done(((bf16[16,8,1024]{2,1,0:T(8,128)(2,1)}), bf16[16,8,1024]{2,1,0:T(8,128)(2,1)S(1)}, u32[]{:S(2)}, u32[]{:S(2)}) %all-to-all-start) | async-done | bytes 262176 | tf_op jit(solution)/shard_map/all_to_all | solution.py:103
  143.4 2.9 %fusion.22 = bf16[16,8,256]{2,1,0:T(8,128)(2,1)} fusion(bf16[1024,256]{1,0:T(8,128)(2,1)S(1)} %copy-done.2, bf16[1024,1024]{1,0:T(8,128)(2,1)} %param.18, bf16[16,8,1024]{2,1,0:T(8,128)(2,1)S(1)} %all-to-all-done), kind=kOutput, calls=%fused_computation.32 | convolution fusion | flops 335839232 | bytes 2949120 | tf_op jit(solution)/shard_map/dot_general | solution.py:39
  146.2 3.5 %all-to-all-start.1 = ((bf16[16,8,256]{2,1,0:T(8,128)(2,1)}), bf16[16,8,256]{2,1,0:T(8,128)(2,1)S(1)}, u32[]{:S(2)}, u32[]{:S(2)}) async-start(bf16[16,8,256]{2,1,0:T(8,128)(2,1)} %fusion.22), calls=%async_computation.1 | async-start | bytes 131072 | tf_op jit(solution)/shard_map/all_to_all | solution.py:107
  149.8 6.8 %all-to-all-done.1 = bf16[16,8,256]{2,1,0:T(8,128)(2,1)S(1)} async-done(((bf16[16,8,256]{2,1,0:T(8,128)(2,1)}), bf16[16,8,256]{2,1,0:T(8,128)(2,1)S(1)}, u32[]{:S(2)}, u32[]{:S(2)}) %all-to-all-start.1) | async-done | bytes 65568 | tf_op jit(solution)/shard_map/all_to_all | solution.py:107
  (66 shorter events, 17.8 us)
Async XLA Ops:
  7.2 1.6 copy-start
  7.2 92.9 %all-gather.3.cloned.1.call-start = ((), (), s32[]{:S(2)}) async-start(), calls=%async_computation.2 | async-start | bytes 8912896 | tf_op jit(solution)/shard_map/all_gather | solution.py:13
  15.7 5.1 %copy-start.1 = (bf16[768,1024]{0,1:T(8,128)(2,1)S(1)}, bf16[768,1024]{0,1:T(8,128)(2,1)}, u32[]{:S(2)}) copy-start(bf16[768,1024]{0,1:T(8,128)(2,1)} %copy.73) | copy-start | bytes 4718596
  19.7 1.1 copy-start.9
  20.9 1.4 copy-start.3
  20.9 2.4 %copy-start.7 = (s32[32]{0:T(128)S(1)}, s32[32]{0:T(128)}, u32[]{:S(2)}) copy-start(s32[32]{0:T(128)} %param.23) | copy-start | bytes 388
  20.9 2.8 %copy-start.8 = (s32[32]{0:T(128)S(1)}, s32[32]{0:T(128)}, u32[]{:S(2)}) copy-start(s32[32]{0:T(128)} %param.21) | copy-start | bytes 388
  120.0 3.3 %copy-start.4 = (bf16[1024,1024]{1,0:T(8,128)(2,1)S(1)}, bf16[1024,1024]{1,0:T(8,128)(2,1)}, u32[]{:S(2)}) copy-start(bf16[1024,1024]{1,0:T(8,128)(2,1)} %param.17) | copy-start | bytes 6291460
  120.1 3.4 %copy-start.5 = (bf16[768,1024]{1,0:T(8,128)(2,1)S(1)}, bf16[768,1024]{1,0:T(8,128)(2,1)}, u32[]{:S(2)}) copy-start(bf16[768,1024]{1,0:T(8,128)(2,1)} %param.13) | copy-start | bytes 4718596
  123.5 9.9 %copy-start.6 = (bf16[1024,32]{0,1:T(8,128)(2,1)S(1)}, bf16[1024,32]{0,1:T(8,128)(2,1)}, u32[]{:S(2)}) copy-start(bf16[1024,32]{0,1:T(8,128)(2,1)} %param.20) | copy-start | bytes 196612
  129.8 13.5 %all-to-all-start = ((bf16[16,8,1024]{2,1,0:T(8,128)(2,1)}), bf16[16,8,1024]{2,1,0:T(8,128)(2,1)S(1)}, u32[]{:S(2)}, u32[]{:S(2)}) async-start(bf16[16,8,1024]{2,1,0:T(8,128)(2,1)} %fusion.20), calls=%async_computation | async-start | bytes 524288 | tf_op jit(solution)/shard_map/all_to_all | solution.py:103
  133.6 9.8 %copy-start.2 = (bf16[1024,256]{1,0:T(8,128)(2,1)S(1)}, bf16[1024,256]{1,0:T(8,128)(2,1)}, u32[]{:S(2)}) copy-start(bf16[1024,256]{1,0:T(8,128)(2,1)} %param.19) | copy-start | bytes 1572868
  146.2 10.4 %all-to-all-start.1 = ((bf16[16,8,256]{2,1,0:T(8,128)(2,1)}), bf16[16,8,256]{2,1,0:T(8,128)(2,1)S(1)}, u32[]{:S(2)}, u32[]{:S(2)}) async-start(bf16[16,8,256]{2,1,0:T(8,128)(2,1)} %fusion.22), calls=%async_computation.1 | async-start | bytes 131072 | tf_op jit(solution)/shard_map/all_to_all | solution.py:107
Sparse Core Ops, SparseCore 0:
  22.4 77.5 all-gather.2
where the time goes:
time: 166 us; the launch traced here: 165 us
  waiting for transfers between devices  76.8 us (46%)
  matrix products  34.8 us (21%)
  other arithmetic  21.1 us (13%)
  between operations  14.3 us (9%)
  local copies, waits for them, and re-layouts  10.5 us (6%)
  starting transfers between devices  7.05 us (4%)
    all_gather x1, waiting for transfers between devices, carried_in(): everything = lax.all_gather(shard, axis)  61.3 us
    select_n x16, other arithmetic, step(): return jnp.where(reached, new, before)  19.6 us
    dot_general x1, matrix products, shards(): jnp.einsum('hts,shd->thd', weight, values, preferred_element_type=jnp.flo...  9.81 us
    all_to_all x1, waiting for transfers between devices, shards(): lax.all_to_all(outgoing, 'seq', split_axis=0, concat_axis=0, tiled=True)  8.76 us
    all_to_all x1, waiting for transfers between devices, shards(): lax.all_to_all(partials.astype(jnp.bfloat16), 'seq', split_axis=0, concat...  6.75 us
    dot_general x1, matrix products, shards(): jnp.dot(events, w_query, preferred_element_type=jnp.float32)  5.01 us
    dot_general x1, matrix products, shards(): jnp.dot(events, w_key, preferred_element_type=jnp.float32)  4.34 us
    dot_general x1, matrix products, shards(): jnp.dot(events, w_value, preferred_element_type=jnp.float32)  3.97 us
  transfers between devices with their start and end apart: 3, of which 3 were waited for; matrix products, arithmetic and copies ran while one was open for 11% of the time, Pallas kernels for 0%

commit v1 on v0

v1 whole, which is shorter than its diff:
```python
import functools

import jax
import jax.numpy as jnp
from jax import lax
from jax.experimental import pallas as pl
from jax.experimental.pallas import tpu as pltpu
from jax.sharding import PartitionSpec as P

HEADS = 8
EXPERTS = 16
CAP = 8
PLANE = 4
F32 = jnp.float32
BF16 = jnp.bfloat16
MIB = 1 << 20


def dot(a, b, contract=((1,), (0,)), **kw):
    return lax.dot_general(a, b, (contract, ((), ())), preferred_element_type=F32, **kw)


def call(kernel, grid, in_specs, out_specs, out_shape, flops, moved, scratch=(), vmem=56):
    return pl.pallas_call(
        kernel,
        grid=grid,
        in_specs=in_specs,
        out_specs=out_specs,
        out_shape=out_shape,
        scratch_shapes=scratch,
        compiler_params=pltpu.CompilerParams(vmem_limit_bytes=vmem * MIB),
        cost_estimate=pl.CostEstimate(flops=flops, bytes_accessed=moved, transcendentals=0),
    )


def whole(shape):
    return pl.BlockSpec(shape, lambda *_: (0,) * len(shape))


def columns(rows, cols):
    return pl.BlockSpec((rows, cols), lambda i: (0, i))


def shaped(shape, kind):
    return jax.ShapeDtypeStruct(shape, kind)


def key_value_kernel(head_dim, tile, events, w_key, w_value, keys, values, inner, state):
    k = dot(events[...], w_key[...]).astype(BF16)
    v = dot(events[...], w_value[...]).astype(BF16)
    keys[...] = k
    values[...] = v
    total = None
    for i in range(events.shape[0] // tile):
        here = slice(i * tile, (i + 1) * tile)
        if i:
            inner[i - 1] = total.astype(BF16)
        both = dot(k[here], v[here], ((0,), (0,)))
        parts = [slice(h * head_dim, (h + 1) * head_dim) for h in range(both.shape[0] // head_dim)]
        own = jnp.concatenate([both[part, part] for part in parts], axis=0)
        total = own if total is None else total + own
    state[...] = total.astype(BF16)


def key_value_state(events, w_key, w_value):
    rows, width = events.shape
    head_dim = width // HEADS
    pair = width // PLANE
    tile = row_tile(rows)
    inner = rows // tile - 1
    return call(
        functools.partial(key_value_kernel, head_dim, tile),
        (PLANE,),
        [whole((rows, width)), columns(width, pair), columns(width, pair)],
        [
            columns(rows, pair),
            columns(rows, pair),
            pl.BlockSpec((inner, pair, head_dim), lambda i: (0, i, 0)),
            pl.BlockSpec((pair, head_dim), lambda i: (i, 0)),
        ],
        [shaped((rows, width), BF16)] * 2
        + [shaped((inner, width, head_dim), BF16), shaped((width, head_dim), BF16)],
        4 * rows * width * width,
        8 * rows * width,
    )(events, w_key, w_value)


def row_tile(rows):
    return 256 if rows % 256 == 0 and rows > 256 else rows // 2


def within_kernel(head_dim, tile, copies, events, w_query, keys, values, inner, labels, experts, tasks, *outs):
    query, within, query_at, within_at, events_at, factor_at, selector, match, column = outs
    rows = events.shape[0]
    pair = w_query.shape[1]
    q = dot(events[...], w_query[...]).astype(BF16)
    query[...] = q
    spot = lax.broadcasted_iota(jnp.int32, (tile, tile), 0)
    causal = lax.broadcasted_iota(jnp.int32, (tile, tile), 1) <= spot
    for i in range(rows // tile):
        here = slice(i * tile, (i + 1) * tile)
        totals = []
        for h in range(pair // head_dim):
            part = slice(h * head_dim, (h + 1) * head_dim)
            weight = dot(q[here, part], keys[here, part], ((1,), (1,)))
            weight = jnp.where(causal, weight, 0.0).astype(BF16)
            totals.append(dot(weight, values[here, part]))
        total = jnp.concatenate(totals, axis=1)
        if i:
            total = total + dot(q[here], on_diagonal(inner[i - 1], head_dim))
        within[here, :] = total.astype(BF16)
    chosen = row_choice(labels[...], rows)
    query_at[...] = dot(chosen, q).astype(BF16)
    within_at[...] = dot(chosen, within[...]).astype(BF16)

    @pl.when(pl.program_id(0) == 0)
    def _():
        events_at[...] = dot(chosen, events[...]).astype(BF16)
        start = lax.axis_index("seq") * rows + 1
        factor_at[...] = upright(lax.rsqrt((labels[...] + start).astype(F32) * head_dim))
        places = slot_of(experts[...])
        target = slot_place(selector.shape, 0, copies)
        selector[...] = jnp.where((target == places[0]) | (target == places[1]), 1.0, 0.0).astype(BF16)
        target = slot_place((labels.shape[1], selector.shape[0]), 1, copies)
        number = lax.broadcasted_iota(jnp.int32, column.shape[1:], 1)
        for k in range(2):
            match[k] = jnp.where(target == upright(places[k]), 1.0, 0.0).astype(BF16)
            chosen_column = upright(tasks[...] * EXPERTS + experts[k : k + 1, :])
            column[k] = jnp.where(number == chosen_column, 1.0, 0.0)


def upright(row):
    many = row.shape[1]
    diagonal = lax.broadcasted_iota(jnp.int32, (many, many), 0) == lax.broadcasted_iota(jnp.int32, (many, many), 1)
    return jnp.sum(jnp.where(diagonal, row, jnp.zeros_like(row)), axis=1, keepdims=True)


def row_choice(labels, rows):
    number = lax.broadcasted_iota(jnp.int32, (labels.shape[1], rows), 1)
    return jnp.where(number == upright(labels), 1.0, 0.0).astype(BF16)


def on_diagonal(block, head_dim):
    pair = block.shape[0]
    row = lax.broadcasted_iota(jnp.int32, (pair, pair), 0) // head_dim
    col = lax.broadcasted_iota(jnp.int32, (pair, pair), 1) // head_dim
    wide = jnp.concatenate([block.astype(F32)] * (pair // head_dim), axis=1)
    return jnp.where(row == col, wide, 0.0).astype(BF16)


def slot_of(experts):
    many = experts.shape[1]
    number = lax.broadcasted_iota(jnp.int32, (EXPERTS, many), 0)
    ones = [jnp.where(number == experts[k : k + 1, :], 1.0, 0.0) for k in range(2)]
    earlier = lax.broadcasted_iota(jnp.int32, (many, many), 0) < lax.broadcasted_iota(jnp.int32, (many, many), 1)
    strict = jnp.where(earlier, 1.0, 0.0).astype(BF16)
    first = dot(ones[0].astype(BF16), strict)
    second = dot(ones[1].astype(BF16), strict) + jnp.sum(ones[0], axis=1, keepdims=True)
    slots = [jnp.sum(o * c, axis=0, keepdims=True).astype(jnp.int32) for o, c in zip(ones, (first, second))]
    return [experts[k : k + 1, :] * CAP + slots[k] for k in range(2)]


def slot_place(shape, axis, copies):
    row = lax.broadcasted_iota(jnp.int32, shape, axis)
    return row if copies == 1 else (row // (copies * CAP)) * CAP + row % CAP


def queries_within(events, w_query, keys, values, inner, labels, experts, tasks, devices):
    rows, width = events.shape
    head_dim = width // HEADS
    pair = width // PLANE
    many = labels.shape[1]
    tile = row_tile(rows)
    slots = devices * CAP
    kinds = 2 * EXPERTS
    return call(
        functools.partial(within_kernel, head_dim, tile, devices // EXPERTS),
        (width // pair,),
        [
            whole((rows, width)),
            columns(width, pair),
            columns(rows, pair),
            columns(rows, pair),
            pl.BlockSpec((inner.shape[0], pair, head_dim), lambda i: (0, i, 0)),
            whole(labels.shape),
            whole(experts.shape),
            whole(tasks.shape),
        ],
        [columns(rows, pair), columns(rows, pair), columns(many, pair), columns(many, pair), whole((many, width))]
        + [whole((many, 1)), whole((slots, many)), whole((2, many, slots)), whole((2, many, kinds))],
        [shaped((rows, width), BF16)] * 2
        + [shaped((many, width), BF16)] * 3
        + [shaped((many, 1), F32), shaped((slots, many), BF16)]
        + [shaped((2, many, slots), BF16), shaped((2, many, kinds), F32)],
        2 * rows * width * width + 4 * tile * rows * width,
        8 * rows * width,
    )(events, w_query, keys, values, inner, labels, experts, tasks)


def sums_before(state):
    devices = lax.axis_size("seq")
    planes = devices // PLANE
    plane = [[p * PLANE + r for r in range(PLANE)] for p in range(planes)]
    line = [[p * PLANE + r for p in range(planes)] for r in range(PLANE)]
    pair = state.shape[0] // PLANE

    def exchange(x, groups):
        return lax.all_to_all(x, "seq", split_axis=0, concat_axis=0, tiled=True, axis_index_groups=groups)

    states = exchange(state, plane).reshape(PLANE, pair, -1).astype(F32)
    total = jnp.sum(states, axis=0).astype(BF16)
    totals = exchange(jnp.tile(total, (planes, 1)), line).reshape(planes, pair, -1).astype(F32)
    earlier = jnp.arange(planes) < lax.axis_index("seq") // PLANE
    running = jnp.sum(jnp.where(earlier[:, None, None], totals, 0.0), axis=0)
    before = []
    for j in range(PLANE):
        before.append(running.astype(BF16))
        running = running + states[j]
    return exchange(jnp.concatenate(before, axis=0), plane)


def earlier_terms(query, prefix, head_dim):
    pair = query.shape[1] // PLANE
    terms = [dot(query[:, p * pair : (p + 1) * pair], prefix[p]) for p in range(PLANE)]
    return jnp.concatenate(terms, axis=1)


def picked_rows(query_at, within_at, events_at, factor_at, prefix, w_output):
    many, width = query_at.shape
    head_dim = width // HEADS
    by_head = prefix.reshape(HEADS, head_dim, head_dim)
    earlier = jnp.einsum("thd,hde->the", query_at.reshape(many, HEADS, head_dim), by_head, preferred_element_type=F32)
    attended = ((within_at.astype(F32) + earlier.reshape(many, width)) * factor_at).astype(BF16)
    return (events_at.astype(F32) + dot(attended, w_output)).astype(BF16)


def hidden_kernel(head_dim, events, query, within, before, w_output, hidden, prefix):
    tile = events.shape[0]
    pair = before.shape[0] // PLANE

    @pl.when(pl.program_id(0) == 0)
    def _():
        for p in range(PLANE):
            prefix[p] = on_diagonal(before[p * pair : (p + 1) * pair, :], head_dim)

    start = lax.axis_index("seq") * (tile * pl.num_programs(0)) + pl.program_id(0) * tile + 1
    place = (lax.broadcasted_iota(jnp.int32, (tile, 1), 0) + start).astype(F32)
    total = within[...].astype(F32) + earlier_terms(query[...], prefix, head_dim)
    attended = (total * lax.rsqrt(place * head_dim)).astype(BF16)
    hidden[...] = (events[...].astype(F32) + dot(attended, w_output[...])).astype(BF16)


def hidden_rows(events, query, within, prefix, w_output):
    rows, width = events.shape
    head_dim = width // HEADS
    tile = row_tile(rows)
    pair = width // PLANE
    strip = pl.BlockSpec((tile, width), lambda i: (i, 0))
    return call(
        functools.partial(hidden_kernel, head_dim),
        (rows // tile,),
        [strip, strip, strip, whole((width, head_dim)), whole((width, width))],
        strip,
        shaped((rows, width), BF16),
        2 * rows * width * width,
        10 * rows * width,
        [pltpu.VMEM((PLANE, pair, pair), BF16)],
    )(events, query, within, prefix, w_output)


def expert_rows(rows, weight_in, weight_out):
    inner = jnp.maximum(dot(rows, weight_in), 0.0).astype(BF16)
    return dot(inner, weight_out).astype(BF16)


def score_rows(picked, gate_weight, column, match, back):
    logits = dot(picked, gate_weight)
    gates = jax.nn.sigmoid(jnp.sum(logits[None] * column, axis=2))
    choices, many, slots = match.shape
    chosen = dot(match.reshape(choices * many, slots), back).reshape(choices, many, -1)
    return jnp.sum(gates[:, :, None] * chosen, axis=0)


def shards(
    events,
    w_query,
    w_key,
    w_value,
    w_output,
    expert_in,
    expert_out,
    gate_weight,
    label_rows,
    label_experts,
    label_tasks,
):
    devices = lax.axis_size("seq")
    labels = label_rows.reshape(1, -1)
    tasks = label_tasks.reshape(1, -1)
    experts = label_experts.T

    def exchange(x):
        return lax.all_to_all(x, "seq", split_axis=0, concat_axis=0, tiled=True)

    keys, values, inner, state = key_value_state(events, w_key, w_value)
    query, within, query_at, within_at, events_at, factor_at, selector, match, column = queries_within(
        events, w_query, keys, values, inner, labels, experts, tasks, devices
    )
    prefix = sums_before(state)
    picked = picked_rows(query_at, within_at, events_at, factor_at, prefix, w_output)
    arrived = exchange(dot(selector, picked).astype(BF16))
    hidden = hidden_rows(events, query, within, prefix, w_output)
    back = exchange(expert_rows(arrived, expert_in, expert_out))
    return hidden, score_rows(picked, gate_weight, column, match, back)


def solution(mesh):
    placed = (
        P(("grp", "seq"), None),
        P(),
        P(),
        P(),
        P(),
        P(None, "seq"),
        P("seq", None),
        P(),
        P(("grp", "seq")),
        P(("grp", "seq"), None),
        P(("grp", "seq")),
    )
    return jax.shard_map(
        shards,
        mesh=mesh,
        in_specs=placed,
        out_specs=(P(("grp", "seq"), None), P(("grp", "seq"), None)),
        check_vma=False,
    )
```

time: 166 us -> 82.4 us (0.50)
  waiting for transfers between devices: 76.8 us -> 18.6 us
  matrix products: 34.8 us -> 6.22 us
  Pallas kernels: 0 us -> 26.4 us
  other arithmetic: 21.1 us -> 1.93 us
  between operations: 14.3 us -> 0.77 us
  blocking collectives: 0 us -> 10.3 us
  local copies, waits for them, and re-layouts: 10.5 us -> 0.78 us
  starting transfers between devices: 7.05 us -> 16.6 us
    all_gather x1 -> x0, waiting for transfers between devices: 61.3 us -> none  [carried_in(): everything = lax.all_gather(shard, axis)]
    dot_general x10 -> x6, matrix products: 34.8 us -> 6.22 us  [the longest x5 5.16 us: dot(): lax.dot_general(a, b, (contract, ((), ())), preferred_element_type=F32, *...]
    pallas_call x0 -> x3, Pallas kernels: none -> 26.4 us  [the longest x1 12.4 us: queries_within(): call(functools.partial(within_kernel, head_dim, tile, devices // EXPERTS)...]
    select_n x18 -> x0, other arithmetic: 19.6 us -> none  [the longest x16 19.6 us: step(): return jnp.where(reached, new, before)]
    all_to_all x0 -> x1, blocking collectives: none -> 10.3 us  [exchange(): lax.all_to_all(x, 'seq', split_axis=0, concat_axis=0, tiled=True, axis_in...]
    all_to_all x2 -> x4, starting transfers between devices: 7.01 us -> 16.6 us  [the longest x2 8.86 us: exchange(): lax.all_to_all(x, 'seq', split_axis=0, concat_axis=0, tiled=True, axis_in...]
    gather x8 -> x0, local copies, waits for them, and re-layouts: 4.17 us -> none  [the longest x1 2.28 us: shards(): picked = jnp.take(hidden, label_rows, axis=0)]
    all_to_all x2 -> x4, waiting for transfers between devices: 15.5 us -> 18.6 us  [the longest x2 10.1 us: exchange(): return lax.all_to_all(x, 'seq', split_axis=0, concat_axis=0, tiled=True)]
  transfers between devices with their start and end apart: 3 -> 4, of which waited for: 3 -> 3; matrix products, arithmetic and copies ran while one was open for 11% -> 1% of each run, Pallas kernels for 0% -> 23%
where the time goes in v1:
time: 82.4 us; the launch traced here: 81.6 us
  Pallas kernels  26.4 us (32%)
  waiting for transfers between devices  18.6 us (23%)
  starting transfers between devices  16.6 us (20%)
  blocking collectives  10.3 us (12%)
  matrix products  6.22 us (8%)
  other arithmetic  1.93 us (2%)
    pallas_call x1, Pallas kernels, queries_within(): call(functools.partial(within_kernel, head_dim, tile, devices // EXPERTS)...  12.4 us
    all_to_all x1, blocking collectives, exchange(): lax.all_to_all(x, 'seq', split_axis=0, concat_axis=0, tiled=True, axis_in...  10.3 us
    all_to_all x2, waiting for transfers between devices, exchange(): return lax.all_to_all(x, 'seq', split_axis=0, concat_axis=0, tiled=True)  10.1 us
    all_to_all x2, starting transfers between devices, exchange(): lax.all_to_all(x, 'seq', split_axis=0, concat_axis=0, tiled=True, axis_in...  8.86 us
    all_to_all x2, waiting for transfers between devices, exchange(): lax.all_to_all(x, 'seq', split_axis=0, concat_axis=0, tiled=True, axis_in...  8.5 us
    all_to_all x2, starting transfers between devices, exchange(): return lax.all_to_all(x, 'seq', split_axis=0, concat_axis=0, tiled=True)  7.74 us
    pallas_call x1, Pallas kernels, key_value_state(): call(functools.partial(key_value_kernel, head_dim, tile), (PLANE,), [whol...  7.54 us
    pallas_call x1, Pallas kernels, hidden_rows(): call(functools.partial(hidden_kernel, head_dim), (rows // tile,), [strip,...  6.53 us
  transfers between devices with their start and end apart: 4, of which 3 were waited for; matrix products, arithmetic and copies ran while one was open for 1% of the time, Pallas kernels for 23%

profile of v1, /device:TPU:0, one launch (start us, length us, event | category | flops | bytes accessed | tf_op | source)
XLA Modules:
  0.0 81.6 jit_solution(7295429255449208908)
XLA Ops:
  0.6 0.0 copy-start
  0.6 7.5 %shard_map.122 = (bf16[768,1024]{1,0:T(8,128)(2,1)}, bf16[768,1024]{1,0:T(8,128)(2,1)}, bf16[2,1024,128]{2,1,0:T(8,128)(2,1)}, bf16[1024,128]{1,0:T(8,128)(2,1)}) custom-call(bf16[768,1024]{1,0:T(8,128)(2,1)} %events.5, bf16[1024,1024]{1,0:T(8,128)(2,1)} %w_key.1, bf16[1024,1024]{1,0:T(8,128)(2,1)} %w_value.1), custom_call_target="tpu_custom_call" | custom-call | flops 3221225472 | bytes 6291456 | tf_op jit(solution)/shard_map/pallas_call | solution.py:71
  8.2 10.3 %all_to_all.50 = bf16[4,256,128]{2,1,0:T(8,128)(2,1)S(1)} all-to-all(bf16[4,256,128]{2,1,0:T(8,128)(2,1)} %bitcast.74), channel_id=1, replica_groups={{0,1,2,3},{4,5,6,7},{8,9,10,11},{12,13,14,15},{16,17,18,19},{20,21,22,2..., dimensions={0} | all-to-all | bytes 524288 | tf_op jit(solution)/shard_map/all_to_all | solution.py:208
  18.5 0.7 tile.2
  19.2 5.5 %all-to-all-start.1 = ((bf16[4,256,128]{2,1,0:T(8,128)(2,1)}), bf16[4,256,128]{2,1,0:T(8,128)(2,1)S(1)}, u32[]{:S(2)}, u32[]{:S(2)}) async-start(bf16[4,256,128]{2,1,0:T(8,128)(2,1)} %tile.2), calls=%async_computation.1 | async-start | bytes 524288 | tf_op jit(solution)/shard_map/all_to_all | solution.py:208
  24.7 8.5 %all-to-all-done.1 = bf16[4,256,128]{2,1,0:T(8,128)(2,1)S(1)} async-done(((bf16[4,256,128]{2,1,0:T(8,128)(2,1)}), bf16[4,256,128]{2,1,0:T(8,128)(2,1)S(1)}, u32[]{:S(2)}, u32[]{:S(2)}) %all-to-all-start.1) | async-done | bytes 262176 | tf_op jit(solution)/shard_map/all_to_all | solution.py:208
  33.2 0.1 select_reduce_fusion
  33.4 0.7 pad_maximum_fusion
  34.1 3.4 %all-to-all-start.2 = ((bf16[4,256,128]{2,1,0:T(8,128)(2,1)}), bf16[4,256,128]{2,1,0:T(8,128)(2,1)S(1)}, u32[]{:S(2)}, u32[]{:S(2)}) async-start(bf16[4,256,128]{2,1,0:T(8,128)(2,1)} %bitcast.7), calls=%async_computation.2 | async-start | bytes 524288 | tf_op jit(solution)/shard_map/all_to_all | solution.py:208
  37.5 12.4 %shard_map.123 = (bf16[768,1024]{1,0:T(8,128)(2,1)}, bf16[768,1024]{1,0:T(8,128)(2,1)}, bf16[32,1024]{1,0:T(8,128)(2,1)}, bf16[32,1024]{1,0:T(8,128)(2,1)}, bf16...) custom-call(bf16[768,1024]{1,0:T(8,128)(2,1)} %events.5, ...), custom_call_target="tpu_custom_call" | custom-call | flops 2415919104 | bytes 6291456 | tf_op jit(solution)/shard_map/pallas_call | solution.py:176
  49.9 0.0 copy-start.2
  49.9 0.9 %reduce.2 = f32[32]{0:T(128)S(1)} reduce(f32[32,1]{1,0:T(8,128)} %get-tuple-element.24, f32[]{:T(128)} %constant.27), dimensions={1}, to_apply=%get-tuple-element.24.reduce_sub_computation | reduce | bytes 260 | tf_op jit(solution)/shard_map/pallas_call | solution.py:176
  50.8 1.1 %convolution_bitcast_fusion = f32[8,4,8,128]{3,2,1,0:T(8,128)S(1)} fusion(bf16[8,128,128]{2,1,0:T(8,128)(2,1)S(1)} %bitcast.72, bf16[32,1024]{1,0:T(8,128)(2,1)} %get-tuple-element.23), kind=kOutput, calls=%fused_computation.5 | convolution fusion | flops 8388608 | bytes 458752 | tf_op jit(solution)/shard_map/thd,hde->the/dot_general | solution.py:232
  51.9 2.1 %fusion.3 = bf16[32,1024]{1,0:T(8,128)(2,1)S(1)} fusion(bf16[1024,1024]{1,0:T(8,128)(2,1)} %w_output.1, bf16[32,1024]{1,0:T(8,128)(2,1)} %get-tuple-element.21, f32[8,4,8,128]{3,2,1,0:T(8,128)S(1)} %convolution_bitcast_fusion, bf16[32,1024]{1,0:T(8,128)(2,1)} %get-tuple-element.22, f32[32]{0:T(128)S(1)} %reduce.2), kind=kOutput, calls=%fused_computation.7 | convolution fusion | flops 67338240 | bytes 2424960 | tf_op jit(solution)/shard_map/dot_general | solution.py:20
  54.0 0.9 %fusion.2 = bf16[16,8,1024]{2,1,0:T(8,128)(2,1)} fusion(bf16[128,32]{1,0:T(8,128)(2,1)S(1)} %copy-done.5, bf16[32,1024]{1,0:T(8,128)(2,1)S(1)} %fusion.3), kind=kOutput, calls=%fused_computation.4 | convolution fusion | flops 8519680 | bytes 335872 | tf_op jit(solution)/shard_map/dot_general | solution.py:20
  54.9 4.2 %all-to-all-start.3 = ((bf16[16,8,1024]{2,1,0:T(8,128)(2,1)}), bf16[16,8,1024]{2,1,0:T(8,128)(2,1)S(1)}, u32[]{:S(2)}, u32[]{:S(2)}) async-start(bf16[16,8,1024]{2,1,0:T(8,128)(2,1)} %fusion.2), calls=%async_computation.3 | async-start | bytes 524288 | tf_op jit(solution)/shard_map/all_to_all | solution.py:303
  59.2 0.1 fusion.25
  59.3 0.1 multiply_reduce_fusion
  59.4 9.8 %all-to-all-done.3 = bf16[16,8,1024]{2,1,0:T(8,128)(2,1)S(1)} async-done(((bf16[16,8,1024]{2,1,0:T(8,128)(2,1)}), bf16[16,8,1024]{2,1,0:T(8,128)(2,1)S(1)}, u32[]{:S(2)}, u32[]{:S(2)}) %all-to-all-start.3) | async-done | bytes 262176 | tf_op jit(solution)/shard_map/all_to_all | solution.py:303
  69.2 1.3 %fusion.5 = bf16[16,8,256]{2,1,0:T(8,128)(2,1)} fusion(bf16[1024,256]{1,0:T(8,128)(2,1)S(1)} %copy-done.2, bf16[1024,1024]{1,0:T(8,128)(2,1)S(1)} %copy-done, bf16[16,8,1024]{2,1,0:T(8,128)(2,1)S(1)} %all-to-all-done.3), kind=kOutput, calls=%fused_computation.9 | convolution fusion | flops 335839232 | bytes 2949120 | tf_op jit(solution)/shard_map/dot_general | solution.py:20
  70.5 3.5 %all-to-all-start.4 = ((bf16[16,8,256]{2,1,0:T(8,128)(2,1)}), bf16[16,8,256]{2,1,0:T(8,128)(2,1)S(1)}, u32[]{:S(2)}, u32[]{:S(2)}) async-start(bf16[16,8,256]{2,1,0:T(8,128)(2,1)} %fusion.5), calls=%async_computation.4 | async-start | bytes 131072 | tf_op jit(solution)/shard_map/all_to_all | solution.py:303
  74.0 6.5 %shard_map.124 = bf16[768,1024]{1,0:T(8,128)(2,1)} custom-call(bf16[768,1024]{1,0:T(8,128)(2,1)} %events.5, bf16[768,1024]{1,0:T(8,128)(2,1)} %get-tuple-element.18.query, bf16[768,1024]{1,0:T(8,128)(2,1)} %get-tuple-element.19.within, bf16[1024,128]{1,0:T(8,128)(2,1)} %bitcast.73, bf16[1024,1024]{1,0:T(8,128)(2,1)} %w_output.1), custom_call_target="tpu_custom_call" | custom-call | flops 1610612736 | bytes 7864320 | tf_op jit(solution)/shard_map/pallas_call | solution.py:259
  80.5 0.3 all-to-all-done.4
  80.9 0.8 fusion.6
  (17 shorter events, 0.1 us)
Async XLA Ops:
  0.6 68.6 %copy-start = (bf16[1024,1024]{1,0:T(8,128)(2,1)S(1)}, bf16[1024,1024]{1,0:T(8,128)(2,1)}, u32[]{:S(2)}) copy-start(bf16[1024,1024]{1,0:T(8,128)(2,1)} %param.16) | copy-start | bytes 6291460
  19.2 14.0 %all-to-all-start.1 = ((bf16[4,256,128]{2,1,0:T(8,128)(2,1)}), bf16[4,256,128]{2,1,0:T(8,128)(2,1)S(1)}, u32[]{:S(2)}, u32[]{:S(2)}) async-start(bf16[4,256,128]{2,1,0:T(8,128)(2,1)} %tile.2), calls=%async_computation.1 | async-start | bytes 524288 | tf_op jit(solution)/shard_map/all_to_all | solution.py:208
  34.1 16.7 %all-to-all-start.2 = ((bf16[4,256,128]{2,1,0:T(8,128)(2,1)}), bf16[4,256,128]{2,1,0:T(8,128)(2,1)S(1)}, u32[]{:S(2)}, u32[]{:S(2)}) async-start(bf16[4,256,128]{2,1,0:T(8,128)(2,1)} %bitcast.7), calls=%async_computation.2 | async-start | bytes 524288 | tf_op jit(solution)/shard_map/all_to_all | solution.py:208
  49.9 4.1 %copy-start.5 = (bf16[128,32]{1,0:T(8,128)(2,1)S(1)}, bf16[128,32]{1,0:T(8,128)(2,1)}, u32[]{:S(2)}) copy-start(bf16[128,32]{1,0:T(8,128)(2,1)} %get-tuple-element.27) | copy-start | bytes 24580
  49.9 9.3 %copy-start.3 = (bf16[1024,32]{0,1:T(8,128)(2,1)S(1)}, bf16[1024,32]{0,1:T(8,128)(2,1)}, u32[]{:S(2)}) copy-start(bf16[1024,32]{0,1:T(8,128)(2,1)} %param.18) | copy-start | bytes 196612
  49.9 9.4 %copy-start.4 = (f32[2,32,32]{2,1,0:T(8,128)S(1)}, f32[2,32,32]{2,1,0:T(8,128)}, u32[]{:S(2)}) copy-start(f32[2,32,32]{2,1,0:T(8,128)} %get-tuple-element.25) | copy-start | bytes 24580
  49.9 19.3 %copy-start.2 = (bf16[1024,256]{1,0:T(8,128)(2,1)S(1)}, bf16[1024,256]{1,0:T(8,128)(2,1)}, u32[]{:S(2)}) copy-start(bf16[1024,256]{1,0:T(8,128)(2,1)} %param.17) | copy-start | bytes 1572868
  50.8 19.7 %copy-start.1 = (bf16[4,256,128]{2,1,0:T(8,128)(2,1)}, bf16[4,256,128]{2,1,0:T(8,128)(2,1)S(1)}, u32[]{:S(2)}) copy-start(bf16[4,256,128]{2,1,0:T(8,128)(2,1)S(1)} %all-to-all-done.2) | copy-start | bytes 786436
  54.9 14.3 %all-to-all-start.3 = ((bf16[16,8,1024]{2,1,0:T(8,128)(2,1)}), bf16[16,8,1024]{2,1,0:T(8,128)(2,1)S(1)}, u32[]{:S(2)}, u32[]{:S(2)}) async-start(bf16[16,8,1024]{2,1,0:T(8,128)(2,1)} %fusion.2), calls=%async_computation.3 | async-start | bytes 524288 | tf_op jit(solution)/shard_map/all_to_all | solution.py:303
  70.5 10.4 %all-to-all-start.4 = ((bf16[16,8,256]{2,1,0:T(8,128)(2,1)}), bf16[16,8,256]{2,1,0:T(8,128)(2,1)S(1)}, u32[]{:S(2)}, u32[]{:S(2)}) async-start(bf16[16,8,256]{2,1,0:T(8,128)(2,1)} %fusion.5), calls=%async_computation.4 | async-start | bytes 131072 | tf_op jit(solution)/shard_map/all_to_all | solution.py:303
  74.0 6.9 %copy-start.6 = (bf16[2,32,128]{2,1,0:T(8,128)(2,1)S(1)}, bf16[2,32,128]{2,1,0:T(8,128)(2,1)}, u32[]{:S(2)}) copy-start(bf16[2,32,128]{2,1,0:T(8,128)(2,1)} %get-tuple-element.26) | copy-start | bytes 49156

commit v2 on v1

v2 whole, which is shorter than its diff:
```python
import functools

import jax
import jax.numpy as jnp
from jax import lax
from jax.experimental import pallas as pl
from jax.experimental.pallas import tpu as pltpu
from jax.sharding import PartitionSpec as P

HEADS = 8
EXPERTS = 16
CAP = 8
PLANE = 4
GROUP = 8
FAR = 1024
F32 = jnp.float32
BF16 = jnp.bfloat16
MIB = 1 << 20


def dot(a, b, contract=((1,), (0,)), **kw):
    return lax.dot_general(a, b, (contract, ((), ())), preferred_element_type=F32, **kw)


def call(kernel, grid, in_specs, out_specs, out_shape, flops, moved, scratch=(), vmem=56):
    return pl.pallas_call(
        kernel,
        grid=grid,
        in_specs=in_specs,
        out_specs=out_specs,
        out_shape=out_shape,
        scratch_shapes=scratch,
        compiler_params=pltpu.CompilerParams(vmem_limit_bytes=vmem * MIB),
        cost_estimate=pl.CostEstimate(flops=flops, bytes_accessed=moved, transcendentals=0),
    )


def whole(shape):
    return pl.BlockSpec(shape, lambda *_: (0,) * len(shape))


def columns(rows, cols):
    return pl.BlockSpec((rows, cols), lambda i: (0, i))


def shaped(shape, kind):
    return jax.ShapeDtypeStruct(shape, kind)


def key_value_kernel(head_dim, tile, events, w_key, w_value, w_query, labels, experts, *outs):
    keys, values, inner, message, query_at, events_at = outs
    rows = events.shape[0]
    many = labels.shape[1]
    k = dot(events[...], w_key[...]).astype(BF16)
    v = dot(events[...], w_value[...]).astype(BF16)
    keys[...] = k
    values[...] = v

    @pl.when(pl.program_id(0) == 0)
    def _():
        events_at[...] = dot(row_choice(labels[...], rows), events[...]).astype(BF16)

    query = dot(events_at[...], w_query[...])
    query_at[...] = query.astype(BF16)
    scaled = (query * factor_at(labels[...], rows, head_dim)).astype(BF16)
    total = None
    for i in range(rows // tile):
        here = slice(i * tile, (i + 1) * tile)
        if i:
            inner[i - 1] = total.astype(BF16)
        both = dot(v[here], k[here], ((0,), (0,)))
        parts = [slice(h * head_dim, (h + 1) * head_dim) for h in range(both.shape[0] // head_dim)]
        own = jnp.concatenate([both[part, part] for part in parts], axis=0)
        total = own if total is None else total + own
    state = total.astype(BF16)
    cut = state.shape[0] // message.shape[0]
    places = slot_rows(experts[...], message.shape[1] - cut - many, message.shape[2])
    for j in range(message.shape[0]):
        head = j * cut // head_dim
        message[j, :cut] = state[j * cut : (j + 1) * cut]
        message[j, cut : cut + many] = scaled[:, head * head_dim : (head + 1) * head_dim]
        message[j, cut + many :] = places


def slot_rows(experts, rows, lanes):
    places = [p.astype(F32) for p in slot_of(experts)]
    many = experts.shape[1]
    number = lax.broadcasted_iota(jnp.int32, (rows, many), 0)
    both = jnp.where(number == 0, places[0], jnp.where(number == 1, places[1], 0.0))
    return jnp.concatenate([both, jnp.zeros((rows, lanes - many), F32)], axis=1).astype(BF16)


def factor_at(labels, rows, head_dim):
    start = lax.axis_index("seq") * rows + 1
    return upright(lax.rsqrt((labels + start).astype(F32) * head_dim))


def key_value_state(events, w_key, w_value, w_query, labels, experts, devices):
    rows, width = events.shape
    head_dim = width // HEADS
    pair = width // PLANE
    many = labels.shape[1]
    tile = row_tile(rows)
    inner = rows // tile - 1
    length = width // devices + many + 16
    return call(
        functools.partial(key_value_kernel, head_dim, tile),
        (PLANE,),
        [whole((rows, width))] + [columns(width, pair)] * 3 + [whole(labels.shape), whole(experts.shape)],
        [
            columns(rows, pair),
            columns(rows, pair),
            pl.BlockSpec((inner, pair, head_dim), lambda i: (0, i, 0)),
            pl.BlockSpec((devices // PLANE, length, head_dim), lambda i: (i, 0, 0)),
            columns(many, pair),
            whole((many, width)),
        ],
        [shaped((rows, width), BF16)] * 2
        + [shaped((inner, width, head_dim), BF16), shaped((devices, length, head_dim), BF16)]
        + [shaped((many, width), BF16)] * 2,
        4 * rows * width * width,
        8 * rows * width,
    )(events, w_key, w_value, w_query, labels, experts)


def base_kernel(head_dim, copies, rows, query_at, events_at, keys, values, w_output, labels, experts, outgoing, total):
    step = pl.program_id(0)
    many = labels.shape[1]

    @pl.when(step == 0)
    def _():
        total[...] = events_at[...].astype(F32)

    causal = lax.broadcasted_iota(jnp.int32, (many, rows), 1) <= upright(labels[...])
    parts = []
    for h in range(keys.shape[1] // head_dim):
        part = slice(h * head_dim, (h + 1) * head_dim)
        weight = dot(query_at[:, part], keys[:, part], ((1,), (1,)))
        parts.append(dot(jnp.where(causal, weight, 0.0).astype(BF16), values[:, part]))
    within = (jnp.concatenate(parts, axis=1) * factor_at(labels[...], rows, head_dim)).astype(BF16)
    total[...] += dot(within, w_output[...])

    @pl.when(step == pl.num_programs(0) - 1)
    def _():
        places = slot_of(experts[...])
        target = slot_place((outgoing.shape[0], many), 0, copies)
        selector = jnp.where((target == places[0]) | (target == places[1]), 1.0, 0.0).astype(BF16)
        outgoing[...] = dot(selector, total[...].astype(BF16)).astype(BF16)


def base_rows(query_at, events_at, keys, values, w_output, labels, experts, devices):
    rows, width = keys.shape
    many = labels.shape[1]
    pair = width // PLANE
    return call(
        functools.partial(base_kernel, width // HEADS, devices // EXPERTS, rows),
        (PLANE,),
        [
            columns(many, pair),
            whole((many, width)),
            columns(rows, pair),
            columns(rows, pair),
            pl.BlockSpec((pair, width), lambda i: (i, 0)),
            whole(labels.shape),
            whole(experts.shape),
        ],
        whole((devices * CAP, width)),
        shaped((devices * CAP, width), BF16),
        4 * many * rows * width,
        6 * rows * width,
        [pltpu.VMEM((many, width), F32)],
    )(query_at, events_at, keys, values, w_output, labels, experts)


def slice_kernel(copies, cut, many, arrived, outgoing, before):
    devices, _, lanes = arrived.shape
    spread = lanes // cut
    total = jnp.zeros((cut, lanes), F32)
    terms, places = [], []
    for b in range(devices):
        sums = total.astype(BF16)
        before[b] = sums
        total = total + arrived[b, :cut].astype(F32)
        low = b // GROUP * cut
        pieces = [sums]
        if low:
            pieces = [jnp.zeros((low, lanes), BF16)] + pieces
        if lanes - low - cut:
            pieces = pieces + [jnp.zeros((lanes - low - cut, lanes), BF16)]
        placed = jnp.concatenate(pieces, axis=0) if len(pieces) > 1 else sums
        terms.append(dot(arrived[b, cut : cut + many], placed, ((1,), (1,))).astype(BF16))
        offset = b % 2 * FAR
        places.append(arrived[b, cut + many :].astype(F32)[:2, :many] + offset)
    rows = devices * 2 * CAP
    row = lax.broadcasted_iota(jnp.int32, (rows, 1), 0)
    target = row // (2 * CAP * copies) * CAP + row % CAP + row // CAP % 2 * FAR
    target = target.astype(F32)
    for q in range(GROUP // 2):
        blocks = [g * GROUP + q * 2 + i for g in range(spread) for i in range(2)]
        place = jnp.concatenate([places[b] for b in blocks], axis=1)
        selector = jnp.where((target == place[0:1]) | (target == place[1:2]), 1.0, 0.0).astype(BF16)
        chosen = dot(selector, jnp.concatenate([terms[b] for b in blocks], axis=0)).astype(BF16)
        outgoing[:, q * 2 * CAP : (q + 1) * 2 * CAP, :] = chosen.reshape(devices, 2 * CAP, lanes)


def slice_terms(arrived, cut, many):
    devices, _, lanes = arrived.shape
    return small(
        functools.partial(slice_kernel, devices // EXPERTS, cut, many),
        [shaped((devices, GROUP * CAP, lanes), BF16), shaped((devices, cut, lanes), BF16)],
        arrived,
    )


def small(kernel, out_shape, *operands):
    vmem = pl.BlockSpec(memory_space=pltpu.VMEM)
    return pl.pallas_call(
        kernel,
        in_specs=[vmem] * len(operands),
        out_specs=jax.tree.map(lambda _: vmem, out_shape),
        out_shape=out_shape,
        cost_estimate=pl.CostEstimate(flops=1 << 22, bytes_accessed=1 << 20, transcendentals=0),
    )(*operands)


def columns_joined(arrived):
    devices, rows, lanes = arrived.shape
    spread = devices // HEADS
    parts = arrived.reshape(HEADS, spread, rows, spread, lanes // spread)
    return parts.transpose(3, 2, 0, 1, 4).reshape(spread * rows, HEADS * lanes)


def row_tile(rows):
    return 256 if rows % 256 == 0 and rows > 256 else rows // 2


def within_kernel(head_dim, tile, copies, events, w_query, keys, values, inner, experts, tasks, *outs):
    query, within, match, column = outs
    rows = events.shape[0]
    pair = w_query.shape[1]
    q = dot(events[...], w_query[...]).astype(BF16)
    query[...] = q
    spot = lax.broadcasted_iota(jnp.int32, (tile, tile), 0)
    causal = lax.broadcasted_iota(jnp.int32, (tile, tile), 1) <= spot
    for i in range(rows // tile):
        here = slice(i * tile, (i + 1) * tile)
        totals = []
        for h in range(pair // head_dim):
            part = slice(h * head_dim, (h + 1) * head_dim)
            weight = dot(q[here, part], keys[here, part], ((1,), (1,)))
            weight = jnp.where(causal, weight, 0.0).astype(BF16)
            totals.append(dot(weight, values[here, part]))
        total = jnp.concatenate(totals, axis=1)
        if i:
            total = total + dot(q[here], on_diagonal(inner[i - 1], head_dim), ((1,), (1,)))
        within[here, :] = total.astype(BF16)

    @pl.when(pl.program_id(0) == 0)
    def _():
        places = slot_of(experts[...])
        target = slot_place(match.shape[1:], 1, copies)
        number = lax.broadcasted_iota(jnp.int32, column.shape[1:], 1)
        for k in range(2):
            match[k] = jnp.where(target == upright(places[k]), 1.0, 0.0).astype(BF16)
            chosen_column = upright(tasks[...] * EXPERTS + experts[k : k + 1, :])
            column[k] = jnp.where(number == chosen_column, 1.0, 0.0)


def upright(row):
    many = row.shape[1]
    diagonal = lax.broadcasted_iota(jnp.int32, (many, many), 0) == lax.broadcasted_iota(jnp.int32, (many, many), 1)
    return jnp.sum(jnp.where(diagonal, row, jnp.zeros_like(row)), axis=1, keepdims=True)


def row_choice(labels, rows):
    number = lax.broadcasted_iota(jnp.int32, (labels.shape[1], rows), 1)
    return jnp.where(number == upright(labels), 1.0, 0.0).astype(BF16)


def on_diagonal(block, head_dim):
    pair = block.shape[0]
    row = lax.broadcasted_iota(jnp.int32, (pair, pair), 0) // head_dim
    col = lax.broadcasted_iota(jnp.int32, (pair, pair), 1) // head_dim
    wide = jnp.concatenate([block.astype(F32)] * (pair // head_dim), axis=1)
    return jnp.where(row == col, wide, 0.0).astype(BF16)


def slot_of(experts):
    many = experts.shape[1]
    number = lax.broadcasted_iota(jnp.int32, (EXPERTS, many), 0)
    ones = [jnp.where(number == experts[k : k + 1, :], 1.0, 0.0) for k in range(2)]
    earlier = lax.broadcasted_iota(jnp.int32, (many, many), 0) < lax.broadcasted_iota(jnp.int32, (many, many), 1)
    strict = jnp.where(earlier, 1.0, 0.0).astype(BF16)
    first = dot(ones[0].astype(BF16), strict)
    second = dot(ones[1].astype(BF16), strict) + jnp.sum(ones[0], axis=1, keepdims=True)
    slots = [jnp.sum(o * c, axis=0, keepdims=True).astype(jnp.int32) for o, c in zip(ones, (first, second))]
    return [experts[k : k + 1, :] * CAP + slots[k] for k in range(2)]


def slot_place(shape, axis, copies):
    row = lax.broadcasted_iota(jnp.int32, shape, axis)
    return row if copies == 1 else (row // (copies * CAP)) * CAP + row % CAP


def queries_within(events, w_query, keys, values, inner, experts, tasks, devices):
    rows, width = events.shape
    head_dim = width // HEADS
    pair = width // PLANE
    many = experts.shape[1]
    tile = row_tile(rows)
    slots = devices * CAP
    kinds = 2 * EXPERTS
    return call(
        functools.partial(within_kernel, head_dim, tile, devices // EXPERTS),
        (width // pair,),
        [
            whole((rows, width)),
            columns(width, pair),
            columns(rows, pair),
            columns(rows, pair),
            pl.BlockSpec((inner.shape[0], pair, head_dim), lambda i: (0, i, 0)),
            whole(experts.shape),
            whole(tasks.shape),
        ],
        [columns(rows, pair), columns(rows, pair), whole((2, many, slots)), whole((2, many, kinds))],
        [shaped((rows, width), BF16)] * 2
        + [shaped((2, many, slots), BF16), shaped((2, many, kinds), F32)],
        2 * rows * width * width + 4 * tile * rows * width,
        8 * rows * width,
    )(events, w_query, keys, values, inner, experts, tasks)


def hidden_kernel(head_dim, events, query, within, before, w_output, labels, hidden, picked, prefix):
    tile = events.shape[0]
    step = pl.program_id(0)
    pair = before.shape[0] // PLANE

    @pl.when(step == 0)
    def _():
        picked[...] = jnp.zeros_like(picked)
        for p in range(PLANE):
            prefix[p] = on_diagonal(before[p * pair : (p + 1) * pair, :], head_dim)

    start = lax.axis_index("seq") * (tile * pl.num_programs(0)) + step * tile + 1
    place = (lax.broadcasted_iota(jnp.int32, (tile, 1), 0) + start).astype(F32)
    cols = [slice(p * pair, (p + 1) * pair) for p in range(PLANE)]
    earlier = jnp.concatenate([dot(query[:, c], prefix[p], ((1,), (1,))) for p, c in enumerate(cols)], axis=1)
    attended = ((within[...].astype(F32) + earlier) * lax.rsqrt(place * head_dim)).astype(BF16)
    rows = (events[...].astype(F32) + dot(attended, w_output[...])).astype(BF16)
    hidden[...] = rows
    picked[...] += dot(row_choice(labels[...] - step * tile, tile), rows).astype(BF16)


def hidden_rows(events, query, within, before, w_output, labels):
    rows, width = events.shape
    many = labels.shape[1]
    head_dim = width // HEADS
    tile = row_tile(rows)
    pair = width // PLANE
    strip = pl.BlockSpec((tile, width), lambda i: (i, 0))
    return call(
        functools.partial(hidden_kernel, head_dim),
        (rows // tile,),
        [strip, strip, strip, whole((width, head_dim)), whole((width, width)), whole(labels.shape)],
        [strip, whole((many, width))],
        [shaped((rows, width), BF16), shaped((many, width), BF16)],
        2 * rows * width * width,
        10 * rows * width,
        [pltpu.VMEM((PLANE, pair, pair), BF16)],
    )(events, query, within, before, w_output, labels)


def expert_rows(rows, weight_in, weight_out):
    inner = jnp.maximum(dot(rows, weight_in), 0.0).astype(BF16)
    return dot(inner, weight_out).astype(BF16)


def score_rows(picked, gate_weight, column, match, back):
    logits = dot(picked, gate_weight)
    gates = jax.nn.sigmoid(jnp.sum(logits[None] * column, axis=2))
    choices, many, slots = match.shape
    chosen = dot(match.reshape(choices * many, slots), back).reshape(choices, many, -1)
    return jnp.sum(gates[:, :, None] * chosen, axis=0)


def shards(
    events,
    w_query,
    w_key,
    w_value,
    w_output,
    expert_in,
    expert_out,
    gate_weight,
    label_rows,
    label_experts,
    label_tasks,
):
    devices = lax.axis_size("seq")
    width = events.shape[1]
    labels = label_rows.reshape(1, -1)
    tasks = label_tasks.reshape(1, -1)
    experts = label_experts.T
    many = labels.shape[1]
    cut = width // devices

    def exchange(x):
        flat = x.reshape(-1, x.shape[-1])
        return lax.all_to_all(flat, "seq", split_axis=0, concat_axis=0, tiled=True).reshape(x.shape)

    keys, values, inner, message, query_at, events_at = key_value_state(
        events, w_key, w_value, w_query, labels, experts, devices
    )
    slices = exchange(message)
    base = base_rows(query_at, events_at, keys, values, w_output, labels, experts, devices)
    slices, base = lax.optimization_barrier((slices, base))
    base = exchange(base)
    terms, before = slice_terms(slices, cut, many)
    keys, values, terms, before = lax.optimization_barrier((keys, values, terms, before))
    terms = exchange(terms)
    before = exchange(before).reshape(width, -1)
    query, within, match, column = queries_within(events, w_query, keys, values, inner, experts, tasks, devices)
    rows = (base.astype(F32) + dot(columns_joined(terms), w_output)).astype(BF16)
    back = exchange(expert_rows(rows, expert_in, expert_out))
    hidden, picked = hidden_rows(events, query, within, before, w_output, labels)
    return hidden, score_rows(picked, gate_weight, column, match, back)


def solution(mesh):
    placed = (
        P(("grp", "seq"), None),
        P(),
        P(),
        P(),
        P(),
        P(None, "seq"),
        P("seq", None),
        P(),
        P(("grp", "seq")),
        P(("grp", "seq"), None),
        P(("grp", "seq")),
    )
    return jax.shard_map(
        shards,
        mesh=mesh,
        in_specs=placed,
        out_specs=(P(("grp", "seq"), None), P(("grp", "seq"), None)),
        check_vma=False,
    )
```

time: 82.4 us -> 92.3 us (1.12)
  Pallas kernels: 26.4 us -> 35.1 us
  waiting for transfers between devices: 18.6 us -> 13.1 us
  starting transfers between devices: 16.6 us -> 20.4 us
  blocking collectives: 10.3 us -> 13.9 us
  other arithmetic: 1.93 us -> 0.11 us
  local copies, waits for them, and re-layouts: 0.78 us -> 1.92 us
    pallas_call x0 -> x2, Pallas kernels: none -> 8.06 us  [the longest x1 5.86 us: base_rows(): call(functools.partial(base_kernel, width // HEADS, devices // EXPERTS, r...]
    all_to_all x4, waiting for transfers between devices: 18.6 us -> 13.1 us  [exchange(): lax.all_to_all(flat, 'seq', split_axis=0, concat_axis=0, tiled=True)]
    all_to_all x4, starting transfers between devices: 16.6 us -> 20.4 us  [exchange(): lax.all_to_all(flat, 'seq', split_axis=0, concat_axis=0, tiled=True)]
    all_to_all x1, blocking collectives: 10.3 us -> 13.9 us  [exchange(): lax.all_to_all(flat, 'seq', split_axis=0, concat_axis=0, tiled=True)]
    pallas_call x1, Pallas kernels: 7.54 us -> 9.02 us  [key_value_state(): call(functools.partial(key_value_kernel, head_dim, tile), (PLANE,), [whol...]
    dot_general x1 -> x0, matrix products: 1.06 us -> none  [picked_rows(): jnp.einsum('thd,hde->the', query_at.reshape(many, HEADS, head_dim), by_he...]
    dot_general x5 -> x4, matrix products: 5.16 us -> 6.08 us  [dot(): lax.dot_general(a, b, (contract, ((), ())), preferred_element_type=F32, *...]
  transfers between devices with their start and end apart: 4 -> 4, of which waited for: 3 -> 2; matrix products, arithmetic and copies ran while one was open for 1% -> 7% of each run, Pallas kernels for 23% -> 26%
where the time goes in v2:
time: 92.3 us; the launch traced here: 91.4 us
  Pallas kernels  35.1 us (38%)
  starting transfers between devices  20.4 us (22%)
  blocking collectives  13.9 us (15%)
  waiting for transfers between devices  13.1 us (14%)
  matrix products  6.08 us (7%)
  local copies, waits for them, and re-layouts  1.92 us (2%)
    all_to_all x4, starting transfers between devices, exchange(): lax.all_to_all(flat, 'seq', split_axis=0, concat_axis=0, tiled=True)  20.4 us
    all_to_all x1, blocking collectives, exchange(): lax.all_to_all(flat, 'seq', split_axis=0, concat_axis=0, tiled=True)  13.9 us
    all_to_all x4, waiting for transfers between devices, exchange(): lax.all_to_all(flat, 'seq', split_axis=0, concat_axis=0, tiled=True)  13.1 us
    pallas_call x1, Pallas kernels, queries_within(): call(functools.partial(within_kernel, head_dim, tile, devices // EXPERTS)...  11.5 us
    pallas_call x1, Pallas kernels, key_value_state(): call(functools.partial(key_value_kernel, head_dim, tile), (PLANE,), [whol...  9.02 us
    pallas_call x1, Pallas kernels, hidden_rows(): call(functools.partial(hidden_kernel, head_dim), (rows // tile,), [strip,...  6.49 us
    dot_general x4, matrix products, dot(): lax.dot_general(a, b, (contract, ((), ())), preferred_element_type=F32, *...  6.08 us
    pallas_call x1, Pallas kernels, base_rows(): call(functools.partial(base_kernel, width // HEADS, devices // EXPERTS, r...  5.86 us
  transfers between devices with their start and end apart: 4, of which 2 were waited for; matrix products, arithmetic and copies ran while one was open for 7% of the time, Pallas kernels for 26%

profile of v2, /device:TPU:0, one launch (start us, length us, event | category | flops | bytes accessed | tf_op | source)
XLA Modules:
  0.0 91.4 jit_solution(4464111746857312669)
XLA Ops:
  0.6 0.0 copy-start
  0.6 9.0 %shard_map.122 = (bf16[768,1024]{1,0:T(8,128)(2,1)}, bf16[768,1024]{1,0:T(8,128)(2,1)}, bf16[2,1024,128]{2,1,0:T(8,128)(2,1)}, bf16[16,112,128]{2,1,0:T(8,128)(2...) custom-call(bf16[768,1024]{1,0:T(8,128)(2,1)} %events.5, bf16[1024,1024]{1,0:T(8,128)(2,1)} %w_key.1, ...), custom_call_target="tpu_custom_call" | custom-call | flops 3221225472 | bytes 6291456 | tf_op jit(solution)/shard_map/pallas_call | solution.py:106
  9.7 7.4 %all-to-all-start = ((bf16[16,112,128]{2,1,0:T(8,128)(2,1)}), bf16[16,112,128]{2,1,0:T(8,128)(2,1)S(1)}, u32[]{:S(2)}, u32[]{:S(2)}) async-start(bf16[16,112,128]{2,1,0:T(8,128)(2,1)} %get-tuple-element.24), calls=%async_computation | async-start | bytes 917504 | tf_op jit(solution)/shard_map/all_to_all | solution.py:409
  17.1 5.9 %shard_map.123 = bf16[128,1024]{1,0:T(8,128)(2,1)} custom-call(bf16[32,1024]{1,0:T(8,128)(2,1)} %get-tuple-element.25.query_at, bf16[32,1024]{1,0:T(8,128)(2,1)} %get-tuple-element.26.events_at, bf16[768,1024]{1,0:T(8,128)(2,1)} %get-tuple-element.30.keys, bf16[768,1024]{1,0:T(8,128)(2,1)} %get-tuple-element.31.values, bf16[1024,1024]{1,0:T(8,128)(2,1)} %w_output.3, ...), custom_call_target="tpu_custom_call" | custom-call | flops 100663296 | bytes 4718592 | tf_op jit(solution)/shard_map/pallas_call | solution.py:155
  22.9 7.4 %all-to-all-done.arrived = bf16[16,112,128]{2,1,0:T(8,128)(2,1)S(1)} async-done(((bf16[16,112,128]{2,1,0:T(8,128)(2,1)}), bf16[16,112,128]{2,1,0:T(8,128)(2,1)S(1)}, u32[]{:S(2)}, u32[]{:S(2)}) %all-to-all-start) | async-done | bytes 458784 | tf_op jit(solution)/shard_map/all_to_all | solution.py:409
  30.3 0.8 copy-done.1
  31.1 2.2 %shard_map.124 = (bf16[16,64,128]{2,1,0:T(8,128)(2,1)}, bf16[16,64,128]{2,1,0:T(8,128)(2,1)}) custom-call(bf16[16,112,128]{2,1,0:T(8,128)(2,1)} %copy-done.1), custom_call_target="tpu_custom_call" | custom-call | flops 4194304 | bytes 1048576 | tf_op jit(solution)/shard_map/pallas_call | solution.py:217
  33.3 13.9 %all_to_all.41 = bf16[16,64,128]{2,1,0:T(8,128)(2,1)S(1)} all-to-all(bf16[16,64,128]{2,1,0:T(8,128)(2,1)} %get-tuple-element.41), channel_id=1, replica_groups=mesh['grp'=2,'seq'=16] {'seq'}, dimensions={0} | all-to-all | bytes 524288 | tf_op jit(solution)/shard_map/all_to_all | solution.py:409
  47.2 3.5 %all-to-all-start.2 = ((bf16[16,8,1024]{2,1,0:T(8,128)(2,1)}), bf16[16,8,1024]{2,1,0:T(8,128)(2,1)S(1)}, u32[]{:S(2)}, u32[]{:S(2)}) async-start(bf16[16,8,1024]{2,1,0:T(8,128)(2,1)} %bitcast.28), calls=%async_computation.2 | async-start | bytes 524288 | tf_op jit(solution)/shard_map/all_to_all | solution.py:409
  50.8 11.5 %shard_map.125 = (bf16[768,1024]{1,0:T(8,128)(2,1)}, bf16[768,1024]{1,0:T(8,128)(2,1)}, bf16[2,32,128]{2,1,0:T(8,128)(2,1)}, f32[2,32,32]{2,1,0:T(8,128)}) custom-call(bf16[768,1024]{1,0:T(8,128)(2,1)} %events.5, bf16[1024,1024]{1,0:T(8,128)(2,1)} %w_query.3, bf16[768,1024]{1,0:T(8,128)(2,1)} %get-tuple-element.30.keys, ...), custom_call_target="tpu_custom_call" | custom-call | flops 2415919104 | bytes 6291456 | tf_op jit(solution)/shard_map/pallas_call | solution.py:313
  62.3 0.2 reshape_reshape.3
  62.5 0.5 copy.15
  63.1 0.3 reshape.47
  63.4 6.0 %all-to-all-start.1 = ((bf16[16,64,128]{2,1,0:T(8,128)(2,1)}), bf16[16,64,128]{2,1,0:T(8,128)(2,1)S(1)}, u32[]{:S(2)}, u32[]{:S(2)}) async-start(bf16[16,64,128]{2,1,0:T(8,128)(2,1)} %get-tuple-element.35), calls=%async_computation.1 | async-start | bytes 524288 | tf_op jit(solution)/shard_map/all_to_all | solution.py:409
  69.4 2.0 %fusion = bf16[128,1024]{1,0:T(8,128)(2,1)S(1)} fusion(bf16[128,1024]{1,0:T(8,128)(2,1)S(1)} %reshape.47, bf16[1024,1024]{1,0:T(8,128)(2,1)} %w_output.3, bf16[16,8,1024]{2,1,0:T(8,128)(2,1)S(1)} %all-to-all-done.2), kind=kOutput, calls=%fused_computation.2 | convolution fusion | flops 268828672 | bytes 2883584 | tf_op jit(solution)/shard_map/dot_general | solution.py:22
  71.5 2.3 %fusion.4 = bf16[16,8,256]{2,1,0:T(8,128)(2,1)} fusion(bf16[1024,256]{1,0:T(8,128)(2,1)} %param.17, bf16[128,1024]{1,0:T(8,128)(2,1)S(1)} %fusion, bf16[1024,1024]{1,0:T(8,128)(2,1)S(1)} %copy-done), kind=kOutput, calls=%fused_computation.6 | convolution fusion | flops 335839232 | bytes 2949120 | tf_op jit(solution)/shard_map/dot_general | solution.py:22
  73.8 5.7 %all-to-all-done.1 = bf16[16,64,128]{2,1,0:T(8,128)(2,1)S(1)} async-done(((bf16[16,64,128]{2,1,0:T(8,128)(2,1)}), bf16[16,64,128]{2,1,0:T(8,128)(2,1)S(1)}, u32[]{:S(2)}, u32[]{:S(2)}) %all-to-all-start.1) | async-done | bytes 262176 | tf_op jit(solution)/shard_map/all_to_all | solution.py:409
  79.5 3.5 %all-to-all-start.4 = ((bf16[16,8,256]{2,1,0:T(8,128)(2,1)}), bf16[16,8,256]{2,1,0:T(8,128)(2,1)S(1)}, u32[]{:S(2)}, u32[]{:S(2)}) async-start(bf16[16,8,256]{2,1,0:T(8,128)(2,1)} %fusion.4), calls=%async_computation.4 | async-start | bytes 131072 | tf_op jit(solution)/shard_map/all_to_all | solution.py:409
  83.0 0.0 copy-start.3
  83.0 0.0 copy-start.4
  83.0 6.5 %shard_map.126 = (bf16[768,1024]{1,0:T(8,128)(2,1)}, bf16[32,1024]{1,0:T(8,128)(2,1)}) custom-call(bf16[768,1024]{1,0:T(8,128)(2,1)} %events.5, bf16[768,1024]{1,0:T(8,128)(2,1)} %get-tuple-element.33.query, bf16[768,1024]{1,0:T(8,128)(2,1)} %get-tuple-element.34.within, bf16[1024,128]{1,0:T(8,128)(2,1)} %bitcast.27, bf16[1024,1024]{1,0:T(8,128)(2,1)} %w_output.3, ...), custom_call_target="tpu_custom_call" | custom-call | flops 1610612736 | bytes 7864320 | tf_op jit(solution)/shard_map/pallas_call | solution.py:361
  89.5 1.0 %fusion.9 = f32[32,32]{1,0:T(8,128)S(1)} fusion(bf16[32,1024]{1,0:T(8,128)(2,1)} %get-tuple-element.37, bf16[1024,32]{0,1:T(8,128)(2,1)S(1)} %copy-done.3), kind=kOutput, calls=%fused_computation.15 | convolution fusion | flops 2097152 | bytes 135168 | tf_op jit(solution)/shard_map/dot_general | solution.py:22
  90.5 0.1 multiply_reduce_fusion
  90.6 0.8 fusion.5
  (11 shorter events, 0.0 us)
Async XLA Ops:
  0.6 70.8 %copy-start = (bf16[1024,1024]{1,0:T(8,128)(2,1)S(1)}, bf16[1024,1024]{1,0:T(8,128)(2,1)}, u32[]{:S(2)}) copy-start(bf16[1024,1024]{1,0:T(8,128)(2,1)} %param.16) | copy-start | bytes 6291460
  9.7 20.7 %all-to-all-start = ((bf16[16,112,128]{2,1,0:T(8,128)(2,1)}), bf16[16,112,128]{2,1,0:T(8,128)(2,1)S(1)}, u32[]{:S(2)}, u32[]{:S(2)}) async-start(bf16[16,112,128]{2,1,0:T(8,128)(2,1)} %get-tuple-element.24), calls=%async_computation | async-start | bytes 917504 | tf_op jit(solution)/shard_map/all_to_all | solution.py:409
  30.3 0.8 copy-start.1
  47.2 16.2 %all-to-all-start.2 = ((bf16[16,8,1024]{2,1,0:T(8,128)(2,1)}), bf16[16,8,1024]{2,1,0:T(8,128)(2,1)S(1)}, u32[]{:S(2)}, u32[]{:S(2)}) async-start(bf16[16,8,1024]{2,1,0:T(8,128)(2,1)} %bitcast.28), calls=%async_computation.2 | async-start | bytes 524288 | tf_op jit(solution)/shard_map/all_to_all | solution.py:409
  63.4 16.0 %all-to-all-start.1 = ((bf16[16,64,128]{2,1,0:T(8,128)(2,1)}), bf16[16,64,128]{2,1,0:T(8,128)(2,1)S(1)}, u32[]{:S(2)}, u32[]{:S(2)}) async-start(bf16[16,64,128]{2,1,0:T(8,128)(2,1)} %get-tuple-element.35), calls=%async_computation.1 | async-start | bytes 524288 | tf_op jit(solution)/shard_map/all_to_all | solution.py:409
  79.5 3.5 %copy-start.2 = (bf16[16,64,128]{2,1,0:T(8,128)(2,1)}, bf16[16,64,128]{2,1,0:T(8,128)(2,1)S(1)}, u32[]{:S(2)}) copy-start(bf16[16,64,128]{2,1,0:T(8,128)(2,1)S(1)} %all-to-all-done.1) | copy-start | bytes 786436
  79.5 11.1 %all-to-all-start.4 = ((bf16[16,8,256]{2,1,0:T(8,128)(2,1)}), bf16[16,8,256]{2,1,0:T(8,128)(2,1)S(1)}, u32[]{:S(2)}, u32[]{:S(2)}) async-start(bf16[16,8,256]{2,1,0:T(8,128)(2,1)} %fusion.4), calls=%async_computation.4 | async-start | bytes 131072 | tf_op jit(solution)/shard_map/all_to_all | solution.py:409
  83.0 6.5 %copy-start.3 = (bf16[1024,32]{0,1:T(8,128)(2,1)S(1)}, bf16[1024,32]{0,1:T(8,128)(2,1)}, u32[]{:S(2)}) copy-start(bf16[1024,32]{0,1:T(8,128)(2,1)} %param.18) | copy-start | bytes 196612
  83.0 7.5 %copy-start.4 = (f32[2,32,32]{2,1,0:T(8,128)S(1)}, f32[2,32,32]{2,1,0:T(8,128)}, u32[]{:S(2)}) copy-start(f32[2,32,32]{2,1,0:T(8,128)} %get-tuple-element.38) | copy-start | bytes 24580
  83.0 7.6 %copy-start.5 = (bf16[2,32,128]{2,1,0:T(8,128)(2,1)S(1)}, bf16[2,32,128]{2,1,0:T(8,128)(2,1)}, u32[]{:S(2)}) copy-start(bf16[2,32,128]{2,1,0:T(8,128)(2,1)} %get-tuple-element.39) | copy-start | bytes 49156

commit v3 on v1

v3 whole, which is shorter than its diff:
```python
import functools

import jax
import jax.numpy as jnp
from jax import lax
from jax.experimental import pallas as pl
from jax.experimental.pallas import tpu as pltpu
from jax.sharding import PartitionSpec as P

HEADS = 8
EXPERTS = 16
CAP = 8
PLANE = 4
F32 = jnp.float32
BF16 = jnp.bfloat16
MIB = 1 << 20


def dot(a, b, contract=((1,), (0,)), **kw):
    return lax.dot_general(a, b, (contract, ((), ())), preferred_element_type=F32, **kw)


def call(kernel, grid, in_specs, out_specs, out_shape, flops, moved, scratch=(), vmem=24):
    return pl.pallas_call(
        kernel,
        grid=grid,
        in_specs=in_specs,
        out_specs=out_specs,
        out_shape=out_shape,
        scratch_shapes=scratch,
        compiler_params=pltpu.CompilerParams(vmem_limit_bytes=vmem * MIB),
        cost_estimate=pl.CostEstimate(flops=flops, bytes_accessed=moved, transcendentals=0),
    )


def whole(shape):
    return pl.BlockSpec(shape, lambda *_: (0,) * len(shape))


def columns(rows, cols):
    return pl.BlockSpec((rows, cols), lambda i: (0, i))


def shaped(shape, kind):
    return jax.ShapeDtypeStruct(shape, kind)


def key_value_kernel(head_dim, tile, rank, events, w_key, w_value, keys, values, inner, *states):
    k = dot(events[...], w_key[...]).astype(BF16)
    v = dot(events[...], w_value[...]).astype(BF16)
    keys[...] = k
    values[...] = v
    total = None
    for i in range(events.shape[0] // tile):
        here = slice(i * tile, (i + 1) * tile)
        if i:
            inner[i - 1] = total.astype(BF16)
        both = dot(k[here], v[here], ((0,), (0,)))
        parts = [slice(h * head_dim, (h + 1) * head_dim) for h in range(both.shape[0] // head_dim)]
        own = jnp.concatenate([both[part, part] for part in parts], axis=0)
        total = own if total is None else total + own
    for i, state in enumerate(states):

        @pl.when(pl.program_id(0) == i)
        def _():
            state[...] = total.astype(BF16)


def key_value_state(events, w_key, w_value, rank):
    rows, width = events.shape
    head_dim = width // HEADS
    pair = width // PLANE
    tile = row_tile(rows)
    inner = rows // tile - 1
    cols = lambda many: pl.BlockSpec((many, pair), lambda i, r: (0, i ^ r[0]))
    return pl.pallas_call(
        functools.partial(key_value_kernel, head_dim, tile),
        grid_spec=pltpu.PrefetchScalarGridSpec(
            num_scalar_prefetch=1,
            grid=(PLANE,),
            in_specs=[whole((rows, width)), cols(width), cols(width)],
            out_specs=[
                cols(rows),
                cols(rows),
                pl.BlockSpec((inner, pair, head_dim), lambda i, r: (0, i ^ r[0], 0)),
            ]
            + [whole((pair, head_dim))] * PLANE,
        ),
        out_shape=[shaped((rows, width), BF16)] * 2
        + [shaped((inner, width, head_dim), BF16)]
        + [shaped((pair, head_dim), BF16)] * PLANE,
        compiler_params=pltpu.CompilerParams(vmem_limit_bytes=60 * MIB),
        cost_estimate=pl.CostEstimate(flops=4 * rows * width * width, bytes_accessed=8 * rows * width, transcendentals=0),
    )(rank, events, w_key, w_value)


def row_tile(rows):
    return 256 if rows % 256 == 0 and rows > 256 else rows // 2


def labelled_kernel(head_dim, copies, events, w_query, keys, values, labels, experts, tasks, *outs):
    query_at, within_at, events_at, factor, selector, match, column = outs
    rows = events.shape[0]
    many = labels.shape[1]

    @pl.when(pl.program_id(0) == 0)
    def _():
        events_at[...] = dot(row_choice(labels[...], rows), events[...]).astype(BF16)
        start = lax.axis_index("seq") * rows + 1
        factor[...] = upright(lax.rsqrt((labels[...] + start).astype(F32) * head_dim))
        places = slot_of(experts[...])
        target = slot_place(selector.shape, 0, copies)
        selector[...] = jnp.where((target == places[0]) | (target == places[1]), 1.0, 0.0).astype(BF16)
        target = slot_place(match.shape[1:], 1, copies)
        number = lax.broadcasted_iota(jnp.int32, column.shape[1:], 1)
        for k in range(2):
            match[k] = jnp.where(target == upright(places[k]), 1.0, 0.0).astype(BF16)
            chosen_column = upright(tasks[...] * EXPERTS + experts[k : k + 1, :])
            column[k] = jnp.where(number == chosen_column, 1.0, 0.0)

    query = dot(events_at[...], w_query[...]).astype(BF16)
    query_at[...] = query
    causal = lax.broadcasted_iota(jnp.int32, (many, rows), 1) <= upright(labels[...])
    for h in range(keys.shape[1] // head_dim):
        part = slice(h * head_dim, (h + 1) * head_dim)
        weight = dot(query[:, part], keys[:, part], ((1,), (1,)))
        within_at[:, part] = dot(jnp.where(causal, weight, 0.0).astype(BF16), values[:, part])


def labelled_rows(events, w_query, keys, values, labels, experts, tasks, devices):
    rows, width = events.shape
    many = labels.shape[1]
    pair = width // PLANE
    slots = devices * CAP
    kinds = 2 * EXPERTS
    return call(
        functools.partial(labelled_kernel, width // HEADS, devices // EXPERTS),
        (PLANE,),
        [whole((rows, width)), columns(width, pair), columns(rows, pair), columns(rows, pair)]
        + [whole(labels.shape), whole(experts.shape), whole(tasks.shape)],
        [columns(many, pair), columns(many, pair), whole((many, width)), whole((many, 1))]
        + [whole((slots, many)), whole((2, many, slots)), whole((2, many, kinds))],
        [shaped((many, width), BF16), shaped((many, width), F32), shaped((many, width), BF16)]
        + [shaped((many, 1), F32), shaped((slots, many), BF16)]
        + [shaped((2, many, slots), BF16), shaped((2, many, kinds), F32)],
        4 * many * rows * width,
        8 * rows * width,
        vmem=12,
    )(events, w_query, keys, values, labels, experts, tasks)


def slot_of(experts):
    many = experts.shape[1]
    number = lax.broadcasted_iota(jnp.int32, (EXPERTS, many), 0)
    ones = [jnp.where(number == experts[k : k + 1, :], 1.0, 0.0) for k in range(2)]
    earlier = lax.broadcasted_iota(jnp.int32, (many, many), 0) < lax.broadcasted_iota(jnp.int32, (many, many), 1)
    strict = jnp.where(earlier, 1.0, 0.0).astype(BF16)
    first = dot(ones[0].astype(BF16), strict)
    second = dot(ones[1].astype(BF16), strict) + jnp.sum(ones[0], axis=1, keepdims=True)
    slots = [jnp.sum(o * c, axis=0, keepdims=True).astype(jnp.int32) for o, c in zip(ones, (first, second))]
    return [experts[k : k + 1, :] * CAP + slots[k] for k in range(2)]


def slot_place(shape, axis, copies):
    row = lax.broadcasted_iota(jnp.int32, shape, axis)
    return row if copies == 1 else (row // (copies * CAP)) * CAP + row % CAP


def within_kernel(head_dim, tile, events, w_query, keys, values, inner, query, within):
    rows = events.shape[0]
    pair = w_query.shape[1]
    q = dot(events[...], w_query[...]).astype(BF16)
    query[...] = q
    spot = lax.broadcasted_iota(jnp.int32, (tile, tile), 0)
    causal = lax.broadcasted_iota(jnp.int32, (tile, tile), 1) <= spot
    for i in range(rows // tile):
        here = slice(i * tile, (i + 1) * tile)
        totals = []
        for h in range(pair // head_dim):
            part = slice(h * head_dim, (h + 1) * head_dim)
            weight = dot(q[here, part], keys[here, part], ((1,), (1,)))
            weight = jnp.where(causal, weight, 0.0).astype(BF16)
            totals.append(dot(weight, values[here, part]))
        total = jnp.concatenate(totals, axis=1)
        if i:
            total = total + dot(q[here], on_diagonal(inner[i - 1], head_dim))
        within[here, :] = total.astype(BF16)


def upright(row):
    many = row.shape[1]
    diagonal = lax.broadcasted_iota(jnp.int32, (many, many), 0) == lax.broadcasted_iota(jnp.int32, (many, many), 1)
    return jnp.sum(jnp.where(diagonal, row, jnp.zeros_like(row)), axis=1, keepdims=True)


def row_choice(labels, rows):
    number = lax.broadcasted_iota(jnp.int32, (labels.shape[1], rows), 1)
    return jnp.where(number == upright(labels), 1.0, 0.0).astype(BF16)


def on_diagonal(block, head_dim):
    pair = block.shape[0]
    row = lax.broadcasted_iota(jnp.int32, (pair, pair), 0) // head_dim
    col = lax.broadcasted_iota(jnp.int32, (pair, pair), 1) // head_dim
    wide = jnp.concatenate([block.astype(F32)] * (pair // head_dim), axis=1)
    return jnp.where(row == col, wide, 0.0).astype(BF16)


def queries_within(events, w_query, keys, values, inner):
    rows, width = events.shape
    head_dim = width // HEADS
    pair = width // PLANE
    tile = row_tile(rows)
    return call(
        functools.partial(within_kernel, head_dim, tile),
        (width // pair,),
        [
            whole((rows, width)),
            columns(width, pair),
            columns(rows, pair),
            columns(rows, pair),
            pl.BlockSpec((inner.shape[0], pair, head_dim), lambda i: (0, i, 0)),
        ],
        [columns(rows, pair), columns(rows, pair)],
        [shaped((rows, width), BF16)] * 2,
        2 * rows * width * width + 4 * tile * rows * width,
        8 * rows * width,
    )(events, w_query, keys, values, inner)


def flip(x, j):
    devices = lax.axis_size("seq")
    return lax.ppermute(x, "seq", [(i, i ^ j) for i in range(devices)])


def later(x, s):
    return lax.ppermute(x, "seq", [(i, i + s) for i in range(lax.axis_size("seq") - s)])


def swapped(states):
    return [states[0]] + [flip(x, j) for j, x in enumerate(states) if j]


def sums_before(states):
    devices = lax.axis_size("seq")
    rank = lax.axis_index("seq") % PLANE
    states = [x.astype(F32) for x in states]
    total = sum(states)
    planes = jnp.zeros_like(total)
    step = PLANE
    while step < devices:
        came = later(total.astype(BF16), step).astype(F32)
        total, planes = total + came, planes + came
        step *= 2
    before = []
    for j in range(PLANE):
        held = [jnp.where((rank ^ i) < (rank ^ j), states[i], 0.0) for i in range(PLANE) if i != j]
        before.append((planes + sum(held)).astype(BF16))
    return swapped(before)


def earlier_terms(query, prefix, head_dim):
    pair = query.shape[1] // PLANE
    terms = [dot(query[:, p * pair : (p + 1) * pair], prefix[p]) for p in range(PLANE)]
    return jnp.concatenate(terms, axis=1)


def put_prefix(prefix, parts, head_dim):
    rank = lax.axis_index("seq") % PLANE
    for j, part in enumerate(parts):
        prefix[rank ^ j] = on_diagonal(part[...], head_dim)


def picked_kernel(head_dim, query_at, within_at, events_at, factor, selector, w_output, *refs):
    parts, (picked, outgoing, prefix) = refs[:PLANE], refs[PLANE:]
    put_prefix(prefix, parts, head_dim)
    total = within_at[...] + earlier_terms(query_at[...], prefix, head_dim)
    attended = (total * factor[...]).astype(BF16)
    rows = (events_at[...].astype(F32) + dot(attended, w_output[...])).astype(BF16)
    picked[...] = rows
    outgoing[...] = dot(selector[...], rows).astype(BF16)


def picked_rows(query_at, within_at, events_at, factor, selector, w_output, prefix):
    many, width = query_at.shape
    slots = selector.shape[0]
    pair = width // PLANE
    operands = (query_at, within_at, events_at, factor, selector, w_output, *prefix)
    return call(
        functools.partial(picked_kernel, width // HEADS),
        (),
        [whole(x.shape) for x in operands],
        [whole((many, width)), whole((slots, width))],
        [shaped((many, width), BF16), shaped((slots, width), BF16)],
        2 * many * width * width,
        2 * width * width,
        [pltpu.VMEM((PLANE, pair, pair), BF16)],
        vmem=10,
    )(*operands)


def hidden_kernel(head_dim, events, query, within, w_output, *refs):
    parts, (hidden, prefix) = refs[:PLANE], refs[PLANE:]
    tile = events.shape[0]

    @pl.when(pl.program_id(0) == 0)
    def _():
        put_prefix(prefix, parts, head_dim)

    start = lax.axis_index("seq") * (tile * pl.num_programs(0)) + pl.program_id(0) * tile + 1
    place = (lax.broadcasted_iota(jnp.int32, (tile, 1), 0) + start).astype(F32)
    total = within[...].astype(F32) + earlier_terms(query[...], prefix, head_dim)
    attended = (total * lax.rsqrt(place * head_dim)).astype(BF16)
    hidden[...] = (events[...].astype(F32) + dot(attended, w_output[...])).astype(BF16)


def hidden_rows(events, query, within, prefix, w_output):
    rows, width = events.shape
    head_dim = width // HEADS
    tile = row_tile(rows)
    pair = width // PLANE
    strip = pl.BlockSpec((tile, width), lambda i: (i, 0))
    return call(
        functools.partial(hidden_kernel, head_dim),
        (rows // tile,),
        [strip, strip, strip, whole((width, width))] + [whole((pair, head_dim))] * PLANE,
        strip,
        shaped((rows, width), BF16),
        2 * rows * width * width,
        10 * rows * width,
        [pltpu.VMEM((PLANE, pair, pair), BF16)],
    )(events, query, within, w_output, *prefix)


def expert_rows(rows, weight_in, weight_out):
    inner = jnp.maximum(dot(rows, weight_in), 0.0).astype(BF16)
    return dot(inner, weight_out).astype(BF16)


def score_rows(picked, gate_weight, column, match, back):
    logits = dot(picked, gate_weight)
    gates = jax.nn.sigmoid(jnp.sum(logits[None] * column, axis=2))
    choices, many, slots = match.shape
    chosen = dot(match.reshape(choices * many, slots), back).reshape(choices, many, -1)
    return jnp.sum(gates[:, :, None] * chosen, axis=0)


def shards(
    events,
    w_query,
    w_key,
    w_value,
    w_output,
    expert_in,
    expert_out,
    gate_weight,
    label_rows,
    label_experts,
    label_tasks,
):
    devices = lax.axis_size("seq")
    labels = label_rows.reshape(1, -1)
    tasks = label_tasks.reshape(1, -1)
    experts = label_experts.T

    def exchange(x):
        return lax.all_to_all(x, "seq", split_axis=0, concat_axis=0, tiled=True)

    rank = (lax.axis_index("seq") % PLANE).reshape(1)
    keys, values, inner, *states = key_value_state(events, w_key, w_value, rank)
    states = swapped(states)
    labelled = labelled_rows(events, w_query, keys, values, labels, experts, tasks, devices)
    states, labelled = lax.optimization_barrier((states, labelled))
    *labelled, match, column = labelled
    prefix = sums_before(states)
    picked, outgoing = picked_rows(*labelled, w_output, prefix)
    outgoing, keys, values = lax.optimization_barrier((outgoing, keys, values))
    arrived = exchange(outgoing)
    query, within = queries_within(events, w_query, keys, values, inner)
    arrived, query, within = lax.optimization_barrier((arrived, query, within))
    partial = expert_rows(arrived, expert_in, expert_out)
    back = exchange(partial)
    hidden = hidden_rows(events, query, within, prefix, w_output)
    return hidden, score_rows(picked, gate_weight, column, match, back)


def solution(mesh):
    placed = (
        P(("grp", "seq"), None),
        P(),
        P(),
        P(),
        P(),
        P(None, "seq"),
        P("seq", None),
        P(),
        P(("grp", "seq")),
        P(("grp", "seq"), None),
        P(("grp", "seq")),
    )
    return jax.shard_map(
        shards,
        mesh=mesh,
        in_specs=placed,
        out_specs=(P(("grp", "seq"), None), P(("grp", "seq"), None)),
        check_vma=False,
    )
```

time: 82.4 us -> 88.4 us (1.073)
  local copies, waits for them, and re-layouts: 0.78 us -> 21.4 us
  waiting for transfers between devices: 18.6 us -> 7.52 us
  starting transfers between devices: 16.6 us -> 27.1 us
  blocking collectives: 10.3 us -> 0 us
  matrix products: 6.22 us -> 3.29 us
  other arithmetic: 1.93 us -> 0.36 us
    unnamed x14 -> x44, local copies, waits for them, and re-layouts: 0.04 us -> 21.4 us
    ppermute x0 -> x8, starting transfers between devices: none -> 14.7 us  [the longest x2 9.31 us: later(): lax.ppermute(x, 'seq', [(i, i + s) for i in range(lax.axis_size('seq') -...]
    all_to_all x1 -> x0, blocking collectives: 10.3 us -> none  [exchange(): lax.all_to_all(x, 'seq', split_axis=0, concat_axis=0, tiled=True, axis_in...]
    all_to_all x2, waiting for transfers between devices: 10.1 us -> 0.01 us  [exchange(): return lax.all_to_all(x, 'seq', split_axis=0, concat_axis=0, tiled=True)]
    all_to_all x2 -> x0, starting transfers between devices: 8.86 us -> none  [exchange(): lax.all_to_all(x, 'seq', split_axis=0, concat_axis=0, tiled=True, axis_in...]
    all_to_all x2 -> x0, waiting for transfers between devices: 8.5 us -> none  [exchange(): lax.all_to_all(x, 'seq', split_axis=0, concat_axis=0, tiled=True, axis_in...]
    ppermute x0 -> x8, waiting for transfers between devices: none -> 7.51 us  [the longest x6 3.76 us: flip(): return lax.ppermute(x, 'seq', [(i, i ^ j) for i in range(devices)])]
    all_to_all x2, starting transfers between devices: 7.74 us -> 12.4 us  [exchange(): return lax.all_to_all(x, 'seq', split_axis=0, concat_axis=0, tiled=True)]
  transfers between devices with their start and end apart: 4 -> 10, of which waited for: 3 -> 4; matrix products, arithmetic and copies ran while one was open for 1% -> 0% of each run, Pallas kernels for 23% -> 20%
where the time goes in v3:
time: 88.4 us; the launch traced here: 87.5 us
  starting transfers between devices  27.1 us (31%)
  Pallas kernels  27 us (31%)
  local copies, waits for them, and re-layouts  21.4 us (24%)
  waiting for transfers between devices  7.52 us (9%)
  matrix products  3.29 us (4%)
  between operations  0.89 us (1%)
    unnamed x44, local copies, waits for them, and re-layouts  21.4 us
    all_to_all x2, starting transfers between devices, exchange(): return lax.all_to_all(x, 'seq', split_axis=0, concat_axis=0, tiled=True)  12.4 us
    pallas_call x1, Pallas kernels, queries_within(): call(functools.partial(within_kernel, head_dim, tile), (width // pair,),...  9.4 us
    ppermute x2, starting transfers between devices, later(): lax.ppermute(x, 'seq', [(i, i + s) for i in range(lax.axis_size('seq') -...  9.31 us
    pallas_call x1, Pallas kernels, key_value_state(): pl.pallas_call(functools.partial(key_value_kernel, head_dim, tile), grid_...  8.24 us
    ppermute x6, starting transfers between devices, flip(): return lax.ppermute(x, 'seq', [(i, i ^ j) for i in range(devices)])  5.38 us
    pallas_call x1, Pallas kernels, labelled_rows(): call(functools.partial(labelled_kernel, width // HEADS, devices // EXPERT...  4.26 us
    ppermute x6, waiting for transfers between devices, flip(): return lax.ppermute(x, 'seq', [(i, i ^ j) for i in range(devices)])  3.76 us
  transfers between devices with their start and end apart: 10, of which 4 were waited for; matrix products, arithmetic and copies ran while one was open for 0% of the time, Pallas kernels for 20%

profile of v3, /device:TPU:0, one launch (start us, length us, event | category | flops | bytes accessed | tf_op | source)
XLA Modules:
  0.0 87.5 jit_solution(2094045261912548982)
XLA Ops:
  0.7 8.2 %shard_map.122 = (bf16[768,1024]{1,0:T(8,128)(2,1)}, bf16[768,1024]{1,0:T(8,128)(2,1)}, bf16[2,1024,128]{2,1,0:T(8,128)(2,1)}, bf16[256,128]{1,0:T(8,128)(2,1)},...) custom-call(s32[1]{0:T(128)} %bitcast.rank, bf16[768,1024]{1,0:T(8,128)(2,1)} %events.7, ...), custom_call_target="tpu_custom_call" | custom-call | flops 3221225472 | bytes 6291456 | tf_op jit(solution)/shard_map/pallas_call | solution.py:76
  9.5 2.6 %collective-permute-start.1 = (bf16[256,128]{1,0:T(8,128)(2,1)}, bf16[256,128]{1,0:T(8,128)(2,1)S(1)}, u32[]{:S(2)}, u32[]{:S(2)}) collective-permute-start(bf16[256,128]{1,0:T(8,128)(2,1)} %get-tuple-element.39), channel_id=1, source_target_pairs={{0,2},{1,3},{2,0},{3,1},{4,6},{5,7},{6,4},{7,5},{8,10},{9,11},{10,... | collective-permute-start | bytes 196616 | tf_op jit(solution)/shard_map/ppermute | solution.py:233
  13.5 1.6 %copy-done.6 = bf16[1024,1024]{1,0:T(8,128)(2,1)S(1)} copy-done((bf16[1024,1024]{1,0:T(8,128)(2,1)S(1)}, bf16[1024,1024]{1,0:T(8,128)(2,1)}, u32[]{:S(2)}) %copy-start.6) | copy-done | bytes 2097176
  15.1 1.4 %copy-done.8 = bf16[768,1024]{1,0:T(8,128)(2,1)S(1)} copy-done((bf16[768,1024]{1,0:T(8,128)(2,1)S(1)}, bf16[768,1024]{1,0:T(8,128)(2,1)}, u32[]{:S(2)}) %copy-start.8) | copy-done | bytes 1572888
  17.9 4.3 %shard_map.123 = (bf16[32,1024]{1,0:T(8,128)(2,1)S(1)}, f32[32,1024]{1,0:T(8,128)S(1)}, bf16[32,1024]{1,0:T(8,128)(2,1)S(1)}, f32[32,1]{1,0:T(8,128)S(1)}, bf16[...) custom-call(bf16[768,1024]{1,0:T(8,128)(2,1)S(1)} %copy-done.3, ...), custom_call_target="tpu_custom_call" | custom-call | flops 100663296 | bytes 6291456 | tf_op jit(solution)/shard_map/pallas_call | solution.py:136
  22.3 3.8 %collective-permute-start.3 = (bf16[256,128]{1,0:T(8,128)(2,1)S(1)}, bf16[256,128]{1,0:T(8,128)(2,1)S(1)}, u32[]{:S(2)}, u32[]{:S(2)}) collective-permute-start(bf16[256,128]{1,0:T(8,128)(2,1)S(1)} %fusion.24), channel_id=1, source_target_pairs={{0,4},{1,5},{2,6},{3,7},{4,8},{5,9},{6,10},{7,11},{8,12},{9,13},{1... | collective-permute-start | bytes 196616 | tf_op jit(solution)/shard_map/ppermute | solution.py:237
  26.1 1.9 %collective-permute-done.3 = bf16[256,128]{1,0:T(8,128)(2,1)S(1)} collective-permute-done((bf16[256,128]{1,0:T(8,128)(2,1)S(1)}, bf16[256,128]{1,0:T(8,128)(2,1)S(1)}, u32[]{:S(2)}, u32[]{:S(2)}) %collective-permute-start.3) | collective-permute-done | bytes 65568 | tf_op jit(solution)/shard_map/ppermute | solution.py:237
  28.1 5.5 %collective-permute-start.4 = (bf16[256,128]{1,0:T(8,128)(2,1)S(1)}, bf16[256,128]{1,0:T(8,128)(2,1)S(1)}, u32[]{:S(2)}, u32[]{:S(2)}) collective-permute-start(bf16[256,128]{1,0:T(8,128)(2,1)S(1)} %fusion.6), channel_id=1, source_target_pairs={{0,8},{1,9},{2,10},{3,11},{4,12},{5,13},{6,14},{7,15},{16,24},{17,... | collective-permute-start | bytes 196616 | tf_op jit(solution)/shard_map/ppermute | solution.py:237
  33.6 1.9 %collective-permute-done.4 = bf16[256,128]{1,0:T(8,128)(2,1)S(1)} collective-permute-done((bf16[256,128]{1,0:T(8,128)(2,1)S(1)}, bf16[256,128]{1,0:T(8,128)(2,1)S(1)}, u32[]{:S(2)}, u32[]{:S(2)}) %collective-permute-start.4) | collective-permute-done | bytes 65568 | tf_op jit(solution)/shard_map/ppermute | solution.py:237
  35.7 1.6 %collective-permute-start.5 = (bf16[256,128]{1,0:T(8,128)(2,1)S(1)}, bf16[256,128]{1,0:T(8,128)(2,1)S(1)}, u32[]{:S(2)}, u32[]{:S(2)}) collective-permute-start(bf16[256,128]{1,0:T(8,128)(2,1)S(1)} %get-tuple-element.74), channel_id=1, source_target_pairs={{0,1},{1,0},{2,3},{3,2},{4,5},{5,4},{6,7},{7,6},{8,9},{9,8},{10,11... | collective-permute-start | bytes 196616 | tf_op jit(solution)/shard_map/ppermute | solution.py:233
  37.8 2.2 %collective-permute-done.7.refs_3_ = bf16[256,128]{1,0:T(8,128)(2,1)S(1)} collective-permute-done((bf16[256,128]{1,0:T(8,128)(2,1)S(1)}, bf16[256,128]{1,0:T(8,128)(2,1)S(1)}, u32[]{:S(2)}, u32[]{:S(2)}) %collective-permute-start.7) | collective-permute-done | bytes 65568 | tf_op jit(solution)/shard_map/ppermute | solution.py:233
  40.0 1.6 %collective-permute-done.6.refs_2_ = bf16[256,128]{1,0:T(8,128)(2,1)S(1)} collective-permute-done((bf16[256,128]{1,0:T(8,128)(2,1)S(1)}, bf16[256,128]{1,0:T(8,128)(2,1)S(1)}, u32[]{:S(2)}, u32[]{:S(2)}) %collective-permute-start.6) | collective-permute-done | bytes 65568 | tf_op jit(solution)/shard_map/ppermute | solution.py:233
  41.6 1.6 %copy-done.1 = bf16[1024,1024]{1,0:T(8,128)(2,1)S(1)} copy-done((bf16[1024,1024]{1,0:T(8,128)(2,1)S(1)}, bf16[1024,1024]{1,0:T(8,128)(2,1)}, u32[]{:S(2)}) %copy-start.1) | copy-done | bytes 2097176
  43.2 1.6 %shard_map.124 = (bf16[32,1024]{1,0:T(8,128)(2,1)S(1)}, bf16[128,1024]{1,0:T(8,128)(2,1)}) custom-call(bf16[32,1024]{1,0:T(8,128)(2,1)S(1)} %get-tuple-element.50.query_at, f32[32,1024]{1,0:T(8,128)S(1)} %get-tuple-element.51.within_at, bf16[32,1024]{1,0:T(8,128)(2,1)S(1)} %get-tuple-element.52.events_at, f32[32,1]{1,0:T(8,128)S(1)} %get-tuple-element.53.factor, ...), custom_call_target="tpu_custom_call" | custom-call | flops 67108864 | bytes 2097152 | tf_op jit(solution)/shard_map/pallas_call | solution.py:289
  44.8 6.4 %all-to-all-start = ((bf16[16,8,1024]{2,1,0:T(8,128)(2,1)}), bf16[16,8,1024]{2,1,0:T(8,128)(2,1)}, u32[]{:S(2)}, u32[]{:S(2)}) async-start(bf16[16,8,1024]{2,1,0:T(8,128)(2,1)} %bitcast.4), calls=%async_computation | async-start | bytes 524288 | tf_op jit(solution)/shard_map/all_to_all | solution.py:367
  52.9 1.6 %copy-done.7 = bf16[1024,1024]{1,0:T(8,128)(2,1)S(1)} copy-done((bf16[1024,1024]{1,0:T(8,128)(2,1)S(1)}, bf16[1024,1024]{1,0:T(8,128)(2,1)}, u32[]{:S(2)}) %copy-start.7) | copy-done | bytes 2097176
  57.3 9.4 %shard_map.125 = (bf16[768,1024]{1,0:T(8,128)(2,1)S(1)}, bf16[768,1024]{1,0:T(8,128)(2,1)S(1)}) custom-call(bf16[768,1024]{1,0:T(8,128)(2,1)S(1)} %copy-done.4, bf16[1024,1024]{1,0:T(8,128)(2,1)S(1)} %copy-done.7, bf16[768,1024]{1,0:T(8,128)(2,1)S(1)} %copy-done.9, bf16[768,1024]{1,0:T(8,128)(2,1)S(1)} %copy-done.11, bf16[2,1024,128]{2,1,0:T(8,128)(2,1)S(1)} %copy-done.19), custom_call_target="tpu_custom_call" | custom-call | flops 2415919104 | bytes 6291456 | tf_op jit(solution)/shard_map/pallas_call | solution.py:214
  69.1 2.4 %fusion.3 = bf16[16,8,256]{2,1,0:T(8,128)(2,1)} fusion(bf16[1024,256]{1,0:T(8,128)(2,1)} %param.17, bf16[128,1024]{1,0:T(8,128)(2,1)} %bitcast.5, bf16[1024,1024]{1,0:T(8,128)(2,1)S(1)} %copy-done), kind=kOutput, calls=%fused_computation.4 | convolution fusion | flops 335839232 | bytes 2949120 | tf_op jit(solution)/shard_map/dot_general | solution.py:20
  71.5 5.9 %all-to-all-start.1 = ((bf16[16,8,256]{2,1,0:T(8,128)(2,1)}), bf16[16,8,256]{2,1,0:T(8,128)(2,1)S(1)}, u32[]{:S(2)}, u32[]{:S(2)}) async-start(bf16[16,8,256]{2,1,0:T(8,128)(2,1)} %fusion.3), calls=%async_computation.1 | async-start | bytes 131072 | tf_op jit(solution)/shard_map/all_to_all | solution.py:367
  77.4 1.6 %copy-done.2 = bf16[1024,1024]{1,0:T(8,128)(2,1)S(1)} copy-done((bf16[1024,1024]{1,0:T(8,128)(2,1)S(1)}, bf16[1024,1024]{1,0:T(8,128)(2,1)}, u32[]{:S(2)}) %copy-start.2) | copy-done | bytes 2097176
  79.0 1.4 %copy-done.5 = bf16[768,1024]{1,0:T(8,128)(2,1)S(1)} copy-done((bf16[768,1024]{1,0:T(8,128)(2,1)S(1)}, bf16[768,1024]{1,0:T(8,128)(2,1)}, u32[]{:S(2)}) %copy-start.5) | copy-done | bytes 1572888
  80.4 1.4 %copy-done.13 = bf16[768,1024]{1,0:T(8,128)(2,1)S(1)} copy-done((bf16[768,1024]{1,0:T(8,128)(2,1)S(1)}, bf16[768,1024]{1,0:T(8,128)(2,1)}, u32[]{:S(2)}) %copy-start.13) | copy-done | bytes 1572888
  81.8 1.4 %copy-done.15 = bf16[768,1024]{1,0:T(8,128)(2,1)S(1)} copy-done((bf16[768,1024]{1,0:T(8,128)(2,1)S(1)}, bf16[768,1024]{1,0:T(8,128)(2,1)}, u32[]{:S(2)}) %copy-start.15) | copy-done | bytes 1572888
  83.3 3.5 %shard_map.126 = bf16[768,1024]{1,0:T(8,128)(2,1)} custom-call(bf16[768,1024]{1,0:T(8,128)(2,1)S(1)} %copy-done.5, bf16[768,1024]{1,0:T(8,128)(2,1)S(1)} %copy-done.13, bf16[768,1024]{1,0:T(8,128)(2,1)S(1)} %copy-done.15, bf16[1024,1024]{1,0:T(8,128)(2,1)S(1)} %copy-done.2, bf16[256,128]{1,0:T(8,128)(2,1)S(1)} %get-tuple-element.73.refs_0_, ...), custom_call_target="tpu_custom_call" | custom-call | flops 1610612736 | bytes 7864320 | tf_op jit(solution)/shard_map/pallas_call | solution.py:323
  (53 shorter events, 11.8 us)
Async XLA Ops:
  0.6 68.4 %copy-start = (bf16[1024,1024]{1,0:T(8,128)(2,1)S(1)}, bf16[1024,1024]{1,0:T(8,128)(2,1)}, u32[]{:S(2)}) copy-start(bf16[1024,1024]{1,0:T(8,128)(2,1)} %param.16) | copy-start | bytes 6291460
  0.7 11.5 %copy-start.16 = (s32[32,2]{0,1:T(2,128)S(1)}, s32[32,2]{0,1:T(2,128)}, u32[]{:S(2)}) copy-start(s32[32,2]{0,1:T(2,128)} %param.20) | copy-start | bytes 772
  0.7 11.5 %copy-start.17 = (s32[32]{0:T(128)S(1)}, s32[32]{0:T(128)}, u32[]{:S(2)}) copy-start(s32[32]{0:T(128)} %param.19) | copy-start | bytes 388
  0.7 11.4 %copy-start.18 = (s32[32]{0:T(128)S(1)}, s32[32]{0:T(128)}, u32[]{:S(2)}) copy-start(s32[32]{0:T(128)} %param.21) | copy-start | bytes 388
  8.9 13.3 %collective-permute-start = (bf16[256,128]{1,0:T(8,128)(2,1)}, bf16[256,128]{1,0:T(8,128)(2,1)S(1)}, u32[]{:S(2)}, u32[]{:S(2)}) collective-permute-start(bf16[256,128]{1,0:T(8,128)(2,1)} %get-tuple-element.38), channel_id=1, source_target_pairs={{0,1},{1,0},{2,3},{3,2},{4,5},{5,4},{6,7},{7,6},{8,9},{9,8},{10,11... | collective-permute-start | bytes 196616 | tf_op jit(solution)/shard_map/ppermute | solution.py:233
  9.5 12.8 %collective-permute-start.1 = (bf16[256,128]{1,0:T(8,128)(2,1)}, bf16[256,128]{1,0:T(8,128)(2,1)S(1)}, u32[]{:S(2)}, u32[]{:S(2)}) collective-permute-start(bf16[256,128]{1,0:T(8,128)(2,1)} %get-tuple-element.39), channel_id=1, source_target_pairs={{0,2},{1,3},{2,0},{3,1},{4,6},{5,7},{6,4},{7,5},{8,10},{9,11},{10,... | collective-permute-start | bytes 196616 | tf_op jit(solution)/shard_map/ppermute | solution.py:233
  12.0 10.2 %collective-permute-start.2 = (bf16[256,128]{1,0:T(8,128)(2,1)}, bf16[256,128]{1,0:T(8,128)(2,1)S(1)}, u32[]{:S(2)}, u32[]{:S(2)}) collective-permute-start(bf16[256,128]{1,0:T(8,128)(2,1)} %get-tuple-element.40), channel_id=1, source_target_pairs={{0,3},{1,2},{2,1},{3,0},{4,7},{5,6},{6,5},{7,4},{8,11},{9,10},{10,... | collective-permute-start | bytes 196616 | tf_op jit(solution)/shard_map/ppermute | solution.py:233
  12.1 1.4 %copy-start.3 = (bf16[768,1024]{1,0:T(8,128)(2,1)S(1)}, bf16[768,1024]{1,0:T(8,128)(2,1)}, u32[]{:S(2)}) copy-start(bf16[768,1024]{1,0:T(8,128)(2,1)} %events.7) | copy-start | bytes 4718596
  13.5 1.6 %copy-start.6 = (bf16[1024,1024]{1,0:T(8,128)(2,1)S(1)}, bf16[1024,1024]{1,0:T(8,128)(2,1)}, u32[]{:S(2)}) copy-start(bf16[1024,1024]{1,0:T(8,128)(2,1)} %w_query.3) | copy-start | bytes 6291460
  15.1 1.4 %copy-start.8 = (bf16[768,1024]{1,0:T(8,128)(2,1)S(1)}, bf16[768,1024]{1,0:T(8,128)(2,1)}, u32[]{:S(2)}) copy-start(bf16[768,1024]{1,0:T(8,128)(2,1)} %get-tuple-element.61.keys) | copy-start | bytes 4718596
  17.9 4.3 %copy-start.20 = (bf16[256,128]{1,0:T(8,128)(2,1)S(1)}, bf16[256,128]{1,0:T(8,128)(2,1)}, u32[]{:S(2)}) copy-start(bf16[256,128]{1,0:T(8,128)(2,1)} %get-tuple-element.55) | copy-start | bytes 196612
  22.3 28.9 %copy-start.21 = (bf16[1024,32]{0,1:T(8,128)(2,1)S(1)}, bf16[1024,32]{0,1:T(8,128)(2,1)}, u32[]{:S(2)}) copy-start(bf16[1024,32]{0,1:T(8,128)(2,1)} %param.18) | copy-start | bytes 196612
  22.3 5.7 %collective-permute-start.3 = (bf16[256,128]{1,0:T(8,128)(2,1)S(1)}, bf16[256,128]{1,0:T(8,128)(2,1)S(1)}, u32[]{:S(2)}, u32[]{:S(2)}) collective-permute-start(bf16[256,128]{1,0:T(8,128)(2,1)S(1)} %fusion.24), channel_id=1, source_target_pairs={{0,4},{1,5},{2,6},{3,7},{4,8},{5,9},{6,10},{7,11},{8,12},{9,13},{1... | collective-permute-start | bytes 196616 | tf_op jit(solution)/shard_map/ppermute | solution.py:237
  28.1 23.4 %copy-start.19 = (bf16[2,1024,128]{2,1,0:T(8,128)(2,1)S(1)}, bf16[2,1024,128]{2,1,0:T(8,128)(2,1)}, u32[]{:S(2)}) copy-start(bf16[2,1024,128]{2,1,0:T(8,128)(2,1)} %get-tuple-element.63.inner) | copy-start | bytes 1572868
  28.1 7.4 %collective-permute-start.4 = (bf16[256,128]{1,0:T(8,128)(2,1)S(1)}, bf16[256,128]{1,0:T(8,128)(2,1)S(1)}, u32[]{:S(2)}, u32[]{:S(2)}) collective-permute-start(bf16[256,128]{1,0:T(8,128)(2,1)S(1)} %fusion.6), channel_id=1, source_target_pairs={{0,8},{1,9},{2,10},{3,11},{4,12},{5,13},{6,14},{7,15},{16,24},{17,... | collective-permute-start | bytes 196616 | tf_op jit(solution)/shard_map/ppermute | solution.py:237
  35.6 4.4 %collective-permute-start.7 = (bf16[256,128]{1,0:T(8,128)(2,1)S(1)}, bf16[256,128]{1,0:T(8,128)(2,1)S(1)}, u32[]{:S(2)}, u32[]{:S(2)}) collective-permute-start(bf16[256,128]{1,0:T(8,128)(2,1)S(1)} %get-tuple-element.72), channel_id=1, source_target_pairs={{0,3},{1,2},{2,1},{3,0},{4,7},{5,6},{6,5},{7,4},{8,11},{9,10},{10,... | collective-permute-start | bytes 196616 | tf_op jit(solution)/shard_map/ppermute | solution.py:233
  35.7 4.3 %collective-permute-start.5 = (bf16[256,128]{1,0:T(8,128)(2,1)S(1)}, bf16[256,128]{1,0:T(8,128)(2,1)S(1)}, u32[]{:S(2)}, u32[]{:S(2)}) collective-permute-start(bf16[256,128]{1,0:T(8,128)(2,1)S(1)} %get-tuple-element.74), channel_id=1, source_target_pairs={{0,1},{1,0},{2,3},{3,2},{4,5},{5,4},{6,7},{7,6},{8,9},{9,8},{10,11... | collective-permute-start | bytes 196616 | tf_op jit(solution)/shard_map/ppermute | solution.py:233
  37.3 4.3 %collective-permute-start.6 = (bf16[256,128]{1,0:T(8,128)(2,1)S(1)}, bf16[256,128]{1,0:T(8,128)(2,1)S(1)}, u32[]{:S(2)}, u32[]{:S(2)}) collective-permute-start(bf16[256,128]{1,0:T(8,128)(2,1)S(1)} %get-tuple-element.75), channel_id=1, source_target_pairs={{0,2},{1,3},{2,0},{3,1},{4,6},{5,7},{6,4},{7,5},{8,10},{9,11},{10,... | collective-permute-start | bytes 196616 | tf_op jit(solution)/shard_map/ppermute | solution.py:233
  41.6 1.6 %copy-start.1 = (bf16[1024,1024]{1,0:T(8,128)(2,1)S(1)}, bf16[1024,1024]{1,0:T(8,128)(2,1)}, u32[]{:S(2)}) copy-start(bf16[1024,1024]{1,0:T(8,128)(2,1)} %w_output.3) | copy-start | bytes 6291460
  44.8 24.3 %all-to-all-start = ((bf16[16,8,1024]{2,1,0:T(8,128)(2,1)}), bf16[16,8,1024]{2,1,0:T(8,128)(2,1)}, u32[]{:S(2)}, u32[]{:S(2)}) async-start(bf16[16,8,1024]{2,1,0:T(8,128)(2,1)} %bitcast.4), calls=%async_computation | async-start | bytes 524288 | tf_op jit(solution)/shard_map/all_to_all | solution.py:367
  51.5 1.4 %copy-start.4 = (bf16[768,1024]{1,0:T(8,128)(2,1)S(1)}, bf16[768,1024]{1,0:T(8,128)(2,1)}, u32[]{:S(2)}) copy-start(bf16[768,1024]{1,0:T(8,128)(2,1)} %events.7) | copy-start | bytes 4718596
  52.9 1.6 %copy-start.7 = (bf16[1024,1024]{1,0:T(8,128)(2,1)S(1)}, bf16[1024,1024]{1,0:T(8,128)(2,1)}, u32[]{:S(2)}) copy-start(bf16[1024,1024]{1,0:T(8,128)(2,1)} %w_query.3) | copy-start | bytes 6291460
  71.5 15.3 %all-to-all-start.1 = ((bf16[16,8,256]{2,1,0:T(8,128)(2,1)}), bf16[16,8,256]{2,1,0:T(8,128)(2,1)S(1)}, u32[]{:S(2)}, u32[]{:S(2)}) async-start(bf16[16,8,256]{2,1,0:T(8,128)(2,1)} %fusion.3), calls=%async_computation.1 | async-start | bytes 131072 | tf_op jit(solution)/shard_map/all_to_all | solution.py:367
  77.4 1.6 %copy-start.2 = (bf16[1024,1024]{1,0:T(8,128)(2,1)S(1)}, bf16[1024,1024]{1,0:T(8,128)(2,1)}, u32[]{:S(2)}) copy-start(bf16[1024,1024]{1,0:T(8,128)(2,1)} %w_output.3) | copy-start | bytes 6291460
  (8 other events, 10.8 us)

commit v4 on v3

v4 whole, which is shorter than its diff:
```python
import functools

import jax
import jax.numpy as jnp
from jax import lax
from jax.experimental import pallas as pl
from jax.experimental.pallas import tpu as pltpu
from jax.sharding import PartitionSpec as P

HEADS = 8
EXPERTS = 16
CAP = 8
PLANE = 4
F32 = jnp.float32
BF16 = jnp.bfloat16
MIB = 1 << 20


def dot(a, b, contract=((1,), (0,)), **kw):
    return lax.dot_general(a, b, (contract, ((), ())), preferred_element_type=F32, **kw)


def call(kernel, grid, in_specs, out_specs, out_shape, flops, moved, scratch=(), vmem=60):
    return pl.pallas_call(
        kernel,
        grid=grid,
        in_specs=in_specs,
        out_specs=out_specs,
        out_shape=out_shape,
        scratch_shapes=scratch,
        compiler_params=pltpu.CompilerParams(vmem_limit_bytes=vmem * MIB),
        cost_estimate=pl.CostEstimate(flops=flops, bytes_accessed=moved, transcendentals=0),
    )


FAR = pl.BlockSpec(memory_space=pltpu.HBM)
VMEM = pl.BlockSpec(memory_space=pltpu.VMEM)


def near(kernel, out_shape, flops, moved, scratch=(), vmem=10):
    return pl.pallas_call(
        kernel,
        out_shape=out_shape,
        scratch_shapes=scratch,
        compiler_params=pltpu.CompilerParams(vmem_limit_bytes=vmem * MIB),
        cost_estimate=pl.CostEstimate(flops=flops, bytes_accessed=moved, transcendentals=0),
    )


def whole(shape):
    return pl.BlockSpec(shape, lambda *_: (0,) * len(shape))


def columns(rows, cols):
    return pl.BlockSpec((rows, cols), lambda i: (0, i))


def shaped(shape, kind):
    return jax.ShapeDtypeStruct(shape, kind)


def key_value_kernel(head_dim, tile, events, w_key, w_value, keys, values, inner, *states):
    k = dot(events[...], w_key[...]).astype(BF16)
    v = dot(events[...], w_value[...]).astype(BF16)
    keys[...] = k
    values[...] = v
    total = None
    for i in range(events.shape[0] // tile):
        here = slice(i * tile, (i + 1) * tile)
        if i:
            inner[i - 1] = total.astype(BF16)
        both = dot(k[here], v[here], ((0,), (0,)))
        parts = [slice(h * head_dim, (h + 1) * head_dim) for h in range(both.shape[0] // head_dim)]
        own = jnp.concatenate([both[part, part] for part in parts], axis=0)
        total = own if total is None else total + own
    for i, state in enumerate(states):

        @pl.when(pl.program_id(0) == i)
        def _():
            state[...] = total.astype(BF16)


def key_value_state(events, w_key, w_value):
    rows, width = events.shape
    head_dim = width // HEADS
    pair = width // PLANE
    tile = row_tile(rows)
    inner = rows // tile - 1

    def turn(i):
        return i ^ (lax.axis_index("seq") % PLANE)

    def cols(many):
        return pl.BlockSpec((many, pair), lambda i: (0, turn(i)))

    return call(
        functools.partial(key_value_kernel, head_dim, tile),
        (PLANE,),
        [whole((rows, width)), cols(width), cols(width)],
        [cols(rows), cols(rows), pl.BlockSpec((inner, pair, head_dim), lambda i: (0, turn(i), 0))]
        + [whole((pair, head_dim))] * PLANE,
        [shaped((rows, width), BF16)] * 2
        + [shaped((inner, width, head_dim), BF16)]
        + [shaped((pair, head_dim), BF16)] * PLANE,
        4 * rows * width * width,
        8 * rows * width,
    )(events, w_key, w_value)


def row_tile(rows):
    return 256 if rows % 256 == 0 and rows > 256 else rows // 2


def labelled_kernel(head_dim, copies, events_far, w_query_far, keys_far, values_far, labels, experts, tasks, *refs):
    (packed, match, column), (events, w_query, keys, values, done) = refs[:3], refs[3:]
    fetches = []
    for far, here in ((events_far, events), (w_query_far, w_query), (keys_far, keys), (values_far, values)):
        fetches.append(pltpu.make_async_copy(far, here, done.at[len(fetches)]))
        fetches[-1].start()
    rows, width = events.shape
    many = labels.shape[1]

    start = lax.axis_index("seq") * rows + 1
    factor = upright(lax.rsqrt((labels[...] + start).astype(F32) * head_dim))
    places = [upright(p) for p in slot_of(experts[...])]
    target = slot_place(match.shape[1:], 1, copies)
    number = lax.broadcasted_iota(jnp.int32, column.shape[1:], 1)
    found = [jnp.where(target == place, 1.0, 0.0) for place in places]
    packed[:, 3 * width : 3 * width + head_dim] = jnp.broadcast_to(factor, (many, head_dim))
    packed[:, 3 * width + head_dim :] = found[0] + found[1]
    for k in range(2):
        match[k] = found[k].astype(BF16)
        chosen_column = upright(tasks[...] * EXPERTS + experts[k : k + 1, :])
        column[k] = jnp.where(number == chosen_column, 1.0, 0.0)
    chosen = row_choice(labels[...], rows)
    causal = lax.broadcasted_iota(jnp.int32, (many, rows), 1) <= upright(labels[...])
    parts = [slice(h, h + head_dim) for h in range(0, width, head_dim)]

    fetches[0].wait()
    chosen_events = dot(chosen, events[...]).astype(BF16)
    packed[:, width : 2 * width] = chosen_events.astype(F32)
    fetches[1].wait()
    query = dot(chosen_events, w_query[...]).astype(BF16)
    packed[:, :width] = query.astype(F32)
    fetches[2].wait()
    weights = [dot(query[:, part], keys[:, part], ((1,), (1,))) for part in parts]
    weights = [jnp.where(causal, weight, 0.0).astype(BF16) for weight in weights]
    fetches[3].wait()
    for part, weight in zip(parts, weights):
        packed[:, 2 * width + part.start : 2 * width + part.stop] = dot(weight, values[:, part])


def labelled_rows(events, w_query, keys, values, labels, experts, tasks, devices):
    rows, width = events.shape
    many = labels.shape[1]
    slots = devices * CAP
    return call(
        functools.partial(labelled_kernel, width // HEADS, devices // EXPERTS),
        (),
        [FAR] * 4 + [VMEM] * 3,
        [VMEM] * 3,
        [shaped((many, 3 * width + width // HEADS + slots), F32)]
        + [shaped((2, many, slots), BF16), shaped((2, many, 2 * EXPERTS), F32)],
        4 * many * rows * width,
        8 * rows * width,
        [pltpu.VMEM(x.shape, BF16) for x in (events, w_query, keys, values)] + [pltpu.SemaphoreType.DMA((4,))],
    )(events, w_query, keys, values, labels, experts, tasks)


def unpacked(packed, width, head_dim):
    query, events, within = (packed[:, i * width : (i + 1) * width] for i in range(3))
    factor = packed[:, 3 * width : 3 * width + head_dim]
    slots = packed[:, 3 * width + head_dim :]
    return query.astype(BF16), events.astype(BF16), within * factor[:, :1], factor, slots.astype(BF16)


def slot_of(experts):
    many = experts.shape[1]
    number = lax.broadcasted_iota(jnp.int32, (EXPERTS, many), 0)
    ones = [jnp.where(number == experts[k : k + 1, :], 1.0, 0.0) for k in range(2)]
    earlier = lax.broadcasted_iota(jnp.int32, (many, many), 0) < lax.broadcasted_iota(jnp.int32, (many, many), 1)
    strict = jnp.where(earlier, 1.0, 0.0).astype(BF16)
    first = dot(ones[0].astype(BF16), strict)
    second = dot(ones[1].astype(BF16), strict) + jnp.sum(ones[0], axis=1, keepdims=True)
    slots = [jnp.sum(o * c, axis=0, keepdims=True).astype(jnp.int32) for o, c in zip(ones, (first, second))]
    return [experts[k : k + 1, :] * CAP + slots[k] for k in range(2)]


def slot_place(shape, axis, copies):
    row = lax.broadcasted_iota(jnp.int32, shape, axis)
    return row if copies == 1 else (row // (copies * CAP)) * CAP + row % CAP


def within_kernel(head_dim, tile, events, w_query, keys, values, inner, query, within):
    rows = events.shape[0]
    q = dot(events[...], w_query[...]).astype(BF16)
    query[...] = q
    half = tile // 2
    spot = lax.broadcasted_iota(jnp.int32, (half, 2 * half), 0)
    causal = lax.broadcasted_iota(jnp.int32, (half, 2 * half), 1) % half <= spot

    def masked(weight):
        return jnp.where(causal, weight, 0.0).astype(BF16)

    tiles = range(rows // tile)
    heres = [slice(i * tile, (i + 1) * tile) for i in tiles]
    firsts = [slice(i * tile, i * tile + half) for i in tiles]
    seconds = [slice(i * tile + half, (i + 1) * tile) for i in tiles]
    early = [dot(q[heres[i]], heads_apart(keys[firsts[i], :], head_dim), ((1,), (1,))) for i in tiles]
    late = [dot(q[seconds[i]], heads_apart(keys[seconds[i], :], head_dim), ((1,), (1,))) for i in tiles]
    before = [dot(q[heres[i]], on_diagonal(inner[i - 1], head_dim)) for i in tiles if i]
    early = [jnp.concatenate([masked(w[:half]), w[half:].astype(BF16)], axis=0) for w in early]
    late = [masked(w) for w in late]
    early = [dot(early[i], heads_apart(values[firsts[i], :], head_dim)) for i in tiles]
    late = [dot(late[i], heads_apart(values[seconds[i], :], head_dim)) for i in tiles]
    for i in tiles:
        total = jnp.concatenate([early[i][:half], early[i][half:] + late[i]], axis=0)
        if i:
            total = total + before[i - 1]
        within[heres[i], :] = total.astype(BF16)


def heads_apart(block, head_dim):
    return on_diagonal(jnp.concatenate([block[:, :head_dim], block[:, head_dim:]], axis=0), head_dim, block.shape[0])


def upright(row):
    many = row.shape[1]
    diagonal = lax.broadcasted_iota(jnp.int32, (many, many), 0) == lax.broadcasted_iota(jnp.int32, (many, many), 1)
    return jnp.sum(jnp.where(diagonal, row, jnp.zeros_like(row)), axis=1, keepdims=True)


def row_choice(labels, rows):
    number = lax.broadcasted_iota(jnp.int32, (labels.shape[1], rows), 1)
    return jnp.where(number == upright(labels), 1.0, 0.0).astype(BF16)


def on_diagonal(block, head_dim, rows=None):
    rows = rows or head_dim
    empty = jnp.zeros((rows, head_dim), block.dtype)
    first = jnp.concatenate([block[:rows], empty], axis=1)
    second = jnp.concatenate([empty, block[rows:]], axis=1)
    return jnp.concatenate([first, second], axis=0)


def queries_within(events, w_query, keys, values, inner):
    rows, width = events.shape
    head_dim = width // HEADS
    pair = width // PLANE
    tile = row_tile(rows)
    return call(
        functools.partial(within_kernel, head_dim, tile),
        (width // pair,),
        [
            whole((rows, width)),
            columns(width, pair),
            columns(rows, pair),
            columns(rows, pair),
            pl.BlockSpec((inner.shape[0], pair, head_dim), lambda i: (0, i, 0)),
        ],
        [columns(rows, pair), columns(rows, pair)],
        [shaped((rows, width), BF16)] * 2,
        2 * rows * width * width + 4 * tile * rows * width,
        8 * rows * width,
    )(events, w_query, keys, values, inner)


def flip(x, j):
    devices = lax.axis_size("seq")
    return lax.ppermute(x, "seq", [(i, i ^ j) for i in range(devices)])


def later(x, s):
    return lax.ppermute(x, "seq", [(i, i + s) for i in range(lax.axis_size("seq") - s)])


def swapped(states):
    return [states[0]] + [flip(x, j) for j, x in enumerate(states) if j]


def sums_before(states):
    devices = lax.axis_size("seq")
    rank = lax.axis_index("seq") % PLANE
    states = [x.astype(F32) for x in states]
    total = sum(states).astype(BF16)
    planes = sum(later(total, s).astype(F32) for s in reversed(range(PLANE, devices, PLANE)))
    before = []
    for j in range(PLANE):
        held = [jnp.where((rank ^ i) < (rank ^ j), states[i], 0.0) for i in range(PLANE) if i != j]
        before.append((planes + sum(held)).astype(BF16))
    return before


def earlier_terms(query, prefix, head_dim):
    pair = query.shape[1] // PLANE
    terms = [dot(query[:, p * pair : (p + 1) * pair], prefix[p]) for p in range(PLANE)]
    return jnp.concatenate(terms, axis=1)


def put_prefix(prefix, parts, head_dim):
    rank = lax.axis_index("seq") % PLANE
    for j, part in enumerate(parts):
        prefix[rank ^ j] = on_diagonal(part[...], head_dim)


def picked_kernel(head_dim, query_at, events_at, within_at, factor, selector, w_output, *refs):
    parts, (picked, outgoing, prefix) = refs[:PLANE], refs[PLANE:]
    put_prefix(prefix, parts, head_dim)
    earlier = earlier_terms(query_at[...], prefix, head_dim)
    attended = (within_at[...] + earlier * factor[:, :1]).astype(BF16)
    rows = (events_at[...].astype(F32) + dot(attended, w_output[...])).astype(BF16)
    picked[...] = rows
    outgoing[...] = dot(selector[...], rows, ((0,), (0,))).astype(BF16)


def picked_rows(query_at, events_at, within_at, factor, selector, w_output, prefix):
    many, width = query_at.shape
    slots = selector.shape[1]
    pair = width // PLANE
    return near(
        functools.partial(picked_kernel, width // HEADS),
        [shaped((many, width), BF16), shaped((slots, width), BF16)],
        2 * many * width * width,
        2 * width * width,
        [pltpu.VMEM((PLANE, pair, pair), BF16)],
    )(query_at, events_at, within_at, factor, selector, w_output, *prefix)


def hidden_kernel(head_dim, tile, *refs):
    events_far, query_far, within_far, w_output_far = refs[:4]
    parts_far, hidden_far = refs[4 : 4 + PLANE], refs[4 + PLANE]
    events, query, within, w_output, parts, hidden, prefix, done, sent = refs[5 + PLANE :]
    rows = events.shape[0]
    tiles = range(rows // tile)
    strips = [slice(i * tile, (i + 1) * tile) for i in tiles]
    number = iter(range(done.shape[0]))

    def fetch(far, here):
        copy = pltpu.make_async_copy(far, here, done.at[next(number)])
        copy.start()
        return copy

    def fetch_strip(far, here, i):
        return fetch(far.at[strips[i], :], here.at[strips[i], :])

    parts_in = [fetch(far, parts.at[j]) for j, far in enumerate(parts_far)]
    query_in = [fetch_strip(query_far, query, 0)]
    within_in = [fetch_strip(within_far, within, 0)]
    w_output_in = fetch(w_output_far, w_output)
    events_in = [fetch_strip(events_far, events, 0)]
    for i in tiles[1:]:
        query_in.append(fetch_strip(query_far, query, i))
        within_in.append(fetch_strip(within_far, within, i))
        events_in.append(fetch_strip(events_far, events, i))
    for copy in parts_in:
        copy.wait()
    put_prefix(prefix, [parts.at[j] for j in range(PLANE)], head_dim)
    results = []
    for i, strip in enumerate(strips):
        query_in[i].wait()
        within_in[i].wait()
        start = lax.axis_index("seq") * rows + i * tile + 1
        place = (lax.broadcasted_iota(jnp.int32, (tile, 1), 0) + start).astype(F32)
        total = within[strip, :].astype(F32) + earlier_terms(query[strip, :], prefix, head_dim)
        attended = (total * lax.rsqrt(place * head_dim)).astype(BF16)
        if not i:
            w_output_in.wait()
        events_in[i].wait()
        hidden[strip, :] = (events[strip, :].astype(F32) + dot(attended, w_output[...])).astype(BF16)
        results.append(pltpu.make_async_copy(hidden.at[strip, :], hidden_far.at[strip, :], sent.at[i]))
        results[-1].start()
    for copy in results:
        copy.wait()


def hidden_rows(events, query, within, prefix, w_output):
    rows, width = events.shape
    head_dim = width // HEADS
    tile = row_tile(rows)
    pair = width // PLANE
    tiles = rows // tile
    return call(
        functools.partial(hidden_kernel, head_dim, tile),
        (),
        [FAR] * (4 + PLANE),
        FAR,
        shaped((rows, width), BF16),
        2 * rows * width * width,
        10 * rows * width,
        [pltpu.VMEM((rows, width), BF16)] * 3
        + [pltpu.VMEM((width, width), BF16), pltpu.VMEM((PLANE, pair, head_dim), BF16)]
        + [pltpu.VMEM((rows, width), BF16), pltpu.VMEM((PLANE, pair, pair), BF16)]
        + [pltpu.SemaphoreType.DMA((PLANE + 1 + 3 * tiles,)), pltpu.SemaphoreType.DMA((tiles,))],
    )(events, query, within, w_output, *prefix)


def expert_rows(rows, weight_in, weight_out):
    inner = jnp.maximum(dot(rows, weight_in), 0.0).astype(BF16)
    return dot(inner, weight_out).astype(BF16)


def score_rows(picked, gate_weight, column, match, back):
    logits = dot(picked, gate_weight)
    gates = jax.nn.sigmoid(jnp.sum(logits[None] * column, axis=2))
    choices, many, slots = match.shape
    chosen = dot(match.reshape(choices * many, slots), back).reshape(choices, many, -1)
    return jnp.sum(gates[:, :, None] * chosen, axis=0)


def shards(
    events,
    w_query,
    w_key,
    w_value,
    w_output,
    expert_in,
    expert_out,
    gate_weight,
    label_rows,
    label_experts,
    label_tasks,
):
    devices = lax.axis_size("seq")
    width = events.shape[1]
    labels = label_rows.reshape(1, -1)
    tasks = label_tasks.reshape(1, -1)
    experts = label_experts.T

    def exchange(x):
        return lax.all_to_all(x, "seq", split_axis=0, concat_axis=0, tiled=True)

    keys, values, inner, *states = key_value_state(events, w_key, w_value)
    states = swapped(states)
    packed, match, column = labelled_rows(events, w_query, keys, values, labels, experts, tasks, devices)
    labelled = unpacked(packed, width, width // HEADS)
    states, labelled = lax.optimization_barrier((states, labelled))
    before = sums_before(states)
    before, one = lax.optimization_barrier((before, jnp.ones((), BF16)))
    prefix = swapped(before)
    picked, outgoing = picked_rows(*labelled, w_output * one, prefix)
    outgoing, keys, values = lax.optimization_barrier((outgoing, keys, values))
    arrived = exchange(outgoing)
    query, within = queries_within(events, w_query, keys, values, inner)
    arrived, query, within = lax.optimization_barrier((arrived, query, within))
    back = exchange(expert_rows(arrived, expert_in, expert_out))
    hidden = hidden_rows(events, query, within, prefix, w_output)
    return hidden, score_rows(picked, gate_weight, column, match, back)


def solution(mesh):
    placed = (
        P(("grp", "seq"), None),
        P(),
        P(),
        P(),
        P(),
        P(None, "seq"),
        P("seq", None),
        P(),
        P(("grp", "seq")),
        P(("grp", "seq"), None),
        P(("grp", "seq")),
    )
    return jax.shard_map(
        shards,
        mesh=mesh,
        in_specs=placed,
        out_specs=(P(("grp", "seq"), None), P(("grp", "seq"), None)),
        check_vma=False,
    )
```

time: 88.4 us -> 71.8 us (0.81)
  local copies, waits for them, and re-layouts: 21.4 us -> 1.61 us
  other arithmetic: 0.36 us -> 4.07 us
  Pallas kernels: 27 us -> 30.5 us
  waiting for transfers between devices: 7.52 us -> 5.02 us
  matrix products: 3.29 us -> 2.15 us
    unnamed x44 -> x20, local copies, waits for them, and re-layouts: 21.4 us -> 0.05 us
    mul x0 -> x2, other arithmetic: none -> 2.71 us  [the longest x1 1.73 us: shards(): picked, outgoing = picked_rows(*labelled, w_output * one, prefix)]
    pallas_call x3, Pallas kernels: 13.4 us -> 15.7 us  [the longest x1 8.32 us: key_value_state(): call(functools.partial(key_value_kernel, head_dim, tile), (PLANE,), [whol...]
    ppermute x2 -> x3, waiting for transfers between devices: 3.75 us -> 1.84 us  [later(): lax.ppermute(x, 'seq', [(i, i + s) for i in range(lax.axis_size('seq') -...]
    ppermute x6, waiting for transfers between devices: 3.76 us -> 2 us  [flip(): return lax.ppermute(x, 'seq', [(i, i ^ j) for i in range(devices)])]
    slice x0 -> x4, local copies, waits for them, and re-layouts: none -> 1.56 us  [the longest x1 0.83 us: unpacked(): factor[:, :1]]
    all_to_all x2, waiting for transfers between devices: 0.01 us -> 1.18 us  [exchange(): return lax.all_to_all(x, 'seq', split_axis=0, concat_axis=0, tiled=True)]
    dot_general x3, matrix products: 3.29 us -> 2.15 us  [dot(): lax.dot_general(a, b, (contract, ((), ())), preferred_element_type=F32, *...]
  transfers between devices with their start and end apart: 10 -> 11, of which waited for: 4 -> 6; matrix products, arithmetic and copies ran while one was open for 0% -> 8% of each run, Pallas kernels for 20% -> 29%
where the time goes in v4:
time: 71.8 us; the launch traced here: 71.2 us
  Pallas kernels  30.5 us (42%)
  starting transfers between devices  26.9 us (37%)
  waiting for transfers between devices  5.02 us (7%)
  other arithmetic  4.07 us (6%)
  matrix products  2.15 us (3%)
  local copies, waits for them, and re-layouts  1.61 us (2%)
  between operations  0.88 us (1%)
    all_to_all x2, starting transfers between devices, exchange(): return lax.all_to_all(x, 'seq', split_axis=0, concat_axis=0, tiled=True)  12.3 us
    pallas_call x1, Pallas kernels, queries_within(): call(functools.partial(within_kernel, head_dim, tile), (width // pair,),...  9.62 us
    ppermute x3, starting transfers between devices, later(): lax.ppermute(x, 'seq', [(i, i + s) for i in range(lax.axis_size('seq') -...  9.48 us
    pallas_call x1, Pallas kernels, key_value_state(): call(functools.partial(key_value_kernel, head_dim, tile), (PLANE,), [whol...  8.32 us
    pallas_call x1, Pallas kernels, hidden_rows(): call(functools.partial(hidden_kernel, head_dim, tile), (), [FAR] * (4 + P...  5.84 us
    pallas_call x1, Pallas kernels, labelled_rows(): call(functools.partial(labelled_kernel, width // HEADS, devices // EXPERT...  5.22 us
    ppermute x6, starting transfers between devices, flip(): return lax.ppermute(x, 'seq', [(i, i ^ j) for i in range(devices)])  5.11 us
    dot_general x3, matrix products, dot(): lax.dot_general(a, b, (contract, ((), ())), preferred_element_type=F32, *...  2.15 us
  transfers between devices with their start and end apart: 11, of which 6 were waited for; matrix products, arithmetic and copies ran while one was open for 8% of the time, Pallas kernels for 29%

profile of v4, /device:TPU:0, one launch (start us, length us, event | category | flops | bytes accessed | tf_op | source)
XLA Modules:
  0.0 71.2 jit_solution(3802706484144260255)
XLA Ops:
  0.6 8.3 %shard_map.122 = (bf16[768,1024]{1,0:T(8,128)(2,1)}, bf16[768,1024]{1,0:T(8,128)(2,1)}, bf16[2,1024,128]{2,1,0:T(8,128)(2,1)}, bf16[256,128]{1,0:T(8,128)(2,1)},...) custom-call(bf16[768,1024]{1,0:T(8,128)(2,1)} %refs_0_.1, bf16[1024,1024]{1,0:T(8,128)(2,1)} %w_key.1, ...), custom_call_target="tpu_custom_call" | custom-call | flops 3221225472 | bytes 6291456 | tf_op jit(solution)/shard_map/pallas_call | solution.py:96
  9.5 2.6 %collective-permute-start.1 = (bf16[256,128]{1,0:T(8,128)(2,1)}, bf16[256,128]{1,0:T(8,128)(2,1)S(1)}, u32[]{:S(2)}, u32[]{:S(2)}) collective-permute-start(bf16[256,128]{1,0:T(8,128)(2,1)} %get-tuple-element.38), channel_id=1, source_target_pairs={{0,2},{1,3},{2,0},{3,1},{4,6},{5,7},{6,4},{7,5},{8,10},{9,11},{10,... | collective-permute-start | bytes 196616 | tf_op jit(solution)/shard_map/ppermute | solution.py:270
  12.2 5.2 %shard_map.123 = (f32[32,3328]{1,0:T(8,128)}, bf16[2,32,128]{2,1,0:T(8,128)(2,1)}, f32[2,32,32]{2,1,0:T(8,128)}) custom-call(bf16[768,1024]{1,0:T(8,128)(2,1)} %refs_0_.1, bf16[1024,1024]{1,0:T(8,128)(2,1)} %w_query.1, bf16[768,1024]{1,0:T(8,128)(2,1)} %get-tuple-element.59.keys_far.keys, bf16[768,1024]{1,0:T(8,128)(2,1)} %get-tuple-element.60.values_far.values, ...), custom_call_target="tpu_custom_call" | custom-call | flops 100663296 | bytes 6291456 | tf_op jit(solution)/shard_map/pallas_call | solution.py:157
  17.4 0.8 %slice_reduce_fusion = f32[32]{0:T(128)S(1)} fusion(f32[32,3328]{1,0:T(8,128)} %get-tuple-element.42), kind=kLoop, calls=%fused_computation.45 | loop fusion | bytes 256 | tf_op jit(solution)/shard_map/slice | solution.py:174
  18.2 1.0 %convert.5 = bf16[32,3328]{1,0:T(8,128)(2,1)S(1)} convert(f32[32,3328]{1,0:T(8,128)} %get-tuple-element.42) | non-fusion elementwise | flops 106496 | bytes 638976 | tf_op jit(solution)/shard_map/convert.2
  19.2 1.0 %slice_multiply_fusion.within_at = f32[32,1024]{1,0:T(8,128)S(1)} fusion(f32[32,3328]{1,0:T(8,128)} %get-tuple-element.42, f32[32]{0:T(128)S(1)} %slice_reduce_fusion), kind=kLoop, calls=%fused_computation.42 | loop fusion | flops 32768 | bytes 262272 | tf_op jit(solution)/shard_map/mul | solution.py:174
  20.3 0.7 %slice.26.factor = f32[32,128]{1,0:T(8,128)S(1)} slice(f32[32,3328]{1,0:T(8,128)} %get-tuple-element.42), slice={[0:32], [3072:3200]} | slice | bytes 32768 | tf_op jit(solution)/shard_map/slice | solution.py:172
  21.1 3.7 %collective-permute-start.5 = (bf16[256,128]{1,0:T(8,128)(2,1)S(1)}, bf16[256,128]{1,0:T(8,128)(2,1)S(1)}, u32[]{:S(2)}, u32[]{:S(2)}) collective-permute-start(bf16[256,128]{1,0:T(8,128)(2,1)S(1)} %fusion.22), channel_id=1, source_target_pairs={{0,4},{1,5},{2,6},{3,7},{4,8},{5,9},{6,10},{7,11},{8,12},{9,13},{1... | collective-permute-start | bytes 196616 | tf_op jit(solution)/shard_map/ppermute | solution.py:274
  24.8 4.5 %collective-permute-start.4 = (bf16[256,128]{1,0:T(8,128)(2,1)S(1)}, bf16[256,128]{1,0:T(8,128)(2,1)S(1)}, u32[]{:S(2)}, u32[]{:S(2)}) collective-permute-start(bf16[256,128]{1,0:T(8,128)(2,1)S(1)} %fusion.22), channel_id=1, source_target_pairs={{0,8},{1,9},{2,10},{3,11},{4,12},{5,13},{6,14},{7,15},{16,24},{17,... | collective-permute-start | bytes 196616 | tf_op jit(solution)/shard_map/ppermute | solution.py:274
  29.3 1.3 %collective-permute-start.3 = (bf16[256,128]{1,0:T(8,128)(2,1)S(1)}, bf16[256,128]{1,0:T(8,128)(2,1)S(1)}, u32[]{:S(2)}, u32[]{:S(2)}) collective-permute-start(bf16[256,128]{1,0:T(8,128)(2,1)S(1)} %fusion.22), channel_id=1, source_target_pairs={{0,12},{1,13},{2,14},{3,15},{16,28},{17,29},{18,30},{19,31}} | collective-permute-start | bytes 196616 | tf_op jit(solution)/shard_map/ppermute | solution.py:274
  30.6 0.8 %collective-permute-done.4 = bf16[256,128]{1,0:T(8,128)(2,1)S(1)} collective-permute-done((bf16[256,128]{1,0:T(8,128)(2,1)S(1)}, bf16[256,128]{1,0:T(8,128)(2,1)S(1)}, u32[]{:S(2)}, u32[]{:S(2)}) %collective-permute-start.4) | collective-permute-done | bytes 65568 | tf_op jit(solution)/shard_map/ppermute | solution.py:274
  31.4 1.0 %collective-permute-done.3 = bf16[256,128]{1,0:T(8,128)(2,1)S(1)} collective-permute-done((bf16[256,128]{1,0:T(8,128)(2,1)S(1)}, bf16[256,128]{1,0:T(8,128)(2,1)S(1)}, u32[]{:S(2)}, u32[]{:S(2)}) %collective-permute-start.3) | collective-permute-done | bytes 65568 | tf_op jit(solution)/shard_map/ppermute | solution.py:274
  32.7 1.6 %collective-permute-start.7 = (bf16[256,128]{1,0:T(8,128)(2,1)S(1)}, bf16[256,128]{1,0:T(8,128)(2,1)S(1)}, u32[]{:S(2)}, u32[]{:S(2)}) collective-permute-start(bf16[256,128]{1,0:T(8,128)(2,1)S(1)} %get-tuple-element.55), channel_id=1, source_target_pairs={{0,2},{1,3},{2,0},{3,1},{4,6},{5,7},{6,4},{7,5},{8,10},{9,11},{10,... | collective-permute-start | bytes 196616 | tf_op jit(solution)/shard_map/ppermute | solution.py:270
  34.6 1.7 %broadcast_multiply_fusion.w_output = bf16[1024,1024]{1,0:T(8,128)(2,1)S(1)} fusion(bf16[1024,1024]{1,0:T(8,128)(2,1)} %refs_3_.1, bf16[]{:T(256)} %constant.27.clone.1), kind=kLoop, calls=%fused_computation.7 | loop fusion | flops 1048576 | bytes 4194306 | tf_op jit(solution)/shard_map/mul | solution.py:440
  36.3 0.9 %collective-permute-done.7.refs_2_.refs_6_ = bf16[256,128]{1,0:T(8,128)(2,1)S(1)} collective-permute-done((bf16[256,128]{1,0:T(8,128)(2,1)S(1)}, bf16[256,128]{1,0:T(8,128)(2,1)S(1)}, u32[]{:S(2)}, u32[]{:S(2)}) %collective-permute-start.7) | collective-permute-done | bytes 65568 | tf_op jit(solution)/shard_map/ppermute | solution.py:270
  37.2 1.1 %collective-permute-done.8.refs_3_.refs_7_ = bf16[256,128]{1,0:T(8,128)(2,1)S(1)} collective-permute-done((bf16[256,128]{1,0:T(8,128)(2,1)S(1)}, bf16[256,128]{1,0:T(8,128)(2,1)S(1)}, u32[]{:S(2)}, u32[]{:S(2)}) %collective-permute-start.8) | collective-permute-done | bytes 65568 | tf_op jit(solution)/shard_map/ppermute | solution.py:270
  38.3 1.5 %shard_map.124 = (bf16[32,1024]{1,0:T(8,128)(2,1)S(1)}, bf16[128,1024]{1,0:T(8,128)(2,1)}) custom-call(bf16[32,1024]{1,0:T(8,128)(2,1)S(1)} %get-tuple-element.43.query_at, bf16[32,1024]{1,0:T(8,128)(2,1)S(1)} %get-tuple-element.44.events_at, f32[32,1024]{1,0:T(8,128)S(1)} %slice_multiply_fusion.within_at, f32[32,128]{1,0:T(8,128)S(1)} %slice.26.factor, ...), custom_call_target="tpu_custom_call" | custom-call | flops 67108864 | bytes 2097152 | tf_op jit(solution)/shard_map/pallas_call | solution.py:320
  39.9 6.4 %all-to-all-start = ((bf16[16,8,1024]{2,1,0:T(8,128)(2,1)}), bf16[16,8,1024]{2,1,0:T(8,128)(2,1)S(1)}, u32[]{:S(2)}, u32[]{:S(2)}) async-start(bf16[16,8,1024]{2,1,0:T(8,128)(2,1)} %bitcast.3), calls=%async_computation | async-start | bytes 524288 | tf_op jit(solution)/shard_map/all_to_all | solution.py:430
  46.6 9.6 %shard_map.125 = (bf16[768,1024]{1,0:T(8,128)(2,1)}, bf16[768,1024]{1,0:T(8,128)(2,1)}) custom-call(bf16[768,1024]{1,0:T(8,128)(2,1)} %refs_0_.1, bf16[1024,1024]{1,0:T(8,128)(2,1)} %w_query.1, bf16[768,1024]{1,0:T(8,128)(2,1)} %get-tuple-element.59.keys_far.keys, bf16[768,1024]{1,0:T(8,128)(2,1)} %get-tuple-element.60.values_far.values, ...), custom_call_target="tpu_custom_call" | custom-call | flops 2415919104 | bytes 6291456 | tf_op jit(solution)/shard_map/pallas_call | solution.py:251
  56.3 1.3 %fusion.3 = bf16[16,8,256]{2,1,0:T(8,128)(2,1)} fusion(bf16[1024,256]{1,0:T(8,128)(2,1)S(1)} %copy-done.5, bf16[128,1024]{1,0:T(8,128)(2,1)S(1)} %bitcast.18, bf16[1024,1024]{1,0:T(8,128)(2,1)S(1)} %copy-done), kind=kOutput, calls=%fused_computation.4 | convolution fusion | flops 335839232 | bytes 2949120 | tf_op jit(solution)/shard_map/dot_general | solution.py:20
  57.6 5.9 %all-to-all-start.1 = ((bf16[16,8,256]{2,1,0:T(8,128)(2,1)}), bf16[16,8,256]{2,1,0:T(8,128)(2,1)S(1)}, u32[]{:S(2)}, u32[]{:S(2)}) async-start(bf16[16,8,256]{2,1,0:T(8,128)(2,1)} %fusion.3), calls=%async_computation.1 | async-start | bytes 131072 | tf_op jit(solution)/shard_map/all_to_all | solution.py:430
  63.5 5.8 %shard_map.126 = bf16[768,1024]{1,0:T(8,128)(2,1)} custom-call(bf16[768,1024]{1,0:T(8,128)(2,1)} %refs_0_.1, bf16[768,1024]{1,0:T(8,128)(2,1)} %get-tuple-element.64.refs_1_, bf16[768,1024]{1,0:T(8,128)(2,1)} %get-tuple-element.65.refs_2_, bf16[1024,1024]{1,0:T(8,128)(2,1)} %refs_3_.1, bf16[256,128]{1,0:T(8,128)(2,1)} %copy-done.1, ...), custom_call_target="tpu_custom_call" | custom-call | flops 1610612736 | bytes 7864320 | tf_op jit(solution)/shard_map/pallas_call | solution.py:382
  69.4 1.0 %all-to-all-done.1 = bf16[16,8,256]{2,1,0:T(8,128)(2,1)S(1)} async-done(((bf16[16,8,256]{2,1,0:T(8,128)(2,1)}), bf16[16,8,256]{2,1,0:T(8,128)(2,1)S(1)}, u32[]{:S(2)}, u32[]{:S(2)}) %all-to-all-start.1) | async-done | bytes 65568 | tf_op jit(solution)/shard_map/all_to_all | solution.py:430
  70.4 0.8 %fusion.4 = f32[32,256]{1,0:T(8,128)} fusion(bf16[2,32,128]{2,1,0:T(8,128)(2,1)S(1)} %copy-done.9, bf16[16,8,256]{2,1,0:T(8,128)(2,1)S(1)} %all-to-all-done.1, f32[2,32]{1,0:T(2,128)S(1)} %add_divide_fusion), kind=kOutput, calls=%fused_computation.6 | convolution fusion | flops 4218880 | bytes 114944 | tf_op jit(solution)/shard_map/dot_general | solution.py:20
  (37 shorter events, 1.6 us)
Async XLA Ops:
  0.6 55.7 %copy-start = (bf16[1024,1024]{1,0:T(8,128)(2,1)S(1)}, bf16[1024,1024]{1,0:T(8,128)(2,1)}, u32[]{:S(2)}) copy-start(bf16[1024,1024]{1,0:T(8,128)(2,1)} %param.16) | copy-start | bytes 6291460
  9.0 12.0 %collective-permute-start = (bf16[256,128]{1,0:T(8,128)(2,1)}, bf16[256,128]{1,0:T(8,128)(2,1)S(1)}, u32[]{:S(2)}, u32[]{:S(2)}) collective-permute-start(bf16[256,128]{1,0:T(8,128)(2,1)} %get-tuple-element.37), channel_id=1, source_target_pairs={{0,1},{1,0},{2,3},{3,2},{4,5},{5,4},{6,7},{7,6},{8,9},{9,8},{10,11... | collective-permute-start | bytes 196616 | tf_op jit(solution)/shard_map/ppermute | solution.py:270
  9.5 11.5 %collective-permute-start.1 = (bf16[256,128]{1,0:T(8,128)(2,1)}, bf16[256,128]{1,0:T(8,128)(2,1)S(1)}, u32[]{:S(2)}, u32[]{:S(2)}) collective-permute-start(bf16[256,128]{1,0:T(8,128)(2,1)} %get-tuple-element.38), channel_id=1, source_target_pairs={{0,2},{1,3},{2,0},{3,1},{4,6},{5,7},{6,4},{7,5},{8,10},{9,11},{10,... | collective-permute-start | bytes 196616 | tf_op jit(solution)/shard_map/ppermute | solution.py:270
  12.1 8.9 %collective-permute-start.2 = (bf16[256,128]{1,0:T(8,128)(2,1)}, bf16[256,128]{1,0:T(8,128)(2,1)S(1)}, u32[]{:S(2)}, u32[]{:S(2)}) collective-permute-start(bf16[256,128]{1,0:T(8,128)(2,1)} %get-tuple-element.39), channel_id=1, source_target_pairs={{0,3},{1,2},{2,1},{3,0},{4,7},{5,6},{6,5},{7,4},{8,11},{9,10},{10,... | collective-permute-start | bytes 196616 | tf_op jit(solution)/shard_map/ppermute | solution.py:270
  12.1 8.9 %copy-start.6 = (bf16[256,128]{1,0:T(8,128)(2,1)S(1)}, bf16[256,128]{1,0:T(8,128)(2,1)}, u32[]{:S(2)}) copy-start(bf16[256,128]{1,0:T(8,128)(2,1)} %get-tuple-element.48) | copy-start | bytes 196612
  21.1 9.5 %collective-permute-start.5 = (bf16[256,128]{1,0:T(8,128)(2,1)S(1)}, bf16[256,128]{1,0:T(8,128)(2,1)S(1)}, u32[]{:S(2)}, u32[]{:S(2)}) collective-permute-start(bf16[256,128]{1,0:T(8,128)(2,1)S(1)} %fusion.22), channel_id=1, source_target_pairs={{0,4},{1,5},{2,6},{3,7},{4,8},{5,9},{6,10},{7,11},{8,12},{9,13},{1... | collective-permute-start | bytes 196616 | tf_op jit(solution)/shard_map/ppermute | solution.py:274
  24.8 6.7 %collective-permute-start.4 = (bf16[256,128]{1,0:T(8,128)(2,1)S(1)}, bf16[256,128]{1,0:T(8,128)(2,1)S(1)}, u32[]{:S(2)}, u32[]{:S(2)}) collective-permute-start(bf16[256,128]{1,0:T(8,128)(2,1)S(1)} %fusion.22), channel_id=1, source_target_pairs={{0,8},{1,9},{2,10},{3,11},{4,12},{5,13},{6,14},{7,15},{16,24},{17,... | collective-permute-start | bytes 196616 | tf_op jit(solution)/shard_map/ppermute | solution.py:274
  29.3 3.2 %collective-permute-start.3 = (bf16[256,128]{1,0:T(8,128)(2,1)S(1)}, bf16[256,128]{1,0:T(8,128)(2,1)S(1)}, u32[]{:S(2)}, u32[]{:S(2)}) collective-permute-start(bf16[256,128]{1,0:T(8,128)(2,1)S(1)} %fusion.22), channel_id=1, source_target_pairs={{0,12},{1,13},{2,14},{3,15},{16,28},{17,29},{18,30},{19,31}} | collective-permute-start | bytes 196616 | tf_op jit(solution)/shard_map/ppermute | solution.py:274
  32.6 5.7 %copy-start.1 = (bf16[256,128]{1,0:T(8,128)(2,1)}, bf16[256,128]{1,0:T(8,128)(2,1)S(1)}, u32[]{:S(2)}) copy-start(bf16[256,128]{1,0:T(8,128)(2,1)S(1)} %get-tuple-element.53.refs_0_.refs_4_) | copy-start | bytes 196612
  32.6 3.7 %collective-permute-start.6 = (bf16[256,128]{1,0:T(8,128)(2,1)S(1)}, bf16[256,128]{1,0:T(8,128)(2,1)S(1)}, u32[]{:S(2)}, u32[]{:S(2)}) collective-permute-start(bf16[256,128]{1,0:T(8,128)(2,1)S(1)} %get-tuple-element.54), channel_id=1, source_target_pairs={{0,1},{1,0},{2,3},{3,2},{4,5},{5,4},{6,7},{7,6},{8,9},{9,8},{10,11... | collective-permute-start | bytes 196616 | tf_op jit(solution)/shard_map/ppermute | solution.py:270
  32.7 4.5 %collective-permute-start.7 = (bf16[256,128]{1,0:T(8,128)(2,1)S(1)}, bf16[256,128]{1,0:T(8,128)(2,1)S(1)}, u32[]{:S(2)}, u32[]{:S(2)}) collective-permute-start(bf16[256,128]{1,0:T(8,128)(2,1)S(1)} %get-tuple-element.55), channel_id=1, source_target_pairs={{0,2},{1,3},{2,0},{3,1},{4,6},{5,7},{6,4},{7,5},{8,10},{9,11},{10,... | collective-permute-start | bytes 196616 | tf_op jit(solution)/shard_map/ppermute | solution.py:270
  34.3 4.0 %collective-permute-start.8 = (bf16[256,128]{1,0:T(8,128)(2,1)S(1)}, bf16[256,128]{1,0:T(8,128)(2,1)S(1)}, u32[]{:S(2)}, u32[]{:S(2)}) collective-permute-start(bf16[256,128]{1,0:T(8,128)(2,1)S(1)} %get-tuple-element.56), channel_id=1, source_target_pairs={{0,3},{1,2},{2,1},{3,0},{4,7},{5,6},{6,5},{7,4},{8,11},{9,10},{10,... | collective-permute-start | bytes 196616 | tf_op jit(solution)/shard_map/ppermute | solution.py:270
  36.3 10.0 %copy-start.7 = (bf16[1024,32]{0,1:T(8,128)(2,1)S(1)}, bf16[1024,32]{0,1:T(8,128)(2,1)}, u32[]{:S(2)}) copy-start(bf16[1024,32]{0,1:T(8,128)(2,1)} %param.18) | copy-start | bytes 196612
  36.3 10.1 %copy-start.8 = (f32[2,32,32]{2,1,0:T(8,128)S(1)}, f32[2,32,32]{2,1,0:T(8,128)}, u32[]{:S(2)}) copy-start(f32[2,32,32]{2,1,0:T(8,128)} %get-tuple-element.67) | copy-start | bytes 24580
  36.3 19.9 %copy-start.2 = (bf16[256,128]{1,0:T(8,128)(2,1)}, bf16[256,128]{1,0:T(8,128)(2,1)S(1)}, u32[]{:S(2)}) copy-start(bf16[256,128]{1,0:T(8,128)(2,1)S(1)} %collective-permute-done.6.refs_1_.refs_5_) | copy-start | bytes 196612
  37.2 19.0 %copy-start.3 = (bf16[256,128]{1,0:T(8,128)(2,1)}, bf16[256,128]{1,0:T(8,128)(2,1)S(1)}, u32[]{:S(2)}) copy-start(bf16[256,128]{1,0:T(8,128)(2,1)S(1)} %collective-permute-done.7.refs_2_.refs_6_) | copy-start | bytes 196612
  38.3 17.9 %copy-start.4 = (bf16[256,128]{1,0:T(8,128)(2,1)}, bf16[256,128]{1,0:T(8,128)(2,1)S(1)}, u32[]{:S(2)}) copy-start(bf16[256,128]{1,0:T(8,128)(2,1)S(1)} %collective-permute-done.8.refs_3_.refs_7_) | copy-start | bytes 196612
  39.9 16.5 %all-to-all-start = ((bf16[16,8,1024]{2,1,0:T(8,128)(2,1)}), bf16[16,8,1024]{2,1,0:T(8,128)(2,1)S(1)}, u32[]{:S(2)}, u32[]{:S(2)}) async-start(bf16[16,8,1024]{2,1,0:T(8,128)(2,1)} %bitcast.3), calls=%async_computation | async-start | bytes 524288 | tf_op jit(solution)/shard_map/all_to_all | solution.py:430
  46.6 9.8 %copy-start.5 = (bf16[1024,256]{1,0:T(8,128)(2,1)S(1)}, bf16[1024,256]{1,0:T(8,128)(2,1)}, u32[]{:S(2)}) copy-start(bf16[1024,256]{1,0:T(8,128)(2,1)} %param.17) | copy-start | bytes 1572868
  57.6 12.8 %all-to-all-start.1 = ((bf16[16,8,256]{2,1,0:T(8,128)(2,1)}), bf16[16,8,256]{2,1,0:T(8,128)(2,1)S(1)}, u32[]{:S(2)}, u32[]{:S(2)}) async-start(bf16[16,8,256]{2,1,0:T(8,128)(2,1)} %fusion.3), calls=%async_computation.1 | async-start | bytes 131072 | tf_op jit(solution)/shard_map/all_to_all | solution.py:430
  63.5 6.9 %copy-start.9 = (bf16[2,32,128]{2,1,0:T(8,128)(2,1)S(1)}, bf16[2,32,128]{2,1,0:T(8,128)(2,1)}, u32[]{:S(2)}) copy-start(bf16[2,32,128]{2,1,0:T(8,128)(2,1)} %get-tuple-element.68) | copy-start | bytes 49156

commit v5 on v4

--- a/solution.py
+++ b/solution.py
@@ -116,7 +116,8 @@
     fetches = []
     for far, here in ((events_far, events), (w_query_far, w_query), (keys_far, keys), (values_far, values)):
         fetches.append(pltpu.make_async_copy(far, here, done.at[len(fetches)]))
-        fetches[-1].start()
+    fetches[0].start()
+    fetches[1].start()
     rows, width = events.shape
     many = labels.shape[1]
 
@@ -137,6 +138,8 @@
     parts = [slice(h, h + head_dim) for h in range(0, width, head_dim)]
 
     fetches[0].wait()
+    fetches[2].start()
+    fetches[3].start()
     chosen_events = dot(chosen, events[...]).astype(BF16)
     packed[:, width : 2 * width] = chosen_events.astype(F32)
     fetches[1].wait()
@@ -165,13 +168,6 @@
         8 * rows * width,
         [pltpu.VMEM(x.shape, BF16) for x in (events, w_query, keys, values)] + [pltpu.SemaphoreType.DMA((4,))],
     )(events, w_query, keys, values, labels, experts, tasks)
-
-
-def unpacked(packed, width, head_dim):
-    query, events, within = (packed[:, i * width : (i + 1) * width] for i in range(3))
-    factor = packed[:, 3 * width : 3 * width + head_dim]
-    slots = packed[:, 3 * width + head_dim :]
-    return query.astype(BF16), events.astype(BF16), within * factor[:, :1], factor, slots.astype(BF16)
 
 
 def slot_of(experts):
@@ -303,27 +299,33 @@
         prefix[rank ^ j] = on_diagonal(part[...], head_dim)
 
 
-def picked_kernel(head_dim, query_at, events_at, within_at, factor, selector, w_output, *refs):
+def picked_kernel(head_dim, packed, w_output, *refs):
     parts, (picked, outgoing, prefix) = refs[:PLANE], refs[PLANE:]
+    width = w_output.shape[0]
+    query, events, within = (packed[:, i * width : (i + 1) * width] for i in range(3))
+    factor = packed[:, 3 * width : 3 * width + 1]
+    selector = packed[:, 3 * width + head_dim :].astype(BF16)
     put_prefix(prefix, parts, head_dim)
-    earlier = earlier_terms(query_at[...], prefix, head_dim)
-    attended = (within_at[...] + earlier * factor[:, :1]).astype(BF16)
-    rows = (events_at[...].astype(F32) + dot(attended, w_output[...])).astype(BF16)
+    earlier = earlier_terms(query.astype(BF16), prefix, head_dim)
+    attended = ((within + earlier) * factor).astype(BF16)
+    rows = (events + dot(attended, w_output[...])).astype(BF16)
     picked[...] = rows
-    outgoing[...] = dot(selector[...], rows, ((0,), (0,))).astype(BF16)
-
-
-def picked_rows(query_at, events_at, within_at, factor, selector, w_output, prefix):
-    many, width = query_at.shape
-    slots = selector.shape[1]
+    outgoing[...] = dot(selector, rows, ((0,), (0,))).astype(BF16)
+
+
+def picked_rows(packed, w_output, prefix):
+    many = packed.shape[0]
+    width = w_output.shape[0]
+    head_dim = width // HEADS
+    slots = packed.shape[1] - 3 * width - head_dim
     pair = width // PLANE
     return near(
-        functools.partial(picked_kernel, width // HEADS),
+        functools.partial(picked_kernel, head_dim),
         [shaped((many, width), BF16), shaped((slots, width), BF16)],
         2 * many * width * width,
         2 * width * width,
         [pltpu.VMEM((PLANE, pair, pair), BF16)],
-    )(query_at, events_at, within_at, factor, selector, w_output, *prefix)
+    )(packed, w_output, *prefix)
 
 
 def hidden_kernel(head_dim, tile, *refs):
@@ -348,10 +350,6 @@
     within_in = [fetch_strip(within_far, within, 0)]
     w_output_in = fetch(w_output_far, w_output)
     events_in = [fetch_strip(events_far, events, 0)]
-    for i in tiles[1:]:
-        query_in.append(fetch_strip(query_far, query, i))
-        within_in.append(fetch_strip(within_far, within, i))
-        events_in.append(fetch_strip(events_far, events, i))
     for copy in parts_in:
         copy.wait()
     put_prefix(prefix, [parts.at[j] for j in range(PLANE)], head_dim)
@@ -359,6 +357,11 @@
     for i, strip in enumerate(strips):
         query_in[i].wait()
         within_in[i].wait()
+        if not i:
+            for k in tiles[1:]:
+                query_in.append(fetch_strip(query_far, query, k))
+                within_in.append(fetch_strip(within_far, within, k))
+                events_in.append(fetch_strip(events_far, events, k))
         start = lax.axis_index("seq") * rows + i * tile + 1
         place = (lax.broadcasted_iota(jnp.int32, (tile, 1), 0) + start).astype(F32)
         total = within[strip, :].astype(F32) + earlier_terms(query[strip, :], prefix, head_dim)
@@ -421,7 +424,6 @@
     label_tasks,
 ):
     devices = lax.axis_size("seq")
-    width = events.shape[1]
     labels = label_rows.reshape(1, -1)
     tasks = label_tasks.reshape(1, -1)
     experts = label_experts.T
@@ -432,12 +434,11 @@
     keys, values, inner, *states = key_value_state(events, w_key, w_value)
     states = swapped(states)
     packed, match, column = labelled_rows(events, w_query, keys, values, labels, experts, tasks, devices)
-    labelled = unpacked(packed, width, width // HEADS)
-    states, labelled = lax.optimization_barrier((states, labelled))
+    states, packed = lax.optimization_barrier((states, packed))
     before = sums_before(states)
     before, one = lax.optimization_barrier((before, jnp.ones((), BF16)))
     prefix = swapped(before)
-    picked, outgoing = picked_rows(*labelled, w_output * one, prefix)
+    picked, outgoing = picked_rows(packed * one.astype(F32), w_output * one, prefix)
     outgoing, keys, values = lax.optimization_barrier((outgoing, keys, values))
     arrived = exchange(outgoing)
     query, within = queries_within(events, w_query, keys, values, inner)

time: 71.8 us -> 68.6 us (0.955)
  local copies, waits for them, and re-layouts: 1.61 us -> 0.05 us
  waiting for transfers between devices: 5.02 us -> 3.97 us
  other arithmetic: 4.07 us -> 3.09 us
    slice x4 -> x0, local copies, waits for them, and re-layouts: 1.56 us -> none  [the longest x1 0.83 us: unpacked(): factor[:, :1]]
    ppermute x6, waiting for transfers between devices: 2 us -> 0.94 us  [flip(): return lax.ppermute(x, 'seq', [(i, i ^ j) for i in range(devices)])]
    another operation x1 -> x0, other arithmetic: 1.04 us -> none
  transfers between devices with their start and end apart: 11 -> 11, of which waited for: 6 -> 5; matrix products, arithmetic and copies ran while one was open for 8% -> 4% of each run, Pallas kernels for 29% -> 31%
where the time goes in v5:
time: 68.6 us; the launch traced here: 68 us
  Pallas kernels  31 us (45%)
  starting transfers between devices  26.9 us (39%)
  waiting for transfers between devices  3.97 us (6%)
  other arithmetic  3.09 us (5%)
  matrix products  2.16 us (3%)
  between operations  0.9 us (1%)
    all_to_all x2, starting transfers between devices, exchange(): return lax.all_to_all(x, 'seq', split_axis=0, concat_axis=0, tiled=True)  12.3 us
    pallas_call x1, Pallas kernels, queries_within(): call(functools.partial(within_kernel, head_dim, tile), (width // pair,),...  9.61 us
    ppermute x3, starting transfers between devices, later(): lax.ppermute(x, 'seq', [(i, i + s) for i in range(lax.axis_size('seq') -...  9.48 us
    pallas_call x1, Pallas kernels, key_value_state(): call(functools.partial(key_value_kernel, head_dim, tile), (PLANE,), [whol...  8.31 us
    pallas_call x1, Pallas kernels, hidden_rows(): call(functools.partial(hidden_kernel, head_dim, tile), (), [FAR] * (4 + P...  5.84 us
    pallas_call x1, Pallas kernels, labelled_rows(): call(functools.partial(labelled_kernel, width // HEADS, devices // EXPERT...  5.68 us
    ppermute x6, starting transfers between devices, flip(): return lax.ppermute(x, 'seq', [(i, i ^ j) for i in range(devices)])  5.11 us
    dot_general x3, matrix products, dot(): lax.dot_general(a, b, (contract, ((), ())), preferred_element_type=F32, *...  2.16 us
  transfers between devices with their start and end apart: 11, of which 5 were waited for; matrix products, arithmetic and copies ran while one was open for 4% of the time, Pallas kernels for 31%

profile of v5, /device:TPU:0, one launch (start us, length us, event | category | flops | bytes accessed | tf_op | source)
XLA Modules:
  0.0 68.0 jit_solution(14671705665385375555)
XLA Ops:
  0.6 8.3 %shard_map.122 = (bf16[768,1024]{1,0:T(8,128)(2,1)}, bf16[768,1024]{1,0:T(8,128)(2,1)}, bf16[2,1024,128]{2,1,0:T(8,128)(2,1)}, bf16[256,128]{1,0:T(8,128)(2,1)},...) custom-call(bf16[768,1024]{1,0:T(8,128)(2,1)} %refs_0_.1, bf16[1024,1024]{1,0:T(8,128)(2,1)} %w_key.1, ...), custom_call_target="tpu_custom_call" | custom-call | flops 3221225472 | bytes 6291456 | tf_op jit(solution)/shard_map/pallas_call | solution.py:96
  9.0 0.5 collective-permute-start
  9.5 2.6 %collective-permute-start.1 = (bf16[256,128]{1,0:T(8,128)(2,1)}, bf16[256,128]{1,0:T(8,128)(2,1)S(1)}, u32[]{:S(2)}, u32[]{:S(2)}) collective-permute-start(bf16[256,128]{1,0:T(8,128)(2,1)} %get-tuple-element.34), channel_id=1, source_target_pairs={{0,2},{1,3},{2,0},{3,1},{4,6},{5,7},{6,4},{7,5},{8,10},{9,11},{10,... | collective-permute-start | bytes 196616 | tf_op jit(solution)/shard_map/ppermute | solution.py:266
  12.1 5.7 %shard_map.123 = (f32[32,3328]{1,0:T(8,128)}, bf16[2,32,128]{2,1,0:T(8,128)(2,1)}, f32[2,32,32]{2,1,0:T(8,128)}) custom-call(bf16[768,1024]{1,0:T(8,128)(2,1)} %refs_0_.1, bf16[1024,1024]{1,0:T(8,128)(2,1)} %w_query.1, bf16[768,1024]{1,0:T(8,128)(2,1)} %get-tuple-element.51.keys_far.keys, bf16[768,1024]{1,0:T(8,128)(2,1)} %get-tuple-element.52.values_far.values, ...), custom_call_target="tpu_custom_call" | custom-call | flops 100663296 | bytes 6291456 | tf_op jit(solution)/shard_map/pallas_call | solution.py:160
  17.9 3.7 %collective-permute-start.5 = (bf16[256,128]{1,0:T(8,128)(2,1)S(1)}, bf16[256,128]{1,0:T(8,128)(2,1)S(1)}, u32[]{:S(2)}, u32[]{:S(2)}) collective-permute-start(bf16[256,128]{1,0:T(8,128)(2,1)S(1)} %fusion.22), channel_id=1, source_target_pairs={{0,4},{1,5},{2,6},{3,7},{4,8},{5,9},{6,10},{7,11},{8,12},{9,13},{1... | collective-permute-start | bytes 196616 | tf_op jit(solution)/shard_map/ppermute | solution.py:270
  21.6 4.5 %collective-permute-start.4 = (bf16[256,128]{1,0:T(8,128)(2,1)S(1)}, bf16[256,128]{1,0:T(8,128)(2,1)S(1)}, u32[]{:S(2)}, u32[]{:S(2)}) collective-permute-start(bf16[256,128]{1,0:T(8,128)(2,1)S(1)} %fusion.22), channel_id=1, source_target_pairs={{0,8},{1,9},{2,10},{3,11},{4,12},{5,13},{6,14},{7,15},{16,24},{17,... | collective-permute-start | bytes 196616 | tf_op jit(solution)/shard_map/ppermute | solution.py:270
  26.1 1.3 %collective-permute-start.3 = (bf16[256,128]{1,0:T(8,128)(2,1)S(1)}, bf16[256,128]{1,0:T(8,128)(2,1)S(1)}, u32[]{:S(2)}, u32[]{:S(2)}) collective-permute-start(bf16[256,128]{1,0:T(8,128)(2,1)S(1)} %fusion.22), channel_id=1, source_target_pairs={{0,12},{1,13},{2,14},{3,15},{16,28},{17,29},{18,30},{19,31}} | collective-permute-start | bytes 196616 | tf_op jit(solution)/shard_map/ppermute | solution.py:270
  27.5 0.8 %collective-permute-done.4 = bf16[256,128]{1,0:T(8,128)(2,1)S(1)} collective-permute-done((bf16[256,128]{1,0:T(8,128)(2,1)S(1)}, bf16[256,128]{1,0:T(8,128)(2,1)S(1)}, u32[]{:S(2)}, u32[]{:S(2)}) %collective-permute-start.4) | collective-permute-done | bytes 65568 | tf_op jit(solution)/shard_map/ppermute | solution.py:270
  28.3 1.0 %collective-permute-done.3 = bf16[256,128]{1,0:T(8,128)(2,1)S(1)} collective-permute-done((bf16[256,128]{1,0:T(8,128)(2,1)S(1)}, bf16[256,128]{1,0:T(8,128)(2,1)S(1)}, u32[]{:S(2)}, u32[]{:S(2)}) %collective-permute-start.3) | collective-permute-done | bytes 65568 | tf_op jit(solution)/shard_map/ppermute | solution.py:270
  29.3 0.2 fusion.17
  29.6 1.6 %collective-permute-start.7 = (bf16[256,128]{1,0:T(8,128)(2,1)S(1)}, bf16[256,128]{1,0:T(8,128)(2,1)S(1)}, u32[]{:S(2)}, u32[]{:S(2)}) collective-permute-start(bf16[256,128]{1,0:T(8,128)(2,1)S(1)} %get-tuple-element.47), channel_id=1, source_target_pairs={{0,2},{1,3},{2,0},{3,1},{4,6},{5,7},{6,4},{7,5},{8,10},{9,11},{10,... | collective-permute-start | bytes 196616 | tf_op jit(solution)/shard_map/ppermute | solution.py:266
  31.2 0.3 collective-permute-start.8
  31.4 1.0 %broadcast_multiply_fusion.1.packed = f32[32,3328]{1,0:T(8,128)S(1)} fusion(f32[32,3328]{1,0:T(8,128)} %get-tuple-element.39, f32[]{:T(128)S(6)} %convert_element_type.57), kind=kLoop, calls=%fused_computation.24 | loop fusion | flops 106496 | bytes 851972 | tf_op jit(solution)/shard_map/mul | solution.py:441
  32.5 1.7 %broadcast_multiply_fusion.w_output = bf16[1024,1024]{1,0:T(8,128)(2,1)S(1)} fusion(bf16[1024,1024]{1,0:T(8,128)(2,1)} %refs_3_.1, bf16[]{:T(256)} %constant.27.clone.1), kind=kLoop, calls=%fused_computation.7 | loop fusion | flops 1048576 | bytes 4194306 | tf_op jit(solution)/shard_map/mul | solution.py:441
  34.3 0.9 %collective-permute-done.8.refs_3_.refs_7_ = bf16[256,128]{1,0:T(8,128)(2,1)S(1)} collective-permute-done((bf16[256,128]{1,0:T(8,128)(2,1)S(1)}, bf16[256,128]{1,0:T(8,128)(2,1)S(1)}, u32[]{:S(2)}, u32[]{:S(2)}) %collective-permute-start.8) | collective-permute-done | bytes 65568 | tf_op jit(solution)/shard_map/ppermute | solution.py:266
  35.2 1.5 %shard_map.124 = (bf16[32,1024]{1,0:T(8,128)(2,1)S(1)}, bf16[128,1024]{1,0:T(8,128)(2,1)}) custom-call(f32[32,3328]{1,0:T(8,128)S(1)} %broadcast_multiply_fusion.1.packed, bf16[1024,1024]{1,0:T(8,128)(2,1)S(1)} %broadcast_multiply_fusion.w_output, bf16[256,128]{1,0:T(8,128)(2,1)S(1)} %get-tuple-element.45.refs_0_.refs_4_, ...), custom_call_target="tpu_custom_call" | custom-call | flops 67108864 | bytes 2097152 | tf_op jit(solution)/shard_map/pallas_call | solution.py:322
  36.7 6.4 %all-to-all-start = ((bf16[16,8,1024]{2,1,0:T(8,128)(2,1)}), bf16[16,8,1024]{2,1,0:T(8,128)(2,1)S(1)}, u32[]{:S(2)}, u32[]{:S(2)}) async-start(bf16[16,8,1024]{2,1,0:T(8,128)(2,1)} %bitcast.3), calls=%async_computation | async-start | bytes 524288 | tf_op jit(solution)/shard_map/all_to_all | solution.py:432
  43.4 9.6 %shard_map.125 = (bf16[768,1024]{1,0:T(8,128)(2,1)}, bf16[768,1024]{1,0:T(8,128)(2,1)}) custom-call(bf16[768,1024]{1,0:T(8,128)(2,1)} %refs_0_.1, bf16[1024,1024]{1,0:T(8,128)(2,1)} %w_query.1, bf16[768,1024]{1,0:T(8,128)(2,1)} %get-tuple-element.51.keys_far.keys, bf16[768,1024]{1,0:T(8,128)(2,1)} %get-tuple-element.52.values_far.values, ...), custom_call_target="tpu_custom_call" | custom-call | flops 2415919104 | bytes 6291456 | tf_op jit(solution)/shard_map/pallas_call | solution.py:247
  53.1 0.1 all-to-all-done
  53.2 1.3 %fusion.3 = bf16[16,8,256]{2,1,0:T(8,128)(2,1)} fusion(bf16[1024,256]{1,0:T(8,128)(2,1)S(1)} %copy-done.5, bf16[128,1024]{1,0:T(8,128)(2,1)S(1)} %bitcast.18, bf16[1024,1024]{1,0:T(8,128)(2,1)S(1)} %copy-done), kind=kOutput, calls=%fused_computation.4 | convolution fusion | flops 335839232 | bytes 2949120 | tf_op jit(solution)/shard_map/dot_general | solution.py:20
  54.5 5.9 %all-to-all-start.1 = ((bf16[16,8,256]{2,1,0:T(8,128)(2,1)}), bf16[16,8,256]{2,1,0:T(8,128)(2,1)S(1)}, u32[]{:S(2)}, u32[]{:S(2)}) async-start(bf16[16,8,256]{2,1,0:T(8,128)(2,1)} %fusion.3), calls=%async_computation.1 | async-start | bytes 131072 | tf_op jit(solution)/shard_map/all_to_all | solution.py:432
  60.4 5.8 %shard_map.126 = bf16[768,1024]{1,0:T(8,128)(2,1)} custom-call(bf16[768,1024]{1,0:T(8,128)(2,1)} %refs_0_.1, bf16[768,1024]{1,0:T(8,128)(2,1)} %get-tuple-element.56.refs_1_, bf16[768,1024]{1,0:T(8,128)(2,1)} %get-tuple-element.57.refs_2_, bf16[1024,1024]{1,0:T(8,128)(2,1)} %refs_3_.1, bf16[256,128]{1,0:T(8,128)(2,1)} %copy-done.1, ...), custom_call_target="tpu_custom_call" | custom-call | flops 1610612736 | bytes 7864320 | tf_op jit(solution)/shard_map/pallas_call | solution.py:385
  66.3 1.0 %all-to-all-done.1 = bf16[16,8,256]{2,1,0:T(8,128)(2,1)S(1)} async-done(((bf16[16,8,256]{2,1,0:T(8,128)(2,1)}), bf16[16,8,256]{2,1,0:T(8,128)(2,1)S(1)}, u32[]{:S(2)}, u32[]{:S(2)}) %all-to-all-start.1) | async-done | bytes 65568 | tf_op jit(solution)/shard_map/all_to_all | solution.py:432
  67.3 0.8 %fusion.4 = f32[32,256]{1,0:T(8,128)} fusion(bf16[2,32,128]{2,1,0:T(8,128)(2,1)S(1)} %copy-done.9, bf16[16,8,256]{2,1,0:T(8,128)(2,1)S(1)} %all-to-all-done.1, f32[2,32]{1,0:T(2,128)S(1)} %add_divide_fusion), kind=kOutput, calls=%fused_computation.6 | convolution fusion | flops 4218880 | bytes 114944 | tf_op jit(solution)/shard_map/dot_general | solution.py:20
  (32 shorter events, 0.5 us)
Async XLA Ops:
  0.6 52.6 %copy-start = (bf16[1024,1024]{1,0:T(8,128)(2,1)S(1)}, bf16[1024,1024]{1,0:T(8,128)(2,1)}, u32[]{:S(2)}) copy-start(bf16[1024,1024]{1,0:T(8,128)(2,1)} %param.16) | copy-start | bytes 6291460
  9.0 8.9 %collective-permute-start = (bf16[256,128]{1,0:T(8,128)(2,1)}, bf16[256,128]{1,0:T(8,128)(2,1)S(1)}, u32[]{:S(2)}, u32[]{:S(2)}) collective-permute-start(bf16[256,128]{1,0:T(8,128)(2,1)} %get-tuple-element.33), channel_id=1, source_target_pairs={{0,1},{1,0},{2,3},{3,2},{4,5},{5,4},{6,7},{7,6},{8,9},{9,8},{10,11... | collective-permute-start | bytes 196616 | tf_op jit(solution)/shard_map/ppermute | solution.py:266
  9.5 8.4 %collective-permute-start.1 = (bf16[256,128]{1,0:T(8,128)(2,1)}, bf16[256,128]{1,0:T(8,128)(2,1)S(1)}, u32[]{:S(2)}, u32[]{:S(2)}) collective-permute-start(bf16[256,128]{1,0:T(8,128)(2,1)} %get-tuple-element.34), channel_id=1, source_target_pairs={{0,2},{1,3},{2,0},{3,1},{4,6},{5,7},{6,4},{7,5},{8,10},{9,11},{10,... | collective-permute-start | bytes 196616 | tf_op jit(solution)/shard_map/ppermute | solution.py:266
  12.1 5.8 %collective-permute-start.2 = (bf16[256,128]{1,0:T(8,128)(2,1)}, bf16[256,128]{1,0:T(8,128)(2,1)S(1)}, u32[]{:S(2)}, u32[]{:S(2)}) collective-permute-start(bf16[256,128]{1,0:T(8,128)(2,1)} %get-tuple-element.35), channel_id=1, source_target_pairs={{0,3},{1,2},{2,1},{3,0},{4,7},{5,6},{6,5},{7,4},{8,11},{9,10},{10,... | collective-permute-start | bytes 196616 | tf_op jit(solution)/shard_map/ppermute | solution.py:266
  12.1 5.7 %copy-start.6 = (bf16[256,128]{1,0:T(8,128)(2,1)S(1)}, bf16[256,128]{1,0:T(8,128)(2,1)}, u32[]{:S(2)}) copy-start(bf16[256,128]{1,0:T(8,128)(2,1)} %get-tuple-element.40) | copy-start | bytes 196612
  17.9 9.5 %collective-permute-start.5 = (bf16[256,128]{1,0:T(8,128)(2,1)S(1)}, bf16[256,128]{1,0:T(8,128)(2,1)S(1)}, u32[]{:S(2)}, u32[]{:S(2)}) collective-permute-start(bf16[256,128]{1,0:T(8,128)(2,1)S(1)} %fusion.22), channel_id=1, source_target_pairs={{0,4},{1,5},{2,6},{3,7},{4,8},{5,9},{6,10},{7,11},{8,12},{9,13},{1... | collective-permute-start | bytes 196616 | tf_op jit(solution)/shard_map/ppermute | solution.py:270
  21.6 6.7 %collective-permute-start.4 = (bf16[256,128]{1,0:T(8,128)(2,1)S(1)}, bf16[256,128]{1,0:T(8,128)(2,1)S(1)}, u32[]{:S(2)}, u32[]{:S(2)}) collective-permute-start(bf16[256,128]{1,0:T(8,128)(2,1)S(1)} %fusion.22), channel_id=1, source_target_pairs={{0,8},{1,9},{2,10},{3,11},{4,12},{5,13},{6,14},{7,15},{16,24},{17,... | collective-permute-start | bytes 196616 | tf_op jit(solution)/shard_map/ppermute | solution.py:270
  26.1 3.2 %collective-permute-start.3 = (bf16[256,128]{1,0:T(8,128)(2,1)S(1)}, bf16[256,128]{1,0:T(8,128)(2,1)S(1)}, u32[]{:S(2)}, u32[]{:S(2)}) collective-permute-start(bf16[256,128]{1,0:T(8,128)(2,1)S(1)} %fusion.22), channel_id=1, source_target_pairs={{0,12},{1,13},{2,14},{3,15},{16,28},{17,29},{18,30},{19,31}} | collective-permute-start | bytes 196616 | tf_op jit(solution)/shard_map/ppermute | solution.py:270
  29.5 5.7 %copy-start.1 = (bf16[256,128]{1,0:T(8,128)(2,1)}, bf16[256,128]{1,0:T(8,128)(2,1)S(1)}, u32[]{:S(2)}) copy-start(bf16[256,128]{1,0:T(8,128)(2,1)S(1)} %get-tuple-element.45.refs_0_.refs_4_) | copy-start | bytes 196612
  29.5 4.7 %collective-permute-start.6 = (bf16[256,128]{1,0:T(8,128)(2,1)S(1)}, bf16[256,128]{1,0:T(8,128)(2,1)S(1)}, u32[]{:S(2)}, u32[]{:S(2)}) collective-permute-start(bf16[256,128]{1,0:T(8,128)(2,1)S(1)} %get-tuple-element.46), channel_id=1, source_target_pairs={{0,1},{1,0},{2,3},{3,2},{4,5},{5,4},{6,7},{7,6},{8,9},{9,8},{10,11... | collective-permute-start | bytes 196616 | tf_op jit(solution)/shard_map/ppermute | solution.py:266
  29.6 4.7 %collective-permute-start.7 = (bf16[256,128]{1,0:T(8,128)(2,1)S(1)}, bf16[256,128]{1,0:T(8,128)(2,1)S(1)}, u32[]{:S(2)}, u32[]{:S(2)}) collective-permute-start(bf16[256,128]{1,0:T(8,128)(2,1)S(1)} %get-tuple-element.47), channel_id=1, source_target_pairs={{0,2},{1,3},{2,0},{3,1},{4,6},{5,7},{6,4},{7,5},{8,10},{9,11},{10,... | collective-permute-start | bytes 196616 | tf_op jit(solution)/shard_map/ppermute | solution.py:266
  31.2 4.0 %collective-permute-start.8 = (bf16[256,128]{1,0:T(8,128)(2,1)S(1)}, bf16[256,128]{1,0:T(8,128)(2,1)S(1)}, u32[]{:S(2)}, u32[]{:S(2)}) collective-permute-start(bf16[256,128]{1,0:T(8,128)(2,1)S(1)} %get-tuple-element.48), channel_id=1, source_target_pairs={{0,3},{1,2},{2,1},{3,0},{4,7},{5,6},{6,5},{7,4},{8,11},{9,10},{10,... | collective-permute-start | bytes 196616 | tf_op jit(solution)/shard_map/ppermute | solution.py:266
  34.2 9.0 %copy-start.7 = (bf16[1024,32]{0,1:T(8,128)(2,1)S(1)}, bf16[1024,32]{0,1:T(8,128)(2,1)}, u32[]{:S(2)}) copy-start(bf16[1024,32]{0,1:T(8,128)(2,1)} %param.18) | copy-start | bytes 196612
  34.2 9.1 %copy-start.8 = (f32[2,32,32]{2,1,0:T(8,128)S(1)}, f32[2,32,32]{2,1,0:T(8,128)}, u32[]{:S(2)}) copy-start(f32[2,32,32]{2,1,0:T(8,128)} %get-tuple-element.59) | copy-start | bytes 24580
  34.2 18.8 %copy-start.2 = (bf16[256,128]{1,0:T(8,128)(2,1)}, bf16[256,128]{1,0:T(8,128)(2,1)S(1)}, u32[]{:S(2)}) copy-start(bf16[256,128]{1,0:T(8,128)(2,1)S(1)} %collective-permute-done.6.refs_1_.refs_5_) | copy-start | bytes 196612
  34.3 18.8 %copy-start.3 = (bf16[256,128]{1,0:T(8,128)(2,1)}, bf16[256,128]{1,0:T(8,128)(2,1)S(1)}, u32[]{:S(2)}) copy-start(bf16[256,128]{1,0:T(8,128)(2,1)S(1)} %collective-permute-done.7.refs_2_.refs_6_) | copy-start | bytes 196612
  35.2 17.9 %copy-start.4 = (bf16[256,128]{1,0:T(8,128)(2,1)}, bf16[256,128]{1,0:T(8,128)(2,1)S(1)}, u32[]{:S(2)}) copy-start(bf16[256,128]{1,0:T(8,128)(2,1)S(1)} %collective-permute-done.8.refs_3_.refs_7_) | copy-start | bytes 196612
  36.7 16.5 %all-to-all-start = ((bf16[16,8,1024]{2,1,0:T(8,128)(2,1)}), bf16[16,8,1024]{2,1,0:T(8,128)(2,1)S(1)}, u32[]{:S(2)}, u32[]{:S(2)}) async-start(bf16[16,8,1024]{2,1,0:T(8,128)(2,1)} %bitcast.3), calls=%async_computation | async-start | bytes 524288 | tf_op jit(solution)/shard_map/all_to_all | solution.py:432
  43.4 9.8 %copy-start.5 = (bf16[1024,256]{1,0:T(8,128)(2,1)S(1)}, bf16[1024,256]{1,0:T(8,128)(2,1)}, u32[]{:S(2)}) copy-start(bf16[1024,256]{1,0:T(8,128)(2,1)} %param.17) | copy-start | bytes 1572868
  54.5 12.8 %all-to-all-start.1 = ((bf16[16,8,256]{2,1,0:T(8,128)(2,1)}), bf16[16,8,256]{2,1,0:T(8,128)(2,1)S(1)}, u32[]{:S(2)}, u32[]{:S(2)}) async-start(bf16[16,8,256]{2,1,0:T(8,128)(2,1)} %fusion.3), calls=%async_computation.1 | async-start | bytes 131072 | tf_op jit(solution)/shard_map/all_to_all | solution.py:432
  60.4 6.9 %copy-start.9 = (bf16[2,32,128]{2,1,0:T(8,128)(2,1)S(1)}, bf16[2,32,128]{2,1,0:T(8,128)(2,1)}, u32[]{:S(2)}) copy-start(bf16[2,32,128]{2,1,0:T(8,128)(2,1)} %get-tuple-element.60) | copy-start | bytes 49156

commit v6 on v5

--- a/solution.py
+++ b/solution.py
@@ -59,11 +59,17 @@
     return jax.ShapeDtypeStruct(shape, kind)
 
 
-def key_value_kernel(head_dim, tile, events, w_key, w_value, keys, values, inner, *states):
+def key_value_kernel(head_dim, tile, events, w_key, w_value, w_query, labels, keys, values, inner, query_at, events_at, *states):
+
+    @pl.when(pl.program_id(0) == 0)
+    def _():
+        events_at[...] = dot(row_choice(labels[...], events.shape[0]), events[...]).astype(BF16)
+
     k = dot(events[...], w_key[...]).astype(BF16)
     v = dot(events[...], w_value[...]).astype(BF16)
     keys[...] = k
     values[...] = v
+    query_at[...] = dot(events_at[...], w_query[...]).astype(BF16)
     total = None
     for i in range(events.shape[0] // tile):
         here = slice(i * tile, (i + 1) * tile)
@@ -80,8 +86,9 @@
             state[...] = total.astype(BF16)
 
 
-def key_value_state(events, w_key, w_value):
+def key_value_state(events, w_key, w_value, w_query, labels):
     rows, width = events.shape
+    many = labels.shape[1]
     head_dim = width // HEADS
     pair = width // PLANE
     tile = row_tile(rows)
@@ -96,30 +103,31 @@
     return call(
         functools.partial(key_value_kernel, head_dim, tile),
         (PLANE,),
-        [whole((rows, width)), cols(width), cols(width)],
+        [whole((rows, width)), cols(width), cols(width), cols(width), whole(labels.shape)],
         [cols(rows), cols(rows), pl.BlockSpec((inner, pair, head_dim), lambda i: (0, turn(i), 0))]
+        + [cols(many), whole((many, width))]
         + [whole((pair, head_dim))] * PLANE,
         [shaped((rows, width), BF16)] * 2
         + [shaped((inner, width, head_dim), BF16)]
+        + [shaped((many, width), BF16)] * 2
         + [shaped((pair, head_dim), BF16)] * PLANE,
         4 * rows * width * width,
         8 * rows * width,
-    )(events, w_key, w_value)
+    )(events, w_key, w_value, w_query, labels)
 
 
 def row_tile(rows):
     return 256 if rows % 256 == 0 and rows > 256 else rows // 2
 
 
-def labelled_kernel(head_dim, copies, events_far, w_query_far, keys_far, values_far, labels, experts, tasks, *refs):
-    (packed, match, column), (events, w_query, keys, values, done) = refs[:3], refs[3:]
-    fetches = []
-    for far, here in ((events_far, events), (w_query_far, w_query), (keys_far, keys), (values_far, values)):
-        fetches.append(pltpu.make_async_copy(far, here, done.at[len(fetches)]))
-    fetches[0].start()
-    fetches[1].start()
-    rows, width = events.shape
+def labelled_kernel(head_dim, copies, keys_far, values_far, query_at, events_at, labels, experts, tasks, *refs):
+    (packed, match, column), (keys, values, came) = refs[:3], refs[3:]
+    rows, width = keys.shape
     many = labels.shape[1]
+    halves = [slice(0, width // 2), slice(width // 2, width)]
+    fars = [far.at[:, half] for far in (keys_far, values_far) for half in halves]
+    heres = [here.at[:, half] for here in (keys, values) for half in halves]
+    fetches = fetch_all(fars, heres, came)
 
     start = lax.axis_index("seq") * rows + 1
     factor = upright(lax.rsqrt((labels[...] + start).astype(F32) * head_dim))
@@ -133,41 +141,50 @@
         match[k] = found[k].astype(BF16)
         chosen_column = upright(tasks[...] * EXPERTS + experts[k : k + 1, :])
         column[k] = jnp.where(number == chosen_column, 1.0, 0.0)
-    chosen = row_choice(labels[...], rows)
+    query = query_at[...]
+    packed[:, :width] = query.astype(F32)
+    packed[:, width : 2 * width] = events_at[...].astype(F32)
     causal = lax.broadcasted_iota(jnp.int32, (many, rows), 1) <= upright(labels[...])
     parts = [slice(h, h + head_dim) for h in range(0, width, head_dim)]
-
-    fetches[0].wait()
-    fetches[2].start()
-    fetches[3].start()
-    chosen_events = dot(chosen, events[...]).astype(BF16)
-    packed[:, width : 2 * width] = chosen_events.astype(F32)
-    fetches[1].wait()
-    query = dot(chosen_events, w_query[...]).astype(BF16)
-    packed[:, :width] = query.astype(F32)
-    fetches[2].wait()
-    weights = [dot(query[:, part], keys[:, part], ((1,), (1,))) for part in parts]
+    weights = []
+    for h, part in enumerate(parts):
+        if h % (HEADS // 2) == 0:
+            fetches[h // (HEADS // 2)].wait()
+        weights.append(dot(query[:, part], keys[:, part], ((1,), (1,))))
     weights = [jnp.where(causal, weight, 0.0).astype(BF16) for weight in weights]
-    fetches[3].wait()
-    for part, weight in zip(parts, weights):
-        packed[:, 2 * width + part.start : 2 * width + part.stop] = dot(weight, values[:, part])
-
-
-def labelled_rows(events, w_query, keys, values, labels, experts, tasks, devices):
-    rows, width = events.shape
+    for h, part in enumerate(parts):
+        if h % (HEADS // 2) == 0:
+            fetches[2 + h // (HEADS // 2)].wait()
+        packed[:, 2 * width + part.start : 2 * width + part.stop] = dot(weights[h], values[:, part])
+
+
+def labelled_rows(keys, values, query_at, events_at, labels, experts, tasks, devices):
+    rows, width = keys.shape
     many = labels.shape[1]
     slots = devices * CAP
     return call(
         functools.partial(labelled_kernel, width // HEADS, devices // EXPERTS),
         (),
-        [FAR] * 4 + [VMEM] * 3,
+        [FAR] * 2 + [VMEM] * 5,
         [VMEM] * 3,
         [shaped((many, 3 * width + width // HEADS + slots), F32)]
         + [shaped((2, many, slots), BF16), shaped((2, many, 2 * EXPERTS), F32)],
         4 * many * rows * width,
-        8 * rows * width,
-        [pltpu.VMEM(x.shape, BF16) for x in (events, w_query, keys, values)] + [pltpu.SemaphoreType.DMA((4,))],
-    )(events, w_query, keys, values, labels, experts, tasks)
+        4 * rows * width,
+        [pltpu.VMEM(x.shape, BF16) for x in (keys, values)] + [pltpu.SemaphoreType.DMA((4,))],
+    )(keys, values, query_at, events_at, labels, experts, tasks)
+
+
+def fetch_all(fars, heres, done):
+    copies = [pltpu.make_async_copy(far, here, done.at[i]) for i, (far, here) in enumerate(zip(fars, heres))]
+    for copy in copies:
+        copy.start()
+    return copies
+
+
+def wait_all(copies):
+    for copy in copies:
+        copy.wait()
 
 
 def slot_of(experts):
@@ -331,49 +348,42 @@
 def hidden_kernel(head_dim, tile, *refs):
     events_far, query_far, within_far, w_output_far = refs[:4]
     parts_far, hidden_far = refs[4 : 4 + PLANE], refs[4 + PLANE]
-    events, query, within, w_output, parts, hidden, prefix, done, sent = refs[5 + PLANE :]
+    events, query, within, w_output, parts, hidden, attended, prefix, came, strips_came, w_came, left = refs[5 + PLANE :]
     rows = events.shape[0]
-    tiles = range(rows // tile)
-    strips = [slice(i * tile, (i + 1) * tile) for i in tiles]
-    number = iter(range(done.shape[0]))
-
-    def fetch(far, here):
-        copy = pltpu.make_async_copy(far, here, done.at[next(number)])
-        copy.start()
-        return copy
-
-    def fetch_strip(far, here, i):
-        return fetch(far.at[strips[i], :], here.at[strips[i], :])
-
-    parts_in = [fetch(far, parts.at[j]) for j, far in enumerate(parts_far)]
-    query_in = [fetch_strip(query_far, query, 0)]
-    within_in = [fetch_strip(within_far, within, 0)]
-    w_output_in = fetch(w_output_far, w_output)
-    events_in = [fetch_strip(events_far, events, 0)]
-    for copy in parts_in:
-        copy.wait()
+    pair = prefix.shape[1]
+    strips = [slice(i, i + tile) for i in range(0, rows, tile)]
+    chunks = [slice(i, i + pair) for i in range(0, w_output.shape[0], pair)]
+
+    def fetch_strip(i):
+        fars = [query_far.at[strips[i], :], within_far.at[strips[i], :]]
+        return fetch_all(fars, [query.at[strips[i], :], within.at[strips[i], :]], strips_came.at[i])
+
+    def fetch_chunk(c):
+        return fetch_all([w_output_far.at[:, chunks[c]]], [w_output.at[:, chunks[c]]], w_came.at[pl.ds(c, 1)])
+
+    parts_in = fetch_all(parts_far, [parts.at[j] for j in range(PLANE)], came)
+    strips_in = [fetch_strip(i) for i in range(len(strips))]
+    chunks_in = [fetch_chunk(0)]
+    events_in = pltpu.make_async_copy(events_far, events, came.at[PLANE])
+    events_in.start()
+    chunks_in += [fetch_chunk(c) for c in range(1, len(chunks))]
+    wait_all(parts_in)
     put_prefix(prefix, [parts.at[j] for j in range(PLANE)], head_dim)
-    results = []
     for i, strip in enumerate(strips):
-        query_in[i].wait()
-        within_in[i].wait()
-        if not i:
-            for k in tiles[1:]:
-                query_in.append(fetch_strip(query_far, query, k))
-                within_in.append(fetch_strip(within_far, within, k))
-                events_in.append(fetch_strip(events_far, events, k))
+        wait_all(strips_in[i])
         start = lax.axis_index("seq") * rows + i * tile + 1
         place = (lax.broadcasted_iota(jnp.int32, (tile, 1), 0) + start).astype(F32)
         total = within[strip, :].astype(F32) + earlier_terms(query[strip, :], prefix, head_dim)
-        attended = (total * lax.rsqrt(place * head_dim)).astype(BF16)
-        if not i:
-            w_output_in.wait()
-        events_in[i].wait()
-        hidden[strip, :] = (events[strip, :].astype(F32) + dot(attended, w_output[...])).astype(BF16)
-        results.append(pltpu.make_async_copy(hidden.at[strip, :], hidden_far.at[strip, :], sent.at[i]))
+        attended[strip, :] = (total * lax.rsqrt(place * head_dim)).astype(BF16)
+    results = []
+    for c, chunk in enumerate(chunks):
+        wait_all(chunks_in[c])
+        if not c:
+            events_in.wait()
+        hidden[:, chunk] = (events[:, chunk].astype(F32) + dot(attended[...], w_output[:, chunk])).astype(BF16)
+        results.append(pltpu.make_async_copy(hidden.at[:, chunk], hidden_far.at[:, chunk], left.at[c]))
         results[-1].start()
-    for copy in results:
-        copy.wait()
+    wait_all(results)
 
 
 def hidden_rows(events, query, within, prefix, w_output):
@@ -381,7 +391,6 @@
     head_dim = width // HEADS
     tile = row_tile(rows)
     pair = width // PLANE
-    tiles = rows // tile
     return call(
         functools.partial(hidden_kernel, head_dim, tile),
         (),
@@ -392,8 +401,10 @@
         10 * rows * width,
         [pltpu.VMEM((rows, width), BF16)] * 3
         + [pltpu.VMEM((width, width), BF16), pltpu.VMEM((PLANE, pair, head_dim), BF16)]
-        + [pltpu.VMEM((rows, width), BF16), pltpu.VMEM((PLANE, pair, pair), BF16)]
-        + [pltpu.SemaphoreType.DMA((PLANE + 1 + 3 * tiles,)), pltpu.SemaphoreType.DMA((tiles,))],
+        + [pltpu.VMEM((rows, width), BF16)] * 2
+        + [pltpu.VMEM((PLANE, pair, pair), BF16), pltpu.SemaphoreType.DMA((PLANE + 1,))]
+        + [pltpu.SemaphoreType.DMA((rows // tile, 2)), pltpu.SemaphoreType.DMA((PLANE,))]
+        + [pltpu.SemaphoreType.DMA((PLANE,))],
     )(events, query, within, w_output, *prefix)
 
 
@@ -431,9 +442,9 @@
     def exchange(x):
         return lax.all_to_all(x, "seq", split_axis=0, concat_axis=0, tiled=True)
 
-    keys, values, inner, *states = key_value_state(events, w_key, w_value)
+    keys, values, inner, query_at, events_at, *states = key_value_state(events, w_key, w_value, w_query, labels)
     states = swapped(states)
-    packed, match, column = labelled_rows(events, w_query, keys, values, labels, experts, tasks, devices)
+    packed, match, column = labelled_rows(keys, values, query_at, events_at, labels, experts, tasks, devices)
     states, packed = lax.optimization_barrier((states, packed))
     before = sums_before(states)
     before, one = lax.optimization_barrier((before, jnp.ones((), BF16)))

time: 68.6 us -> 69 us (level)
  Pallas kernels: 31 us -> 32.4 us
  waiting for transfers between devices: 3.97 us -> 2.94 us
    pallas_call x1, Pallas kernels: 5.84 us -> 7.72 us  [hidden_rows(): call(functools.partial(hidden_kernel, head_dim, tile), (), [FAR] * (4 + P...]
    pallas_call x1, Pallas kernels: 5.68 us -> 4.24 us  [labelled_rows(): call(functools.partial(labelled_kernel, width // HEADS, devices // EXPERT...]
    pallas_call x1, Pallas kernels: 8.31 us -> 9.36 us  [key_value_state(): call(functools.partial(key_value_kernel, head_dim, tile), (PLANE,), [whol...]
    all_to_all x2, waiting for transfers between devices: 1.18 us -> 0.14 us  [exchange(): return lax.all_to_all(x, 'seq', split_axis=0, concat_axis=0, tiled=True)]
  transfers between devices with their start and end apart: 11 -> 11, of which waited for: 5 -> 4; matrix products, arithmetic and copies ran while one was open for 4% -> 4% of each run, Pallas kernels for 31% -> 31%
where the time goes in v6:
time: 69 us; the launch traced here: 68.5 us
  Pallas kernels  32.4 us (47%)
  starting transfers between devices  26.9 us (39%)
  other arithmetic  3.09 us (4%)
  waiting for transfers between devices  2.94 us (4%)
  matrix products  2.16 us (3%)
  between operations  0.91 us (1%)
    all_to_all x2, starting transfers between devices, exchange(): return lax.all_to_all(x, 'seq', split_axis=0, concat_axis=0, tiled=True)  12.3 us
    pallas_call x1, Pallas kernels, queries_within(): call(functools.partial(within_kernel, head_dim, tile), (width // pair,),...  9.61 us
    ppermute x3, starting transfers between devices, later(): lax.ppermute(x, 'seq', [(i, i + s) for i in range(lax.axis_size('seq') -...  9.48 us
    pallas_call x1, Pallas kernels, key_value_state(): call(functools.partial(key_value_kernel, head_dim, tile), (PLANE,), [whol...  9.36 us
    pallas_call x1, Pallas kernels, hidden_rows(): call(functools.partial(hidden_kernel, head_dim, tile), (), [FAR] * (4 + P...  7.72 us
    ppermute x6, starting transfers between devices, flip(): return lax.ppermute(x, 'seq', [(i, i ^ j) for i in range(devices)])  5.11 us
    pallas_call x1, Pallas kernels, labelled_rows(): call(functools.partial(labelled_kernel, width // HEADS, devices // EXPERT...  4.24 us
    dot_general x3, matrix products, dot(): lax.dot_general(a, b, (contract, ((), ())), preferred_element_type=F32, *...  2.16 us
  transfers between devices with their start and end apart: 11, of which 4 were waited for; matrix products, arithmetic and copies ran while one was open for 4% of the time, Pallas kernels for 31%

profile of v6, /device:TPU:0, one launch (start us, length us, event | category | flops | bytes accessed | tf_op | source)
XLA Modules:
  0.0 68.5 jit_solution(7544109843897343748)
XLA Ops:
  0.6 9.4 %shard_map.122 = (bf16[768,1024]{1,0:T(8,128)(2,1)}, bf16[768,1024]{1,0:T(8,128)(2,1)}, bf16[2,1024,128]{2,1,0:T(8,128)(2,1)}, bf16[32,1024]{1,0:T(8,128)(2,1)},...) custom-call(bf16[768,1024]{1,0:T(8,128)(2,1)} %refs_0_.1, ...), custom_call_target="tpu_custom_call" | custom-call | flops 3221225472 | bytes 6291456 | tf_op jit(solution)/shard_map/pallas_call | solution.py:103
  10.0 0.5 collective-permute-start
  10.5 2.6 %collective-permute-start.1 = (bf16[256,128]{1,0:T(8,128)(2,1)}, bf16[256,128]{1,0:T(8,128)(2,1)S(1)}, u32[]{:S(2)}, u32[]{:S(2)}) collective-permute-start(bf16[256,128]{1,0:T(8,128)(2,1)} %get-tuple-element.36), channel_id=1, source_target_pairs={{0,2},{1,3},{2,0},{3,1},{4,6},{5,7},{6,4},{7,5},{8,10},{9,11},{10,... | collective-permute-start | bytes 196616 | tf_op jit(solution)/shard_map/ppermute | solution.py:283
  13.2 4.2 %shard_map.123 = (f32[32,3328]{1,0:T(8,128)}, bf16[2,32,128]{2,1,0:T(8,128)(2,1)}, f32[2,32,32]{2,1,0:T(8,128)}) custom-call(bf16[768,1024]{1,0:T(8,128)(2,1)} %get-tuple-element.55.keys_far.keys, bf16[768,1024]{1,0:T(8,128)(2,1)} %get-tuple-element.56.values_far.values, bf16[32,1024]{1,0:T(8,128)(2,1)} %get-tuple-element.40.query_at, ...), custom_call_target="tpu_custom_call" | custom-call | flops 100663296 | bytes 3145728 | tf_op jit(solution)/shard_map/pallas_call | solution.py:165
  17.5 3.7 %collective-permute-start.5 = (bf16[256,128]{1,0:T(8,128)(2,1)S(1)}, bf16[256,128]{1,0:T(8,128)(2,1)S(1)}, u32[]{:S(2)}, u32[]{:S(2)}) collective-permute-start(bf16[256,128]{1,0:T(8,128)(2,1)S(1)} %fusion.22), channel_id=1, source_target_pairs={{0,4},{1,5},{2,6},{3,7},{4,8},{5,9},{6,10},{7,11},{8,12},{9,13},{1... | collective-permute-start | bytes 196616 | tf_op jit(solution)/shard_map/ppermute | solution.py:287
  21.2 4.5 %collective-permute-start.4 = (bf16[256,128]{1,0:T(8,128)(2,1)S(1)}, bf16[256,128]{1,0:T(8,128)(2,1)S(1)}, u32[]{:S(2)}, u32[]{:S(2)}) collective-permute-start(bf16[256,128]{1,0:T(8,128)(2,1)S(1)} %fusion.22), channel_id=1, source_target_pairs={{0,8},{1,9},{2,10},{3,11},{4,12},{5,13},{6,14},{7,15},{16,24},{17,... | collective-permute-start | bytes 196616 | tf_op jit(solution)/shard_map/ppermute | solution.py:287
  25.7 1.3 %collective-permute-start.3 = (bf16[256,128]{1,0:T(8,128)(2,1)S(1)}, bf16[256,128]{1,0:T(8,128)(2,1)S(1)}, u32[]{:S(2)}, u32[]{:S(2)}) collective-permute-start(bf16[256,128]{1,0:T(8,128)(2,1)S(1)} %fusion.22), channel_id=1, source_target_pairs={{0,12},{1,13},{2,14},{3,15},{16,28},{17,29},{18,30},{19,31}} | collective-permute-start | bytes 196616 | tf_op jit(solution)/shard_map/ppermute | solution.py:287
  27.1 0.8 %collective-permute-done.4 = bf16[256,128]{1,0:T(8,128)(2,1)S(1)} collective-permute-done((bf16[256,128]{1,0:T(8,128)(2,1)S(1)}, bf16[256,128]{1,0:T(8,128)(2,1)S(1)}, u32[]{:S(2)}, u32[]{:S(2)}) %collective-permute-start.4) | collective-permute-done | bytes 65568 | tf_op jit(solution)/shard_map/ppermute | solution.py:287
  27.9 1.0 %collective-permute-done.3 = bf16[256,128]{1,0:T(8,128)(2,1)S(1)} collective-permute-done((bf16[256,128]{1,0:T(8,128)(2,1)S(1)}, bf16[256,128]{1,0:T(8,128)(2,1)S(1)}, u32[]{:S(2)}, u32[]{:S(2)}) %collective-permute-start.3) | collective-permute-done | bytes 65568 | tf_op jit(solution)/shard_map/ppermute | solution.py:287
  28.9 0.2 fusion.17
  29.2 1.6 %collective-permute-start.7 = (bf16[256,128]{1,0:T(8,128)(2,1)S(1)}, bf16[256,128]{1,0:T(8,128)(2,1)S(1)}, u32[]{:S(2)}, u32[]{:S(2)}) collective-permute-start(bf16[256,128]{1,0:T(8,128)(2,1)S(1)} %get-tuple-element.51), channel_id=1, source_target_pairs={{0,2},{1,3},{2,0},{3,1},{4,6},{5,7},{6,4},{7,5},{8,10},{9,11},{10,... | collective-permute-start | bytes 196616 | tf_op jit(solution)/shard_map/ppermute | solution.py:283
  30.8 0.3 collective-permute-start.8
  31.0 1.0 %broadcast_multiply_fusion.1.packed = f32[32,3328]{1,0:T(8,128)S(1)} fusion(f32[32,3328]{1,0:T(8,128)} %get-tuple-element.43, f32[]{:T(128)S(6)} %convert_element_type.57), kind=kLoop, calls=%fused_computation.24 | loop fusion | flops 106496 | bytes 851972 | tf_op jit(solution)/shard_map/mul | solution.py:452
  32.1 1.7 %broadcast_multiply_fusion.w_output = bf16[1024,1024]{1,0:T(8,128)(2,1)S(1)} fusion(bf16[1024,1024]{1,0:T(8,128)(2,1)} %refs_3_.1, bf16[]{:T(256)} %constant.27.clone.1), kind=kLoop, calls=%fused_computation.7 | loop fusion | flops 1048576 | bytes 4194306 | tf_op jit(solution)/shard_map/mul | solution.py:452
  33.9 0.9 %collective-permute-done.8.refs_3_.refs_7_ = bf16[256,128]{1,0:T(8,128)(2,1)S(1)} collective-permute-done((bf16[256,128]{1,0:T(8,128)(2,1)S(1)}, bf16[256,128]{1,0:T(8,128)(2,1)S(1)}, u32[]{:S(2)}, u32[]{:S(2)}) %collective-permute-start.8) | collective-permute-done | bytes 65568 | tf_op jit(solution)/shard_map/ppermute | solution.py:283
  34.8 1.5 %shard_map.124 = (bf16[32,1024]{1,0:T(8,128)(2,1)S(1)}, bf16[128,1024]{1,0:T(8,128)(2,1)}) custom-call(f32[32,3328]{1,0:T(8,128)S(1)} %broadcast_multiply_fusion.1.packed, bf16[1024,1024]{1,0:T(8,128)(2,1)S(1)} %broadcast_multiply_fusion.w_output, bf16[256,128]{1,0:T(8,128)(2,1)S(1)} %get-tuple-element.49.refs_0_.refs_4_, ...), custom_call_target="tpu_custom_call" | custom-call | flops 67108864 | bytes 2097152 | tf_op jit(solution)/shard_map/pallas_call | solution.py:339
  36.3 6.4 %all-to-all-start = ((bf16[16,8,1024]{2,1,0:T(8,128)(2,1)}), bf16[16,8,1024]{2,1,0:T(8,128)(2,1)S(1)}, u32[]{:S(2)}, u32[]{:S(2)}) async-start(bf16[16,8,1024]{2,1,0:T(8,128)(2,1)} %bitcast.3), calls=%async_computation | async-start | bytes 524288 | tf_op jit(solution)/shard_map/all_to_all | solution.py:443
  42.8 0.1 fusion.25
  43.0 9.6 %shard_map.125 = (bf16[768,1024]{1,0:T(8,128)(2,1)}, bf16[768,1024]{1,0:T(8,128)(2,1)}) custom-call(bf16[768,1024]{1,0:T(8,128)(2,1)} %refs_0_.1, bf16[1024,1024]{1,0:T(8,128)(2,1)} %w_query.3, bf16[768,1024]{1,0:T(8,128)(2,1)} %get-tuple-element.55.keys_far.keys, bf16[768,1024]{1,0:T(8,128)(2,1)} %get-tuple-element.56.values_far.values, ...), custom_call_target="tpu_custom_call" | custom-call | flops 2415919104 | bytes 6291456 | tf_op jit(solution)/shard_map/pallas_call | solution.py:264
  52.7 0.1 all-to-all-done
  52.8 1.3 %fusion.3 = bf16[16,8,256]{2,1,0:T(8,128)(2,1)} fusion(bf16[1024,256]{1,0:T(8,128)(2,1)S(1)} %copy-done.5, bf16[128,1024]{1,0:T(8,128)(2,1)S(1)} %bitcast.18, bf16[1024,1024]{1,0:T(8,128)(2,1)S(1)} %copy-done), kind=kOutput, calls=%fused_computation.4 | convolution fusion | flops 335839232 | bytes 2949120 | tf_op jit(solution)/shard_map/dot_general | solution.py:20
  54.1 5.9 %all-to-all-start.1 = ((bf16[16,8,256]{2,1,0:T(8,128)(2,1)}), bf16[16,8,256]{2,1,0:T(8,128)(2,1)S(1)}, u32[]{:S(2)}, u32[]{:S(2)}) async-start(bf16[16,8,256]{2,1,0:T(8,128)(2,1)} %fusion.3), calls=%async_computation.1 | async-start | bytes 131072 | tf_op jit(solution)/shard_map/all_to_all | solution.py:443
  60.0 7.7 %shard_map.126 = bf16[768,1024]{1,0:T(8,128)(2,1)} custom-call(bf16[768,1024]{1,0:T(8,128)(2,1)} %refs_0_.1, bf16[768,1024]{1,0:T(8,128)(2,1)} %get-tuple-element.60.refs_1_, bf16[768,1024]{1,0:T(8,128)(2,1)} %get-tuple-element.61.refs_2_, bf16[1024,1024]{1,0:T(8,128)(2,1)} %refs_3_.1, bf16[256,128]{1,0:T(8,128)(2,1)} %copy-done.1, ...), custom_call_target="tpu_custom_call" | custom-call | flops 1610612736 | bytes 7864320 | tf_op jit(solution)/shard_map/pallas_call | solution.py:394
  67.8 0.8 %fusion.4 = f32[32,256]{1,0:T(8,128)} fusion(bf16[2,32,128]{2,1,0:T(8,128)(2,1)S(1)} %copy-done.9, bf16[16,8,256]{2,1,0:T(8,128)(2,1)S(1)} %all-to-all-done.1, f32[2,32]{1,0:T(2,128)S(1)} %add_divide_fusion), kind=kOutput, calls=%fused_computation.6 | convolution fusion | flops 4218880 | bytes 114944 | tf_op jit(solution)/shard_map/dot_general | solution.py:20
  (32 shorter events, 0.4 us)
Async XLA Ops:
  0.6 52.2 %copy-start = (bf16[1024,1024]{1,0:T(8,128)(2,1)S(1)}, bf16[1024,1024]{1,0:T(8,128)(2,1)}, u32[]{:S(2)}) copy-start(bf16[1024,1024]{1,0:T(8,128)(2,1)} %param.16) | copy-start | bytes 6291460
  10.0 7.5 %copy-start.6 = (bf16[256,128]{1,0:T(8,128)(2,1)S(1)}, bf16[256,128]{1,0:T(8,128)(2,1)}, u32[]{:S(2)}) copy-start(bf16[256,128]{1,0:T(8,128)(2,1)} %get-tuple-element.44) | copy-start | bytes 196612
  10.0 7.4 %collective-permute-start = (bf16[256,128]{1,0:T(8,128)(2,1)}, bf16[256,128]{1,0:T(8,128)(2,1)S(1)}, u32[]{:S(2)}, u32[]{:S(2)}) collective-permute-start(bf16[256,128]{1,0:T(8,128)(2,1)} %get-tuple-element.35), channel_id=1, source_target_pairs={{0,1},{1,0},{2,3},{3,2},{4,5},{5,4},{6,7},{7,6},{8,9},{9,8},{10,11... | collective-permute-start | bytes 196616 | tf_op jit(solution)/shard_map/ppermute | solution.py:283
  10.5 6.9 %collective-permute-start.1 = (bf16[256,128]{1,0:T(8,128)(2,1)}, bf16[256,128]{1,0:T(8,128)(2,1)S(1)}, u32[]{:S(2)}, u32[]{:S(2)}) collective-permute-start(bf16[256,128]{1,0:T(8,128)(2,1)} %get-tuple-element.36), channel_id=1, source_target_pairs={{0,2},{1,3},{2,0},{3,1},{4,6},{5,7},{6,4},{7,5},{8,10},{9,11},{10,... | collective-permute-start | bytes 196616 | tf_op jit(solution)/shard_map/ppermute | solution.py:283
  13.1 4.3 %collective-permute-start.2 = (bf16[256,128]{1,0:T(8,128)(2,1)}, bf16[256,128]{1,0:T(8,128)(2,1)S(1)}, u32[]{:S(2)}, u32[]{:S(2)}) collective-permute-start(bf16[256,128]{1,0:T(8,128)(2,1)} %get-tuple-element.37), channel_id=1, source_target_pairs={{0,3},{1,2},{2,1},{3,0},{4,7},{5,6},{6,5},{7,4},{8,11},{9,10},{10,... | collective-permute-start | bytes 196616 | tf_op jit(solution)/shard_map/ppermute | solution.py:283
  17.5 9.5 %collective-permute-start.5 = (bf16[256,128]{1,0:T(8,128)(2,1)S(1)}, bf16[256,128]{1,0:T(8,128)(2,1)S(1)}, u32[]{:S(2)}, u32[]{:S(2)}) collective-permute-start(bf16[256,128]{1,0:T(8,128)(2,1)S(1)} %fusion.22), channel_id=1, source_target_pairs={{0,4},{1,5},{2,6},{3,7},{4,8},{5,9},{6,10},{7,11},{8,12},{9,13},{1... | collective-permute-start | bytes 196616 | tf_op jit(solution)/shard_map/ppermute | solution.py:287
  21.2 6.7 %collective-permute-start.4 = (bf16[256,128]{1,0:T(8,128)(2,1)S(1)}, bf16[256,128]{1,0:T(8,128)(2,1)S(1)}, u32[]{:S(2)}, u32[]{:S(2)}) collective-permute-start(bf16[256,128]{1,0:T(8,128)(2,1)S(1)} %fusion.22), channel_id=1, source_target_pairs={{0,8},{1,9},{2,10},{3,11},{4,12},{5,13},{6,14},{7,15},{16,24},{17,... | collective-permute-start | bytes 196616 | tf_op jit(solution)/shard_map/ppermute | solution.py:287
  25.7 3.2 %collective-permute-start.3 = (bf16[256,128]{1,0:T(8,128)(2,1)S(1)}, bf16[256,128]{1,0:T(8,128)(2,1)S(1)}, u32[]{:S(2)}, u32[]{:S(2)}) collective-permute-start(bf16[256,128]{1,0:T(8,128)(2,1)S(1)} %fusion.22), channel_id=1, source_target_pairs={{0,12},{1,13},{2,14},{3,15},{16,28},{17,29},{18,30},{19,31}} | collective-permute-start | bytes 196616 | tf_op jit(solution)/shard_map/ppermute | solution.py:287
  29.1 5.7 %copy-start.1 = (bf16[256,128]{1,0:T(8,128)(2,1)}, bf16[256,128]{1,0:T(8,128)(2,1)S(1)}, u32[]{:S(2)}) copy-start(bf16[256,128]{1,0:T(8,128)(2,1)S(1)} %get-tuple-element.49.refs_0_.refs_4_) | copy-start | bytes 196612
  29.1 4.7 %collective-permute-start.6 = (bf16[256,128]{1,0:T(8,128)(2,1)S(1)}, bf16[256,128]{1,0:T(8,128)(2,1)S(1)}, u32[]{:S(2)}, u32[]{:S(2)}) collective-permute-start(bf16[256,128]{1,0:T(8,128)(2,1)S(1)} %get-tuple-element.50), channel_id=1, source_target_pairs={{0,1},{1,0},{2,3},{3,2},{4,5},{5,4},{6,7},{7,6},{8,9},{9,8},{10,11... | collective-permute-start | bytes 196616 | tf_op jit(solution)/shard_map/ppermute | solution.py:283
  29.2 4.7 %collective-permute-start.7 = (bf16[256,128]{1,0:T(8,128)(2,1)S(1)}, bf16[256,128]{1,0:T(8,128)(2,1)S(1)}, u32[]{:S(2)}, u32[]{:S(2)}) collective-permute-start(bf16[256,128]{1,0:T(8,128)(2,1)S(1)} %get-tuple-element.51), channel_id=1, source_target_pairs={{0,2},{1,3},{2,0},{3,1},{4,6},{5,7},{6,4},{7,5},{8,10},{9,11},{10,... | collective-permute-start | bytes 196616 | tf_op jit(solution)/shard_map/ppermute | solution.py:283
  30.8 4.0 %collective-permute-start.8 = (bf16[256,128]{1,0:T(8,128)(2,1)S(1)}, bf16[256,128]{1,0:T(8,128)(2,1)S(1)}, u32[]{:S(2)}, u32[]{:S(2)}) collective-permute-start(bf16[256,128]{1,0:T(8,128)(2,1)S(1)} %get-tuple-element.52), channel_id=1, source_target_pairs={{0,3},{1,2},{2,1},{3,0},{4,7},{5,6},{6,5},{7,4},{8,11},{9,10},{10,... | collective-permute-start | bytes 196616 | tf_op jit(solution)/shard_map/ppermute | solution.py:283
  33.8 9.0 %copy-start.7 = (bf16[1024,32]{0,1:T(8,128)(2,1)S(1)}, bf16[1024,32]{0,1:T(8,128)(2,1)}, u32[]{:S(2)}) copy-start(bf16[1024,32]{0,1:T(8,128)(2,1)} %param.18) | copy-start | bytes 196612
  33.8 9.1 %copy-start.8 = (f32[2,32,32]{2,1,0:T(8,128)S(1)}, f32[2,32,32]{2,1,0:T(8,128)}, u32[]{:S(2)}) copy-start(f32[2,32,32]{2,1,0:T(8,128)} %get-tuple-element.63) | copy-start | bytes 24580
  33.8 18.8 %copy-start.2 = (bf16[256,128]{1,0:T(8,128)(2,1)}, bf16[256,128]{1,0:T(8,128)(2,1)S(1)}, u32[]{:S(2)}) copy-start(bf16[256,128]{1,0:T(8,128)(2,1)S(1)} %collective-permute-done.6.refs_1_.refs_5_) | copy-start | bytes 196612
  33.9 18.8 %copy-start.3 = (bf16[256,128]{1,0:T(8,128)(2,1)}, bf16[256,128]{1,0:T(8,128)(2,1)S(1)}, u32[]{:S(2)}) copy-start(bf16[256,128]{1,0:T(8,128)(2,1)S(1)} %collective-permute-done.7.refs_2_.refs_6_) | copy-start | bytes 196612
  34.8 17.9 %copy-start.4 = (bf16[256,128]{1,0:T(8,128)(2,1)}, bf16[256,128]{1,0:T(8,128)(2,1)S(1)}, u32[]{:S(2)}) copy-start(bf16[256,128]{1,0:T(8,128)(2,1)S(1)} %collective-permute-done.8.refs_3_.refs_7_) | copy-start | bytes 196612
  36.3 16.5 %all-to-all-start = ((bf16[16,8,1024]{2,1,0:T(8,128)(2,1)}), bf16[16,8,1024]{2,1,0:T(8,128)(2,1)S(1)}, u32[]{:S(2)}, u32[]{:S(2)}) async-start(bf16[16,8,1024]{2,1,0:T(8,128)(2,1)} %bitcast.3), calls=%async_computation | async-start | bytes 524288 | tf_op jit(solution)/shard_map/all_to_all | solution.py:443
  43.0 9.8 %copy-start.5 = (bf16[1024,256]{1,0:T(8,128)(2,1)S(1)}, bf16[1024,256]{1,0:T(8,128)(2,1)}, u32[]{:S(2)}) copy-start(bf16[1024,256]{1,0:T(8,128)(2,1)} %param.17) | copy-start | bytes 1572868
  54.1 13.6 %all-to-all-start.1 = ((bf16[16,8,256]{2,1,0:T(8,128)(2,1)}), bf16[16,8,256]{2,1,0:T(8,128)(2,1)S(1)}, u32[]{:S(2)}, u32[]{:S(2)}) async-start(bf16[16,8,256]{2,1,0:T(8,128)(2,1)} %fusion.3), calls=%async_computation.1 | async-start | bytes 131072 | tf_op jit(solution)/shard_map/all_to_all | solution.py:443
  60.0 7.7 %copy-start.9 = (bf16[2,32,128]{2,1,0:T(8,128)(2,1)S(1)}, bf16[2,32,128]{2,1,0:T(8,128)(2,1)}, u32[]{:S(2)}) copy-start(bf16[2,32,128]{2,1,0:T(8,128)(2,1)} %get-tuple-element.64) | copy-start | bytes 49156

commit v7 on v5

--- a/solution.py
+++ b/solution.py
@@ -60,8 +60,9 @@
 
 
 def key_value_kernel(head_dim, tile, events, w_key, w_value, keys, values, inner, *states):
-    k = dot(events[...], w_key[...]).astype(BF16)
-    v = dot(events[...], w_value[...]).astype(BF16)
+    pair = w_key.shape[1]
+    both = dot(events[...], jnp.concatenate([w_key[...], w_value[...]], axis=1)).astype(BF16)
+    k, v = both[:, :pair], both[:, pair:]
     keys[...] = k
     values[...] = v
     total = None
@@ -69,9 +70,9 @@
         here = slice(i * tile, (i + 1) * tile)
         if i:
             inner[i - 1] = total.astype(BF16)
-        both = dot(k[here], v[here], ((0,), (0,)))
-        parts = [slice(h * head_dim, (h + 1) * head_dim) for h in range(both.shape[0] // head_dim)]
-        own = jnp.concatenate([both[part, part] for part in parts], axis=0)
+        product = dot(k[here], v[here], ((0,), (0,)))
+        parts = [slice(h, h + head_dim) for h in range(0, pair, head_dim)]
+        own = jnp.concatenate([product[part, part] for part in parts], axis=0)
         total = own if total is None else total + own
     for i, state in enumerate(states):
 
@@ -88,7 +89,7 @@
     inner = rows // tile - 1
 
     def turn(i):
-        return i ^ (lax.axis_index("seq") % PLANE)
+        return (lax.axis_index("seq") ^ i) & (PLANE - 1)
 
     def cols(many):
         return pl.BlockSpec((many, pair), lambda i: (0, turn(i)))
@@ -97,9 +98,10 @@
         functools.partial(key_value_kernel, head_dim, tile),
         (PLANE,),
         [whole((rows, width)), cols(width), cols(width)],
-        [cols(rows), cols(rows), pl.BlockSpec((inner, pair, head_dim), lambda i: (0, turn(i), 0))]
+        [pl.BlockSpec((None, rows, pair), lambda i: (turn(i), 0, 0))] * 2
+        + [pl.BlockSpec((inner, pair, head_dim), lambda i: (0, turn(i), 0))]
         + [whole((pair, head_dim))] * PLANE,
-        [shaped((rows, width), BF16)] * 2
+        [shaped((PLANE, rows, pair), BF16)] * 2
         + [shaped((inner, width, head_dim), BF16)]
         + [shaped((pair, head_dim), BF16)] * PLANE,
         4 * rows * width * width,
@@ -116,8 +118,7 @@
     fetches = []
     for far, here in ((events_far, events), (w_query_far, w_query), (keys_far, keys), (values_far, values)):
         fetches.append(pltpu.make_async_copy(far, here, done.at[len(fetches)]))
-    fetches[0].start()
-    fetches[1].start()
+        fetches[-1].start()
     rows, width = events.shape
     many = labels.shape[1]
 
@@ -135,22 +136,25 @@
         column[k] = jnp.where(number == chosen_column, 1.0, 0.0)
     chosen = row_choice(labels[...], rows)
     causal = lax.broadcasted_iota(jnp.int32, (many, rows), 1) <= upright(labels[...])
-    parts = [slice(h, h + head_dim) for h in range(0, width, head_dim)]
+    pair = 2 * head_dim
+    parts = [slice(c, c + pair) for c in range(0, width, pair)]
 
     fetches[0].wait()
-    fetches[2].start()
-    fetches[3].start()
     chosen_events = dot(chosen, events[...]).astype(BF16)
     packed[:, width : 2 * width] = chosen_events.astype(F32)
     fetches[1].wait()
     query = dot(chosen_events, w_query[...]).astype(BF16)
     packed[:, :width] = query.astype(F32)
+    causal = jnp.concatenate([causal, causal], axis=0)
+    apart = [heads_apart(query[:, part], head_dim) for part in parts]
     fetches[2].wait()
-    weights = [dot(query[:, part], keys[:, part], ((1,), (1,))) for part in parts]
+    weights = [dot(q, keys[p], ((1,), (1,))) for p, q in enumerate(apart)]
     weights = [jnp.where(causal, weight, 0.0).astype(BF16) for weight in weights]
     fetches[3].wait()
-    for part, weight in zip(parts, weights):
-        packed[:, 2 * width + part.start : 2 * width + part.stop] = dot(weight, values[:, part])
+    for p, (part, weight) in enumerate(zip(parts, weights)):
+        terms = dot(weight, values[p])
+        terms = jnp.concatenate([terms[:many, :head_dim], terms[many:, head_dim:]], axis=1)
+        packed[:, 2 * width + part.start : 2 * width + part.stop] = terms
 
 
 def labelled_rows(events, w_query, keys, values, labels, experts, tasks, devices):
@@ -250,8 +254,8 @@
         [
             whole((rows, width)),
             columns(width, pair),
-            columns(rows, pair),
-            columns(rows, pair),
+            pl.BlockSpec((None, rows, pair), lambda i: (i, 0, 0)),
+            pl.BlockSpec((None, rows, pair), lambda i: (i, 0, 0)),
             pl.BlockSpec((inner.shape[0], pair, head_dim), lambda i: (0, i, 0)),
         ],
         [columns(rows, pair), columns(rows, pair)],
@@ -276,7 +280,7 @@
 
 def sums_before(states):
     devices = lax.axis_size("seq")
-    rank = lax.axis_index("seq") % PLANE
+    rank = lax.axis_index("seq") & (PLANE - 1)
     states = [x.astype(F32) for x in states]
     total = sum(states).astype(BF16)
     planes = sum(later(total, s).astype(F32) for s in reversed(range(PLANE, devices, PLANE)))
@@ -294,7 +298,7 @@
 
 
 def put_prefix(prefix, parts, head_dim):
-    rank = lax.axis_index("seq") % PLANE
+    rank = lax.axis_index("seq") & (PLANE - 1)
     for j, part in enumerate(parts):
         prefix[rank ^ j] = on_diagonal(part[...], head_dim)
 

time: 68.6 us -> 67.9 us (0.990)
  Pallas kernels: 31 us -> 30.3 us
  transfers between devices with their start and end apart: 11 -> 11, of which waited for: 5 -> 5; matrix products, arithmetic and copies ran while one was open for 4% -> 4% of each run, Pallas kernels for 31% -> 30%
where the time goes in v7:
time: 67.9 us; the launch traced here: 67.4 us
  Pallas kernels  30.3 us (45%)
  starting transfers between devices  26.9 us (40%)
  waiting for transfers between devices  3.99 us (6%)
  other arithmetic  3.09 us (5%)
  matrix products  2.16 us (3%)
  between operations  0.89 us (1%)
    all_to_all x2, starting transfers between devices, exchange(): return lax.all_to_all(x, 'seq', split_axis=0, concat_axis=0, tiled=True)  12.3 us
    pallas_call x1, Pallas kernels, queries_within(): call(functools.partial(within_kernel, head_dim, tile), (width // pair,),...  9.6 us
    ppermute x3, starting transfers between devices, later(): lax.ppermute(x, 'seq', [(i, i + s) for i in range(lax.axis_size('seq') -...  9.48 us
    pallas_call x1, Pallas kernels, key_value_state(): call(functools.partial(key_value_kernel, head_dim, tile), (PLANE,), [whol...  8.3 us
    pallas_call x1, Pallas kernels, hidden_rows(): call(functools.partial(hidden_kernel, head_dim, tile), (), [FAR] * (4 + P...  5.84 us
    ppermute x6, starting transfers between devices, flip(): return lax.ppermute(x, 'seq', [(i, i ^ j) for i in range(devices)])  5.11 us
    pallas_call x1, Pallas kernels, labelled_rows(): call(functools.partial(labelled_kernel, width // HEADS, devices // EXPERT...  5.08 us
    dot_general x3, matrix products, dot(): lax.dot_general(a, b, (contract, ((), ())), preferred_element_type=F32, *...  2.16 us
  transfers between devices with their start and end apart: 11, of which 5 were waited for; matrix products, arithmetic and copies ran while one was open for 4% of the time, Pallas kernels for 30%

profile of v7, /device:TPU:0, one launch (start us, length us, event | category | flops | bytes accessed | tf_op | source)
XLA Modules:
  0.0 67.4 jit_solution(5886822238923086790)
XLA Ops:
  0.6 8.3 %shard_map.122 = (bf16[4,768,256]{2,1,0:T(8,128)(2,1)}, bf16[4,768,256]{2,1,0:T(8,128)(2,1)}, bf16[2,1024,128]{2,1,0:T(8,128)(2,1)}, bf16[256,128]{1,0:T(8,128)(...) custom-call(bf16[768,1024]{1,0:T(8,128)(2,1)} %refs_0_.1, ...), custom_call_target="tpu_custom_call" | custom-call | flops 3221225472 | bytes 6291456 | tf_op jit(solution)/shard_map/pallas_call | solution.py:97
  8.9 0.5 collective-permute-start
  9.5 2.6 %collective-permute-start.1 = (bf16[256,128]{1,0:T(8,128)(2,1)}, bf16[256,128]{1,0:T(8,128)(2,1)S(1)}, u32[]{:S(2)}, u32[]{:S(2)}) collective-permute-start(bf16[256,128]{1,0:T(8,128)(2,1)} %get-tuple-element.34), channel_id=1, source_target_pairs={{0,2},{1,3},{2,0},{3,1},{4,6},{5,7},{6,4},{7,5},{8,10},{9,11},{10,... | collective-permute-start | bytes 196616 | tf_op jit(solution)/shard_map/ppermute | solution.py:270
  12.1 5.1 %shard_map.123 = (f32[32,3328]{1,0:T(8,128)}, bf16[2,32,128]{2,1,0:T(8,128)(2,1)}, f32[2,32,32]{2,1,0:T(8,128)}) custom-call(bf16[768,1024]{1,0:T(8,128)(2,1)} %refs_0_.1, bf16[1024,1024]{1,0:T(8,128)(2,1)} %w_query.1, bf16[4,768,256]{2,1,0:T(8,128)(2,1)} %get-tuple-element.51.keys_far.keys, bf16[4,768,256]{2,1,0:T(8,128)(2,1)} %get-tuple-element.52.values_far.values, ...), custom_call_target="tpu_custom_call" | custom-call | flops 100663296 | bytes 6291456 | tf_op jit(solution)/shard_map/pallas_call | solution.py:164
  17.3 3.7 %collective-permute-start.5 = (bf16[256,128]{1,0:T(8,128)(2,1)S(1)}, bf16[256,128]{1,0:T(8,128)(2,1)S(1)}, u32[]{:S(2)}, u32[]{:S(2)}) collective-permute-start(bf16[256,128]{1,0:T(8,128)(2,1)S(1)} %fusion.22), channel_id=1, source_target_pairs={{0,4},{1,5},{2,6},{3,7},{4,8},{5,9},{6,10},{7,11},{8,12},{9,13},{1... | collective-permute-start | bytes 196616 | tf_op jit(solution)/shard_map/ppermute | solution.py:274
  21.0 4.5 %collective-permute-start.4 = (bf16[256,128]{1,0:T(8,128)(2,1)S(1)}, bf16[256,128]{1,0:T(8,128)(2,1)S(1)}, u32[]{:S(2)}, u32[]{:S(2)}) collective-permute-start(bf16[256,128]{1,0:T(8,128)(2,1)S(1)} %fusion.22), channel_id=1, source_target_pairs={{0,8},{1,9},{2,10},{3,11},{4,12},{5,13},{6,14},{7,15},{16,24},{17,... | collective-permute-start | bytes 196616 | tf_op jit(solution)/shard_map/ppermute | solution.py:274
  25.5 1.3 %collective-permute-start.3 = (bf16[256,128]{1,0:T(8,128)(2,1)S(1)}, bf16[256,128]{1,0:T(8,128)(2,1)S(1)}, u32[]{:S(2)}, u32[]{:S(2)}) collective-permute-start(bf16[256,128]{1,0:T(8,128)(2,1)S(1)} %fusion.22), channel_id=1, source_target_pairs={{0,12},{1,13},{2,14},{3,15},{16,28},{17,29},{18,30},{19,31}} | collective-permute-start | bytes 196616 | tf_op jit(solution)/shard_map/ppermute | solution.py:274
  26.9 0.8 %collective-permute-done.4 = bf16[256,128]{1,0:T(8,128)(2,1)S(1)} collective-permute-done((bf16[256,128]{1,0:T(8,128)(2,1)S(1)}, bf16[256,128]{1,0:T(8,128)(2,1)S(1)}, u32[]{:S(2)}, u32[]{:S(2)}) %collective-permute-start.4) | collective-permute-done | bytes 65568 | tf_op jit(solution)/shard_map/ppermute | solution.py:274
  27.7 1.0 %collective-permute-done.3 = bf16[256,128]{1,0:T(8,128)(2,1)S(1)} collective-permute-done((bf16[256,128]{1,0:T(8,128)(2,1)S(1)}, bf16[256,128]{1,0:T(8,128)(2,1)S(1)}, u32[]{:S(2)}, u32[]{:S(2)}) %collective-permute-start.3) | collective-permute-done | bytes 65568 | tf_op jit(solution)/shard_map/ppermute | solution.py:274
  28.7 0.2 fusion.17
  29.0 1.6 %collective-permute-start.7 = (bf16[256,128]{1,0:T(8,128)(2,1)S(1)}, bf16[256,128]{1,0:T(8,128)(2,1)S(1)}, u32[]{:S(2)}, u32[]{:S(2)}) collective-permute-start(bf16[256,128]{1,0:T(8,128)(2,1)S(1)} %get-tuple-element.47), channel_id=1, source_target_pairs={{0,2},{1,3},{2,0},{3,1},{4,6},{5,7},{6,4},{7,5},{8,10},{9,11},{10,... | collective-permute-start | bytes 196616 | tf_op jit(solution)/shard_map/ppermute | solution.py:270
  30.5 0.3 collective-permute-start.8
  30.8 1.0 %broadcast_multiply_fusion.1.packed = f32[32,3328]{1,0:T(8,128)S(1)} fusion(f32[32,3328]{1,0:T(8,128)} %get-tuple-element.39, f32[]{:T(128)S(6)} %convert_element_type.57), kind=kLoop, calls=%fused_computation.24 | loop fusion | flops 106496 | bytes 851972 | tf_op jit(solution)/shard_map/mul | solution.py:445
  31.9 1.7 %broadcast_multiply_fusion.w_output = bf16[1024,1024]{1,0:T(8,128)(2,1)S(1)} fusion(bf16[1024,1024]{1,0:T(8,128)(2,1)} %refs_3_.1, bf16[]{:T(256)} %constant.4.clone.1), kind=kLoop, calls=%fused_computation.7 | loop fusion | flops 1048576 | bytes 4194306 | tf_op jit(solution)/shard_map/mul | solution.py:445
  33.7 0.9 %collective-permute-done.8.refs_3_.refs_7_ = bf16[256,128]{1,0:T(8,128)(2,1)S(1)} collective-permute-done((bf16[256,128]{1,0:T(8,128)(2,1)S(1)}, bf16[256,128]{1,0:T(8,128)(2,1)S(1)}, u32[]{:S(2)}, u32[]{:S(2)}) %collective-permute-start.8) | collective-permute-done | bytes 65568 | tf_op jit(solution)/shard_map/ppermute | solution.py:270
  34.6 1.5 %shard_map.124 = (bf16[32,1024]{1,0:T(8,128)(2,1)S(1)}, bf16[128,1024]{1,0:T(8,128)(2,1)}) custom-call(f32[32,3328]{1,0:T(8,128)S(1)} %broadcast_multiply_fusion.1.packed, bf16[1024,1024]{1,0:T(8,128)(2,1)S(1)} %broadcast_multiply_fusion.w_output, bf16[256,128]{1,0:T(8,128)(2,1)S(1)} %get-tuple-element.45.refs_0_.refs_4_, ...), custom_call_target="tpu_custom_call" | custom-call | flops 67108864 | bytes 2097152 | tf_op jit(solution)/shard_map/pallas_call | solution.py:326
  36.1 6.4 %all-to-all-start = ((bf16[16,8,1024]{2,1,0:T(8,128)(2,1)}), bf16[16,8,1024]{2,1,0:T(8,128)(2,1)S(1)}, u32[]{:S(2)}, u32[]{:S(2)}) async-start(bf16[16,8,1024]{2,1,0:T(8,128)(2,1)} %bitcast.3), calls=%async_computation | async-start | bytes 524288 | tf_op jit(solution)/shard_map/all_to_all | solution.py:436
  42.8 9.6 %shard_map.125 = (bf16[768,1024]{1,0:T(8,128)(2,1)}, bf16[768,1024]{1,0:T(8,128)(2,1)}) custom-call(bf16[768,1024]{1,0:T(8,128)(2,1)} %refs_0_.1, bf16[1024,1024]{1,0:T(8,128)(2,1)} %w_query.1, bf16[4,768,256]{2,1,0:T(8,128)(2,1)} %get-tuple-element.51.keys_far.keys, bf16[4,768,256]{2,1,0:T(8,128)(2,1)} %get-tuple-element.52.values_far.values, ...), custom_call_target="tpu_custom_call" | custom-call | flops 2415919104 | bytes 6291456 | tf_op jit(solution)/shard_map/pallas_call | solution.py:251
  52.4 0.2 all-to-all-done
  52.6 1.3 %fusion.3 = bf16[16,8,256]{2,1,0:T(8,128)(2,1)} fusion(bf16[1024,256]{1,0:T(8,128)(2,1)S(1)} %copy-done.5, bf16[128,1024]{1,0:T(8,128)(2,1)S(1)} %bitcast.18, bf16[1024,1024]{1,0:T(8,128)(2,1)S(1)} %copy-done), kind=kOutput, calls=%fused_computation.4 | convolution fusion | flops 335839232 | bytes 2949120 | tf_op jit(solution)/shard_map/dot_general | solution.py:20
  53.9 5.9 %all-to-all-start.1 = ((bf16[16,8,256]{2,1,0:T(8,128)(2,1)}), bf16[16,8,256]{2,1,0:T(8,128)(2,1)S(1)}, u32[]{:S(2)}, u32[]{:S(2)}) async-start(bf16[16,8,256]{2,1,0:T(8,128)(2,1)} %fusion.3), calls=%async_computation.1 | async-start | bytes 131072 | tf_op jit(solution)/shard_map/all_to_all | solution.py:436
  59.8 5.8 %shard_map.126 = bf16[768,1024]{1,0:T(8,128)(2,1)} custom-call(bf16[768,1024]{1,0:T(8,128)(2,1)} %refs_0_.1, bf16[768,1024]{1,0:T(8,128)(2,1)} %get-tuple-element.56.refs_1_, bf16[768,1024]{1,0:T(8,128)(2,1)} %get-tuple-element.57.refs_2_, bf16[1024,1024]{1,0:T(8,128)(2,1)} %refs_3_.1, bf16[256,128]{1,0:T(8,128)(2,1)} %copy-done.1, ...), custom_call_target="tpu_custom_call" | custom-call | flops 1610612736 | bytes 7864320 | tf_op jit(solution)/shard_map/pallas_call | solution.py:389
  65.6 1.0 %all-to-all-done.1 = bf16[16,8,256]{2,1,0:T(8,128)(2,1)S(1)} async-done(((bf16[16,8,256]{2,1,0:T(8,128)(2,1)}), bf16[16,8,256]{2,1,0:T(8,128)(2,1)S(1)}, u32[]{:S(2)}, u32[]{:S(2)}) %all-to-all-start.1) | async-done | bytes 65568 | tf_op jit(solution)/shard_map/all_to_all | solution.py:436
  66.7 0.8 %fusion.4 = f32[32,256]{1,0:T(8,128)} fusion(bf16[2,32,128]{2,1,0:T(8,128)(2,1)S(1)} %copy-done.9, bf16[16,8,256]{2,1,0:T(8,128)(2,1)S(1)} %all-to-all-done.1, f32[2,32]{1,0:T(2,128)S(1)} %add_divide_fusion), kind=kOutput, calls=%fused_computation.6 | convolution fusion | flops 4218880 | bytes 114944 | tf_op jit(solution)/shard_map/dot_general | solution.py:20
  (32 shorter events, 0.5 us)
Async XLA Ops:
  0.6 52.0 %copy-start = (bf16[1024,1024]{1,0:T(8,128)(2,1)S(1)}, bf16[1024,1024]{1,0:T(8,128)(2,1)}, u32[]{:S(2)}) copy-start(bf16[1024,1024]{1,0:T(8,128)(2,1)} %param.16) | copy-start | bytes 6291460
  8.9 8.3 %collective-permute-start = (bf16[256,128]{1,0:T(8,128)(2,1)}, bf16[256,128]{1,0:T(8,128)(2,1)S(1)}, u32[]{:S(2)}, u32[]{:S(2)}) collective-permute-start(bf16[256,128]{1,0:T(8,128)(2,1)} %get-tuple-element.33), channel_id=1, source_target_pairs={{0,1},{1,0},{2,3},{3,2},{4,5},{5,4},{6,7},{7,6},{8,9},{9,8},{10,11... | collective-permute-start | bytes 196616 | tf_op jit(solution)/shard_map/ppermute | solution.py:270
  9.5 7.8 %collective-permute-start.1 = (bf16[256,128]{1,0:T(8,128)(2,1)}, bf16[256,128]{1,0:T(8,128)(2,1)S(1)}, u32[]{:S(2)}, u32[]{:S(2)}) collective-permute-start(bf16[256,128]{1,0:T(8,128)(2,1)} %get-tuple-element.34), channel_id=1, source_target_pairs={{0,2},{1,3},{2,0},{3,1},{4,6},{5,7},{6,4},{7,5},{8,10},{9,11},{10,... | collective-permute-start | bytes 196616 | tf_op jit(solution)/shard_map/ppermute | solution.py:270
  12.1 5.2 %collective-permute-start.2 = (bf16[256,128]{1,0:T(8,128)(2,1)}, bf16[256,128]{1,0:T(8,128)(2,1)S(1)}, u32[]{:S(2)}, u32[]{:S(2)}) collective-permute-start(bf16[256,128]{1,0:T(8,128)(2,1)} %get-tuple-element.35), channel_id=1, source_target_pairs={{0,3},{1,2},{2,1},{3,0},{4,7},{5,6},{6,5},{7,4},{8,11},{9,10},{10,... | collective-permute-start | bytes 196616 | tf_op jit(solution)/shard_map/ppermute | solution.py:270
  12.1 5.1 %copy-start.6 = (bf16[256,128]{1,0:T(8,128)(2,1)S(1)}, bf16[256,128]{1,0:T(8,128)(2,1)}, u32[]{:S(2)}) copy-start(bf16[256,128]{1,0:T(8,128)(2,1)} %get-tuple-element.40) | copy-start | bytes 196612
  17.3 9.5 %collective-permute-start.5 = (bf16[256,128]{1,0:T(8,128)(2,1)S(1)}, bf16[256,128]{1,0:T(8,128)(2,1)S(1)}, u32[]{:S(2)}, u32[]{:S(2)}) collective-permute-start(bf16[256,128]{1,0:T(8,128)(2,1)S(1)} %fusion.22), channel_id=1, source_target_pairs={{0,4},{1,5},{2,6},{3,7},{4,8},{5,9},{6,10},{7,11},{8,12},{9,13},{1... | collective-permute-start | bytes 196616 | tf_op jit(solution)/shard_map/ppermute | solution.py:274
  21.0 6.6 %collective-permute-start.4 = (bf16[256,128]{1,0:T(8,128)(2,1)S(1)}, bf16[256,128]{1,0:T(8,128)(2,1)S(1)}, u32[]{:S(2)}, u32[]{:S(2)}) collective-permute-start(bf16[256,128]{1,0:T(8,128)(2,1)S(1)} %fusion.22), channel_id=1, source_target_pairs={{0,8},{1,9},{2,10},{3,11},{4,12},{5,13},{6,14},{7,15},{16,24},{17,... | collective-permute-start | bytes 196616 | tf_op jit(solution)/shard_map/ppermute | solution.py:274
  25.5 3.2 %collective-permute-start.3 = (bf16[256,128]{1,0:T(8,128)(2,1)S(1)}, bf16[256,128]{1,0:T(8,128)(2,1)S(1)}, u32[]{:S(2)}, u32[]{:S(2)}) collective-permute-start(bf16[256,128]{1,0:T(8,128)(2,1)S(1)} %fusion.22), channel_id=1, source_target_pairs={{0,12},{1,13},{2,14},{3,15},{16,28},{17,29},{18,30},{19,31}} | collective-permute-start | bytes 196616 | tf_op jit(solution)/shard_map/ppermute | solution.py:274
  28.9 5.7 %copy-start.1 = (bf16[256,128]{1,0:T(8,128)(2,1)}, bf16[256,128]{1,0:T(8,128)(2,1)S(1)}, u32[]{:S(2)}) copy-start(bf16[256,128]{1,0:T(8,128)(2,1)S(1)} %get-tuple-element.45.refs_0_.refs_4_) | copy-start | bytes 196612
  28.9 4.7 %collective-permute-start.6 = (bf16[256,128]{1,0:T(8,128)(2,1)S(1)}, bf16[256,128]{1,0:T(8,128)(2,1)S(1)}, u32[]{:S(2)}, u32[]{:S(2)}) collective-permute-start(bf16[256,128]{1,0:T(8,128)(2,1)S(1)} %get-tuple-element.46), channel_id=1, source_target_pairs={{0,1},{1,0},{2,3},{3,2},{4,5},{5,4},{6,7},{7,6},{8,9},{9,8},{10,11... | collective-permute-start | bytes 196616 | tf_op jit(solution)/shard_map/ppermute | solution.py:270
  29.0 4.7 %collective-permute-start.7 = (bf16[256,128]{1,0:T(8,128)(2,1)S(1)}, bf16[256,128]{1,0:T(8,128)(2,1)S(1)}, u32[]{:S(2)}, u32[]{:S(2)}) collective-permute-start(bf16[256,128]{1,0:T(8,128)(2,1)S(1)} %get-tuple-element.47), channel_id=1, source_target_pairs={{0,2},{1,3},{2,0},{3,1},{4,6},{5,7},{6,4},{7,5},{8,10},{9,11},{10,... | collective-permute-start | bytes 196616 | tf_op jit(solution)/shard_map/ppermute | solution.py:270
  30.5 4.0 %collective-permute-start.8 = (bf16[256,128]{1,0:T(8,128)(2,1)S(1)}, bf16[256,128]{1,0:T(8,128)(2,1)S(1)}, u32[]{:S(2)}, u32[]{:S(2)}) collective-permute-start(bf16[256,128]{1,0:T(8,128)(2,1)S(1)} %get-tuple-element.48), channel_id=1, source_target_pairs={{0,3},{1,2},{2,1},{3,0},{4,7},{5,6},{6,5},{7,4},{8,11},{9,10},{10,... | collective-permute-start | bytes 196616 | tf_op jit(solution)/shard_map/ppermute | solution.py:270
  33.6 9.0 %copy-start.7 = (bf16[1024,32]{0,1:T(8,128)(2,1)S(1)}, bf16[1024,32]{0,1:T(8,128)(2,1)}, u32[]{:S(2)}) copy-start(bf16[1024,32]{0,1:T(8,128)(2,1)} %param.18) | copy-start | bytes 196612
  33.6 9.1 %copy-start.8 = (f32[2,32,32]{2,1,0:T(8,128)S(1)}, f32[2,32,32]{2,1,0:T(8,128)}, u32[]{:S(2)}) copy-start(f32[2,32,32]{2,1,0:T(8,128)} %get-tuple-element.59) | copy-start | bytes 24580
  33.6 18.8 %copy-start.2 = (bf16[256,128]{1,0:T(8,128)(2,1)}, bf16[256,128]{1,0:T(8,128)(2,1)S(1)}, u32[]{:S(2)}) copy-start(bf16[256,128]{1,0:T(8,128)(2,1)S(1)} %collective-permute-done.6.refs_1_.refs_5_) | copy-start | bytes 196612
  33.6 18.8 %copy-start.3 = (bf16[256,128]{1,0:T(8,128)(2,1)}, bf16[256,128]{1,0:T(8,128)(2,1)S(1)}, u32[]{:S(2)}) copy-start(bf16[256,128]{1,0:T(8,128)(2,1)S(1)} %collective-permute-done.7.refs_2_.refs_6_) | copy-start | bytes 196612
  34.6 17.8 %copy-start.4 = (bf16[256,128]{1,0:T(8,128)(2,1)}, bf16[256,128]{1,0:T(8,128)(2,1)S(1)}, u32[]{:S(2)}) copy-start(bf16[256,128]{1,0:T(8,128)(2,1)S(1)} %collective-permute-done.8.refs_3_.refs_7_) | copy-start | bytes 196612
  36.1 16.5 %all-to-all-start = ((bf16[16,8,1024]{2,1,0:T(8,128)(2,1)}), bf16[16,8,1024]{2,1,0:T(8,128)(2,1)S(1)}, u32[]{:S(2)}, u32[]{:S(2)}) async-start(bf16[16,8,1024]{2,1,0:T(8,128)(2,1)} %bitcast.3), calls=%async_computation | async-start | bytes 524288 | tf_op jit(solution)/shard_map/all_to_all | solution.py:436
  42.8 9.8 %copy-start.5 = (bf16[1024,256]{1,0:T(8,128)(2,1)S(1)}, bf16[1024,256]{1,0:T(8,128)(2,1)}, u32[]{:S(2)}) copy-start(bf16[1024,256]{1,0:T(8,128)(2,1)} %param.17) | copy-start | bytes 1572868
  53.9 12.8 %all-to-all-start.1 = ((bf16[16,8,256]{2,1,0:T(8,128)(2,1)}), bf16[16,8,256]{2,1,0:T(8,128)(2,1)S(1)}, u32[]{:S(2)}, u32[]{:S(2)}) async-start(bf16[16,8,256]{2,1,0:T(8,128)(2,1)} %fusion.3), calls=%async_computation.1 | async-start | bytes 131072 | tf_op jit(solution)/shard_map/all_to_all | solution.py:436
  59.8 6.9 %copy-start.9 = (bf16[2,32,128]{2,1,0:T(8,128)(2,1)S(1)}, bf16[2,32,128]{2,1,0:T(8,128)(2,1)}, u32[]{:S(2)}) copy-start(bf16[2,32,128]{2,1,0:T(8,128)(2,1)} %get-tuple-element.60) | copy-start | bytes 49156

commit v8 on v7

--- a/solution.py
+++ b/solution.py
@@ -47,6 +47,18 @@
     )
 
 
+def fetch_all(fars, heres, done):
+    copies = [pltpu.make_async_copy(far, here, done.at[i]) for i, (far, here) in enumerate(zip(fars, heres))]
+    for copy in copies:
+        copy.start()
+    return copies
+
+
+def wait_all(copies):
+    for copy in copies:
+        copy.wait()
+
+
 def whole(shape):
     return pl.BlockSpec(shape, lambda *_: (0,) * len(shape))
 
@@ -59,14 +71,17 @@
     return jax.ShapeDtypeStruct(shape, kind)
 
 
-def key_value_kernel(head_dim, tile, events, w_key, w_value, keys, values, inner, *states):
+def key_value_kernel(head_dim, tiles, *refs):
+    strips, (w_key, w_value, keys, values, inner), states = refs[:tiles], refs[tiles : tiles + 5], refs[tiles + 5 :]
+    tile = strips[0].shape[0]
+    events = jnp.concatenate([strip[...] for strip in strips], axis=0)
     pair = w_key.shape[1]
-    both = dot(events[...], jnp.concatenate([w_key[...], w_value[...]], axis=1)).astype(BF16)
+    both = dot(events, jnp.concatenate([w_key[...], w_value[...]], axis=1)).astype(BF16)
     k, v = both[:, :pair], both[:, pair:]
     keys[...] = k
     values[...] = v
     total = None
-    for i in range(events.shape[0] // tile):
+    for i in range(tiles):
         here = slice(i * tile, (i + 1) * tile)
         if i:
             inner[i - 1] = total.astype(BF16)
@@ -86,7 +101,8 @@
     head_dim = width // HEADS
     pair = width // PLANE
     tile = row_tile(rows)
-    inner = rows // tile - 1
+    tiles = rows // tile
+    inner = tiles - 1
 
     def turn(i):
         return (lax.axis_index("seq") ^ i) & (PLANE - 1)
@@ -95,9 +111,9 @@
         return pl.BlockSpec((many, pair), lambda i: (0, turn(i)))
 
     return call(
-        functools.partial(key_value_kernel, head_dim, tile),
+        functools.partial(key_value_kernel, head_dim, tiles),
         (PLANE,),
-        [whole((rows, width)), cols(width), cols(width)],
+        [pl.BlockSpec((tile, width), lambda i, t=t: (t, 0)) for t in range(tiles)] + [cols(width), cols(width)],
         [pl.BlockSpec((None, rows, pair), lambda i: (turn(i), 0, 0))] * 2
         + [pl.BlockSpec((inner, pair, head_dim), lambda i: (0, turn(i), 0))]
         + [whole((pair, head_dim))] * PLANE,
@@ -106,7 +122,7 @@
         + [shaped((pair, head_dim), BF16)] * PLANE,
         4 * rows * width * width,
         8 * rows * width,
-    )(events, w_key, w_value)
+    )(*[events] * tiles, w_key, w_value)
 
 
 def row_tile(rows):
@@ -115,10 +131,16 @@
 
 def labelled_kernel(head_dim, copies, events_far, w_query_far, keys_far, values_far, labels, experts, tasks, *refs):
     (packed, match, column), (events, w_query, keys, values, done) = refs[:3], refs[3:]
-    fetches = []
-    for far, here in ((events_far, events), (w_query_far, w_query), (keys_far, keys), (values_far, values)):
-        fetches.append(pltpu.make_async_copy(far, here, done.at[len(fetches)]))
-        fetches[-1].start()
+    step = row_tile(events.shape[0])
+    strips = [slice(i, i + step) for i in range(0, events.shape[0], step)]
+    step = keys.shape[2]
+    parts = [slice(c, c + step) for c in range(0, w_query.shape[1], step)]
+    fars = [events_far.at[strip, :] for strip in strips] + [w_query_far.at[:, part] for part in parts]
+    heres = [events.at[strip, :] for strip in strips] + [w_query.at[:, part] for part in parts]
+    fars += [far.at[p] for far in (keys_far, values_far) for p in range(PLANE)]
+    heres += [here.at[p] for here in (keys, values) for p in range(PLANE)]
+    fetches = fetch_all(fars, heres, done)
+    events_in, fetches = fetches[: len(strips)], fetches[len(strips) :]
     rows, width = events.shape
     many = labels.shape[1]
 
@@ -136,23 +158,24 @@
         column[k] = jnp.where(number == chosen_column, 1.0, 0.0)
     chosen = row_choice(labels[...], rows)
     causal = lax.broadcasted_iota(jnp.int32, (many, rows), 1) <= upright(labels[...])
-    pair = 2 * head_dim
-    parts = [slice(c, c + pair) for c in range(0, width, pair)]
-
-    fetches[0].wait()
+    causal = jnp.concatenate([causal, causal], axis=0)
+    wait_all(events_in)
     chosen_events = dot(chosen, events[...]).astype(BF16)
     packed[:, width : 2 * width] = chosen_events.astype(F32)
-    fetches[1].wait()
-    query = dot(chosen_events, w_query[...]).astype(BF16)
-    packed[:, :width] = query.astype(F32)
-    causal = jnp.concatenate([causal, causal], axis=0)
-    apart = [heads_apart(query[:, part], head_dim) for part in parts]
-    fetches[2].wait()
-    weights = [dot(q, keys[p], ((1,), (1,))) for p, q in enumerate(apart)]
-    weights = [jnp.where(causal, weight, 0.0).astype(BF16) for weight in weights]
-    fetches[3].wait()
-    for p, (part, weight) in enumerate(zip(parts, weights)):
-        terms = dot(weight, values[p])
+    apart = []
+    for p, part in enumerate(parts):
+        fetches[p].wait()
+        query = dot(chosen_events, w_query[:, part]).astype(BF16)
+        packed[:, part] = query.astype(F32)
+        apart.append(heads_apart(query, head_dim))
+    weights = []
+    for p, q in enumerate(apart):
+        fetches[PLANE + p].wait()
+        weight = dot(q, keys[p], ((1,), (1,)))
+        weights.append(jnp.where(causal, weight, 0.0).astype(BF16))
+    for p, part in enumerate(parts):
+        fetches[2 * PLANE + p].wait()
+        terms = dot(weights[p], values[p])
         terms = jnp.concatenate([terms[:many, :head_dim], terms[many:, head_dim:]], axis=1)
         packed[:, 2 * width + part.start : 2 * width + part.stop] = terms
 
@@ -170,7 +193,8 @@
         + [shaped((2, many, slots), BF16), shaped((2, many, 2 * EXPERTS), F32)],
         4 * many * rows * width,
         8 * rows * width,
-        [pltpu.VMEM(x.shape, BF16) for x in (events, w_query, keys, values)] + [pltpu.SemaphoreType.DMA((4,))],
+        [pltpu.VMEM(x.shape, BF16) for x in (events, w_query, keys, values)]
+        + [pltpu.SemaphoreType.DMA((rows // row_tile(rows) + 3 * PLANE,))],
     )(events, w_query, keys, values, labels, experts, tasks)
 
 

time: 67.9 us -> 69.3 us (1.021)
  Pallas kernels: 30.3 us -> 31.7 us
    pallas_call x1, Pallas kernels: 5.08 us -> 6.48 us  [labelled_rows(): call(functools.partial(labelled_kernel, width // HEADS, devices // EXPERT...]
  transfers between devices with their start and end apart: 11 -> 11, of which waited for: 5 -> 5; matrix products, arithmetic and copies ran while one was open for 4% -> 4% of each run, Pallas kernels for 30% -> 32%
where the time goes in v8:
time: 69.3 us; the launch traced here: 68.8 us
  Pallas kernels  31.7 us (46%)
  starting transfers between devices  26.9 us (39%)
  waiting for transfers between devices  3.99 us (6%)
  other arithmetic  3.09 us (4%)
  matrix products  2.16 us (3%)
  between operations  0.89 us (1%)
    all_to_all x2, starting transfers between devices, exchange(): return lax.all_to_all(x, 'seq', split_axis=0, concat_axis=0, tiled=True)  12.3 us
    pallas_call x1, Pallas kernels, queries_within(): call(functools.partial(within_kernel, head_dim, tile), (width // pair,),...  9.6 us
    ppermute x3, starting transfers between devices, later(): lax.ppermute(x, 'seq', [(i, i + s) for i in range(lax.axis_size('seq') -...  9.49 us
    pallas_call x1, Pallas kernels, key_value_state(): call(functools.partial(key_value_kernel, head_dim, tiles), (PLANE,), [pl....  8.25 us
    pallas_call x1, Pallas kernels, labelled_rows(): call(functools.partial(labelled_kernel, width // HEADS, devices // EXPERT...  6.48 us
    pallas_call x1, Pallas kernels, hidden_rows(): call(functools.partial(hidden_kernel, head_dim, tile), (), [FAR] * (4 + P...  5.84 us
    ppermute x6, starting transfers between devices, flip(): return lax.ppermute(x, 'seq', [(i, i ^ j) for i in range(devices)])  5.11 us
    dot_general x3, matrix products, dot(): lax.dot_general(a, b, (contract, ((), ())), preferred_element_type=F32, *...  2.16 us
  transfers between devices with their start and end apart: 11, of which 5 were waited for; matrix products, arithmetic and copies ran while one was open for 4% of the time, Pallas kernels for 32%

profile of v8, /device:TPU:0, one launch (start us, length us, event | category | flops | bytes accessed | tf_op | source)
XLA Modules:
  0.0 68.8 jit_solution(385918910239508284)
XLA Ops:
  0.6 8.3 %shard_map.122 = (bf16[4,768,256]{2,1,0:T(8,128)(2,1)}, bf16[4,768,256]{2,1,0:T(8,128)(2,1)}, bf16[2,1024,128]{2,1,0:T(8,128)(2,1)}, bf16[256,128]{1,0:T(8,128)(...) custom-call(bf16[768,1024]{1,0:T(8,128)(2,1)} %refs_0_.3, ...), custom_call_target="tpu_custom_call" | custom-call | flops 3221225472 | bytes 6291456 | tf_op jit(solution)/shard_map/pallas_call | solution.py:113
  8.9 0.5 collective-permute-start
  9.4 2.6 %collective-permute-start.1 = (bf16[256,128]{1,0:T(8,128)(2,1)}, bf16[256,128]{1,0:T(8,128)(2,1)S(1)}, u32[]{:S(2)}, u32[]{:S(2)}) collective-permute-start(bf16[256,128]{1,0:T(8,128)(2,1)} %get-tuple-element.34), channel_id=1, source_target_pairs={{0,2},{1,3},{2,0},{3,1},{4,6},{5,7},{6,4},{7,5},{8,10},{9,11},{10,... | collective-permute-start | bytes 196616 | tf_op jit(solution)/shard_map/ppermute | solution.py:294
  12.1 6.5 %shard_map.123 = (f32[32,3328]{1,0:T(8,128)}, bf16[2,32,128]{2,1,0:T(8,128)(2,1)}, f32[2,32,32]{2,1,0:T(8,128)}) custom-call(bf16[768,1024]{1,0:T(8,128)(2,1)} %refs_0_.3, bf16[1024,1024]{1,0:T(8,128)(2,1)} %w_query.1, bf16[4,768,256]{2,1,0:T(8,128)(2,1)} %get-tuple-element.51.keys_far.keys, bf16[4,768,256]{2,1,0:T(8,128)(2,1)} %get-tuple-element.52.values_far.values, ...), custom_call_target="tpu_custom_call" | custom-call | flops 100663296 | bytes 6291456 | tf_op jit(solution)/shard_map/pallas_call | solution.py:187
  18.7 3.7 %collective-permute-start.5 = (bf16[256,128]{1,0:T(8,128)(2,1)S(1)}, bf16[256,128]{1,0:T(8,128)(2,1)S(1)}, u32[]{:S(2)}, u32[]{:S(2)}) collective-permute-start(bf16[256,128]{1,0:T(8,128)(2,1)S(1)} %fusion.22), channel_id=1, source_target_pairs={{0,4},{1,5},{2,6},{3,7},{4,8},{5,9},{6,10},{7,11},{8,12},{9,13},{1... | collective-permute-start | bytes 196616 | tf_op jit(solution)/shard_map/ppermute | solution.py:298
  22.4 4.5 %collective-permute-start.4 = (bf16[256,128]{1,0:T(8,128)(2,1)S(1)}, bf16[256,128]{1,0:T(8,128)(2,1)S(1)}, u32[]{:S(2)}, u32[]{:S(2)}) collective-permute-start(bf16[256,128]{1,0:T(8,128)(2,1)S(1)} %fusion.22), channel_id=1, source_target_pairs={{0,8},{1,9},{2,10},{3,11},{4,12},{5,13},{6,14},{7,15},{16,24},{17,... | collective-permute-start | bytes 196616 | tf_op jit(solution)/shard_map/ppermute | solution.py:298
  26.9 1.3 %collective-permute-start.3 = (bf16[256,128]{1,0:T(8,128)(2,1)S(1)}, bf16[256,128]{1,0:T(8,128)(2,1)S(1)}, u32[]{:S(2)}, u32[]{:S(2)}) collective-permute-start(bf16[256,128]{1,0:T(8,128)(2,1)S(1)} %fusion.22), channel_id=1, source_target_pairs={{0,12},{1,13},{2,14},{3,15},{16,28},{17,29},{18,30},{19,31}} | collective-permute-start | bytes 196616 | tf_op jit(solution)/shard_map/ppermute | solution.py:298
  28.2 0.8 %collective-permute-done.4 = bf16[256,128]{1,0:T(8,128)(2,1)S(1)} collective-permute-done((bf16[256,128]{1,0:T(8,128)(2,1)S(1)}, bf16[256,128]{1,0:T(8,128)(2,1)S(1)}, u32[]{:S(2)}, u32[]{:S(2)}) %collective-permute-start.4) | collective-permute-done | bytes 65568 | tf_op jit(solution)/shard_map/ppermute | solution.py:298
  29.0 1.0 %collective-permute-done.3 = bf16[256,128]{1,0:T(8,128)(2,1)S(1)} collective-permute-done((bf16[256,128]{1,0:T(8,128)(2,1)S(1)}, bf16[256,128]{1,0:T(8,128)(2,1)S(1)}, u32[]{:S(2)}, u32[]{:S(2)}) %collective-permute-start.3) | collective-permute-done | bytes 65568 | tf_op jit(solution)/shard_map/ppermute | solution.py:298
  30.1 0.2 fusion.17
  30.3 1.6 %collective-permute-start.7 = (bf16[256,128]{1,0:T(8,128)(2,1)S(1)}, bf16[256,128]{1,0:T(8,128)(2,1)S(1)}, u32[]{:S(2)}, u32[]{:S(2)}) collective-permute-start(bf16[256,128]{1,0:T(8,128)(2,1)S(1)} %get-tuple-element.47), channel_id=1, source_target_pairs={{0,2},{1,3},{2,0},{3,1},{4,6},{5,7},{6,4},{7,5},{8,10},{9,11},{10,... | collective-permute-start | bytes 196616 | tf_op jit(solution)/shard_map/ppermute | solution.py:294
  31.9 0.3 collective-permute-start.8
  32.2 1.0 %broadcast_multiply_fusion.1.packed = f32[32,3328]{1,0:T(8,128)S(1)} fusion(f32[32,3328]{1,0:T(8,128)} %get-tuple-element.39, f32[]{:T(128)S(6)} %convert_element_type.57), kind=kLoop, calls=%fused_computation.24 | loop fusion | flops 106496 | bytes 851972 | tf_op jit(solution)/shard_map/mul | solution.py:469
  33.2 1.7 %broadcast_multiply_fusion.w_output = bf16[1024,1024]{1,0:T(8,128)(2,1)S(1)} fusion(bf16[1024,1024]{1,0:T(8,128)(2,1)} %refs_3_.3, bf16[]{:T(256)} %constant.4.clone.1), kind=kLoop, calls=%fused_computation.7 | loop fusion | flops 1048576 | bytes 4194306 | tf_op jit(solution)/shard_map/mul | solution.py:469
  35.0 0.9 %collective-permute-done.8.refs_3_.refs_7_ = bf16[256,128]{1,0:T(8,128)(2,1)S(1)} collective-permute-done((bf16[256,128]{1,0:T(8,128)(2,1)S(1)}, bf16[256,128]{1,0:T(8,128)(2,1)S(1)}, u32[]{:S(2)}, u32[]{:S(2)}) %collective-permute-start.8) | collective-permute-done | bytes 65568 | tf_op jit(solution)/shard_map/ppermute | solution.py:294
  35.9 1.5 %shard_map.124 = (bf16[32,1024]{1,0:T(8,128)(2,1)S(1)}, bf16[128,1024]{1,0:T(8,128)(2,1)}) custom-call(f32[32,3328]{1,0:T(8,128)S(1)} %broadcast_multiply_fusion.1.packed, bf16[1024,1024]{1,0:T(8,128)(2,1)S(1)} %broadcast_multiply_fusion.w_output, bf16[256,128]{1,0:T(8,128)(2,1)S(1)} %get-tuple-element.45.refs_0_.refs_4_, ...), custom_call_target="tpu_custom_call" | custom-call | flops 67108864 | bytes 2097152 | tf_op jit(solution)/shard_map/pallas_call | solution.py:350
  37.5 6.4 %all-to-all-start = ((bf16[16,8,1024]{2,1,0:T(8,128)(2,1)}), bf16[16,8,1024]{2,1,0:T(8,128)(2,1)S(1)}, u32[]{:S(2)}, u32[]{:S(2)}) async-start(bf16[16,8,1024]{2,1,0:T(8,128)(2,1)} %bitcast.3), calls=%async_computation | async-start | bytes 524288 | tf_op jit(solution)/shard_map/all_to_all | solution.py:460
  44.2 9.6 %shard_map.125 = (bf16[768,1024]{1,0:T(8,128)(2,1)}, bf16[768,1024]{1,0:T(8,128)(2,1)}) custom-call(bf16[768,1024]{1,0:T(8,128)(2,1)} %refs_0_.3, bf16[1024,1024]{1,0:T(8,128)(2,1)} %w_query.1, bf16[4,768,256]{2,1,0:T(8,128)(2,1)} %get-tuple-element.51.keys_far.keys, bf16[4,768,256]{2,1,0:T(8,128)(2,1)} %get-tuple-element.52.values_far.values, ...), custom_call_target="tpu_custom_call" | custom-call | flops 2415919104 | bytes 6291456 | tf_op jit(solution)/shard_map/pallas_call | solution.py:275
  53.8 0.2 all-to-all-done
  54.0 1.3 %fusion.3 = bf16[16,8,256]{2,1,0:T(8,128)(2,1)} fusion(bf16[1024,256]{1,0:T(8,128)(2,1)S(1)} %copy-done.5, bf16[128,1024]{1,0:T(8,128)(2,1)S(1)} %bitcast.18, bf16[1024,1024]{1,0:T(8,128)(2,1)S(1)} %copy-done), kind=kOutput, calls=%fused_computation.4 | convolution fusion | flops 335839232 | bytes 2949120 | tf_op jit(solution)/shard_map/dot_general | solution.py:20
  55.2 5.9 %all-to-all-start.1 = ((bf16[16,8,256]{2,1,0:T(8,128)(2,1)}), bf16[16,8,256]{2,1,0:T(8,128)(2,1)S(1)}, u32[]{:S(2)}, u32[]{:S(2)}) async-start(bf16[16,8,256]{2,1,0:T(8,128)(2,1)} %fusion.3), calls=%async_computation.1 | async-start | bytes 131072 | tf_op jit(solution)/shard_map/all_to_all | solution.py:460
  61.1 5.8 %shard_map.126 = bf16[768,1024]{1,0:T(8,128)(2,1)} custom-call(bf16[768,1024]{1,0:T(8,128)(2,1)} %refs_0_.3, bf16[768,1024]{1,0:T(8,128)(2,1)} %get-tuple-element.56.refs_1_, bf16[768,1024]{1,0:T(8,128)(2,1)} %get-tuple-element.57.refs_2_, bf16[1024,1024]{1,0:T(8,128)(2,1)} %refs_3_.3, bf16[256,128]{1,0:T(8,128)(2,1)} %copy-done.1, ...), custom_call_target="tpu_custom_call" | custom-call | flops 1610612736 | bytes 7864320 | tf_op jit(solution)/shard_map/pallas_call | solution.py:413
  67.0 1.0 %all-to-all-done.1 = bf16[16,8,256]{2,1,0:T(8,128)(2,1)S(1)} async-done(((bf16[16,8,256]{2,1,0:T(8,128)(2,1)}), bf16[16,8,256]{2,1,0:T(8,128)(2,1)S(1)}, u32[]{:S(2)}, u32[]{:S(2)}) %all-to-all-start.1) | async-done | bytes 65568 | tf_op jit(solution)/shard_map/all_to_all | solution.py:460
  68.0 0.8 %fusion.4 = f32[32,256]{1,0:T(8,128)} fusion(bf16[2,32,128]{2,1,0:T(8,128)(2,1)S(1)} %copy-done.9, bf16[16,8,256]{2,1,0:T(8,128)(2,1)S(1)} %all-to-all-done.1, f32[2,32]{1,0:T(2,128)S(1)} %add_divide_fusion), kind=kOutput, calls=%fused_computation.6 | convolution fusion | flops 4218880 | bytes 114944 | tf_op jit(solution)/shard_map/dot_general | solution.py:20
  (32 shorter events, 0.5 us)
Async XLA Ops:
  0.6 53.3 %copy-start = (bf16[1024,1024]{1,0:T(8,128)(2,1)S(1)}, bf16[1024,1024]{1,0:T(8,128)(2,1)}, u32[]{:S(2)}) copy-start(bf16[1024,1024]{1,0:T(8,128)(2,1)} %param.16) | copy-start | bytes 6291460
  8.9 9.7 %collective-permute-start = (bf16[256,128]{1,0:T(8,128)(2,1)}, bf16[256,128]{1,0:T(8,128)(2,1)S(1)}, u32[]{:S(2)}, u32[]{:S(2)}) collective-permute-start(bf16[256,128]{1,0:T(8,128)(2,1)} %get-tuple-element.33), channel_id=1, source_target_pairs={{0,1},{1,0},{2,3},{3,2},{4,5},{5,4},{6,7},{7,6},{8,9},{9,8},{10,11... | collective-permute-start | bytes 196616 | tf_op jit(solution)/shard_map/ppermute | solution.py:294
  9.4 9.2 %collective-permute-start.1 = (bf16[256,128]{1,0:T(8,128)(2,1)}, bf16[256,128]{1,0:T(8,128)(2,1)S(1)}, u32[]{:S(2)}, u32[]{:S(2)}) collective-permute-start(bf16[256,128]{1,0:T(8,128)(2,1)} %get-tuple-element.34), channel_id=1, source_target_pairs={{0,2},{1,3},{2,0},{3,1},{4,6},{5,7},{6,4},{7,5},{8,10},{9,11},{10,... | collective-permute-start | bytes 196616 | tf_op jit(solution)/shard_map/ppermute | solution.py:294
  12.0 6.6 %collective-permute-start.2 = (bf16[256,128]{1,0:T(8,128)(2,1)}, bf16[256,128]{1,0:T(8,128)(2,1)S(1)}, u32[]{:S(2)}, u32[]{:S(2)}) collective-permute-start(bf16[256,128]{1,0:T(8,128)(2,1)} %get-tuple-element.35), channel_id=1, source_target_pairs={{0,3},{1,2},{2,1},{3,0},{4,7},{5,6},{6,5},{7,4},{8,11},{9,10},{10,... | collective-permute-start | bytes 196616 | tf_op jit(solution)/shard_map/ppermute | solution.py:294
  12.1 6.5 %copy-start.6 = (bf16[256,128]{1,0:T(8,128)(2,1)S(1)}, bf16[256,128]{1,0:T(8,128)(2,1)}, u32[]{:S(2)}) copy-start(bf16[256,128]{1,0:T(8,128)(2,1)} %get-tuple-element.40) | copy-start | bytes 196612
  18.7 9.5 %collective-permute-start.5 = (bf16[256,128]{1,0:T(8,128)(2,1)S(1)}, bf16[256,128]{1,0:T(8,128)(2,1)S(1)}, u32[]{:S(2)}, u32[]{:S(2)}) collective-permute-start(bf16[256,128]{1,0:T(8,128)(2,1)S(1)} %fusion.22), channel_id=1, source_target_pairs={{0,4},{1,5},{2,6},{3,7},{4,8},{5,9},{6,10},{7,11},{8,12},{9,13},{1... | collective-permute-start | bytes 196616 | tf_op jit(solution)/shard_map/ppermute | solution.py:298
  22.4 6.7 %collective-permute-start.4 = (bf16[256,128]{1,0:T(8,128)(2,1)S(1)}, bf16[256,128]{1,0:T(8,128)(2,1)S(1)}, u32[]{:S(2)}, u32[]{:S(2)}) collective-permute-start(bf16[256,128]{1,0:T(8,128)(2,1)S(1)} %fusion.22), channel_id=1, source_target_pairs={{0,8},{1,9},{2,10},{3,11},{4,12},{5,13},{6,14},{7,15},{16,24},{17,... | collective-permute-start | bytes 196616 | tf_op jit(solution)/shard_map/ppermute | solution.py:298
  26.9 3.2 %collective-permute-start.3 = (bf16[256,128]{1,0:T(8,128)(2,1)S(1)}, bf16[256,128]{1,0:T(8,128)(2,1)S(1)}, u32[]{:S(2)}, u32[]{:S(2)}) collective-permute-start(bf16[256,128]{1,0:T(8,128)(2,1)S(1)} %fusion.22), channel_id=1, source_target_pairs={{0,12},{1,13},{2,14},{3,15},{16,28},{17,29},{18,30},{19,31}} | collective-permute-start | bytes 196616 | tf_op jit(solution)/shard_map/ppermute | solution.py:298
  30.2 5.7 %copy-start.1 = (bf16[256,128]{1,0:T(8,128)(2,1)}, bf16[256,128]{1,0:T(8,128)(2,1)S(1)}, u32[]{:S(2)}) copy-start(bf16[256,128]{1,0:T(8,128)(2,1)S(1)} %get-tuple-element.45.refs_0_.refs_4_) | copy-start | bytes 196612
  30.2 4.7 %collective-permute-start.6 = (bf16[256,128]{1,0:T(8,128)(2,1)S(1)}, bf16[256,128]{1,0:T(8,128)(2,1)S(1)}, u32[]{:S(2)}, u32[]{:S(2)}) collective-permute-start(bf16[256,128]{1,0:T(8,128)(2,1)S(1)} %get-tuple-element.46), channel_id=1, source_target_pairs={{0,1},{1,0},{2,3},{3,2},{4,5},{5,4},{6,7},{7,6},{8,9},{9,8},{10,11... | collective-permute-start | bytes 196616 | tf_op jit(solution)/shard_map/ppermute | solution.py:294
  30.3 4.7 %collective-permute-start.7 = (bf16[256,128]{1,0:T(8,128)(2,1)S(1)}, bf16[256,128]{1,0:T(8,128)(2,1)S(1)}, u32[]{:S(2)}, u32[]{:S(2)}) collective-permute-start(bf16[256,128]{1,0:T(8,128)(2,1)S(1)} %get-tuple-element.47), channel_id=1, source_target_pairs={{0,2},{1,3},{2,0},{3,1},{4,6},{5,7},{6,4},{7,5},{8,10},{9,11},{10,... | collective-permute-start | bytes 196616 | tf_op jit(solution)/shard_map/ppermute | solution.py:294
  31.9 4.0 %collective-permute-start.8 = (bf16[256,128]{1,0:T(8,128)(2,1)S(1)}, bf16[256,128]{1,0:T(8,128)(2,1)S(1)}, u32[]{:S(2)}, u32[]{:S(2)}) collective-permute-start(bf16[256,128]{1,0:T(8,128)(2,1)S(1)} %get-tuple-element.48), channel_id=1, source_target_pairs={{0,3},{1,2},{2,1},{3,0},{4,7},{5,6},{6,5},{7,4},{8,11},{9,10},{10,... | collective-permute-start | bytes 196616 | tf_op jit(solution)/shard_map/ppermute | solution.py:294
  34.9 9.0 %copy-start.7 = (bf16[1024,32]{0,1:T(8,128)(2,1)S(1)}, bf16[1024,32]{0,1:T(8,128)(2,1)}, u32[]{:S(2)}) copy-start(bf16[1024,32]{0,1:T(8,128)(2,1)} %param.18) | copy-start | bytes 196612
  35.0 9.1 %copy-start.8 = (f32[2,32,32]{2,1,0:T(8,128)S(1)}, f32[2,32,32]{2,1,0:T(8,128)}, u32[]{:S(2)}) copy-start(f32[2,32,32]{2,1,0:T(8,128)} %get-tuple-element.59) | copy-start | bytes 24580
  35.0 18.8 %copy-start.2 = (bf16[256,128]{1,0:T(8,128)(2,1)}, bf16[256,128]{1,0:T(8,128)(2,1)S(1)}, u32[]{:S(2)}) copy-start(bf16[256,128]{1,0:T(8,128)(2,1)S(1)} %collective-permute-done.6.refs_1_.refs_5_) | copy-start | bytes 196612
  35.0 18.8 %copy-start.3 = (bf16[256,128]{1,0:T(8,128)(2,1)}, bf16[256,128]{1,0:T(8,128)(2,1)S(1)}, u32[]{:S(2)}) copy-start(bf16[256,128]{1,0:T(8,128)(2,1)S(1)} %collective-permute-done.7.refs_2_.refs_6_) | copy-start | bytes 196612
  35.9 17.8 %copy-start.4 = (bf16[256,128]{1,0:T(8,128)(2,1)}, bf16[256,128]{1,0:T(8,128)(2,1)S(1)}, u32[]{:S(2)}) copy-start(bf16[256,128]{1,0:T(8,128)(2,1)S(1)} %collective-permute-done.8.refs_3_.refs_7_) | copy-start | bytes 196612
  37.5 16.5 %all-to-all-start = ((bf16[16,8,1024]{2,1,0:T(8,128)(2,1)}), bf16[16,8,1024]{2,1,0:T(8,128)(2,1)S(1)}, u32[]{:S(2)}, u32[]{:S(2)}) async-start(bf16[16,8,1024]{2,1,0:T(8,128)(2,1)} %bitcast.3), calls=%async_computation | async-start | bytes 524288 | tf_op jit(solution)/shard_map/all_to_all | solution.py:460
  44.2 9.8 %copy-start.5 = (bf16[1024,256]{1,0:T(8,128)(2,1)S(1)}, bf16[1024,256]{1,0:T(8,128)(2,1)}, u32[]{:S(2)}) copy-start(bf16[1024,256]{1,0:T(8,128)(2,1)} %param.17) | copy-start | bytes 1572868
  55.2 12.8 %all-to-all-start.1 = ((bf16[16,8,256]{2,1,0:T(8,128)(2,1)}), bf16[16,8,256]{2,1,0:T(8,128)(2,1)S(1)}, u32[]{:S(2)}, u32[]{:S(2)}) async-start(bf16[16,8,256]{2,1,0:T(8,128)(2,1)} %fusion.3), calls=%async_computation.1 | async-start | bytes 131072 | tf_op jit(solution)/shard_map/all_to_all | solution.py:460
  61.1 6.9 %copy-start.9 = (bf16[2,32,128]{2,1,0:T(8,128)(2,1)S(1)}, bf16[2,32,128]{2,1,0:T(8,128)(2,1)}, u32[]{:S(2)}) copy-start(bf16[2,32,128]{2,1,0:T(8,128)(2,1)} %get-tuple-element.60) | copy-start | bytes 49156

commit v9 on v7

--- a/solution.py
+++ b/solution.py
@@ -45,6 +45,18 @@
         compiler_params=pltpu.CompilerParams(vmem_limit_bytes=vmem * MIB),
         cost_estimate=pl.CostEstimate(flops=flops, bytes_accessed=moved, transcendentals=0),
     )
+
+
+def fetch_all(fars, heres, done):
+    copies = [pltpu.make_async_copy(far, here, done.at[i]) for i, (far, here) in enumerate(zip(fars, heres))]
+    for copy in copies:
+        copy.start()
+    return copies
+
+
+def wait_all(copies):
+    for copy in copies:
+        copy.wait()
 
 
 def whole(shape):
@@ -115,10 +127,10 @@
 
 def labelled_kernel(head_dim, copies, events_far, w_query_far, keys_far, values_far, labels, experts, tasks, *refs):
     (packed, match, column), (events, w_query, keys, values, done) = refs[:3], refs[3:]
-    fetches = []
-    for far, here in ((events_far, events), (w_query_far, w_query), (keys_far, keys), (values_far, values)):
-        fetches.append(pltpu.make_async_copy(far, here, done.at[len(fetches)]))
-        fetches[-1].start()
+    middle = w_query.shape[0] // 2
+    fars = [w_query_far.at[:middle, :], w_query_far.at[middle:, :], events_far, keys_far, values_far]
+    heres = [w_query.at[:middle, :], w_query.at[middle:, :], events, keys, values]
+    fetches = fetch_all(fars, heres, done)
     rows, width = events.shape
     many = labels.shape[1]
 
@@ -139,18 +151,18 @@
     pair = 2 * head_dim
     parts = [slice(c, c + pair) for c in range(0, width, pair)]
 
-    fetches[0].wait()
+    fetches[2].wait()
     chosen_events = dot(chosen, events[...]).astype(BF16)
     packed[:, width : 2 * width] = chosen_events.astype(F32)
-    fetches[1].wait()
+    wait_all(fetches[:2])
     query = dot(chosen_events, w_query[...]).astype(BF16)
     packed[:, :width] = query.astype(F32)
     causal = jnp.concatenate([causal, causal], axis=0)
     apart = [heads_apart(query[:, part], head_dim) for part in parts]
-    fetches[2].wait()
+    fetches[3].wait()
     weights = [dot(q, keys[p], ((1,), (1,))) for p, q in enumerate(apart)]
     weights = [jnp.where(causal, weight, 0.0).astype(BF16) for weight in weights]
-    fetches[3].wait()
+    fetches[4].wait()
     for p, (part, weight) in enumerate(zip(parts, weights)):
         terms = dot(weight, values[p])
         terms = jnp.concatenate([terms[:many, :head_dim], terms[many:, head_dim:]], axis=1)
@@ -170,7 +182,7 @@
         + [shaped((2, many, slots), BF16), shaped((2, many, 2 * EXPERTS), F32)],
         4 * many * rows * width,
         8 * rows * width,
-        [pltpu.VMEM(x.shape, BF16) for x in (events, w_query, keys, values)] + [pltpu.SemaphoreType.DMA((4,))],
+        [pltpu.VMEM(x.shape, BF16) for x in (events, w_query, keys, values)] + [pltpu.SemaphoreType.DMA((5,))],
     )(events, w_query, keys, values, labels, experts, tasks)
 
 
@@ -283,7 +295,8 @@
     rank = lax.axis_index("seq") & (PLANE - 1)
     states = [x.astype(F32) for x in states]
     total = sum(states).astype(BF16)
-    planes = sum(later(total, s).astype(F32) for s in reversed(range(PLANE, devices, PLANE)))
+    shifts = list(range(PLANE, devices, PLANE))
+    planes = sum(later(total, s).astype(F32) for s in shifts[:1] + shifts[:0:-1])
     before = []
     for j in range(PLANE):
         held = [jnp.where((rank ^ i) < (rank ^ j), states[i], 0.0) for i in range(PLANE) if i != j]

time: 67.9 us -> 67.7 us (level)
  transfers between devices with their start and end apart: 11 -> 11, of which waited for: 5 -> 4; matrix products, arithmetic and copies ran while one was open for 4% -> 4% of each run, Pallas kernels for 30% -> 31%
where the time goes in v9:
time: 67.7 us; the launch traced here: 67.2 us
  Pallas kernels  30.7 us (45%)
  starting transfers between devices  26.3 us (39%)
  waiting for transfers between devices  3.98 us (6%)
  other arithmetic  3.09 us (5%)
  matrix products  2.16 us (3%)
  between operations  0.9 us (1%)
    all_to_all x2, starting transfers between devices, exchange(): return lax.all_to_all(x, 'seq', split_axis=0, concat_axis=0, tiled=True)  12.3 us
    pallas_call x1, Pallas kernels, queries_within(): call(functools.partial(within_kernel, head_dim, tile), (width // pair,),...  9.6 us
    ppermute x3, starting transfers between devices, later(): lax.ppermute(x, 'seq', [(i, i + s) for i in range(lax.axis_size('seq') -...  8.85 us
    pallas_call x1, Pallas kernels, key_value_state(): call(functools.partial(key_value_kernel, head_dim, tile), (PLANE,), [whol...  8.3 us
    pallas_call x1, Pallas kernels, hidden_rows(): call(functools.partial(hidden_kernel, head_dim, tile), (), [FAR] * (4 + P...  5.84 us
    pallas_call x1, Pallas kernels, labelled_rows(): call(functools.partial(labelled_kernel, width // HEADS, devices // EXPERT...  5.45 us
    ppermute x6, starting transfers between devices, flip(): return lax.ppermute(x, 'seq', [(i, i ^ j) for i in range(devices)])  5.11 us
    dot_general x3, matrix products, dot(): lax.dot_general(a, b, (contract, ((), ())), preferred_element_type=F32, *...  2.16 us
  transfers between devices with their start and end apart: 11, of which 4 were waited for; matrix products, arithmetic and copies ran while one was open for 4% of the time, Pallas kernels for 31%

profile of v9, /device:TPU:0, one launch (start us, length us, event | category | flops | bytes accessed | tf_op | source)
XLA Modules:
  0.0 67.2 jit_solution(16882973618063245408)
XLA Ops:
  0.6 8.3 %shard_map.122 = (bf16[4,768,256]{2,1,0:T(8,128)(2,1)}, bf16[4,768,256]{2,1,0:T(8,128)(2,1)}, bf16[2,1024,128]{2,1,0:T(8,128)(2,1)}, bf16[256,128]{1,0:T(8,128)(...) custom-call(bf16[768,1024]{1,0:T(8,128)(2,1)} %refs_0_.1, ...), custom_call_target="tpu_custom_call" | custom-call | flops 3221225472 | bytes 6291456 | tf_op jit(solution)/shard_map/pallas_call | solution.py:109
  8.9 0.5 collective-permute-start
  9.5 2.6 %collective-permute-start.1 = (bf16[256,128]{1,0:T(8,128)(2,1)}, bf16[256,128]{1,0:T(8,128)(2,1)S(1)}, u32[]{:S(2)}, u32[]{:S(2)}) collective-permute-start(bf16[256,128]{1,0:T(8,128)(2,1)} %get-tuple-element.34), channel_id=1, source_target_pairs={{0,2},{1,3},{2,0},{3,1},{4,6},{5,7},{6,4},{7,5},{8,10},{9,11},{10,... | collective-permute-start | bytes 196616 | tf_op jit(solution)/shard_map/ppermute | solution.py:282
  12.1 5.5 %shard_map.123 = (f32[32,3328]{1,0:T(8,128)}, bf16[2,32,128]{2,1,0:T(8,128)(2,1)}, f32[2,32,32]{2,1,0:T(8,128)}) custom-call(bf16[768,1024]{1,0:T(8,128)(2,1)} %refs_0_.1, bf16[1024,1024]{1,0:T(8,128)(2,1)} %w_query.1, bf16[4,768,256]{2,1,0:T(8,128)(2,1)} %get-tuple-element.51.keys_far.keys, bf16[4,768,256]{2,1,0:T(8,128)(2,1)} %get-tuple-element.52.values_far.values, ...), custom_call_target="tpu_custom_call" | custom-call | flops 100663296 | bytes 6291456 | tf_op jit(solution)/shard_map/pallas_call | solution.py:176
  17.7 4.7 %collective-permute-start.5 = (bf16[256,128]{1,0:T(8,128)(2,1)S(1)}, bf16[256,128]{1,0:T(8,128)(2,1)S(1)}, u32[]{:S(2)}, u32[]{:S(2)}) collective-permute-start(bf16[256,128]{1,0:T(8,128)(2,1)S(1)} %fusion.22), channel_id=1, source_target_pairs={{0,8},{1,9},{2,10},{3,11},{4,12},{5,13},{6,14},{7,15},{16,24},{17,... | collective-permute-start | bytes 196616 | tf_op jit(solution)/shard_map/ppermute | solution.py:286
  22.4 2.3 %collective-permute-start.4 = (bf16[256,128]{1,0:T(8,128)(2,1)S(1)}, bf16[256,128]{1,0:T(8,128)(2,1)S(1)}, u32[]{:S(2)}, u32[]{:S(2)}) collective-permute-start(bf16[256,128]{1,0:T(8,128)(2,1)S(1)} %fusion.22), channel_id=1, source_target_pairs={{0,12},{1,13},{2,14},{3,15},{16,28},{17,29},{18,30},{19,31}} | collective-permute-start | bytes 196616 | tf_op jit(solution)/shard_map/ppermute | solution.py:286
  24.7 1.8 %collective-permute-start.3 = (bf16[256,128]{1,0:T(8,128)(2,1)S(1)}, bf16[256,128]{1,0:T(8,128)(2,1)S(1)}, u32[]{:S(2)}, u32[]{:S(2)}) collective-permute-start(bf16[256,128]{1,0:T(8,128)(2,1)S(1)} %fusion.22), channel_id=1, source_target_pairs={{0,4},{1,5},{2,6},{3,7},{4,8},{5,9},{6,10},{7,11},{8,12},{9,13},{1... | collective-permute-start | bytes 196616 | tf_op jit(solution)/shard_map/ppermute | solution.py:286
  26.6 1.8 %collective-permute-done.3 = bf16[256,128]{1,0:T(8,128)(2,1)S(1)} collective-permute-done((bf16[256,128]{1,0:T(8,128)(2,1)S(1)}, bf16[256,128]{1,0:T(8,128)(2,1)S(1)}, u32[]{:S(2)}, u32[]{:S(2)}) %collective-permute-start.3) | collective-permute-done | bytes 65568 | tf_op jit(solution)/shard_map/ppermute | solution.py:286
  28.4 0.2 fusion.17
  28.7 1.6 %collective-permute-start.7 = (bf16[256,128]{1,0:T(8,128)(2,1)S(1)}, bf16[256,128]{1,0:T(8,128)(2,1)S(1)}, u32[]{:S(2)}, u32[]{:S(2)}) collective-permute-start(bf16[256,128]{1,0:T(8,128)(2,1)S(1)} %get-tuple-element.47), channel_id=1, source_target_pairs={{0,2},{1,3},{2,0},{3,1},{4,6},{5,7},{6,4},{7,5},{8,10},{9,11},{10,... | collective-permute-start | bytes 196616 | tf_op jit(solution)/shard_map/ppermute | solution.py:282
  30.3 0.3 collective-permute-start.8
  30.6 1.0 %broadcast_multiply_fusion.1.packed = f32[32,3328]{1,0:T(8,128)S(1)} fusion(f32[32,3328]{1,0:T(8,128)} %get-tuple-element.39, f32[]{:T(128)S(6)} %convert_element_type.57), kind=kLoop, calls=%fused_computation.24 | loop fusion | flops 106496 | bytes 851972 | tf_op jit(solution)/shard_map/mul | solution.py:458
  31.6 1.7 %broadcast_multiply_fusion.w_output = bf16[1024,1024]{1,0:T(8,128)(2,1)S(1)} fusion(bf16[1024,1024]{1,0:T(8,128)(2,1)} %refs_3_.1, bf16[]{:T(256)} %constant.4.clone.1), kind=kLoop, calls=%fused_computation.7 | loop fusion | flops 1048576 | bytes 4194306 | tf_op jit(solution)/shard_map/mul | solution.py:458
  33.4 0.9 %collective-permute-done.8.refs_3_.refs_7_ = bf16[256,128]{1,0:T(8,128)(2,1)S(1)} collective-permute-done((bf16[256,128]{1,0:T(8,128)(2,1)S(1)}, bf16[256,128]{1,0:T(8,128)(2,1)S(1)}, u32[]{:S(2)}, u32[]{:S(2)}) %collective-permute-start.8) | collective-permute-done | bytes 65568 | tf_op jit(solution)/shard_map/ppermute | solution.py:282
  34.3 1.5 %shard_map.124 = (bf16[32,1024]{1,0:T(8,128)(2,1)S(1)}, bf16[128,1024]{1,0:T(8,128)(2,1)}) custom-call(f32[32,3328]{1,0:T(8,128)S(1)} %broadcast_multiply_fusion.1.packed, bf16[1024,1024]{1,0:T(8,128)(2,1)S(1)} %broadcast_multiply_fusion.w_output, bf16[256,128]{1,0:T(8,128)(2,1)S(1)} %get-tuple-element.45.refs_0_.refs_4_, ...), custom_call_target="tpu_custom_call" | custom-call | flops 67108864 | bytes 2097152 | tf_op jit(solution)/shard_map/pallas_call | solution.py:339
  35.9 6.4 %all-to-all-start = ((bf16[16,8,1024]{2,1,0:T(8,128)(2,1)}), bf16[16,8,1024]{2,1,0:T(8,128)(2,1)S(1)}, u32[]{:S(2)}, u32[]{:S(2)}) async-start(bf16[16,8,1024]{2,1,0:T(8,128)(2,1)} %bitcast.3), calls=%async_computation | async-start | bytes 524288 | tf_op jit(solution)/shard_map/all_to_all | solution.py:449
  42.3 0.1 fusion.25
  42.6 9.6 %shard_map.125 = (bf16[768,1024]{1,0:T(8,128)(2,1)}, bf16[768,1024]{1,0:T(8,128)(2,1)}) custom-call(bf16[768,1024]{1,0:T(8,128)(2,1)} %refs_0_.1, bf16[1024,1024]{1,0:T(8,128)(2,1)} %w_query.1, bf16[4,768,256]{2,1,0:T(8,128)(2,1)} %get-tuple-element.51.keys_far.keys, bf16[4,768,256]{2,1,0:T(8,128)(2,1)} %get-tuple-element.52.values_far.values, ...), custom_call_target="tpu_custom_call" | custom-call | flops 2415919104 | bytes 6291456 | tf_op jit(solution)/shard_map/pallas_call | solution.py:263
  52.2 0.2 all-to-all-done
  52.4 1.3 %fusion.3 = bf16[16,8,256]{2,1,0:T(8,128)(2,1)} fusion(bf16[1024,256]{1,0:T(8,128)(2,1)S(1)} %copy-done.5, bf16[128,1024]{1,0:T(8,128)(2,1)S(1)} %bitcast.18, bf16[1024,1024]{1,0:T(8,128)(2,1)S(1)} %copy-done), kind=kOutput, calls=%fused_computation.4 | convolution fusion | flops 335839232 | bytes 2949120 | tf_op jit(solution)/shard_map/dot_general | solution.py:20
  53.6 5.9 %all-to-all-start.1 = ((bf16[16,8,256]{2,1,0:T(8,128)(2,1)}), bf16[16,8,256]{2,1,0:T(8,128)(2,1)S(1)}, u32[]{:S(2)}, u32[]{:S(2)}) async-start(bf16[16,8,256]{2,1,0:T(8,128)(2,1)} %fusion.3), calls=%async_computation.1 | async-start | bytes 131072 | tf_op jit(solution)/shard_map/all_to_all | solution.py:449
  59.5 5.8 %shard_map.126 = bf16[768,1024]{1,0:T(8,128)(2,1)} custom-call(bf16[768,1024]{1,0:T(8,128)(2,1)} %refs_0_.1, bf16[768,1024]{1,0:T(8,128)(2,1)} %get-tuple-element.56.refs_1_, bf16[768,1024]{1,0:T(8,128)(2,1)} %get-tuple-element.57.refs_2_, bf16[1024,1024]{1,0:T(8,128)(2,1)} %refs_3_.1, bf16[256,128]{1,0:T(8,128)(2,1)} %copy-done.1, ...), custom_call_target="tpu_custom_call" | custom-call | flops 1610612736 | bytes 7864320 | tf_op jit(solution)/shard_map/pallas_call | solution.py:402
  65.4 1.0 %all-to-all-done.1 = bf16[16,8,256]{2,1,0:T(8,128)(2,1)S(1)} async-done(((bf16[16,8,256]{2,1,0:T(8,128)(2,1)}), bf16[16,8,256]{2,1,0:T(8,128)(2,1)S(1)}, u32[]{:S(2)}, u32[]{:S(2)}) %all-to-all-start.1) | async-done | bytes 65568 | tf_op jit(solution)/shard_map/all_to_all | solution.py:449
  66.4 0.8 %fusion.4 = f32[32,256]{1,0:T(8,128)} fusion(bf16[2,32,128]{2,1,0:T(8,128)(2,1)S(1)} %copy-done.9, bf16[16,8,256]{2,1,0:T(8,128)(2,1)S(1)} %all-to-all-done.1, f32[2,32]{1,0:T(2,128)S(1)} %add_divide_fusion), kind=kOutput, calls=%fused_computation.6 | convolution fusion | flops 4218880 | bytes 114944 | tf_op jit(solution)/shard_map/dot_general | solution.py:20
  (32 shorter events, 0.4 us)
Async XLA Ops:
  0.6 51.7 %copy-start = (bf16[1024,1024]{1,0:T(8,128)(2,1)S(1)}, bf16[1024,1024]{1,0:T(8,128)(2,1)}, u32[]{:S(2)}) copy-start(bf16[1024,1024]{1,0:T(8,128)(2,1)} %param.16) | copy-start | bytes 6291460
  8.9 8.6 %collective-permute-start = (bf16[256,128]{1,0:T(8,128)(2,1)}, bf16[256,128]{1,0:T(8,128)(2,1)S(1)}, u32[]{:S(2)}, u32[]{:S(2)}) collective-permute-start(bf16[256,128]{1,0:T(8,128)(2,1)} %get-tuple-element.33), channel_id=1, source_target_pairs={{0,1},{1,0},{2,3},{3,2},{4,5},{5,4},{6,7},{7,6},{8,9},{9,8},{10,11... | collective-permute-start | bytes 196616 | tf_op jit(solution)/shard_map/ppermute | solution.py:282
  9.5 8.1 %collective-permute-start.1 = (bf16[256,128]{1,0:T(8,128)(2,1)}, bf16[256,128]{1,0:T(8,128)(2,1)S(1)}, u32[]{:S(2)}, u32[]{:S(2)}) collective-permute-start(bf16[256,128]{1,0:T(8,128)(2,1)} %get-tuple-element.34), channel_id=1, source_target_pairs={{0,2},{1,3},{2,0},{3,1},{4,6},{5,7},{6,4},{7,5},{8,10},{9,11},{10,... | collective-permute-start | bytes 196616 | tf_op jit(solution)/shard_map/ppermute | solution.py:282
  12.1 5.6 %collective-permute-start.2 = (bf16[256,128]{1,0:T(8,128)(2,1)}, bf16[256,128]{1,0:T(8,128)(2,1)S(1)}, u32[]{:S(2)}, u32[]{:S(2)}) collective-permute-start(bf16[256,128]{1,0:T(8,128)(2,1)} %get-tuple-element.35), channel_id=1, source_target_pairs={{0,3},{1,2},{2,1},{3,0},{4,7},{5,6},{6,5},{7,4},{8,11},{9,10},{10,... | collective-permute-start | bytes 196616 | tf_op jit(solution)/shard_map/ppermute | solution.py:282
  12.1 5.5 %copy-start.6 = (bf16[256,128]{1,0:T(8,128)(2,1)S(1)}, bf16[256,128]{1,0:T(8,128)(2,1)}, u32[]{:S(2)}) copy-start(bf16[256,128]{1,0:T(8,128)(2,1)} %get-tuple-element.40) | copy-start | bytes 196612
  17.7 8.9 %collective-permute-start.5 = (bf16[256,128]{1,0:T(8,128)(2,1)S(1)}, bf16[256,128]{1,0:T(8,128)(2,1)S(1)}, u32[]{:S(2)}, u32[]{:S(2)}) collective-permute-start(bf16[256,128]{1,0:T(8,128)(2,1)S(1)} %fusion.22), channel_id=1, source_target_pairs={{0,8},{1,9},{2,10},{3,11},{4,12},{5,13},{6,14},{7,15},{16,24},{17,... | collective-permute-start | bytes 196616 | tf_op jit(solution)/shard_map/ppermute | solution.py:286
  22.4 4.2 %collective-permute-start.4 = (bf16[256,128]{1,0:T(8,128)(2,1)S(1)}, bf16[256,128]{1,0:T(8,128)(2,1)S(1)}, u32[]{:S(2)}, u32[]{:S(2)}) collective-permute-start(bf16[256,128]{1,0:T(8,128)(2,1)S(1)} %fusion.22), channel_id=1, source_target_pairs={{0,12},{1,13},{2,14},{3,15},{16,28},{17,29},{18,30},{19,31}} | collective-permute-start | bytes 196616 | tf_op jit(solution)/shard_map/ppermute | solution.py:286
  24.7 3.7 %collective-permute-start.3 = (bf16[256,128]{1,0:T(8,128)(2,1)S(1)}, bf16[256,128]{1,0:T(8,128)(2,1)S(1)}, u32[]{:S(2)}, u32[]{:S(2)}) collective-permute-start(bf16[256,128]{1,0:T(8,128)(2,1)S(1)} %fusion.22), channel_id=1, source_target_pairs={{0,4},{1,5},{2,6},{3,7},{4,8},{5,9},{6,10},{7,11},{8,12},{9,13},{1... | collective-permute-start | bytes 196616 | tf_op jit(solution)/shard_map/ppermute | solution.py:286
  28.6 5.7 %copy-start.1 = (bf16[256,128]{1,0:T(8,128)(2,1)}, bf16[256,128]{1,0:T(8,128)(2,1)S(1)}, u32[]{:S(2)}) copy-start(bf16[256,128]{1,0:T(8,128)(2,1)S(1)} %get-tuple-element.45.refs_0_.refs_4_) | copy-start | bytes 196612
  28.6 4.7 %collective-permute-start.6 = (bf16[256,128]{1,0:T(8,128)(2,1)S(1)}, bf16[256,128]{1,0:T(8,128)(2,1)S(1)}, u32[]{:S(2)}, u32[]{:S(2)}) collective-permute-start(bf16[256,128]{1,0:T(8,128)(2,1)S(1)} %get-tuple-element.46), channel_id=1, source_target_pairs={{0,1},{1,0},{2,3},{3,2},{4,5},{5,4},{6,7},{7,6},{8,9},{9,8},{10,11... | collective-permute-start | bytes 196616 | tf_op jit(solution)/shard_map/ppermute | solution.py:282
  28.7 4.7 %collective-permute-start.7 = (bf16[256,128]{1,0:T(8,128)(2,1)S(1)}, bf16[256,128]{1,0:T(8,128)(2,1)S(1)}, u32[]{:S(2)}, u32[]{:S(2)}) collective-permute-start(bf16[256,128]{1,0:T(8,128)(2,1)S(1)} %get-tuple-element.47), channel_id=1, source_target_pairs={{0,2},{1,3},{2,0},{3,1},{4,6},{5,7},{6,4},{7,5},{8,10},{9,11},{10,... | collective-permute-start | bytes 196616 | tf_op jit(solution)/shard_map/ppermute | solution.py:282
  30.3 4.0 %collective-permute-start.8 = (bf16[256,128]{1,0:T(8,128)(2,1)S(1)}, bf16[256,128]{1,0:T(8,128)(2,1)S(1)}, u32[]{:S(2)}, u32[]{:S(2)}) collective-permute-start(bf16[256,128]{1,0:T(8,128)(2,1)S(1)} %get-tuple-element.48), channel_id=1, source_target_pairs={{0,3},{1,2},{2,1},{3,0},{4,7},{5,6},{6,5},{7,4},{8,11},{9,10},{10,... | collective-permute-start | bytes 196616 | tf_op jit(solution)/shard_map/ppermute | solution.py:282
  33.3 9.0 %copy-start.7 = (bf16[1024,32]{0,1:T(8,128)(2,1)S(1)}, bf16[1024,32]{0,1:T(8,128)(2,1)}, u32[]{:S(2)}) copy-start(bf16[1024,32]{0,1:T(8,128)(2,1)} %param.18) | copy-start | bytes 196612
  33.3 9.1 %copy-start.8 = (f32[2,32,32]{2,1,0:T(8,128)S(1)}, f32[2,32,32]{2,1,0:T(8,128)}, u32[]{:S(2)}) copy-start(f32[2,32,32]{2,1,0:T(8,128)} %get-tuple-element.59) | copy-start | bytes 24580
  33.4 18.8 %copy-start.2 = (bf16[256,128]{1,0:T(8,128)(2,1)}, bf16[256,128]{1,0:T(8,128)(2,1)S(1)}, u32[]{:S(2)}) copy-start(bf16[256,128]{1,0:T(8,128)(2,1)S(1)} %collective-permute-done.6.refs_1_.refs_5_) | copy-start | bytes 196612
  33.4 18.8 %copy-start.3 = (bf16[256,128]{1,0:T(8,128)(2,1)}, bf16[256,128]{1,0:T(8,128)(2,1)S(1)}, u32[]{:S(2)}) copy-start(bf16[256,128]{1,0:T(8,128)(2,1)S(1)} %collective-permute-done.7.refs_2_.refs_6_) | copy-start | bytes 196612
  34.3 17.9 %copy-start.4 = (bf16[256,128]{1,0:T(8,128)(2,1)}, bf16[256,128]{1,0:T(8,128)(2,1)S(1)}, u32[]{:S(2)}) copy-start(bf16[256,128]{1,0:T(8,128)(2,1)S(1)} %collective-permute-done.8.refs_3_.refs_7_) | copy-start | bytes 196612
  35.9 16.5 %all-to-all-start = ((bf16[16,8,1024]{2,1,0:T(8,128)(2,1)}), bf16[16,8,1024]{2,1,0:T(8,128)(2,1)S(1)}, u32[]{:S(2)}, u32[]{:S(2)}) async-start(bf16[16,8,1024]{2,1,0:T(8,128)(2,1)} %bitcast.3), calls=%async_computation | async-start | bytes 524288 | tf_op jit(solution)/shard_map/all_to_all | solution.py:449
  42.6 9.8 %copy-start.5 = (bf16[1024,256]{1,0:T(8,128)(2,1)S(1)}, bf16[1024,256]{1,0:T(8,128)(2,1)}, u32[]{:S(2)}) copy-start(bf16[1024,256]{1,0:T(8,128)(2,1)} %param.17) | copy-start | bytes 1572868
  53.6 12.8 %all-to-all-start.1 = ((bf16[16,8,256]{2,1,0:T(8,128)(2,1)}), bf16[16,8,256]{2,1,0:T(8,128)(2,1)S(1)}, u32[]{:S(2)}, u32[]{:S(2)}) async-start(bf16[16,8,256]{2,1,0:T(8,128)(2,1)} %fusion.3), calls=%async_computation.1 | async-start | bytes 131072 | tf_op jit(solution)/shard_map/all_to_all | solution.py:449
  59.5 6.9 %copy-start.9 = (bf16[2,32,128]{2,1,0:T(8,128)(2,1)S(1)}, bf16[2,32,128]{2,1,0:T(8,128)(2,1)}, u32[]{:S(2)}) copy-start(bf16[2,32,128]{2,1,0:T(8,128)(2,1)} %get-tuple-element.60) | copy-start | bytes 49156

commit v10 on v7

--- a/solution.py
+++ b/solution.py
@@ -59,7 +59,8 @@
     return jax.ShapeDtypeStruct(shape, kind)
 
 
-def key_value_kernel(head_dim, tile, events, w_key, w_value, keys, values, inner, *states):
+def key_value_kernel(head_dim, tile, events, w_key, w_value, keys, values, inner, *refs):
+    states, kept = refs[:PLANE], refs[PLANE]
     pair = w_key.shape[1]
     both = dot(events[...], jnp.concatenate([w_key[...], w_value[...]], axis=1)).astype(BF16)
     k, v = both[:, :pair], both[:, pair:]
@@ -74,11 +75,12 @@
         parts = [slice(h, h + head_dim) for h in range(0, pair, head_dim)]
         own = jnp.concatenate([product[part, part] for part in parts], axis=0)
         total = own if total is None else total + own
-    for i, state in enumerate(states):
-
-        @pl.when(pl.program_id(0) == i)
-        def _():
-            state[...] = total.astype(BF16)
+    kept[pl.program_id(0)] = total.astype(BF16)
+
+    @pl.when(pl.program_id(0) == PLANE - 1)
+    def _():
+        for i, state in enumerate(states):
+            state[...] = kept[i]
 
 
 def key_value_state(events, w_key, w_value):
@@ -106,6 +108,7 @@
         + [shaped((pair, head_dim), BF16)] * PLANE,
         4 * rows * width * width,
         8 * rows * width,
+        [pltpu.VMEM((PLANE, pair, head_dim), BF16)],
     )(events, w_key, w_value)
 
 
@@ -283,7 +286,8 @@
     rank = lax.axis_index("seq") & (PLANE - 1)
     states = [x.astype(F32) for x in states]
     total = sum(states).astype(BF16)
-    planes = sum(later(total, s).astype(F32) for s in reversed(range(PLANE, devices, PLANE)))
+    shifts = list(range(PLANE, devices, PLANE))
+    planes = sum(later(total, s).astype(F32) for s in shifts[:1] + shifts[:0:-1])
     before = []
     for j in range(PLANE):
         held = [jnp.where((rank ^ i) < (rank ^ j), states[i], 0.0) for i in range(PLANE) if i != j]

time: 67.9 us -> 67.3 us (level)
  transfers between devices with their start and end apart: 11 -> 11, of which waited for: 5 -> 4; matrix products, arithmetic and copies ran while one was open for 4% -> 5% of each run, Pallas kernels for 30% -> 31%
where the time goes in v10:
time: 67.3 us; the launch traced here: 66.8 us
  Pallas kernels  30.3 us (45%)
  starting transfers between devices  26.3 us (39%)
  waiting for transfers between devices  3.98 us (6%)
  other arithmetic  3.09 us (5%)
  matrix products  2.16 us (3%)
  between operations  0.9 us (1%)
    all_to_all x2, starting transfers between devices, exchange(): return lax.all_to_all(x, 'seq', split_axis=0, concat_axis=0, tiled=True)  12.3 us
    pallas_call x1, Pallas kernels, queries_within(): call(functools.partial(within_kernel, head_dim, tile), (width // pair,),...  9.6 us
    ppermute x3, starting transfers between devices, later(): lax.ppermute(x, 'seq', [(i, i + s) for i in range(lax.axis_size('seq') -...  8.85 us
    pallas_call x1, Pallas kernels, key_value_state(): call(functools.partial(key_value_kernel, head_dim, tile), (PLANE,), [whol...  8.28 us
    pallas_call x1, Pallas kernels, hidden_rows(): call(functools.partial(hidden_kernel, head_dim, tile), (), [FAR] * (4 + P...  5.84 us
    ppermute x6, starting transfers between devices, flip(): return lax.ppermute(x, 'seq', [(i, i ^ j) for i in range(devices)])  5.11 us
    pallas_call x1, Pallas kernels, labelled_rows(): call(functools.partial(labelled_kernel, width // HEADS, devices // EXPERT...  5.09 us
    dot_general x3, matrix products, dot(): lax.dot_general(a, b, (contract, ((), ())), preferred_element_type=F32, *...  2.16 us
  transfers between devices with their start and end apart: 11, of which 4 were waited for; matrix products, arithmetic and copies ran while one was open for 5% of the time, Pallas kernels for 31%

profile of v10, /device:TPU:0, one launch (start us, length us, event | category | flops | bytes accessed | tf_op | source)
XLA Modules:
  0.0 66.8 jit_solution(5885360611657503028)
XLA Ops:
  0.6 8.3 %shard_map.122 = (bf16[4,768,256]{2,1,0:T(8,128)(2,1)}, bf16[4,768,256]{2,1,0:T(8,128)(2,1)}, bf16[2,1024,128]{2,1,0:T(8,128)(2,1)}, bf16[256,128]{1,0:T(8,128)(...) custom-call(bf16[768,1024]{1,0:T(8,128)(2,1)} %refs_0_.1, ...), custom_call_target="tpu_custom_call" | custom-call | flops 3221225472 | bytes 6291456 | tf_op jit(solution)/shard_map/pallas_call | solution.py:99
  8.9 0.5 collective-permute-start
  9.4 2.6 %collective-permute-start.1 = (bf16[256,128]{1,0:T(8,128)(2,1)}, bf16[256,128]{1,0:T(8,128)(2,1)S(1)}, u32[]{:S(2)}, u32[]{:S(2)}) collective-permute-start(bf16[256,128]{1,0:T(8,128)(2,1)} %get-tuple-element.34), channel_id=1, source_target_pairs={{0,2},{1,3},{2,0},{3,1},{4,6},{5,7},{6,4},{7,5},{8,10},{9,11},{10,... | collective-permute-start | bytes 196616 | tf_op jit(solution)/shard_map/ppermute | solution.py:273
  12.1 5.1 %shard_map.123 = (f32[32,3328]{1,0:T(8,128)}, bf16[2,32,128]{2,1,0:T(8,128)(2,1)}, f32[2,32,32]{2,1,0:T(8,128)}) custom-call(bf16[768,1024]{1,0:T(8,128)(2,1)} %refs_0_.1, bf16[1024,1024]{1,0:T(8,128)(2,1)} %w_query.1, bf16[4,768,256]{2,1,0:T(8,128)(2,1)} %get-tuple-element.51.keys_far.keys, bf16[4,768,256]{2,1,0:T(8,128)(2,1)} %get-tuple-element.52.values_far.values, ...), custom_call_target="tpu_custom_call" | custom-call | flops 100663296 | bytes 6291456 | tf_op jit(solution)/shard_map/pallas_call | solution.py:167
  17.3 4.7 %collective-permute-start.5 = (bf16[256,128]{1,0:T(8,128)(2,1)S(1)}, bf16[256,128]{1,0:T(8,128)(2,1)S(1)}, u32[]{:S(2)}, u32[]{:S(2)}) collective-permute-start(bf16[256,128]{1,0:T(8,128)(2,1)S(1)} %fusion.22), channel_id=1, source_target_pairs={{0,8},{1,9},{2,10},{3,11},{4,12},{5,13},{6,14},{7,15},{16,24},{17,... | collective-permute-start | bytes 196616 | tf_op jit(solution)/shard_map/ppermute | solution.py:277
  22.0 2.3 %collective-permute-start.4 = (bf16[256,128]{1,0:T(8,128)(2,1)S(1)}, bf16[256,128]{1,0:T(8,128)(2,1)S(1)}, u32[]{:S(2)}, u32[]{:S(2)}) collective-permute-start(bf16[256,128]{1,0:T(8,128)(2,1)S(1)} %fusion.22), channel_id=1, source_target_pairs={{0,12},{1,13},{2,14},{3,15},{16,28},{17,29},{18,30},{19,31}} | collective-permute-start | bytes 196616 | tf_op jit(solution)/shard_map/ppermute | solution.py:277
  24.3 1.8 %collective-permute-start.3 = (bf16[256,128]{1,0:T(8,128)(2,1)S(1)}, bf16[256,128]{1,0:T(8,128)(2,1)S(1)}, u32[]{:S(2)}, u32[]{:S(2)}) collective-permute-start(bf16[256,128]{1,0:T(8,128)(2,1)S(1)} %fusion.22), channel_id=1, source_target_pairs={{0,4},{1,5},{2,6},{3,7},{4,8},{5,9},{6,10},{7,11},{8,12},{9,13},{1... | collective-permute-start | bytes 196616 | tf_op jit(solution)/shard_map/ppermute | solution.py:277
  26.2 1.8 %collective-permute-done.3 = bf16[256,128]{1,0:T(8,128)(2,1)S(1)} collective-permute-done((bf16[256,128]{1,0:T(8,128)(2,1)S(1)}, bf16[256,128]{1,0:T(8,128)(2,1)S(1)}, u32[]{:S(2)}, u32[]{:S(2)}) %collective-permute-start.3) | collective-permute-done | bytes 65568 | tf_op jit(solution)/shard_map/ppermute | solution.py:277
  28.1 0.2 fusion.17
  28.3 1.6 %collective-permute-start.7 = (bf16[256,128]{1,0:T(8,128)(2,1)S(1)}, bf16[256,128]{1,0:T(8,128)(2,1)S(1)}, u32[]{:S(2)}, u32[]{:S(2)}) collective-permute-start(bf16[256,128]{1,0:T(8,128)(2,1)S(1)} %get-tuple-element.47), channel_id=1, source_target_pairs={{0,2},{1,3},{2,0},{3,1},{4,6},{5,7},{6,4},{7,5},{8,10},{9,11},{10,... | collective-permute-start | bytes 196616 | tf_op jit(solution)/shard_map/ppermute | solution.py:273
  29.9 0.3 collective-permute-start.8
  30.2 1.0 %broadcast_multiply_fusion.1.packed = f32[32,3328]{1,0:T(8,128)S(1)} fusion(f32[32,3328]{1,0:T(8,128)} %get-tuple-element.39, f32[]{:T(128)S(6)} %convert_element_type.57), kind=kLoop, calls=%fused_computation.24 | loop fusion | flops 106496 | bytes 851972 | tf_op jit(solution)/shard_map/mul | solution.py:449
  31.2 1.7 %broadcast_multiply_fusion.w_output = bf16[1024,1024]{1,0:T(8,128)(2,1)S(1)} fusion(bf16[1024,1024]{1,0:T(8,128)(2,1)} %refs_3_.1, bf16[]{:T(256)} %constant.4.clone.1), kind=kLoop, calls=%fused_computation.7 | loop fusion | flops 1048576 | bytes 4194306 | tf_op jit(solution)/shard_map/mul | solution.py:449
  33.0 0.9 %collective-permute-done.8.refs_3_.refs_7_ = bf16[256,128]{1,0:T(8,128)(2,1)S(1)} collective-permute-done((bf16[256,128]{1,0:T(8,128)(2,1)S(1)}, bf16[256,128]{1,0:T(8,128)(2,1)S(1)}, u32[]{:S(2)}, u32[]{:S(2)}) %collective-permute-start.8) | collective-permute-done | bytes 65568 | tf_op jit(solution)/shard_map/ppermute | solution.py:273
  33.9 1.5 %shard_map.124 = (bf16[32,1024]{1,0:T(8,128)(2,1)S(1)}, bf16[128,1024]{1,0:T(8,128)(2,1)}) custom-call(f32[32,3328]{1,0:T(8,128)S(1)} %broadcast_multiply_fusion.1.packed, bf16[1024,1024]{1,0:T(8,128)(2,1)S(1)} %broadcast_multiply_fusion.w_output, bf16[256,128]{1,0:T(8,128)(2,1)S(1)} %get-tuple-element.45.refs_0_.refs_4_, ...), custom_call_target="tpu_custom_call" | custom-call | flops 67108864 | bytes 2097152 | tf_op jit(solution)/shard_map/pallas_call | solution.py:330
  35.5 6.4 %all-to-all-start = ((bf16[16,8,1024]{2,1,0:T(8,128)(2,1)}), bf16[16,8,1024]{2,1,0:T(8,128)(2,1)S(1)}, u32[]{:S(2)}, u32[]{:S(2)}) async-start(bf16[16,8,1024]{2,1,0:T(8,128)(2,1)} %bitcast.3), calls=%async_computation | async-start | bytes 524288 | tf_op jit(solution)/shard_map/all_to_all | solution.py:440
  41.9 0.1 fusion.25
  42.2 9.6 %shard_map.125 = (bf16[768,1024]{1,0:T(8,128)(2,1)}, bf16[768,1024]{1,0:T(8,128)(2,1)}) custom-call(bf16[768,1024]{1,0:T(8,128)(2,1)} %refs_0_.1, bf16[1024,1024]{1,0:T(8,128)(2,1)} %w_query.1, bf16[4,768,256]{2,1,0:T(8,128)(2,1)} %get-tuple-element.51.keys_far.keys, bf16[4,768,256]{2,1,0:T(8,128)(2,1)} %get-tuple-element.52.values_far.values, ...), custom_call_target="tpu_custom_call" | custom-call | flops 2415919104 | bytes 6291456 | tf_op jit(solution)/shard_map/pallas_call | solution.py:254
  51.8 0.2 all-to-all-done
  52.0 1.3 %fusion.3 = bf16[16,8,256]{2,1,0:T(8,128)(2,1)} fusion(bf16[1024,256]{1,0:T(8,128)(2,1)S(1)} %copy-done.5, bf16[128,1024]{1,0:T(8,128)(2,1)S(1)} %bitcast.18, bf16[1024,1024]{1,0:T(8,128)(2,1)S(1)} %copy-done), kind=kOutput, calls=%fused_computation.4 | convolution fusion | flops 335839232 | bytes 2949120 | tf_op jit(solution)/shard_map/dot_general | solution.py:20
  53.3 5.9 %all-to-all-start.1 = ((bf16[16,8,256]{2,1,0:T(8,128)(2,1)}), bf16[16,8,256]{2,1,0:T(8,128)(2,1)S(1)}, u32[]{:S(2)}, u32[]{:S(2)}) async-start(bf16[16,8,256]{2,1,0:T(8,128)(2,1)} %fusion.3), calls=%async_computation.1 | async-start | bytes 131072 | tf_op jit(solution)/shard_map/all_to_all | solution.py:440
  59.2 5.8 %shard_map.126 = bf16[768,1024]{1,0:T(8,128)(2,1)} custom-call(bf16[768,1024]{1,0:T(8,128)(2,1)} %refs_0_.1, bf16[768,1024]{1,0:T(8,128)(2,1)} %get-tuple-element.56.refs_1_, bf16[768,1024]{1,0:T(8,128)(2,1)} %get-tuple-element.57.refs_2_, bf16[1024,1024]{1,0:T(8,128)(2,1)} %refs_3_.1, bf16[256,128]{1,0:T(8,128)(2,1)} %copy-done.1, ...), custom_call_target="tpu_custom_call" | custom-call | flops 1610612736 | bytes 7864320 | tf_op jit(solution)/shard_map/pallas_call | solution.py:393
  65.0 1.0 %all-to-all-done.1 = bf16[16,8,256]{2,1,0:T(8,128)(2,1)S(1)} async-done(((bf16[16,8,256]{2,1,0:T(8,128)(2,1)}), bf16[16,8,256]{2,1,0:T(8,128)(2,1)S(1)}, u32[]{:S(2)}, u32[]{:S(2)}) %all-to-all-start.1) | async-done | bytes 65568 | tf_op jit(solution)/shard_map/all_to_all | solution.py:440
  66.0 0.8 %fusion.4 = f32[32,256]{1,0:T(8,128)} fusion(bf16[2,32,128]{2,1,0:T(8,128)(2,1)S(1)} %copy-done.9, bf16[16,8,256]{2,1,0:T(8,128)(2,1)S(1)} %all-to-all-done.1, f32[2,32]{1,0:T(2,128)S(1)} %add_divide_fusion), kind=kOutput, calls=%fused_computation.6 | convolution fusion | flops 4218880 | bytes 114944 | tf_op jit(solution)/shard_map/dot_general | solution.py:20
  (32 shorter events, 0.4 us)
Async XLA Ops:
  0.6 51.3 %copy-start = (bf16[1024,1024]{1,0:T(8,128)(2,1)S(1)}, bf16[1024,1024]{1,0:T(8,128)(2,1)}, u32[]{:S(2)}) copy-start(bf16[1024,1024]{1,0:T(8,128)(2,1)} %param.16) | copy-start | bytes 6291460
  8.9 8.3 %collective-permute-start = (bf16[256,128]{1,0:T(8,128)(2,1)}, bf16[256,128]{1,0:T(8,128)(2,1)S(1)}, u32[]{:S(2)}, u32[]{:S(2)}) collective-permute-start(bf16[256,128]{1,0:T(8,128)(2,1)} %get-tuple-element.33), channel_id=1, source_target_pairs={{0,1},{1,0},{2,3},{3,2},{4,5},{5,4},{6,7},{7,6},{8,9},{9,8},{10,11... | collective-permute-start | bytes 196616 | tf_op jit(solution)/shard_map/ppermute | solution.py:273
  9.4 7.8 %collective-permute-start.1 = (bf16[256,128]{1,0:T(8,128)(2,1)}, bf16[256,128]{1,0:T(8,128)(2,1)S(1)}, u32[]{:S(2)}, u32[]{:S(2)}) collective-permute-start(bf16[256,128]{1,0:T(8,128)(2,1)} %get-tuple-element.34), channel_id=1, source_target_pairs={{0,2},{1,3},{2,0},{3,1},{4,6},{5,7},{6,4},{7,5},{8,10},{9,11},{10,... | collective-permute-start | bytes 196616 | tf_op jit(solution)/shard_map/ppermute | solution.py:273
  12.0 5.2 %collective-permute-start.2 = (bf16[256,128]{1,0:T(8,128)(2,1)}, bf16[256,128]{1,0:T(8,128)(2,1)S(1)}, u32[]{:S(2)}, u32[]{:S(2)}) collective-permute-start(bf16[256,128]{1,0:T(8,128)(2,1)} %get-tuple-element.35), channel_id=1, source_target_pairs={{0,3},{1,2},{2,1},{3,0},{4,7},{5,6},{6,5},{7,4},{8,11},{9,10},{10,... | collective-permute-start | bytes 196616 | tf_op jit(solution)/shard_map/ppermute | solution.py:273
  12.1 5.1 %copy-start.6 = (bf16[256,128]{1,0:T(8,128)(2,1)S(1)}, bf16[256,128]{1,0:T(8,128)(2,1)}, u32[]{:S(2)}) copy-start(bf16[256,128]{1,0:T(8,128)(2,1)} %get-tuple-element.40) | copy-start | bytes 196612
  17.3 8.9 %collective-permute-start.5 = (bf16[256,128]{1,0:T(8,128)(2,1)S(1)}, bf16[256,128]{1,0:T(8,128)(2,1)S(1)}, u32[]{:S(2)}, u32[]{:S(2)}) collective-permute-start(bf16[256,128]{1,0:T(8,128)(2,1)S(1)} %fusion.22), channel_id=1, source_target_pairs={{0,8},{1,9},{2,10},{3,11},{4,12},{5,13},{6,14},{7,15},{16,24},{17,... | collective-permute-start | bytes 196616 | tf_op jit(solution)/shard_map/ppermute | solution.py:277
  22.0 4.2 %collective-permute-start.4 = (bf16[256,128]{1,0:T(8,128)(2,1)S(1)}, bf16[256,128]{1,0:T(8,128)(2,1)S(1)}, u32[]{:S(2)}, u32[]{:S(2)}) collective-permute-start(bf16[256,128]{1,0:T(8,128)(2,1)S(1)} %fusion.22), channel_id=1, source_target_pairs={{0,12},{1,13},{2,14},{3,15},{16,28},{17,29},{18,30},{19,31}} | collective-permute-start | bytes 196616 | tf_op jit(solution)/shard_map/ppermute | solution.py:277
  24.3 3.7 %collective-permute-start.3 = (bf16[256,128]{1,0:T(8,128)(2,1)S(1)}, bf16[256,128]{1,0:T(8,128)(2,1)S(1)}, u32[]{:S(2)}, u32[]{:S(2)}) collective-permute-start(bf16[256,128]{1,0:T(8,128)(2,1)S(1)} %fusion.22), channel_id=1, source_target_pairs={{0,4},{1,5},{2,6},{3,7},{4,8},{5,9},{6,10},{7,11},{8,12},{9,13},{1... | collective-permute-start | bytes 196616 | tf_op jit(solution)/shard_map/ppermute | solution.py:277
  28.2 5.7 %copy-start.1 = (bf16[256,128]{1,0:T(8,128)(2,1)}, bf16[256,128]{1,0:T(8,128)(2,1)S(1)}, u32[]{:S(2)}) copy-start(bf16[256,128]{1,0:T(8,128)(2,1)S(1)} %get-tuple-element.45.refs_0_.refs_4_) | copy-start | bytes 196612
  28.2 4.7 %collective-permute-start.6 = (bf16[256,128]{1,0:T(8,128)(2,1)S(1)}, bf16[256,128]{1,0:T(8,128)(2,1)S(1)}, u32[]{:S(2)}, u32[]{:S(2)}) collective-permute-start(bf16[256,128]{1,0:T(8,128)(2,1)S(1)} %get-tuple-element.46), channel_id=1, source_target_pairs={{0,1},{1,0},{2,3},{3,2},{4,5},{5,4},{6,7},{7,6},{8,9},{9,8},{10,11... | collective-permute-start | bytes 196616 | tf_op jit(solution)/shard_map/ppermute | solution.py:273
  28.3 4.7 %collective-permute-start.7 = (bf16[256,128]{1,0:T(8,128)(2,1)S(1)}, bf16[256,128]{1,0:T(8,128)(2,1)S(1)}, u32[]{:S(2)}, u32[]{:S(2)}) collective-permute-start(bf16[256,128]{1,0:T(8,128)(2,1)S(1)} %get-tuple-element.47), channel_id=1, source_target_pairs={{0,2},{1,3},{2,0},{3,1},{4,6},{5,7},{6,4},{7,5},{8,10},{9,11},{10,... | collective-permute-start | bytes 196616 | tf_op jit(solution)/shard_map/ppermute | solution.py:273
  29.9 4.0 %collective-permute-start.8 = (bf16[256,128]{1,0:T(8,128)(2,1)S(1)}, bf16[256,128]{1,0:T(8,128)(2,1)S(1)}, u32[]{:S(2)}, u32[]{:S(2)}) collective-permute-start(bf16[256,128]{1,0:T(8,128)(2,1)S(1)} %get-tuple-element.48), channel_id=1, source_target_pairs={{0,3},{1,2},{2,1},{3,0},{4,7},{5,6},{6,5},{7,4},{8,11},{9,10},{10,... | collective-permute-start | bytes 196616 | tf_op jit(solution)/shard_map/ppermute | solution.py:273
  32.9 9.0 %copy-start.7 = (bf16[1024,32]{0,1:T(8,128)(2,1)S(1)}, bf16[1024,32]{0,1:T(8,128)(2,1)}, u32[]{:S(2)}) copy-start(bf16[1024,32]{0,1:T(8,128)(2,1)} %param.18) | copy-start | bytes 196612
  33.0 9.1 %copy-start.8 = (f32[2,32,32]{2,1,0:T(8,128)S(1)}, f32[2,32,32]{2,1,0:T(8,128)}, u32[]{:S(2)}) copy-start(f32[2,32,32]{2,1,0:T(8,128)} %get-tuple-element.59) | copy-start | bytes 24580
  33.0 18.8 %copy-start.2 = (bf16[256,128]{1,0:T(8,128)(2,1)}, bf16[256,128]{1,0:T(8,128)(2,1)S(1)}, u32[]{:S(2)}) copy-start(bf16[256,128]{1,0:T(8,128)(2,1)S(1)} %collective-permute-done.6.refs_1_.refs_5_) | copy-start | bytes 196612
  33.0 18.8 %copy-start.3 = (bf16[256,128]{1,0:T(8,128)(2,1)}, bf16[256,128]{1,0:T(8,128)(2,1)S(1)}, u32[]{:S(2)}) copy-start(bf16[256,128]{1,0:T(8,128)(2,1)S(1)} %collective-permute-done.7.refs_2_.refs_6_) | copy-start | bytes 196612
  33.9 17.9 %copy-start.4 = (bf16[256,128]{1,0:T(8,128)(2,1)}, bf16[256,128]{1,0:T(8,128)(2,1)S(1)}, u32[]{:S(2)}) copy-start(bf16[256,128]{1,0:T(8,128)(2,1)S(1)} %collective-permute-done.8.refs_3_.refs_7_) | copy-start | bytes 196612
  35.5 16.5 %all-to-all-start = ((bf16[16,8,1024]{2,1,0:T(8,128)(2,1)}), bf16[16,8,1024]{2,1,0:T(8,128)(2,1)S(1)}, u32[]{:S(2)}, u32[]{:S(2)}) async-start(bf16[16,8,1024]{2,1,0:T(8,128)(2,1)} %bitcast.3), calls=%async_computation | async-start | bytes 524288 | tf_op jit(solution)/shard_map/all_to_all | solution.py:440
  42.2 9.8 %copy-start.5 = (bf16[1024,256]{1,0:T(8,128)(2,1)S(1)}, bf16[1024,256]{1,0:T(8,128)(2,1)}, u32[]{:S(2)}) copy-start(bf16[1024,256]{1,0:T(8,128)(2,1)} %param.17) | copy-start | bytes 1572868
  53.3 12.8 %all-to-all-start.1 = ((bf16[16,8,256]{2,1,0:T(8,128)(2,1)}), bf16[16,8,256]{2,1,0:T(8,128)(2,1)S(1)}, u32[]{:S(2)}, u32[]{:S(2)}) async-start(bf16[16,8,256]{2,1,0:T(8,128)(2,1)} %fusion.3), calls=%async_computation.1 | async-start | bytes 131072 | tf_op jit(solution)/shard_map/all_to_all | solution.py:440
  59.1 6.9 %copy-start.9 = (bf16[2,32,128]{2,1,0:T(8,128)(2,1)S(1)}, bf16[2,32,128]{2,1,0:T(8,128)(2,1)}, u32[]{:S(2)}) copy-start(bf16[2,32,128]{2,1,0:T(8,128)(2,1)} %get-tuple-element.60) | copy-start | bytes 49156

commit v11 on v10

--- a/solution.py
+++ b/solution.py
@@ -79,8 +79,9 @@
 
     @pl.when(pl.program_id(0) == PLANE - 1)
     def _():
+        rank = lax.axis_index("seq") & (PLANE - 1)
         for i, state in enumerate(states):
-            state[...] = kept[i]
+            state[...] = kept[rank ^ i]
 
 
 def key_value_state(events, w_key, w_value):
@@ -90,18 +91,12 @@
     tile = row_tile(rows)
     inner = rows // tile - 1
 
-    def turn(i):
-        return (lax.axis_index("seq") ^ i) & (PLANE - 1)
-
-    def cols(many):
-        return pl.BlockSpec((many, pair), lambda i: (0, turn(i)))
-
     return call(
         functools.partial(key_value_kernel, head_dim, tile),
         (PLANE,),
-        [whole((rows, width)), cols(width), cols(width)],
-        [pl.BlockSpec((None, rows, pair), lambda i: (turn(i), 0, 0))] * 2
-        + [pl.BlockSpec((inner, pair, head_dim), lambda i: (0, turn(i), 0))]
+        [whole((rows, width)), columns(width, pair), columns(width, pair)],
+        [pl.BlockSpec((None, rows, pair), lambda i: (i, 0, 0))] * 2
+        + [pl.BlockSpec((inner, pair, head_dim), lambda i: (0, i, 0))]
         + [whole((pair, head_dim))] * PLANE,
         [shaped((PLANE, rows, pair), BF16)] * 2
         + [shaped((inner, width, head_dim), BF16)]

time: 67.3 us -> 67.2 us (level)
  no operation moved by 1% of the time
where the time goes in v11:
time: 67.2 us; the launch traced here: 66.7 us
  Pallas kernels  30.3 us (45%)
  starting transfers between devices  26.3 us (39%)
  waiting for transfers between devices  3.98 us (6%)
  other arithmetic  3.09 us (5%)
  matrix products  2.16 us (3%)
  between operations  0.9 us (1%)
    all_to_all x2, starting transfers between devices, exchange(): return lax.all_to_all(x, 'seq', split_axis=0, concat_axis=0, tiled=True)  12.3 us
    pallas_call x1, Pallas kernels, queries_within(): call(functools.partial(within_kernel, head_dim, tile), (width // pair,),...  9.6 us
    ppermute x3, starting transfers between devices, later(): lax.ppermute(x, 'seq', [(i, i + s) for i in range(lax.axis_size('seq') -...  8.86 us
    pallas_call x1, Pallas kernels, key_value_state(): call(functools.partial(key_value_kernel, head_dim, tile), (PLANE,), [whol...  8.22 us
    pallas_call x1, Pallas kernels, hidden_rows(): call(functools.partial(hidden_kernel, head_dim, tile), (), [FAR] * (4 + P...  5.84 us
    ppermute x6, starting transfers between devices, flip(): return lax.ppermute(x, 'seq', [(i, i ^ j) for i in range(devices)])  5.11 us
    pallas_call x1, Pallas kernels, labelled_rows(): call(functools.partial(labelled_kernel, width // HEADS, devices // EXPERT...  5.08 us
    dot_general x3, matrix products, dot(): lax.dot_general(a, b, (contract, ((), ())), preferred_element_type=F32, *...  2.16 us
  transfers between devices with their start and end apart: 11, of which 4 were waited for; matrix products, arithmetic and copies ran while one was open for 5% of the time, Pallas kernels for 31%

profile of v11, /device:TPU:0, one launch (start us, length us, event | category | flops | bytes accessed | tf_op | source)
XLA Modules:
  0.0 66.7 jit_solution(15951187773530934672)
XLA Ops:
  0.6 8.2 %shard_map.122 = (bf16[4,768,256]{2,1,0:T(8,128)(2,1)}, bf16[4,768,256]{2,1,0:T(8,128)(2,1)}, bf16[2,1024,128]{2,1,0:T(8,128)(2,1)}, bf16[256,128]{1,0:T(8,128)(...) custom-call(bf16[768,1024]{1,0:T(8,128)(2,1)} %refs_0_.1, ...), custom_call_target="tpu_custom_call" | custom-call | flops 3221225472 | bytes 6291456 | tf_op jit(solution)/shard_map/pallas_call | solution.py:94
  8.9 0.5 collective-permute-start
  9.4 2.6 %collective-permute-start.1 = (bf16[256,128]{1,0:T(8,128)(2,1)}, bf16[256,128]{1,0:T(8,128)(2,1)S(1)}, u32[]{:S(2)}, u32[]{:S(2)}) collective-permute-start(bf16[256,128]{1,0:T(8,128)(2,1)} %get-tuple-element.34), channel_id=1, source_target_pairs={{0,2},{1,3},{2,0},{3,1},{4,6},{5,7},{6,4},{7,5},{8,10},{9,11},{10,... | collective-permute-start | bytes 196616 | tf_op jit(solution)/shard_map/ppermute | solution.py:268
  12.1 5.1 %shard_map.123 = (f32[32,3328]{1,0:T(8,128)}, bf16[2,32,128]{2,1,0:T(8,128)(2,1)}, f32[2,32,32]{2,1,0:T(8,128)}) custom-call(bf16[768,1024]{1,0:T(8,128)(2,1)} %refs_0_.1, bf16[1024,1024]{1,0:T(8,128)(2,1)} %w_query.1, bf16[4,768,256]{2,1,0:T(8,128)(2,1)} %get-tuple-element.51.keys_far.keys, bf16[4,768,256]{2,1,0:T(8,128)(2,1)} %get-tuple-element.52.values_far.values, ...), custom_call_target="tpu_custom_call" | custom-call | flops 100663296 | bytes 6291456 | tf_op jit(solution)/shard_map/pallas_call | solution.py:162
  17.2 4.7 %collective-permute-start.5 = (bf16[256,128]{1,0:T(8,128)(2,1)S(1)}, bf16[256,128]{1,0:T(8,128)(2,1)S(1)}, u32[]{:S(2)}, u32[]{:S(2)}) collective-permute-start(bf16[256,128]{1,0:T(8,128)(2,1)S(1)} %fusion.22), channel_id=1, source_target_pairs={{0,8},{1,9},{2,10},{3,11},{4,12},{5,13},{6,14},{7,15},{16,24},{17,... | collective-permute-start | bytes 196616 | tf_op jit(solution)/shard_map/ppermute | solution.py:272
  21.9 2.3 %collective-permute-start.4 = (bf16[256,128]{1,0:T(8,128)(2,1)S(1)}, bf16[256,128]{1,0:T(8,128)(2,1)S(1)}, u32[]{:S(2)}, u32[]{:S(2)}) collective-permute-start(bf16[256,128]{1,0:T(8,128)(2,1)S(1)} %fusion.22), channel_id=1, source_target_pairs={{0,12},{1,13},{2,14},{3,15},{16,28},{17,29},{18,30},{19,31}} | collective-permute-start | bytes 196616 | tf_op jit(solution)/shard_map/ppermute | solution.py:272
  24.3 1.8 %collective-permute-start.3 = (bf16[256,128]{1,0:T(8,128)(2,1)S(1)}, bf16[256,128]{1,0:T(8,128)(2,1)S(1)}, u32[]{:S(2)}, u32[]{:S(2)}) collective-permute-start(bf16[256,128]{1,0:T(8,128)(2,1)S(1)} %fusion.22), channel_id=1, source_target_pairs={{0,4},{1,5},{2,6},{3,7},{4,8},{5,9},{6,10},{7,11},{8,12},{9,13},{1... | collective-permute-start | bytes 196616 | tf_op jit(solution)/shard_map/ppermute | solution.py:272
  26.2 1.8 %collective-permute-done.3 = bf16[256,128]{1,0:T(8,128)(2,1)S(1)} collective-permute-done((bf16[256,128]{1,0:T(8,128)(2,1)S(1)}, bf16[256,128]{1,0:T(8,128)(2,1)S(1)}, u32[]{:S(2)}, u32[]{:S(2)}) %collective-permute-start.3) | collective-permute-done | bytes 65568 | tf_op jit(solution)/shard_map/ppermute | solution.py:272
  28.0 0.2 fusion.17
  28.3 1.6 %collective-permute-start.7 = (bf16[256,128]{1,0:T(8,128)(2,1)S(1)}, bf16[256,128]{1,0:T(8,128)(2,1)S(1)}, u32[]{:S(2)}, u32[]{:S(2)}) collective-permute-start(bf16[256,128]{1,0:T(8,128)(2,1)S(1)} %get-tuple-element.47), channel_id=1, source_target_pairs={{0,2},{1,3},{2,0},{3,1},{4,6},{5,7},{6,4},{7,5},{8,10},{9,11},{10,... | collective-permute-start | bytes 196616 | tf_op jit(solution)/shard_map/ppermute | solution.py:268
  29.8 0.3 collective-permute-start.8
  30.1 1.0 %broadcast_multiply_fusion.1.packed = f32[32,3328]{1,0:T(8,128)S(1)} fusion(f32[32,3328]{1,0:T(8,128)} %get-tuple-element.39, f32[]{:T(128)S(6)} %convert_element_type.57), kind=kLoop, calls=%fused_computation.24 | loop fusion | flops 106496 | bytes 851972 | tf_op jit(solution)/shard_map/mul | solution.py:444
  31.2 1.7 %broadcast_multiply_fusion.w_output = bf16[1024,1024]{1,0:T(8,128)(2,1)S(1)} fusion(bf16[1024,1024]{1,0:T(8,128)(2,1)} %refs_3_.1, bf16[]{:T(256)} %constant.4.clone.1), kind=kLoop, calls=%fused_computation.7 | loop fusion | flops 1048576 | bytes 4194306 | tf_op jit(solution)/shard_map/mul | solution.py:444
  33.0 0.9 %collective-permute-done.8.refs_3_.refs_7_ = bf16[256,128]{1,0:T(8,128)(2,1)S(1)} collective-permute-done((bf16[256,128]{1,0:T(8,128)(2,1)S(1)}, bf16[256,128]{1,0:T(8,128)(2,1)S(1)}, u32[]{:S(2)}, u32[]{:S(2)}) %collective-permute-start.8) | collective-permute-done | bytes 65568 | tf_op jit(solution)/shard_map/ppermute | solution.py:268
  33.9 1.5 %shard_map.124 = (bf16[32,1024]{1,0:T(8,128)(2,1)S(1)}, bf16[128,1024]{1,0:T(8,128)(2,1)}) custom-call(f32[32,3328]{1,0:T(8,128)S(1)} %broadcast_multiply_fusion.1.packed, bf16[1024,1024]{1,0:T(8,128)(2,1)S(1)} %broadcast_multiply_fusion.w_output, bf16[256,128]{1,0:T(8,128)(2,1)S(1)} %get-tuple-element.45.refs_0_.refs_4_, ...), custom_call_target="tpu_custom_call" | custom-call | flops 67108864 | bytes 2097152 | tf_op jit(solution)/shard_map/pallas_call | solution.py:325
  35.4 6.4 %all-to-all-start = ((bf16[16,8,1024]{2,1,0:T(8,128)(2,1)}), bf16[16,8,1024]{2,1,0:T(8,128)(2,1)S(1)}, u32[]{:S(2)}, u32[]{:S(2)}) async-start(bf16[16,8,1024]{2,1,0:T(8,128)(2,1)} %bitcast.3), calls=%async_computation | async-start | bytes 524288 | tf_op jit(solution)/shard_map/all_to_all | solution.py:435
  41.9 0.1 fusion.25
  42.1 9.6 %shard_map.125 = (bf16[768,1024]{1,0:T(8,128)(2,1)}, bf16[768,1024]{1,0:T(8,128)(2,1)}) custom-call(bf16[768,1024]{1,0:T(8,128)(2,1)} %refs_0_.1, bf16[1024,1024]{1,0:T(8,128)(2,1)} %w_query.1, bf16[4,768,256]{2,1,0:T(8,128)(2,1)} %get-tuple-element.51.keys_far.keys, bf16[4,768,256]{2,1,0:T(8,128)(2,1)} %get-tuple-element.52.values_far.values, ...), custom_call_target="tpu_custom_call" | custom-call | flops 2415919104 | bytes 6291456 | tf_op jit(solution)/shard_map/pallas_call | solution.py:249
  51.8 0.2 all-to-all-done
  51.9 1.3 %fusion.3 = bf16[16,8,256]{2,1,0:T(8,128)(2,1)} fusion(bf16[1024,256]{1,0:T(8,128)(2,1)S(1)} %copy-done.5, bf16[128,1024]{1,0:T(8,128)(2,1)S(1)} %bitcast.18, bf16[1024,1024]{1,0:T(8,128)(2,1)S(1)} %copy-done), kind=kOutput, calls=%fused_computation.4 | convolution fusion | flops 335839232 | bytes 2949120 | tf_op jit(solution)/shard_map/dot_general | solution.py:20
  53.2 5.9 %all-to-all-start.1 = ((bf16[16,8,256]{2,1,0:T(8,128)(2,1)}), bf16[16,8,256]{2,1,0:T(8,128)(2,1)S(1)}, u32[]{:S(2)}, u32[]{:S(2)}) async-start(bf16[16,8,256]{2,1,0:T(8,128)(2,1)} %fusion.3), calls=%async_computation.1 | async-start | bytes 131072 | tf_op jit(solution)/shard_map/all_to_all | solution.py:435
  59.1 5.8 %shard_map.126 = bf16[768,1024]{1,0:T(8,128)(2,1)} custom-call(bf16[768,1024]{1,0:T(8,128)(2,1)} %refs_0_.1, bf16[768,1024]{1,0:T(8,128)(2,1)} %get-tuple-element.56.refs_1_, bf16[768,1024]{1,0:T(8,128)(2,1)} %get-tuple-element.57.refs_2_, bf16[1024,1024]{1,0:T(8,128)(2,1)} %refs_3_.1, bf16[256,128]{1,0:T(8,128)(2,1)} %copy-done.1, ...), custom_call_target="tpu_custom_call" | custom-call | flops 1610612736 | bytes 7864320 | tf_op jit(solution)/shard_map/pallas_call | solution.py:388
  64.9 1.0 %all-to-all-done.1 = bf16[16,8,256]{2,1,0:T(8,128)(2,1)S(1)} async-done(((bf16[16,8,256]{2,1,0:T(8,128)(2,1)}), bf16[16,8,256]{2,1,0:T(8,128)(2,1)S(1)}, u32[]{:S(2)}, u32[]{:S(2)}) %all-to-all-start.1) | async-done | bytes 65568 | tf_op jit(solution)/shard_map/all_to_all | solution.py:435
  66.0 0.8 %fusion.4 = f32[32,256]{1,0:T(8,128)} fusion(bf16[2,32,128]{2,1,0:T(8,128)(2,1)S(1)} %copy-done.9, bf16[16,8,256]{2,1,0:T(8,128)(2,1)S(1)} %all-to-all-done.1, f32[2,32]{1,0:T(2,128)S(1)} %add_divide_fusion), kind=kOutput, calls=%fused_computation.6 | convolution fusion | flops 4218880 | bytes 114944 | tf_op jit(solution)/shard_map/dot_general | solution.py:20
  (32 shorter events, 0.4 us)
Async XLA Ops:
  0.6 51.3 %copy-start = (bf16[1024,1024]{1,0:T(8,128)(2,1)S(1)}, bf16[1024,1024]{1,0:T(8,128)(2,1)}, u32[]{:S(2)}) copy-start(bf16[1024,1024]{1,0:T(8,128)(2,1)} %param.16) | copy-start | bytes 6291460
  8.9 8.3 %collective-permute-start = (bf16[256,128]{1,0:T(8,128)(2,1)}, bf16[256,128]{1,0:T(8,128)(2,1)S(1)}, u32[]{:S(2)}, u32[]{:S(2)}) collective-permute-start(bf16[256,128]{1,0:T(8,128)(2,1)} %get-tuple-element.33), channel_id=1, source_target_pairs={{0,1},{1,0},{2,3},{3,2},{4,5},{5,4},{6,7},{7,6},{8,9},{9,8},{10,11... | collective-permute-start | bytes 196616 | tf_op jit(solution)/shard_map/ppermute | solution.py:268
  9.4 7.8 %collective-permute-start.1 = (bf16[256,128]{1,0:T(8,128)(2,1)}, bf16[256,128]{1,0:T(8,128)(2,1)S(1)}, u32[]{:S(2)}, u32[]{:S(2)}) collective-permute-start(bf16[256,128]{1,0:T(8,128)(2,1)} %get-tuple-element.34), channel_id=1, source_target_pairs={{0,2},{1,3},{2,0},{3,1},{4,6},{5,7},{6,4},{7,5},{8,10},{9,11},{10,... | collective-permute-start | bytes 196616 | tf_op jit(solution)/shard_map/ppermute | solution.py:268
  12.0 5.2 %collective-permute-start.2 = (bf16[256,128]{1,0:T(8,128)(2,1)}, bf16[256,128]{1,0:T(8,128)(2,1)S(1)}, u32[]{:S(2)}, u32[]{:S(2)}) collective-permute-start(bf16[256,128]{1,0:T(8,128)(2,1)} %get-tuple-element.35), channel_id=1, source_target_pairs={{0,3},{1,2},{2,1},{3,0},{4,7},{5,6},{6,5},{7,4},{8,11},{9,10},{10,... | collective-permute-start | bytes 196616 | tf_op jit(solution)/shard_map/ppermute | solution.py:268
  12.0 5.1 %copy-start.6 = (bf16[256,128]{1,0:T(8,128)(2,1)S(1)}, bf16[256,128]{1,0:T(8,128)(2,1)}, u32[]{:S(2)}) copy-start(bf16[256,128]{1,0:T(8,128)(2,1)} %get-tuple-element.40) | copy-start | bytes 196612
  17.2 8.9 %collective-permute-start.5 = (bf16[256,128]{1,0:T(8,128)(2,1)S(1)}, bf16[256,128]{1,0:T(8,128)(2,1)S(1)}, u32[]{:S(2)}, u32[]{:S(2)}) collective-permute-start(bf16[256,128]{1,0:T(8,128)(2,1)S(1)} %fusion.22), channel_id=1, source_target_pairs={{0,8},{1,9},{2,10},{3,11},{4,12},{5,13},{6,14},{7,15},{16,24},{17,... | collective-permute-start | bytes 196616 | tf_op jit(solution)/shard_map/ppermute | solution.py:272
  21.9 4.2 %collective-permute-start.4 = (bf16[256,128]{1,0:T(8,128)(2,1)S(1)}, bf16[256,128]{1,0:T(8,128)(2,1)S(1)}, u32[]{:S(2)}, u32[]{:S(2)}) collective-permute-start(bf16[256,128]{1,0:T(8,128)(2,1)S(1)} %fusion.22), channel_id=1, source_target_pairs={{0,12},{1,13},{2,14},{3,15},{16,28},{17,29},{18,30},{19,31}} | collective-permute-start | bytes 196616 | tf_op jit(solution)/shard_map/ppermute | solution.py:272
  24.3 3.7 %collective-permute-start.3 = (bf16[256,128]{1,0:T(8,128)(2,1)S(1)}, bf16[256,128]{1,0:T(8,128)(2,1)S(1)}, u32[]{:S(2)}, u32[]{:S(2)}) collective-permute-start(bf16[256,128]{1,0:T(8,128)(2,1)S(1)} %fusion.22), channel_id=1, source_target_pairs={{0,4},{1,5},{2,6},{3,7},{4,8},{5,9},{6,10},{7,11},{8,12},{9,13},{1... | collective-permute-start | bytes 196616 | tf_op jit(solution)/shard_map/ppermute | solution.py:272
  28.2 5.7 %copy-start.1 = (bf16[256,128]{1,0:T(8,128)(2,1)}, bf16[256,128]{1,0:T(8,128)(2,1)S(1)}, u32[]{:S(2)}) copy-start(bf16[256,128]{1,0:T(8,128)(2,1)S(1)} %get-tuple-element.45.refs_0_.refs_4_) | copy-start | bytes 196612
  28.2 4.7 %collective-permute-start.6 = (bf16[256,128]{1,0:T(8,128)(2,1)S(1)}, bf16[256,128]{1,0:T(8,128)(2,1)S(1)}, u32[]{:S(2)}, u32[]{:S(2)}) collective-permute-start(bf16[256,128]{1,0:T(8,128)(2,1)S(1)} %get-tuple-element.46), channel_id=1, source_target_pairs={{0,1},{1,0},{2,3},{3,2},{4,5},{5,4},{6,7},{7,6},{8,9},{9,8},{10,11... | collective-permute-start | bytes 196616 | tf_op jit(solution)/shard_map/ppermute | solution.py:268
  28.3 4.7 %collective-permute-start.7 = (bf16[256,128]{1,0:T(8,128)(2,1)S(1)}, bf16[256,128]{1,0:T(8,128)(2,1)S(1)}, u32[]{:S(2)}, u32[]{:S(2)}) collective-permute-start(bf16[256,128]{1,0:T(8,128)(2,1)S(1)} %get-tuple-element.47), channel_id=1, source_target_pairs={{0,2},{1,3},{2,0},{3,1},{4,6},{5,7},{6,4},{7,5},{8,10},{9,11},{10,... | collective-permute-start | bytes 196616 | tf_op jit(solution)/shard_map/ppermute | solution.py:268
  29.8 4.0 %collective-permute-start.8 = (bf16[256,128]{1,0:T(8,128)(2,1)S(1)}, bf16[256,128]{1,0:T(8,128)(2,1)S(1)}, u32[]{:S(2)}, u32[]{:S(2)}) collective-permute-start(bf16[256,128]{1,0:T(8,128)(2,1)S(1)} %get-tuple-element.48), channel_id=1, source_target_pairs={{0,3},{1,2},{2,1},{3,0},{4,7},{5,6},{6,5},{7,4},{8,11},{9,10},{10,... | collective-permute-start | bytes 196616 | tf_op jit(solution)/shard_map/ppermute | solution.py:268
  32.9 9.0 %copy-start.7 = (bf16[1024,32]{0,1:T(8,128)(2,1)S(1)}, bf16[1024,32]{0,1:T(8,128)(2,1)}, u32[]{:S(2)}) copy-start(bf16[1024,32]{0,1:T(8,128)(2,1)} %param.18) | copy-start | bytes 196612
  32.9 9.1 %copy-start.8 = (f32[2,32,32]{2,1,0:T(8,128)S(1)}, f32[2,32,32]{2,1,0:T(8,128)}, u32[]{:S(2)}) copy-start(f32[2,32,32]{2,1,0:T(8,128)} %get-tuple-element.59) | copy-start | bytes 24580
  32.9 18.8 %copy-start.2 = (bf16[256,128]{1,0:T(8,128)(2,1)}, bf16[256,128]{1,0:T(8,128)(2,1)S(1)}, u32[]{:S(2)}) copy-start(bf16[256,128]{1,0:T(8,128)(2,1)S(1)} %collective-permute-done.6.refs_1_.refs_5_) | copy-start | bytes 196612
  32.9 18.8 %copy-start.3 = (bf16[256,128]{1,0:T(8,128)(2,1)}, bf16[256,128]{1,0:T(8,128)(2,1)S(1)}, u32[]{:S(2)}) copy-start(bf16[256,128]{1,0:T(8,128)(2,1)S(1)} %collective-permute-done.7.refs_2_.refs_6_) | copy-start | bytes 196612
  33.9 17.9 %copy-start.4 = (bf16[256,128]{1,0:T(8,128)(2,1)}, bf16[256,128]{1,0:T(8,128)(2,1)S(1)}, u32[]{:S(2)}) copy-start(bf16[256,128]{1,0:T(8,128)(2,1)S(1)} %collective-permute-done.8.refs_3_.refs_7_) | copy-start | bytes 196612
  35.4 16.5 %all-to-all-start = ((bf16[16,8,1024]{2,1,0:T(8,128)(2,1)}), bf16[16,8,1024]{2,1,0:T(8,128)(2,1)S(1)}, u32[]{:S(2)}, u32[]{:S(2)}) async-start(bf16[16,8,1024]{2,1,0:T(8,128)(2,1)} %bitcast.3), calls=%async_computation | async-start | bytes 524288 | tf_op jit(solution)/shard_map/all_to_all | solution.py:435
  42.1 9.8 %copy-start.5 = (bf16[1024,256]{1,0:T(8,128)(2,1)S(1)}, bf16[1024,256]{1,0:T(8,128)(2,1)}, u32[]{:S(2)}) copy-start(bf16[1024,256]{1,0:T(8,128)(2,1)} %param.17) | copy-start | bytes 1572868
  53.2 12.8 %all-to-all-start.1 = ((bf16[16,8,256]{2,1,0:T(8,128)(2,1)}), bf16[16,8,256]{2,1,0:T(8,128)(2,1)S(1)}, u32[]{:S(2)}, u32[]{:S(2)}) async-start(bf16[16,8,256]{2,1,0:T(8,128)(2,1)} %fusion.3), calls=%async_computation.1 | async-start | bytes 131072 | tf_op jit(solution)/shard_map/all_to_all | solution.py:435
  59.1 6.9 %copy-start.9 = (bf16[2,32,128]{2,1,0:T(8,128)(2,1)S(1)}, bf16[2,32,128]{2,1,0:T(8,128)(2,1)}, u32[]{:S(2)}) copy-start(bf16[2,32,128]{2,1,0:T(8,128)(2,1)} %get-tuple-element.60) | copy-start | bytes 49156

commit v12 on v11

--- a/solution.py
+++ b/solution.py
@@ -59,13 +59,13 @@
     return jax.ShapeDtypeStruct(shape, kind)
 
 
-def key_value_kernel(head_dim, tile, events, w_key, w_value, keys, values, inner, *refs):
+def key_value_kernel(head_dim, tile, events, w_key, w_value, keys_values, inner, *refs):
     states, kept = refs[:PLANE], refs[PLANE]
     pair = w_key.shape[1]
     both = dot(events[...], jnp.concatenate([w_key[...], w_value[...]], axis=1)).astype(BF16)
     k, v = both[:, :pair], both[:, pair:]
-    keys[...] = k
-    values[...] = v
+    keys_values[0] = k
+    keys_values[1] = v
     total = None
     for i in range(events.shape[0] // tile):
         here = slice(i * tile, (i + 1) * tile)
@@ -95,10 +95,10 @@
         functools.partial(key_value_kernel, head_dim, tile),
         (PLANE,),
         [whole((rows, width)), columns(width, pair), columns(width, pair)],
-        [pl.BlockSpec((None, rows, pair), lambda i: (i, 0, 0))] * 2
+        [pl.BlockSpec((2, None, rows, pair), lambda i: (0, i, 0, 0))]
         + [pl.BlockSpec((inner, pair, head_dim), lambda i: (0, i, 0))]
         + [whole((pair, head_dim))] * PLANE,
-        [shaped((PLANE, rows, pair), BF16)] * 2
+        [shaped((2, PLANE, rows, pair), BF16)]
         + [shaped((inner, width, head_dim), BF16)]
         + [shaped((pair, head_dim), BF16)] * PLANE,
         4 * rows * width * width,
@@ -111,10 +111,11 @@
     return 256 if rows % 256 == 0 and rows > 256 else rows // 2
 
 
-def labelled_kernel(head_dim, copies, events_far, w_query_far, keys_far, values_far, labels, experts, tasks, *refs):
+def labelled_kernel(head_dim, copies, events_far, w_query_far, keys_values_far, labels, experts, tasks, *refs):
     (packed, match, column), (events, w_query, keys, values, done) = refs[:3], refs[3:]
     fetches = []
-    for far, here in ((events_far, events), (w_query_far, w_query), (keys_far, keys), (values_far, values)):
+    fars = (events_far, w_query_far, keys_values_far.at[0], keys_values_far.at[1])
+    for far, here in zip(fars, (events, w_query, keys, values)):
         fetches.append(pltpu.make_async_copy(far, here, done.at[len(fetches)]))
         fetches[-1].start()
     rows, width = events.shape
@@ -155,21 +156,22 @@
         packed[:, 2 * width + part.start : 2 * width + part.stop] = terms
 
 
-def labelled_rows(events, w_query, keys, values, labels, experts, tasks, devices):
+def labelled_rows(events, w_query, keys_values, labels, experts, tasks, devices):
     rows, width = events.shape
     many = labels.shape[1]
     slots = devices * CAP
     return call(
         functools.partial(labelled_kernel, width // HEADS, devices // EXPERTS),
         (),
-        [FAR] * 4 + [VMEM] * 3,
+        [FAR] * 3 + [VMEM] * 3,
         [VMEM] * 3,
         [shaped((many, 3 * width + width // HEADS + slots), F32)]
         + [shaped((2, many, slots), BF16), shaped((2, many, 2 * EXPERTS), F32)],
         4 * many * rows * width,
         8 * rows * width,
-        [pltpu.VMEM(x.shape, BF16) for x in (events, w_query, keys, values)] + [pltpu.SemaphoreType.DMA((4,))],
-    )(events, w_query, keys, values, labels, experts, tasks)
+        [pltpu.VMEM(x.shape, BF16) for x in (events, w_query)]
+        + [pltpu.VMEM(keys_values.shape[1:], BF16)] * 2 + [pltpu.SemaphoreType.DMA((4,))],
+    )(events, w_query, keys_values, labels, experts, tasks)
 
 
 def slot_of(experts):
@@ -241,7 +243,7 @@
     return jnp.concatenate([first, second], axis=0)
 
 
-def queries_within(events, w_query, keys, values, inner):
+def queries_within(events, w_query, keys_values, inner):
     rows, width = events.shape
     head_dim = width // HEADS
     pair = width // PLANE
@@ -252,15 +254,15 @@
         [
             whole((rows, width)),
             columns(width, pair),
-            pl.BlockSpec((None, rows, pair), lambda i: (i, 0, 0)),
-            pl.BlockSpec((None, rows, pair), lambda i: (i, 0, 0)),
+            pl.BlockSpec((None, None, rows, pair), lambda i: (0, i, 0, 0)),
+            pl.BlockSpec((None, None, rows, pair), lambda i: (1, i, 0, 0)),
             pl.BlockSpec((inner.shape[0], pair, head_dim), lambda i: (0, i, 0)),
         ],
         [columns(rows, pair), columns(rows, pair)],
         [shaped((rows, width), BF16)] * 2,
         2 * rows * width * width + 4 * tile * rows * width,
         8 * rows * width,
-    )(events, w_query, keys, values, inner)
+    )(events, w_query, keys_values, keys_values, inner)
 
 
 def flip(x, j):
@@ -434,17 +436,17 @@
     def exchange(x):
         return lax.all_to_all(x, "seq", split_axis=0, concat_axis=0, tiled=True)
 
-    keys, values, inner, *states = key_value_state(events, w_key, w_value)
+    keys_values, inner, *states = key_value_state(events, w_key, w_value)
     states = swapped(states)
-    packed, match, column = labelled_rows(events, w_query, keys, values, labels, experts, tasks, devices)
+    packed, match, column = labelled_rows(events, w_query, keys_values, labels, experts, tasks, devices)
     states, packed = lax.optimization_barrier((states, packed))
     before = sums_before(states)
     before, one = lax.optimization_barrier((before, jnp.ones((), BF16)))
     prefix = swapped(before)
     picked, outgoing = picked_rows(packed * one.astype(F32), w_output * one, prefix)
-    outgoing, keys, values = lax.optimization_barrier((outgoing, keys, values))
+    outgoing, keys_values = lax.optimization_barrier((outgoing, keys_values))
     arrived = exchange(outgoing)
-    query, within = queries_within(events, w_query, keys, values, inner)
+    query, within = queries_within(events, w_query, keys_values, inner)
     arrived, query, within = lax.optimization_barrier((arrived, query, within))
     back = exchange(expert_rows(arrived, expert_in, expert_out))
     hidden = hidden_rows(events, query, within, prefix, w_output)

time: 67.2 us -> 67.2 us (level)
  no operation moved by 1% of the time
where the time goes in v12:
time: 67.2 us; the launch traced here: 66.7 us
  Pallas kernels  30.2 us (45%)
  starting transfers between devices  26.3 us (39%)
  waiting for transfers between devices  4 us (6%)
  other arithmetic  3.09 us (5%)
  matrix products  2.16 us (3%)
  between operations  0.9 us (1%)
    all_to_all x2, starting transfers between devices, exchange(): return lax.all_to_all(x, 'seq', split_axis=0, concat_axis=0, tiled=True)  12.3 us
    pallas_call x1, Pallas kernels, queries_within(): call(functools.partial(within_kernel, head_dim, tile), (width // pair,),...  9.58 us
    ppermute x3, starting transfers between devices, later(): lax.ppermute(x, 'seq', [(i, i + s) for i in range(lax.axis_size('seq') -...  8.85 us
    pallas_call x1, Pallas kernels, key_value_state(): call(functools.partial(key_value_kernel, head_dim, tile), (PLANE,), [whol...  8.21 us
    pallas_call x1, Pallas kernels, hidden_rows(): call(functools.partial(hidden_kernel, head_dim, tile), (), [FAR] * (4 + P...  5.84 us
    ppermute x6, starting transfers between devices, flip(): return lax.ppermute(x, 'seq', [(i, i ^ j) for i in range(devices)])  5.11 us
    pallas_call x1, Pallas kernels, labelled_rows(): call(functools.partial(labelled_kernel, width // HEADS, devices // EXPERT...  5.04 us
    dot_general x3, matrix products, dot(): lax.dot_general(a, b, (contract, ((), ())), preferred_element_type=F32, *...  2.16 us
  transfers between devices with their start and end apart: 11, of which 4 were waited for; matrix products, arithmetic and copies ran while one was open for 5% of the time, Pallas kernels for 31%

profile of v12, /device:TPU:0, one launch (start us, length us, event | category | flops | bytes accessed | tf_op | source)
XLA Modules:
  0.0 66.7 jit_solution(4063096491715808611)
XLA Ops:
  0.6 8.2 %shard_map.122 = (bf16[2,4,768,256]{3,2,1,0:T(8,128)(2,1)}, bf16[2,1024,128]{2,1,0:T(8,128)(2,1)}, bf16[256,128]{1,0:T(8,128)(2,1)}, bf16[256,128]{1,0:T(8,128)(...) custom-call(bf16[768,1024]{1,0:T(8,128)(2,1)} %refs_0_.1, bf16[1024,1024]{1,0:T(8,128)(2,1)} %w_key.1, ...), custom_call_target="tpu_custom_call" | custom-call | flops 3221225472 | bytes 6291456 | tf_op jit(solution)/shard_map/pallas_call | solution.py:94
  8.9 0.5 collective-permute-start
  9.4 2.6 %collective-permute-start.1 = (bf16[256,128]{1,0:T(8,128)(2,1)}, bf16[256,128]{1,0:T(8,128)(2,1)S(1)}, u32[]{:S(2)}, u32[]{:S(2)}) collective-permute-start(bf16[256,128]{1,0:T(8,128)(2,1)} %get-tuple-element.32), channel_id=1, source_target_pairs={{0,2},{1,3},{2,0},{3,1},{4,6},{5,7},{6,4},{7,5},{8,10},{9,11},{10,... | collective-permute-start | bytes 196616 | tf_op jit(solution)/shard_map/ppermute | solution.py:270
  12.0 5.0 %shard_map.123 = (f32[32,3328]{1,0:T(8,128)}, bf16[2,32,128]{2,1,0:T(8,128)(2,1)}, f32[2,32,32]{2,1,0:T(8,128)}) custom-call(bf16[768,1024]{1,0:T(8,128)(2,1)} %refs_0_.1, bf16[1024,1024]{1,0:T(8,128)(2,1)} %w_query.1, bf16[2,4,768,256]{3,2,1,0:T(8,128)(2,1)} %get-tuple-element.48.keys_values_far.keys.values, s32[1,32]{1,0:T(1,128)} %bitcast.20, ...), custom_call_target="tpu_custom_call" | custom-call | flops 100663296 | bytes 6291456 | tf_op jit(solution)/shard_map/pallas_call | solution.py:163
  17.2 4.7 %collective-permute-start.5 = (bf16[256,128]{1,0:T(8,128)(2,1)S(1)}, bf16[256,128]{1,0:T(8,128)(2,1)S(1)}, u32[]{:S(2)}, u32[]{:S(2)}) collective-permute-start(bf16[256,128]{1,0:T(8,128)(2,1)S(1)} %fusion.22), channel_id=1, source_target_pairs={{0,8},{1,9},{2,10},{3,11},{4,12},{5,13},{6,14},{7,15},{16,24},{17,... | collective-permute-start | bytes 196616 | tf_op jit(solution)/shard_map/ppermute | solution.py:274
  21.9 2.3 %collective-permute-start.4 = (bf16[256,128]{1,0:T(8,128)(2,1)S(1)}, bf16[256,128]{1,0:T(8,128)(2,1)S(1)}, u32[]{:S(2)}, u32[]{:S(2)}) collective-permute-start(bf16[256,128]{1,0:T(8,128)(2,1)S(1)} %fusion.22), channel_id=1, source_target_pairs={{0,12},{1,13},{2,14},{3,15},{16,28},{17,29},{18,30},{19,31}} | collective-permute-start | bytes 196616 | tf_op jit(solution)/shard_map/ppermute | solution.py:274
  24.2 1.8 %collective-permute-start.3 = (bf16[256,128]{1,0:T(8,128)(2,1)S(1)}, bf16[256,128]{1,0:T(8,128)(2,1)S(1)}, u32[]{:S(2)}, u32[]{:S(2)}) collective-permute-start(bf16[256,128]{1,0:T(8,128)(2,1)S(1)} %fusion.22), channel_id=1, source_target_pairs={{0,4},{1,5},{2,6},{3,7},{4,8},{5,9},{6,10},{7,11},{8,12},{9,13},{1... | collective-permute-start | bytes 196616 | tf_op jit(solution)/shard_map/ppermute | solution.py:274
  26.1 1.8 %collective-permute-done.3 = bf16[256,128]{1,0:T(8,128)(2,1)S(1)} collective-permute-done((bf16[256,128]{1,0:T(8,128)(2,1)S(1)}, bf16[256,128]{1,0:T(8,128)(2,1)S(1)}, u32[]{:S(2)}, u32[]{:S(2)}) %collective-permute-start.3) | collective-permute-done | bytes 65568 | tf_op jit(solution)/shard_map/ppermute | solution.py:274
  27.9 0.2 fusion.17
  28.2 1.6 %collective-permute-start.7 = (bf16[256,128]{1,0:T(8,128)(2,1)S(1)}, bf16[256,128]{1,0:T(8,128)(2,1)S(1)}, u32[]{:S(2)}, u32[]{:S(2)}) collective-permute-start(bf16[256,128]{1,0:T(8,128)(2,1)S(1)} %get-tuple-element.44), channel_id=1, source_target_pairs={{0,2},{1,3},{2,0},{3,1},{4,6},{5,7},{6,4},{7,5},{8,10},{9,11},{10,... | collective-permute-start | bytes 196616 | tf_op jit(solution)/shard_map/ppermute | solution.py:270
  29.8 0.3 collective-permute-start.8
  30.1 1.0 %broadcast_multiply_fusion.1.packed = f32[32,3328]{1,0:T(8,128)S(1)} fusion(f32[32,3328]{1,0:T(8,128)} %get-tuple-element.36, f32[]{:T(128)S(6)} %convert_element_type.57), kind=kLoop, calls=%fused_computation.24 | loop fusion | flops 106496 | bytes 851972 | tf_op jit(solution)/shard_map/mul | solution.py:446
  31.1 1.7 %broadcast_multiply_fusion.w_output = bf16[1024,1024]{1,0:T(8,128)(2,1)S(1)} fusion(bf16[1024,1024]{1,0:T(8,128)(2,1)} %refs_3_.1, bf16[]{:T(256)} %constant.4.clone.1), kind=kLoop, calls=%fused_computation.7 | loop fusion | flops 1048576 | bytes 4194306 | tf_op jit(solution)/shard_map/mul | solution.py:446
  32.9 0.9 %collective-permute-done.8.refs_3_.refs_7_ = bf16[256,128]{1,0:T(8,128)(2,1)S(1)} collective-permute-done((bf16[256,128]{1,0:T(8,128)(2,1)S(1)}, bf16[256,128]{1,0:T(8,128)(2,1)S(1)}, u32[]{:S(2)}, u32[]{:S(2)}) %collective-permute-start.8) | collective-permute-done | bytes 65568 | tf_op jit(solution)/shard_map/ppermute | solution.py:270
  33.8 1.5 %shard_map.124 = (bf16[32,1024]{1,0:T(8,128)(2,1)S(1)}, bf16[128,1024]{1,0:T(8,128)(2,1)}) custom-call(f32[32,3328]{1,0:T(8,128)S(1)} %broadcast_multiply_fusion.1.packed, bf16[1024,1024]{1,0:T(8,128)(2,1)S(1)} %broadcast_multiply_fusion.w_output, bf16[256,128]{1,0:T(8,128)(2,1)S(1)} %get-tuple-element.42.refs_0_.refs_4_, ...), custom_call_target="tpu_custom_call" | custom-call | flops 67108864 | bytes 2097152 | tf_op jit(solution)/shard_map/pallas_call | solution.py:327
  35.4 6.4 %all-to-all-start = ((bf16[16,8,1024]{2,1,0:T(8,128)(2,1)}), bf16[16,8,1024]{2,1,0:T(8,128)(2,1)S(1)}, u32[]{:S(2)}, u32[]{:S(2)}) async-start(bf16[16,8,1024]{2,1,0:T(8,128)(2,1)} %bitcast.3), calls=%async_computation | async-start | bytes 524288 | tf_op jit(solution)/shard_map/all_to_all | solution.py:437
  41.8 0.1 fusion.25
  42.1 9.6 %shard_map.125 = (bf16[768,1024]{1,0:T(8,128)(2,1)}, bf16[768,1024]{1,0:T(8,128)(2,1)}) custom-call(bf16[768,1024]{1,0:T(8,128)(2,1)} %refs_0_.1, bf16[1024,1024]{1,0:T(8,128)(2,1)} %w_query.1, bf16[2,4,768,256]{3,2,1,0:T(8,128)(2,1)} %get-tuple-element.48.keys_values_far.keys.values, bf16[2,4,768,256]{3,2,1,0:T(8,128)(2,1)} %get-tuple-element.48.keys_values_far.keys.values, ...), custom_call_target="tpu_custom_call" | custom-call | flops 2415919104 | bytes 6291456 | tf_op jit(solution)/shard_map/pallas_call | solution.py:251
  51.7 0.2 all-to-all-done
  51.9 1.3 %fusion.3 = bf16[16,8,256]{2,1,0:T(8,128)(2,1)} fusion(bf16[1024,256]{1,0:T(8,128)(2,1)S(1)} %copy-done.5, bf16[128,1024]{1,0:T(8,128)(2,1)S(1)} %bitcast.18, bf16[1024,1024]{1,0:T(8,128)(2,1)S(1)} %copy-done), kind=kOutput, calls=%fused_computation.4 | convolution fusion | flops 335839232 | bytes 2949120 | tf_op jit(solution)/shard_map/dot_general | solution.py:20
  53.1 5.9 %all-to-all-start.1 = ((bf16[16,8,256]{2,1,0:T(8,128)(2,1)}), bf16[16,8,256]{2,1,0:T(8,128)(2,1)S(1)}, u32[]{:S(2)}, u32[]{:S(2)}) async-start(bf16[16,8,256]{2,1,0:T(8,128)(2,1)} %fusion.3), calls=%async_computation.1 | async-start | bytes 131072 | tf_op jit(solution)/shard_map/all_to_all | solution.py:437
  59.0 5.8 %shard_map.126 = bf16[768,1024]{1,0:T(8,128)(2,1)} custom-call(bf16[768,1024]{1,0:T(8,128)(2,1)} %refs_0_.1, bf16[768,1024]{1,0:T(8,128)(2,1)} %get-tuple-element.52.refs_1_, bf16[768,1024]{1,0:T(8,128)(2,1)} %get-tuple-element.53.refs_2_, bf16[1024,1024]{1,0:T(8,128)(2,1)} %refs_3_.1, bf16[256,128]{1,0:T(8,128)(2,1)} %copy-done.1, ...), custom_call_target="tpu_custom_call" | custom-call | flops 1610612736 | bytes 7864320 | tf_op jit(solution)/shard_map/pallas_call | solution.py:390
  64.9 1.0 %all-to-all-done.1 = bf16[16,8,256]{2,1,0:T(8,128)(2,1)S(1)} async-done(((bf16[16,8,256]{2,1,0:T(8,128)(2,1)}), bf16[16,8,256]{2,1,0:T(8,128)(2,1)S(1)}, u32[]{:S(2)}, u32[]{:S(2)}) %all-to-all-start.1) | async-done | bytes 65568 | tf_op jit(solution)/shard_map/all_to_all | solution.py:437
  65.9 0.8 %fusion.4 = f32[32,256]{1,0:T(8,128)} fusion(bf16[2,32,128]{2,1,0:T(8,128)(2,1)S(1)} %copy-done.9, bf16[16,8,256]{2,1,0:T(8,128)(2,1)S(1)} %all-to-all-done.1, f32[2,32]{1,0:T(2,128)S(1)} %add_divide_fusion), kind=kOutput, calls=%fused_computation.6 | convolution fusion | flops 4218880 | bytes 114944 | tf_op jit(solution)/shard_map/dot_general | solution.py:20
  (32 shorter events, 0.4 us)
Async XLA Ops:
  0.6 51.2 %copy-start = (bf16[1024,1024]{1,0:T(8,128)(2,1)S(1)}, bf16[1024,1024]{1,0:T(8,128)(2,1)}, u32[]{:S(2)}) copy-start(bf16[1024,1024]{1,0:T(8,128)(2,1)} %param.16) | copy-start | bytes 6291460
  8.9 8.2 %collective-permute-start = (bf16[256,128]{1,0:T(8,128)(2,1)}, bf16[256,128]{1,0:T(8,128)(2,1)S(1)}, u32[]{:S(2)}, u32[]{:S(2)}) collective-permute-start(bf16[256,128]{1,0:T(8,128)(2,1)} %get-tuple-element.31), channel_id=1, source_target_pairs={{0,1},{1,0},{2,3},{3,2},{4,5},{5,4},{6,7},{7,6},{8,9},{9,8},{10,11... | collective-permute-start | bytes 196616 | tf_op jit(solution)/shard_map/ppermute | solution.py:270
  9.4 7.7 %collective-permute-start.1 = (bf16[256,128]{1,0:T(8,128)(2,1)}, bf16[256,128]{1,0:T(8,128)(2,1)S(1)}, u32[]{:S(2)}, u32[]{:S(2)}) collective-permute-start(bf16[256,128]{1,0:T(8,128)(2,1)} %get-tuple-element.32), channel_id=1, source_target_pairs={{0,2},{1,3},{2,0},{3,1},{4,6},{5,7},{6,4},{7,5},{8,10},{9,11},{10,... | collective-permute-start | bytes 196616 | tf_op jit(solution)/shard_map/ppermute | solution.py:270
  12.0 5.1 %collective-permute-start.2 = (bf16[256,128]{1,0:T(8,128)(2,1)}, bf16[256,128]{1,0:T(8,128)(2,1)S(1)}, u32[]{:S(2)}, u32[]{:S(2)}) collective-permute-start(bf16[256,128]{1,0:T(8,128)(2,1)} %get-tuple-element.33), channel_id=1, source_target_pairs={{0,3},{1,2},{2,1},{3,0},{4,7},{5,6},{6,5},{7,4},{8,11},{9,10},{10,... | collective-permute-start | bytes 196616 | tf_op jit(solution)/shard_map/ppermute | solution.py:270
  12.0 5.1 %copy-start.6 = (bf16[256,128]{1,0:T(8,128)(2,1)S(1)}, bf16[256,128]{1,0:T(8,128)(2,1)}, u32[]{:S(2)}) copy-start(bf16[256,128]{1,0:T(8,128)(2,1)} %get-tuple-element.37) | copy-start | bytes 196612
  17.2 8.9 %collective-permute-start.5 = (bf16[256,128]{1,0:T(8,128)(2,1)S(1)}, bf16[256,128]{1,0:T(8,128)(2,1)S(1)}, u32[]{:S(2)}, u32[]{:S(2)}) collective-permute-start(bf16[256,128]{1,0:T(8,128)(2,1)S(1)} %fusion.22), channel_id=1, source_target_pairs={{0,8},{1,9},{2,10},{3,11},{4,12},{5,13},{6,14},{7,15},{16,24},{17,... | collective-permute-start | bytes 196616 | tf_op jit(solution)/shard_map/ppermute | solution.py:274
  21.9 4.2 %collective-permute-start.4 = (bf16[256,128]{1,0:T(8,128)(2,1)S(1)}, bf16[256,128]{1,0:T(8,128)(2,1)S(1)}, u32[]{:S(2)}, u32[]{:S(2)}) collective-permute-start(bf16[256,128]{1,0:T(8,128)(2,1)S(1)} %fusion.22), channel_id=1, source_target_pairs={{0,12},{1,13},{2,14},{3,15},{16,28},{17,29},{18,30},{19,31}} | collective-permute-start | bytes 196616 | tf_op jit(solution)/shard_map/ppermute | solution.py:274
  24.2 3.7 %collective-permute-start.3 = (bf16[256,128]{1,0:T(8,128)(2,1)S(1)}, bf16[256,128]{1,0:T(8,128)(2,1)S(1)}, u32[]{:S(2)}, u32[]{:S(2)}) collective-permute-start(bf16[256,128]{1,0:T(8,128)(2,1)S(1)} %fusion.22), channel_id=1, source_target_pairs={{0,4},{1,5},{2,6},{3,7},{4,8},{5,9},{6,10},{7,11},{8,12},{9,13},{1... | collective-permute-start | bytes 196616 | tf_op jit(solution)/shard_map/ppermute | solution.py:274
  28.1 5.7 %copy-start.1 = (bf16[256,128]{1,0:T(8,128)(2,1)}, bf16[256,128]{1,0:T(8,128)(2,1)S(1)}, u32[]{:S(2)}) copy-start(bf16[256,128]{1,0:T(8,128)(2,1)S(1)} %get-tuple-element.42.refs_0_.refs_4_) | copy-start | bytes 196612
  28.1 4.7 %collective-permute-start.6 = (bf16[256,128]{1,0:T(8,128)(2,1)S(1)}, bf16[256,128]{1,0:T(8,128)(2,1)S(1)}, u32[]{:S(2)}, u32[]{:S(2)}) collective-permute-start(bf16[256,128]{1,0:T(8,128)(2,1)S(1)} %get-tuple-element.43), channel_id=1, source_target_pairs={{0,1},{1,0},{2,3},{3,2},{4,5},{5,4},{6,7},{7,6},{8,9},{9,8},{10,11... | collective-permute-start | bytes 196616 | tf_op jit(solution)/shard_map/ppermute | solution.py:270
  28.2 4.7 %collective-permute-start.7 = (bf16[256,128]{1,0:T(8,128)(2,1)S(1)}, bf16[256,128]{1,0:T(8,128)(2,1)S(1)}, u32[]{:S(2)}, u32[]{:S(2)}) collective-permute-start(bf16[256,128]{1,0:T(8,128)(2,1)S(1)} %get-tuple-element.44), channel_id=1, source_target_pairs={{0,2},{1,3},{2,0},{3,1},{4,6},{5,7},{6,4},{7,5},{8,10},{9,11},{10,... | collective-permute-start | bytes 196616 | tf_op jit(solution)/shard_map/ppermute | solution.py:270
  29.8 4.0 %collective-permute-start.8 = (bf16[256,128]{1,0:T(8,128)(2,1)S(1)}, bf16[256,128]{1,0:T(8,128)(2,1)S(1)}, u32[]{:S(2)}, u32[]{:S(2)}) collective-permute-start(bf16[256,128]{1,0:T(8,128)(2,1)S(1)} %get-tuple-element.45), channel_id=1, source_target_pairs={{0,3},{1,2},{2,1},{3,0},{4,7},{5,6},{6,5},{7,4},{8,11},{9,10},{10,... | collective-permute-start | bytes 196616 | tf_op jit(solution)/shard_map/ppermute | solution.py:270
  32.8 9.0 %copy-start.7 = (bf16[1024,32]{0,1:T(8,128)(2,1)S(1)}, bf16[1024,32]{0,1:T(8,128)(2,1)}, u32[]{:S(2)}) copy-start(bf16[1024,32]{0,1:T(8,128)(2,1)} %param.18) | copy-start | bytes 196612
  32.8 9.1 %copy-start.8 = (f32[2,32,32]{2,1,0:T(8,128)S(1)}, f32[2,32,32]{2,1,0:T(8,128)}, u32[]{:S(2)}) copy-start(f32[2,32,32]{2,1,0:T(8,128)} %get-tuple-element.55) | copy-start | bytes 24580
  32.9 18.8 %copy-start.2 = (bf16[256,128]{1,0:T(8,128)(2,1)}, bf16[256,128]{1,0:T(8,128)(2,1)S(1)}, u32[]{:S(2)}) copy-start(bf16[256,128]{1,0:T(8,128)(2,1)S(1)} %collective-permute-done.6.refs_1_.refs_5_) | copy-start | bytes 196612
  32.9 18.8 %copy-start.3 = (bf16[256,128]{1,0:T(8,128)(2,1)}, bf16[256,128]{1,0:T(8,128)(2,1)S(1)}, u32[]{:S(2)}) copy-start(bf16[256,128]{1,0:T(8,128)(2,1)S(1)} %collective-permute-done.7.refs_2_.refs_6_) | copy-start | bytes 196612
  33.8 17.9 %copy-start.4 = (bf16[256,128]{1,0:T(8,128)(2,1)}, bf16[256,128]{1,0:T(8,128)(2,1)S(1)}, u32[]{:S(2)}) copy-start(bf16[256,128]{1,0:T(8,128)(2,1)S(1)} %collective-permute-done.8.refs_3_.refs_7_) | copy-start | bytes 196612
  35.4 16.5 %all-to-all-start = ((bf16[16,8,1024]{2,1,0:T(8,128)(2,1)}), bf16[16,8,1024]{2,1,0:T(8,128)(2,1)S(1)}, u32[]{:S(2)}, u32[]{:S(2)}) async-start(bf16[16,8,1024]{2,1,0:T(8,128)(2,1)} %bitcast.3), calls=%async_computation | async-start | bytes 524288 | tf_op jit(solution)/shard_map/all_to_all | solution.py:437
  42.1 9.8 %copy-start.5 = (bf16[1024,256]{1,0:T(8,128)(2,1)S(1)}, bf16[1024,256]{1,0:T(8,128)(2,1)}, u32[]{:S(2)}) copy-start(bf16[1024,256]{1,0:T(8,128)(2,1)} %param.17) | copy-start | bytes 1572868
  53.1 12.8 %all-to-all-start.1 = ((bf16[16,8,256]{2,1,0:T(8,128)(2,1)}), bf16[16,8,256]{2,1,0:T(8,128)(2,1)S(1)}, u32[]{:S(2)}, u32[]{:S(2)}) async-start(bf16[16,8,256]{2,1,0:T(8,128)(2,1)} %fusion.3), calls=%async_computation.1 | async-start | bytes 131072 | tf_op jit(solution)/shard_map/all_to_all | solution.py:437
  59.0 6.9 %copy-start.9 = (bf16[2,32,128]{2,1,0:T(8,128)(2,1)S(1)}, bf16[2,32,128]{2,1,0:T(8,128)(2,1)}, u32[]{:S(2)}) copy-start(bf16[2,32,128]{2,1,0:T(8,128)(2,1)} %get-tuple-element.56) | copy-start | bytes 49156

commit v13 on v12

--- a/solution.py
+++ b/solution.py
@@ -61,23 +61,27 @@
 
 def key_value_kernel(head_dim, tile, events, w_key, w_value, keys_values, inner, *refs):
     states, kept = refs[:PLANE], refs[PLANE]
-    pair = w_key.shape[1]
+    wide = w_key.shape[1]
+    pair = keys_values.shape[3]
+    step = wide // pair
     both = dot(events[...], jnp.concatenate([w_key[...], w_value[...]], axis=1)).astype(BF16)
-    k, v = both[:, :pair], both[:, pair:]
-    keys_values[0] = k
-    keys_values[1] = v
-    total = None
-    for i in range(events.shape[0] // tile):
-        here = slice(i * tile, (i + 1) * tile)
-        if i:
-            inner[i - 1] = total.astype(BF16)
-        product = dot(k[here], v[here], ((0,), (0,)))
-        parts = [slice(h, h + head_dim) for h in range(0, pair, head_dim)]
-        own = jnp.concatenate([product[part, part] for part in parts], axis=0)
-        total = own if total is None else total + own
-    kept[pl.program_id(0)] = total.astype(BF16)
-
-    @pl.when(pl.program_id(0) == PLANE - 1)
+    for p in range(step):
+        cols = slice(p * pair, (p + 1) * pair)
+        k, v = both[:, cols], both[:, wide + cols.start : wide + cols.stop]
+        keys_values[0, p] = k
+        keys_values[1, p] = v
+        total = None
+        for i in range(events.shape[0] // tile):
+            here = slice(i * tile, (i + 1) * tile)
+            if i:
+                inner[i - 1, cols, :] = total.astype(BF16)
+            product = dot(k[here], v[here], ((0,), (0,)))
+            parts = [slice(h, h + head_dim) for h in range(0, pair, head_dim)]
+            own = jnp.concatenate([product[part, part] for part in parts], axis=0)
+            total = own if total is None else total + own
+        kept[pl.program_id(0) * step + p] = total.astype(BF16)
+
+    @pl.when(pl.program_id(0) == pl.num_programs(0) - 1)
     def _():
         rank = lax.axis_index("seq") & (PLANE - 1)
         for i, state in enumerate(states):
@@ -88,15 +92,16 @@
     rows, width = events.shape
     head_dim = width // HEADS
     pair = width // PLANE
+    step = 2
     tile = row_tile(rows)
     inner = rows // tile - 1
 
     return call(
         functools.partial(key_value_kernel, head_dim, tile),
-        (PLANE,),
-        [whole((rows, width)), columns(width, pair), columns(width, pair)],
-        [pl.BlockSpec((2, None, rows, pair), lambda i: (0, i, 0, 0))]
-        + [pl.BlockSpec((inner, pair, head_dim), lambda i: (0, i, 0))]
+        (PLANE // step,),
+        [whole((rows, width)), columns(width, step * pair), columns(width, step * pair)],
+        [pl.BlockSpec((2, step, rows, pair), lambda i: (0, i, 0, 0))]
+        + [pl.BlockSpec((inner, step * pair, head_dim), lambda i: (0, i, 0))]
         + [whole((pair, head_dim))] * PLANE,
         [shaped((2, PLANE, rows, pair), BF16)]
         + [shaped((inner, width, head_dim), BF16)]

time: 67.2 us -> 66.9 us (level)
  no operation moved by 1% of the time
where the time goes in v13:
time: 66.9 us; the launch traced here: 66.4 us
  Pallas kernels  30 us (45%)
  starting transfers between devices  26.3 us (39%)
  waiting for transfers between devices  4 us (6%)
  other arithmetic  3.09 us (5%)
  matrix products  2.16 us (3%)
  between operations  0.9 us (1%)
    all_to_all x2, starting transfers between devices, exchange(): return lax.all_to_all(x, 'seq', split_axis=0, concat_axis=0, tiled=True)  12.3 us
    pallas_call x1, Pallas kernels, queries_within(): call(functools.partial(within_kernel, head_dim, tile), (width // pair,),...  9.58 us
    ppermute x3, starting transfers between devices, later(): lax.ppermute(x, 'seq', [(i, i + s) for i in range(lax.axis_size('seq') -...  8.85 us
    pallas_call x1, Pallas kernels, key_value_state(): call(functools.partial(key_value_kernel, head_dim, tile), (PLANE // step,...  7.97 us
    pallas_call x1, Pallas kernels, hidden_rows(): call(functools.partial(hidden_kernel, head_dim, tile), (), [FAR] * (4 + P...  5.84 us
    ppermute x6, starting transfers between devices, flip(): return lax.ppermute(x, 'seq', [(i, i ^ j) for i in range(devices)])  5.11 us
    pallas_call x1, Pallas kernels, labelled_rows(): call(functools.partial(labelled_kernel, width // HEADS, devices // EXPERT...  5.04 us
    dot_general x3, matrix products, dot(): lax.dot_general(a, b, (contract, ((), ())), preferred_element_type=F32, *...  2.16 us
  transfers between devices with their start and end apart: 11, of which 4 were waited for; matrix products, arithmetic and copies ran while one was open for 5% of the time, Pallas kernels for 31%

profile of v13, /device:TPU:0, one launch (start us, length us, event | category | flops | bytes accessed | tf_op | source)
XLA Modules:
  0.0 66.4 jit_solution(16123859997371997566)
XLA Ops:
  0.6 8.0 %shard_map.122 = (bf16[2,4,768,256]{3,2,1,0:T(8,128)(2,1)}, bf16[2,1024,128]{2,1,0:T(8,128)(2,1)}, bf16[256,128]{1,0:T(8,128)(2,1)}, bf16[256,128]{1,0:T(8,128)(...) custom-call(bf16[768,1024]{1,0:T(8,128)(2,1)} %refs_0_.1, bf16[1024,1024]{1,0:T(8,128)(2,1)} %w_key.1, ...), custom_call_target="tpu_custom_call" | custom-call | flops 3221225472 | bytes 6291456 | tf_op jit(solution)/shard_map/pallas_call | solution.py:99
  8.6 0.5 collective-permute-start
  9.1 2.6 %collective-permute-start.1 = (bf16[256,128]{1,0:T(8,128)(2,1)}, bf16[256,128]{1,0:T(8,128)(2,1)S(1)}, u32[]{:S(2)}, u32[]{:S(2)}) collective-permute-start(bf16[256,128]{1,0:T(8,128)(2,1)} %get-tuple-element.32), channel_id=1, source_target_pairs={{0,2},{1,3},{2,0},{3,1},{4,6},{5,7},{6,4},{7,5},{8,10},{9,11},{10,... | collective-permute-start | bytes 196616 | tf_op jit(solution)/shard_map/ppermute | solution.py:275
  11.8 5.0 %shard_map.123 = (f32[32,3328]{1,0:T(8,128)}, bf16[2,32,128]{2,1,0:T(8,128)(2,1)}, f32[2,32,32]{2,1,0:T(8,128)}) custom-call(bf16[768,1024]{1,0:T(8,128)(2,1)} %refs_0_.1, bf16[1024,1024]{1,0:T(8,128)(2,1)} %w_query.1, bf16[2,4,768,256]{3,2,1,0:T(8,128)(2,1)} %get-tuple-element.48.keys_values_far.keys.values, s32[1,32]{1,0:T(1,128)} %bitcast.20, ...), custom_call_target="tpu_custom_call" | custom-call | flops 100663296 | bytes 6291456 | tf_op jit(solution)/shard_map/pallas_call | solution.py:168
  16.9 4.7 %collective-permute-start.5 = (bf16[256,128]{1,0:T(8,128)(2,1)S(1)}, bf16[256,128]{1,0:T(8,128)(2,1)S(1)}, u32[]{:S(2)}, u32[]{:S(2)}) collective-permute-start(bf16[256,128]{1,0:T(8,128)(2,1)S(1)} %fusion.22), channel_id=1, source_target_pairs={{0,8},{1,9},{2,10},{3,11},{4,12},{5,13},{6,14},{7,15},{16,24},{17,... | collective-permute-start | bytes 196616 | tf_op jit(solution)/shard_map/ppermute | solution.py:279
  21.7 2.3 %collective-permute-start.4 = (bf16[256,128]{1,0:T(8,128)(2,1)S(1)}, bf16[256,128]{1,0:T(8,128)(2,1)S(1)}, u32[]{:S(2)}, u32[]{:S(2)}) collective-permute-start(bf16[256,128]{1,0:T(8,128)(2,1)S(1)} %fusion.22), channel_id=1, source_target_pairs={{0,12},{1,13},{2,14},{3,15},{16,28},{17,29},{18,30},{19,31}} | collective-permute-start | bytes 196616 | tf_op jit(solution)/shard_map/ppermute | solution.py:279
  24.0 1.8 %collective-permute-start.3 = (bf16[256,128]{1,0:T(8,128)(2,1)S(1)}, bf16[256,128]{1,0:T(8,128)(2,1)S(1)}, u32[]{:S(2)}, u32[]{:S(2)}) collective-permute-start(bf16[256,128]{1,0:T(8,128)(2,1)S(1)} %fusion.22), channel_id=1, source_target_pairs={{0,4},{1,5},{2,6},{3,7},{4,8},{5,9},{6,10},{7,11},{8,12},{9,13},{1... | collective-permute-start | bytes 196616 | tf_op jit(solution)/shard_map/ppermute | solution.py:279
  25.9 1.8 %collective-permute-done.3 = bf16[256,128]{1,0:T(8,128)(2,1)S(1)} collective-permute-done((bf16[256,128]{1,0:T(8,128)(2,1)S(1)}, bf16[256,128]{1,0:T(8,128)(2,1)S(1)}, u32[]{:S(2)}, u32[]{:S(2)}) %collective-permute-start.3) | collective-permute-done | bytes 65568 | tf_op jit(solution)/shard_map/ppermute | solution.py:279
  27.7 0.2 fusion.17
  28.0 1.6 %collective-permute-start.7 = (bf16[256,128]{1,0:T(8,128)(2,1)S(1)}, bf16[256,128]{1,0:T(8,128)(2,1)S(1)}, u32[]{:S(2)}, u32[]{:S(2)}) collective-permute-start(bf16[256,128]{1,0:T(8,128)(2,1)S(1)} %get-tuple-element.44), channel_id=1, source_target_pairs={{0,2},{1,3},{2,0},{3,1},{4,6},{5,7},{6,4},{7,5},{8,10},{9,11},{10,... | collective-permute-start | bytes 196616 | tf_op jit(solution)/shard_map/ppermute | solution.py:275
  29.5 0.3 collective-permute-start.8
  29.8 1.0 %broadcast_multiply_fusion.1.packed = f32[32,3328]{1,0:T(8,128)S(1)} fusion(f32[32,3328]{1,0:T(8,128)} %get-tuple-element.36, f32[]{:T(128)S(6)} %convert_element_type.57), kind=kLoop, calls=%fused_computation.24 | loop fusion | flops 106496 | bytes 851972 | tf_op jit(solution)/shard_map/mul | solution.py:451
  30.9 1.7 %broadcast_multiply_fusion.w_output = bf16[1024,1024]{1,0:T(8,128)(2,1)S(1)} fusion(bf16[1024,1024]{1,0:T(8,128)(2,1)} %refs_3_.1, bf16[]{:T(256)} %constant.4.clone.1), kind=kLoop, calls=%fused_computation.7 | loop fusion | flops 1048576 | bytes 4194306 | tf_op jit(solution)/shard_map/mul | solution.py:451
  32.7 0.9 %collective-permute-done.8.refs_3_.refs_7_ = bf16[256,128]{1,0:T(8,128)(2,1)S(1)} collective-permute-done((bf16[256,128]{1,0:T(8,128)(2,1)S(1)}, bf16[256,128]{1,0:T(8,128)(2,1)S(1)}, u32[]{:S(2)}, u32[]{:S(2)}) %collective-permute-start.8) | collective-permute-done | bytes 65568 | tf_op jit(solution)/shard_map/ppermute | solution.py:275
  33.6 1.5 %shard_map.124 = (bf16[32,1024]{1,0:T(8,128)(2,1)S(1)}, bf16[128,1024]{1,0:T(8,128)(2,1)}) custom-call(f32[32,3328]{1,0:T(8,128)S(1)} %broadcast_multiply_fusion.1.packed, bf16[1024,1024]{1,0:T(8,128)(2,1)S(1)} %broadcast_multiply_fusion.w_output, bf16[256,128]{1,0:T(8,128)(2,1)S(1)} %get-tuple-element.42.refs_0_.refs_4_, ...), custom_call_target="tpu_custom_call" | custom-call | flops 67108864 | bytes 2097152 | tf_op jit(solution)/shard_map/pallas_call | solution.py:332
  35.1 6.4 %all-to-all-start = ((bf16[16,8,1024]{2,1,0:T(8,128)(2,1)}), bf16[16,8,1024]{2,1,0:T(8,128)(2,1)S(1)}, u32[]{:S(2)}, u32[]{:S(2)}) async-start(bf16[16,8,1024]{2,1,0:T(8,128)(2,1)} %bitcast.3), calls=%async_computation | async-start | bytes 524288 | tf_op jit(solution)/shard_map/all_to_all | solution.py:442
  41.6 0.1 fusion.25
  41.8 9.6 %shard_map.125 = (bf16[768,1024]{1,0:T(8,128)(2,1)}, bf16[768,1024]{1,0:T(8,128)(2,1)}) custom-call(bf16[768,1024]{1,0:T(8,128)(2,1)} %refs_0_.1, bf16[1024,1024]{1,0:T(8,128)(2,1)} %w_query.1, bf16[2,4,768,256]{3,2,1,0:T(8,128)(2,1)} %get-tuple-element.48.keys_values_far.keys.values, bf16[2,4,768,256]{3,2,1,0:T(8,128)(2,1)} %get-tuple-element.48.keys_values_far.keys.values, ...), custom_call_target="tpu_custom_call" | custom-call | flops 2415919104 | bytes 6291456 | tf_op jit(solution)/shard_map/pallas_call | solution.py:256
  51.4 0.2 all-to-all-done
  51.6 1.3 %fusion.3 = bf16[16,8,256]{2,1,0:T(8,128)(2,1)} fusion(bf16[1024,256]{1,0:T(8,128)(2,1)S(1)} %copy-done.5, bf16[128,1024]{1,0:T(8,128)(2,1)S(1)} %bitcast.18, bf16[1024,1024]{1,0:T(8,128)(2,1)S(1)} %copy-done), kind=kOutput, calls=%fused_computation.4 | convolution fusion | flops 335839232 | bytes 2949120 | tf_op jit(solution)/shard_map/dot_general | solution.py:20
  52.9 5.9 %all-to-all-start.1 = ((bf16[16,8,256]{2,1,0:T(8,128)(2,1)}), bf16[16,8,256]{2,1,0:T(8,128)(2,1)S(1)}, u32[]{:S(2)}, u32[]{:S(2)}) async-start(bf16[16,8,256]{2,1,0:T(8,128)(2,1)} %fusion.3), calls=%async_computation.1 | async-start | bytes 131072 | tf_op jit(solution)/shard_map/all_to_all | solution.py:442
  58.8 5.8 %shard_map.126 = bf16[768,1024]{1,0:T(8,128)(2,1)} custom-call(bf16[768,1024]{1,0:T(8,128)(2,1)} %refs_0_.1, bf16[768,1024]{1,0:T(8,128)(2,1)} %get-tuple-element.52.refs_1_, bf16[768,1024]{1,0:T(8,128)(2,1)} %get-tuple-element.53.refs_2_, bf16[1024,1024]{1,0:T(8,128)(2,1)} %refs_3_.1, bf16[256,128]{1,0:T(8,128)(2,1)} %copy-done.1, ...), custom_call_target="tpu_custom_call" | custom-call | flops 1610612736 | bytes 7864320 | tf_op jit(solution)/shard_map/pallas_call | solution.py:395
  64.6 1.0 %all-to-all-done.1 = bf16[16,8,256]{2,1,0:T(8,128)(2,1)S(1)} async-done(((bf16[16,8,256]{2,1,0:T(8,128)(2,1)}), bf16[16,8,256]{2,1,0:T(8,128)(2,1)S(1)}, u32[]{:S(2)}, u32[]{:S(2)}) %all-to-all-start.1) | async-done | bytes 65568 | tf_op jit(solution)/shard_map/all_to_all | solution.py:442
  65.7 0.8 %fusion.4 = f32[32,256]{1,0:T(8,128)} fusion(bf16[2,32,128]{2,1,0:T(8,128)(2,1)S(1)} %copy-done.9, bf16[16,8,256]{2,1,0:T(8,128)(2,1)S(1)} %all-to-all-done.1, f32[2,32]{1,0:T(2,128)S(1)} %add_divide_fusion), kind=kOutput, calls=%fused_computation.6 | convolution fusion | flops 4218880 | bytes 114944 | tf_op jit(solution)/shard_map/dot_general | solution.py:20
  (32 shorter events, 0.4 us)
Async XLA Ops:
  0.6 51.0 %copy-start = (bf16[1024,1024]{1,0:T(8,128)(2,1)S(1)}, bf16[1024,1024]{1,0:T(8,128)(2,1)}, u32[]{:S(2)}) copy-start(bf16[1024,1024]{1,0:T(8,128)(2,1)} %param.16) | copy-start | bytes 6291460
  8.6 8.2 %collective-permute-start = (bf16[256,128]{1,0:T(8,128)(2,1)}, bf16[256,128]{1,0:T(8,128)(2,1)S(1)}, u32[]{:S(2)}, u32[]{:S(2)}) collective-permute-start(bf16[256,128]{1,0:T(8,128)(2,1)} %get-tuple-element.31), channel_id=1, source_target_pairs={{0,1},{1,0},{2,3},{3,2},{4,5},{5,4},{6,7},{7,6},{8,9},{9,8},{10,11... | collective-permute-start | bytes 196616 | tf_op jit(solution)/shard_map/ppermute | solution.py:275
  9.1 7.7 %collective-permute-start.1 = (bf16[256,128]{1,0:T(8,128)(2,1)}, bf16[256,128]{1,0:T(8,128)(2,1)S(1)}, u32[]{:S(2)}, u32[]{:S(2)}) collective-permute-start(bf16[256,128]{1,0:T(8,128)(2,1)} %get-tuple-element.32), channel_id=1, source_target_pairs={{0,2},{1,3},{2,0},{3,1},{4,6},{5,7},{6,4},{7,5},{8,10},{9,11},{10,... | collective-permute-start | bytes 196616 | tf_op jit(solution)/shard_map/ppermute | solution.py:275
  11.7 5.1 %collective-permute-start.2 = (bf16[256,128]{1,0:T(8,128)(2,1)}, bf16[256,128]{1,0:T(8,128)(2,1)S(1)}, u32[]{:S(2)}, u32[]{:S(2)}) collective-permute-start(bf16[256,128]{1,0:T(8,128)(2,1)} %get-tuple-element.33), channel_id=1, source_target_pairs={{0,3},{1,2},{2,1},{3,0},{4,7},{5,6},{6,5},{7,4},{8,11},{9,10},{10,... | collective-permute-start | bytes 196616 | tf_op jit(solution)/shard_map/ppermute | solution.py:275
  11.8 5.1 %copy-start.6 = (bf16[256,128]{1,0:T(8,128)(2,1)S(1)}, bf16[256,128]{1,0:T(8,128)(2,1)}, u32[]{:S(2)}) copy-start(bf16[256,128]{1,0:T(8,128)(2,1)} %get-tuple-element.37) | copy-start | bytes 196612
  16.9 8.9 %collective-permute-start.5 = (bf16[256,128]{1,0:T(8,128)(2,1)S(1)}, bf16[256,128]{1,0:T(8,128)(2,1)S(1)}, u32[]{:S(2)}, u32[]{:S(2)}) collective-permute-start(bf16[256,128]{1,0:T(8,128)(2,1)S(1)} %fusion.22), channel_id=1, source_target_pairs={{0,8},{1,9},{2,10},{3,11},{4,12},{5,13},{6,14},{7,15},{16,24},{17,... | collective-permute-start | bytes 196616 | tf_op jit(solution)/shard_map/ppermute | solution.py:279
  21.7 4.2 %collective-permute-start.4 = (bf16[256,128]{1,0:T(8,128)(2,1)S(1)}, bf16[256,128]{1,0:T(8,128)(2,1)S(1)}, u32[]{:S(2)}, u32[]{:S(2)}) collective-permute-start(bf16[256,128]{1,0:T(8,128)(2,1)S(1)} %fusion.22), channel_id=1, source_target_pairs={{0,12},{1,13},{2,14},{3,15},{16,28},{17,29},{18,30},{19,31}} | collective-permute-start | bytes 196616 | tf_op jit(solution)/shard_map/ppermute | solution.py:279
  24.0 3.7 %collective-permute-start.3 = (bf16[256,128]{1,0:T(8,128)(2,1)S(1)}, bf16[256,128]{1,0:T(8,128)(2,1)S(1)}, u32[]{:S(2)}, u32[]{:S(2)}) collective-permute-start(bf16[256,128]{1,0:T(8,128)(2,1)S(1)} %fusion.22), channel_id=1, source_target_pairs={{0,4},{1,5},{2,6},{3,7},{4,8},{5,9},{6,10},{7,11},{8,12},{9,13},{1... | collective-permute-start | bytes 196616 | tf_op jit(solution)/shard_map/ppermute | solution.py:279
  27.9 5.7 %copy-start.1 = (bf16[256,128]{1,0:T(8,128)(2,1)}, bf16[256,128]{1,0:T(8,128)(2,1)S(1)}, u32[]{:S(2)}) copy-start(bf16[256,128]{1,0:T(8,128)(2,1)S(1)} %get-tuple-element.42.refs_0_.refs_4_) | copy-start | bytes 196612
  27.9 4.7 %collective-permute-start.6 = (bf16[256,128]{1,0:T(8,128)(2,1)S(1)}, bf16[256,128]{1,0:T(8,128)(2,1)S(1)}, u32[]{:S(2)}, u32[]{:S(2)}) collective-permute-start(bf16[256,128]{1,0:T(8,128)(2,1)S(1)} %get-tuple-element.43), channel_id=1, source_target_pairs={{0,1},{1,0},{2,3},{3,2},{4,5},{5,4},{6,7},{7,6},{8,9},{9,8},{10,11... | collective-permute-start | bytes 196616 | tf_op jit(solution)/shard_map/ppermute | solution.py:275
  28.0 4.7 %collective-permute-start.7 = (bf16[256,128]{1,0:T(8,128)(2,1)S(1)}, bf16[256,128]{1,0:T(8,128)(2,1)S(1)}, u32[]{:S(2)}, u32[]{:S(2)}) collective-permute-start(bf16[256,128]{1,0:T(8,128)(2,1)S(1)} %get-tuple-element.44), channel_id=1, source_target_pairs={{0,2},{1,3},{2,0},{3,1},{4,6},{5,7},{6,4},{7,5},{8,10},{9,11},{10,... | collective-permute-start | bytes 196616 | tf_op jit(solution)/shard_map/ppermute | solution.py:275
  29.5 4.0 %collective-permute-start.8 = (bf16[256,128]{1,0:T(8,128)(2,1)S(1)}, bf16[256,128]{1,0:T(8,128)(2,1)S(1)}, u32[]{:S(2)}, u32[]{:S(2)}) collective-permute-start(bf16[256,128]{1,0:T(8,128)(2,1)S(1)} %get-tuple-element.45), channel_id=1, source_target_pairs={{0,3},{1,2},{2,1},{3,0},{4,7},{5,6},{6,5},{7,4},{8,11},{9,10},{10,... | collective-permute-start | bytes 196616 | tf_op jit(solution)/shard_map/ppermute | solution.py:275
  32.6 9.0 %copy-start.7 = (bf16[1024,32]{0,1:T(8,128)(2,1)S(1)}, bf16[1024,32]{0,1:T(8,128)(2,1)}, u32[]{:S(2)}) copy-start(bf16[1024,32]{0,1:T(8,128)(2,1)} %param.18) | copy-start | bytes 196612
  32.6 9.1 %copy-start.8 = (f32[2,32,32]{2,1,0:T(8,128)S(1)}, f32[2,32,32]{2,1,0:T(8,128)}, u32[]{:S(2)}) copy-start(f32[2,32,32]{2,1,0:T(8,128)} %get-tuple-element.55) | copy-start | bytes 24580
  32.6 18.8 %copy-start.2 = (bf16[256,128]{1,0:T(8,128)(2,1)}, bf16[256,128]{1,0:T(8,128)(2,1)S(1)}, u32[]{:S(2)}) copy-start(bf16[256,128]{1,0:T(8,128)(2,1)S(1)} %collective-permute-done.6.refs_1_.refs_5_) | copy-start | bytes 196612
  32.7 18.8 %copy-start.3 = (bf16[256,128]{1,0:T(8,128)(2,1)}, bf16[256,128]{1,0:T(8,128)(2,1)S(1)}, u32[]{:S(2)}) copy-start(bf16[256,128]{1,0:T(8,128)(2,1)S(1)} %collective-permute-done.7.refs_2_.refs_6_) | copy-start | bytes 196612
  33.6 17.8 %copy-start.4 = (bf16[256,128]{1,0:T(8,128)(2,1)}, bf16[256,128]{1,0:T(8,128)(2,1)S(1)}, u32[]{:S(2)}) copy-start(bf16[256,128]{1,0:T(8,128)(2,1)S(1)} %collective-permute-done.8.refs_3_.refs_7_) | copy-start | bytes 196612
  35.1 16.5 %all-to-all-start = ((bf16[16,8,1024]{2,1,0:T(8,128)(2,1)}), bf16[16,8,1024]{2,1,0:T(8,128)(2,1)S(1)}, u32[]{:S(2)}, u32[]{:S(2)}) async-start(bf16[16,8,1024]{2,1,0:T(8,128)(2,1)} %bitcast.3), calls=%async_computation | async-start | bytes 524288 | tf_op jit(solution)/shard_map/all_to_all | solution.py:442
  41.8 9.8 %copy-start.5 = (bf16[1024,256]{1,0:T(8,128)(2,1)S(1)}, bf16[1024,256]{1,0:T(8,128)(2,1)}, u32[]{:S(2)}) copy-start(bf16[1024,256]{1,0:T(8,128)(2,1)} %param.17) | copy-start | bytes 1572868
  52.9 12.8 %all-to-all-start.1 = ((bf16[16,8,256]{2,1,0:T(8,128)(2,1)}), bf16[16,8,256]{2,1,0:T(8,128)(2,1)S(1)}, u32[]{:S(2)}, u32[]{:S(2)}) async-start(bf16[16,8,256]{2,1,0:T(8,128)(2,1)} %fusion.3), calls=%async_computation.1 | async-start | bytes 131072 | tf_op jit(solution)/shard_map/all_to_all | solution.py:442
  58.8 6.9 %copy-start.9 = (bf16[2,32,128]{2,1,0:T(8,128)(2,1)S(1)}, bf16[2,32,128]{2,1,0:T(8,128)(2,1)}, u32[]{:S(2)}) copy-start(bf16[2,32,128]{2,1,0:T(8,128)(2,1)} %get-tuple-element.56) | copy-start | bytes 49156

commit v14 on v13

--- a/solution.py
+++ b/solution.py
@@ -64,10 +64,11 @@
     wide = w_key.shape[1]
     pair = keys_values.shape[3]
     step = wide // pair
-    both = dot(events[...], jnp.concatenate([w_key[...], w_value[...]], axis=1)).astype(BF16)
+    wide_k = dot(events[...], w_key[...]).astype(BF16)
+    wide_v = dot(events[...], w_value[...]).astype(BF16)
     for p in range(step):
         cols = slice(p * pair, (p + 1) * pair)
-        k, v = both[:, cols], both[:, wide + cols.start : wide + cols.stop]
+        k, v = wide_k[:, cols], wide_v[:, cols]
         keys_values[0, p] = k
         keys_values[1, p] = v
         total = None

time: 66.9 us -> 66.9 us (level)
  no operation moved by 1% of the time
where the time goes in v14:
time: 66.9 us; the launch traced here: 66.4 us
  Pallas kernels  30 us (45%)
  starting transfers between devices  26.3 us (39%)
  waiting for transfers between devices  4 us (6%)
  other arithmetic  3.09 us (5%)
  matrix products  2.16 us (3%)
  between operations  0.9 us (1%)
    all_to_all x2, starting transfers between devices, exchange(): return lax.all_to_all(x, 'seq', split_axis=0, concat_axis=0, tiled=True)  12.3 us
    pallas_call x1, Pallas kernels, queries_within(): call(functools.partial(within_kernel, head_dim, tile), (width // pair,),...  9.58 us
    ppermute x3, starting transfers between devices, later(): lax.ppermute(x, 'seq', [(i, i + s) for i in range(lax.axis_size('seq') -...  8.85 us
    pallas_call x1, Pallas kernels, key_value_state(): call(functools.partial(key_value_kernel, head_dim, tile), (PLANE // step,...  7.97 us
    pallas_call x1, Pallas kernels, hidden_rows(): call(functools.partial(hidden_kernel, head_dim, tile), (), [FAR] * (4 + P...  5.84 us
    ppermute x6, starting transfers between devices, flip(): return lax.ppermute(x, 'seq', [(i, i ^ j) for i in range(devices)])  5.11 us
    pallas_call x1, Pallas kernels, labelled_rows(): call(functools.partial(labelled_kernel, width // HEADS, devices // EXPERT...  5.04 us
    dot_general x3, matrix products, dot(): lax.dot_general(a, b, (contract, ((), ())), preferred_element_type=F32, *...  2.16 us
  transfers between devices with their start and end apart: 11, of which 4 were waited for; matrix products, arithmetic and copies ran while one was open for 5% of the time, Pallas kernels for 31%

profile of v14, /device:TPU:0, one launch (start us, length us, event | category | flops | bytes accessed | tf_op | source)
XLA Modules:
  0.0 66.4 jit_solution(16123859997371997566)
XLA Ops:
  0.6 8.0 %shard_map.122 = (bf16[2,4,768,256]{3,2,1,0:T(8,128)(2,1)}, bf16[2,1024,128]{2,1,0:T(8,128)(2,1)}, bf16[256,128]{1,0:T(8,128)(2,1)}, bf16[256,128]{1,0:T(8,128)(...) custom-call(bf16[768,1024]{1,0:T(8,128)(2,1)} %refs_0_.1, bf16[1024,1024]{1,0:T(8,128)(2,1)} %w_key.1, ...), custom_call_target="tpu_custom_call" | custom-call | flops 3221225472 | bytes 6291456 | tf_op jit(solution)/shard_map/pallas_call | solution.py:100
  8.6 0.5 collective-permute-start
  9.1 2.6 %collective-permute-start.1 = (bf16[256,128]{1,0:T(8,128)(2,1)}, bf16[256,128]{1,0:T(8,128)(2,1)S(1)}, u32[]{:S(2)}, u32[]{:S(2)}) collective-permute-start(bf16[256,128]{1,0:T(8,128)(2,1)} %get-tuple-element.32), channel_id=1, source_target_pairs={{0,2},{1,3},{2,0},{3,1},{4,6},{5,7},{6,4},{7,5},{8,10},{9,11},{10,... | collective-permute-start | bytes 196616 | tf_op jit(solution)/shard_map/ppermute | solution.py:276
  11.8 5.0 %shard_map.123 = (f32[32,3328]{1,0:T(8,128)}, bf16[2,32,128]{2,1,0:T(8,128)(2,1)}, f32[2,32,32]{2,1,0:T(8,128)}) custom-call(bf16[768,1024]{1,0:T(8,128)(2,1)} %refs_0_.1, bf16[1024,1024]{1,0:T(8,128)(2,1)} %w_query.1, bf16[2,4,768,256]{3,2,1,0:T(8,128)(2,1)} %get-tuple-element.48.keys_values_far.keys.values, s32[1,32]{1,0:T(1,128)} %bitcast.20, ...), custom_call_target="tpu_custom_call" | custom-call | flops 100663296 | bytes 6291456 | tf_op jit(solution)/shard_map/pallas_call | solution.py:169
  16.9 4.7 %collective-permute-start.5 = (bf16[256,128]{1,0:T(8,128)(2,1)S(1)}, bf16[256,128]{1,0:T(8,128)(2,1)S(1)}, u32[]{:S(2)}, u32[]{:S(2)}) collective-permute-start(bf16[256,128]{1,0:T(8,128)(2,1)S(1)} %fusion.22), channel_id=1, source_target_pairs={{0,8},{1,9},{2,10},{3,11},{4,12},{5,13},{6,14},{7,15},{16,24},{17,... | collective-permute-start | bytes 196616 | tf_op jit(solution)/shard_map/ppermute | solution.py:280
  21.7 2.3 %collective-permute-start.4 = (bf16[256,128]{1,0:T(8,128)(2,1)S(1)}, bf16[256,128]{1,0:T(8,128)(2,1)S(1)}, u32[]{:S(2)}, u32[]{:S(2)}) collective-permute-start(bf16[256,128]{1,0:T(8,128)(2,1)S(1)} %fusion.22), channel_id=1, source_target_pairs={{0,12},{1,13},{2,14},{3,15},{16,28},{17,29},{18,30},{19,31}} | collective-permute-start | bytes 196616 | tf_op jit(solution)/shard_map/ppermute | solution.py:280
  24.0 1.8 %collective-permute-start.3 = (bf16[256,128]{1,0:T(8,128)(2,1)S(1)}, bf16[256,128]{1,0:T(8,128)(2,1)S(1)}, u32[]{:S(2)}, u32[]{:S(2)}) collective-permute-start(bf16[256,128]{1,0:T(8,128)(2,1)S(1)} %fusion.22), channel_id=1, source_target_pairs={{0,4},{1,5},{2,6},{3,7},{4,8},{5,9},{6,10},{7,11},{8,12},{9,13},{1... | collective-permute-start | bytes 196616 | tf_op jit(solution)/shard_map/ppermute | solution.py:280
  25.9 1.8 %collective-permute-done.3 = bf16[256,128]{1,0:T(8,128)(2,1)S(1)} collective-permute-done((bf16[256,128]{1,0:T(8,128)(2,1)S(1)}, bf16[256,128]{1,0:T(8,128)(2,1)S(1)}, u32[]{:S(2)}, u32[]{:S(2)}) %collective-permute-start.3) | collective-permute-done | bytes 65568 | tf_op jit(solution)/shard_map/ppermute | solution.py:280
  27.7 0.2 fusion.17
  28.0 1.6 %collective-permute-start.7 = (bf16[256,128]{1,0:T(8,128)(2,1)S(1)}, bf16[256,128]{1,0:T(8,128)(2,1)S(1)}, u32[]{:S(2)}, u32[]{:S(2)}) collective-permute-start(bf16[256,128]{1,0:T(8,128)(2,1)S(1)} %get-tuple-element.44), channel_id=1, source_target_pairs={{0,2},{1,3},{2,0},{3,1},{4,6},{5,7},{6,4},{7,5},{8,10},{9,11},{10,... | collective-permute-start | bytes 196616 | tf_op jit(solution)/shard_map/ppermute | solution.py:276
  29.5 0.3 collective-permute-start.8
  29.8 1.0 %broadcast_multiply_fusion.1.packed = f32[32,3328]{1,0:T(8,128)S(1)} fusion(f32[32,3328]{1,0:T(8,128)} %get-tuple-element.36, f32[]{:T(128)S(6)} %convert_element_type.57), kind=kLoop, calls=%fused_computation.24 | loop fusion | flops 106496 | bytes 851972 | tf_op jit(solution)/shard_map/mul | solution.py:452
  30.9 1.7 %broadcast_multiply_fusion.w_output = bf16[1024,1024]{1,0:T(8,128)(2,1)S(1)} fusion(bf16[1024,1024]{1,0:T(8,128)(2,1)} %refs_3_.1, bf16[]{:T(256)} %constant.4.clone.1), kind=kLoop, calls=%fused_computation.7 | loop fusion | flops 1048576 | bytes 4194306 | tf_op jit(solution)/shard_map/mul | solution.py:452
  32.7 0.9 %collective-permute-done.8.refs_3_.refs_7_ = bf16[256,128]{1,0:T(8,128)(2,1)S(1)} collective-permute-done((bf16[256,128]{1,0:T(8,128)(2,1)S(1)}, bf16[256,128]{1,0:T(8,128)(2,1)S(1)}, u32[]{:S(2)}, u32[]{:S(2)}) %collective-permute-start.8) | collective-permute-done | bytes 65568 | tf_op jit(solution)/shard_map/ppermute | solution.py:276
  33.6 1.5 %shard_map.124 = (bf16[32,1024]{1,0:T(8,128)(2,1)S(1)}, bf16[128,1024]{1,0:T(8,128)(2,1)}) custom-call(f32[32,3328]{1,0:T(8,128)S(1)} %broadcast_multiply_fusion.1.packed, bf16[1024,1024]{1,0:T(8,128)(2,1)S(1)} %broadcast_multiply_fusion.w_output, bf16[256,128]{1,0:T(8,128)(2,1)S(1)} %get-tuple-element.42.refs_0_.refs_4_, ...), custom_call_target="tpu_custom_call" | custom-call | flops 67108864 | bytes 2097152 | tf_op jit(solution)/shard_map/pallas_call | solution.py:333
  35.1 6.4 %all-to-all-start = ((bf16[16,8,1024]{2,1,0:T(8,128)(2,1)}), bf16[16,8,1024]{2,1,0:T(8,128)(2,1)S(1)}, u32[]{:S(2)}, u32[]{:S(2)}) async-start(bf16[16,8,1024]{2,1,0:T(8,128)(2,1)} %bitcast.3), calls=%async_computation | async-start | bytes 524288 | tf_op jit(solution)/shard_map/all_to_all | solution.py:443
  41.6 0.1 fusion.25
  41.8 9.6 %shard_map.125 = (bf16[768,1024]{1,0:T(8,128)(2,1)}, bf16[768,1024]{1,0:T(8,128)(2,1)}) custom-call(bf16[768,1024]{1,0:T(8,128)(2,1)} %refs_0_.1, bf16[1024,1024]{1,0:T(8,128)(2,1)} %w_query.1, bf16[2,4,768,256]{3,2,1,0:T(8,128)(2,1)} %get-tuple-element.48.keys_values_far.keys.values, bf16[2,4,768,256]{3,2,1,0:T(8,128)(2,1)} %get-tuple-element.48.keys_values_far.keys.values, ...), custom_call_target="tpu_custom_call" | custom-call | flops 2415919104 | bytes 6291456 | tf_op jit(solution)/shard_map/pallas_call | solution.py:257
  51.4 0.2 all-to-all-done
  51.6 1.3 %fusion.3 = bf16[16,8,256]{2,1,0:T(8,128)(2,1)} fusion(bf16[1024,256]{1,0:T(8,128)(2,1)S(1)} %copy-done.5, bf16[128,1024]{1,0:T(8,128)(2,1)S(1)} %bitcast.18, bf16[1024,1024]{1,0:T(8,128)(2,1)S(1)} %copy-done), kind=kOutput, calls=%fused_computation.4 | convolution fusion | flops 335839232 | bytes 2949120 | tf_op jit(solution)/shard_map/dot_general | solution.py:20
  52.9 5.9 %all-to-all-start.1 = ((bf16[16,8,256]{2,1,0:T(8,128)(2,1)}), bf16[16,8,256]{2,1,0:T(8,128)(2,1)S(1)}, u32[]{:S(2)}, u32[]{:S(2)}) async-start(bf16[16,8,256]{2,1,0:T(8,128)(2,1)} %fusion.3), calls=%async_computation.1 | async-start | bytes 131072 | tf_op jit(solution)/shard_map/all_to_all | solution.py:443
  58.8 5.8 %shard_map.126 = bf16[768,1024]{1,0:T(8,128)(2,1)} custom-call(bf16[768,1024]{1,0:T(8,128)(2,1)} %refs_0_.1, bf16[768,1024]{1,0:T(8,128)(2,1)} %get-tuple-element.52.refs_1_, bf16[768,1024]{1,0:T(8,128)(2,1)} %get-tuple-element.53.refs_2_, bf16[1024,1024]{1,0:T(8,128)(2,1)} %refs_3_.1, bf16[256,128]{1,0:T(8,128)(2,1)} %copy-done.1, ...), custom_call_target="tpu_custom_call" | custom-call | flops 1610612736 | bytes 7864320 | tf_op jit(solution)/shard_map/pallas_call | solution.py:396
  64.6 1.0 %all-to-all-done.1 = bf16[16,8,256]{2,1,0:T(8,128)(2,1)S(1)} async-done(((bf16[16,8,256]{2,1,0:T(8,128)(2,1)}), bf16[16,8,256]{2,1,0:T(8,128)(2,1)S(1)}, u32[]{:S(2)}, u32[]{:S(2)}) %all-to-all-start.1) | async-done | bytes 65568 | tf_op jit(solution)/shard_map/all_to_all | solution.py:443
  65.7 0.8 %fusion.4 = f32[32,256]{1,0:T(8,128)} fusion(bf16[2,32,128]{2,1,0:T(8,128)(2,1)S(1)} %copy-done.9, bf16[16,8,256]{2,1,0:T(8,128)(2,1)S(1)} %all-to-all-done.1, f32[2,32]{1,0:T(2,128)S(1)} %add_divide_fusion), kind=kOutput, calls=%fused_computation.6 | convolution fusion | flops 4218880 | bytes 114944 | tf_op jit(solution)/shard_map/dot_general | solution.py:20
  (32 shorter events, 0.4 us)
Async XLA Ops:
  0.6 51.0 %copy-start = (bf16[1024,1024]{1,0:T(8,128)(2,1)S(1)}, bf16[1024,1024]{1,0:T(8,128)(2,1)}, u32[]{:S(2)}) copy-start(bf16[1024,1024]{1,0:T(8,128)(2,1)} %param.16) | copy-start | bytes 6291460
  8.6 8.2 %collective-permute-start = (bf16[256,128]{1,0:T(8,128)(2,1)}, bf16[256,128]{1,0:T(8,128)(2,1)S(1)}, u32[]{:S(2)}, u32[]{:S(2)}) collective-permute-start(bf16[256,128]{1,0:T(8,128)(2,1)} %get-tuple-element.31), channel_id=1, source_target_pairs={{0,1},{1,0},{2,3},{3,2},{4,5},{5,4},{6,7},{7,6},{8,9},{9,8},{10,11... | collective-permute-start | bytes 196616 | tf_op jit(solution)/shard_map/ppermute | solution.py:276
  9.1 7.7 %collective-permute-start.1 = (bf16[256,128]{1,0:T(8,128)(2,1)}, bf16[256,128]{1,0:T(8,128)(2,1)S(1)}, u32[]{:S(2)}, u32[]{:S(2)}) collective-permute-start(bf16[256,128]{1,0:T(8,128)(2,1)} %get-tuple-element.32), channel_id=1, source_target_pairs={{0,2},{1,3},{2,0},{3,1},{4,6},{5,7},{6,4},{7,5},{8,10},{9,11},{10,... | collective-permute-start | bytes 196616 | tf_op jit(solution)/shard_map/ppermute | solution.py:276
  11.7 5.1 %collective-permute-start.2 = (bf16[256,128]{1,0:T(8,128)(2,1)}, bf16[256,128]{1,0:T(8,128)(2,1)S(1)}, u32[]{:S(2)}, u32[]{:S(2)}) collective-permute-start(bf16[256,128]{1,0:T(8,128)(2,1)} %get-tuple-element.33), channel_id=1, source_target_pairs={{0,3},{1,2},{2,1},{3,0},{4,7},{5,6},{6,5},{7,4},{8,11},{9,10},{10,... | collective-permute-start | bytes 196616 | tf_op jit(solution)/shard_map/ppermute | solution.py:276
  11.8 5.1 %copy-start.6 = (bf16[256,128]{1,0:T(8,128)(2,1)S(1)}, bf16[256,128]{1,0:T(8,128)(2,1)}, u32[]{:S(2)}) copy-start(bf16[256,128]{1,0:T(8,128)(2,1)} %get-tuple-element.37) | copy-start | bytes 196612
  16.9 8.9 %collective-permute-start.5 = (bf16[256,128]{1,0:T(8,128)(2,1)S(1)}, bf16[256,128]{1,0:T(8,128)(2,1)S(1)}, u32[]{:S(2)}, u32[]{:S(2)}) collective-permute-start(bf16[256,128]{1,0:T(8,128)(2,1)S(1)} %fusion.22), channel_id=1, source_target_pairs={{0,8},{1,9},{2,10},{3,11},{4,12},{5,13},{6,14},{7,15},{16,24},{17,... | collective-permute-start | bytes 196616 | tf_op jit(solution)/shard_map/ppermute | solution.py:280
  21.7 4.2 %collective-permute-start.4 = (bf16[256,128]{1,0:T(8,128)(2,1)S(1)}, bf16[256,128]{1,0:T(8,128)(2,1)S(1)}, u32[]{:S(2)}, u32[]{:S(2)}) collective-permute-start(bf16[256,128]{1,0:T(8,128)(2,1)S(1)} %fusion.22), channel_id=1, source_target_pairs={{0,12},{1,13},{2,14},{3,15},{16,28},{17,29},{18,30},{19,31}} | collective-permute-start | bytes 196616 | tf_op jit(solution)/shard_map/ppermute | solution.py:280
  24.0 3.7 %collective-permute-start.3 = (bf16[256,128]{1,0:T(8,128)(2,1)S(1)}, bf16[256,128]{1,0:T(8,128)(2,1)S(1)}, u32[]{:S(2)}, u32[]{:S(2)}) collective-permute-start(bf16[256,128]{1,0:T(8,128)(2,1)S(1)} %fusion.22), channel_id=1, source_target_pairs={{0,4},{1,5},{2,6},{3,7},{4,8},{5,9},{6,10},{7,11},{8,12},{9,13},{1... | collective-permute-start | bytes 196616 | tf_op jit(solution)/shard_map/ppermute | solution.py:280
  27.9 5.7 %copy-start.1 = (bf16[256,128]{1,0:T(8,128)(2,1)}, bf16[256,128]{1,0:T(8,128)(2,1)S(1)}, u32[]{:S(2)}) copy-start(bf16[256,128]{1,0:T(8,128)(2,1)S(1)} %get-tuple-element.42.refs_0_.refs_4_) | copy-start | bytes 196612
  27.9 4.7 %collective-permute-start.6 = (bf16[256,128]{1,0:T(8,128)(2,1)S(1)}, bf16[256,128]{1,0:T(8,128)(2,1)S(1)}, u32[]{:S(2)}, u32[]{:S(2)}) collective-permute-start(bf16[256,128]{1,0:T(8,128)(2,1)S(1)} %get-tuple-element.43), channel_id=1, source_target_pairs={{0,1},{1,0},{2,3},{3,2},{4,5},{5,4},{6,7},{7,6},{8,9},{9,8},{10,11... | collective-permute-start | bytes 196616 | tf_op jit(solution)/shard_map/ppermute | solution.py:276
  28.0 4.7 %collective-permute-start.7 = (bf16[256,128]{1,0:T(8,128)(2,1)S(1)}, bf16[256,128]{1,0:T(8,128)(2,1)S(1)}, u32[]{:S(2)}, u32[]{:S(2)}) collective-permute-start(bf16[256,128]{1,0:T(8,128)(2,1)S(1)} %get-tuple-element.44), channel_id=1, source_target_pairs={{0,2},{1,3},{2,0},{3,1},{4,6},{5,7},{6,4},{7,5},{8,10},{9,11},{10,... | collective-permute-start | bytes 196616 | tf_op jit(solution)/shard_map/ppermute | solution.py:276
  29.5 4.0 %collective-permute-start.8 = (bf16[256,128]{1,0:T(8,128)(2,1)S(1)}, bf16[256,128]{1,0:T(8,128)(2,1)S(1)}, u32[]{:S(2)}, u32[]{:S(2)}) collective-permute-start(bf16[256,128]{1,0:T(8,128)(2,1)S(1)} %get-tuple-element.45), channel_id=1, source_target_pairs={{0,3},{1,2},{2,1},{3,0},{4,7},{5,6},{6,5},{7,4},{8,11},{9,10},{10,... | collective-permute-start | bytes 196616 | tf_op jit(solution)/shard_map/ppermute | solution.py:276
  32.6 9.0 %copy-start.7 = (bf16[1024,32]{0,1:T(8,128)(2,1)S(1)}, bf16[1024,32]{0,1:T(8,128)(2,1)}, u32[]{:S(2)}) copy-start(bf16[1024,32]{0,1:T(8,128)(2,1)} %param.18) | copy-start | bytes 196612
  32.6 9.1 %copy-start.8 = (f32[2,32,32]{2,1,0:T(8,128)S(1)}, f32[2,32,32]{2,1,0:T(8,128)}, u32[]{:S(2)}) copy-start(f32[2,32,32]{2,1,0:T(8,128)} %get-tuple-element.55) | copy-start | bytes 24580
  32.6 18.8 %copy-start.2 = (bf16[256,128]{1,0:T(8,128)(2,1)}, bf16[256,128]{1,0:T(8,128)(2,1)S(1)}, u32[]{:S(2)}) copy-start(bf16[256,128]{1,0:T(8,128)(2,1)S(1)} %collective-permute-done.6.refs_1_.refs_5_) | copy-start | bytes 196612
  32.7 18.8 %copy-start.3 = (bf16[256,128]{1,0:T(8,128)(2,1)}, bf16[256,128]{1,0:T(8,128)(2,1)S(1)}, u32[]{:S(2)}) copy-start(bf16[256,128]{1,0:T(8,128)(2,1)S(1)} %collective-permute-done.7.refs_2_.refs_6_) | copy-start | bytes 196612
  33.6 17.8 %copy-start.4 = (bf16[256,128]{1,0:T(8,128)(2,1)}, bf16[256,128]{1,0:T(8,128)(2,1)S(1)}, u32[]{:S(2)}) copy-start(bf16[256,128]{1,0:T(8,128)(2,1)S(1)} %collective-permute-done.8.refs_3_.refs_7_) | copy-start | bytes 196612
  35.1 16.5 %all-to-all-start = ((bf16[16,8,1024]{2,1,0:T(8,128)(2,1)}), bf16[16,8,1024]{2,1,0:T(8,128)(2,1)S(1)}, u32[]{:S(2)}, u32[]{:S(2)}) async-start(bf16[16,8,1024]{2,1,0:T(8,128)(2,1)} %bitcast.3), calls=%async_computation | async-start | bytes 524288 | tf_op jit(solution)/shard_map/all_to_all | solution.py:443
  41.8 9.8 %copy-start.5 = (bf16[1024,256]{1,0:T(8,128)(2,1)S(1)}, bf16[1024,256]{1,0:T(8,128)(2,1)}, u32[]{:S(2)}) copy-start(bf16[1024,256]{1,0:T(8,128)(2,1)} %param.17) | copy-start | bytes 1572868
  52.9 12.8 %all-to-all-start.1 = ((bf16[16,8,256]{2,1,0:T(8,128)(2,1)}), bf16[16,8,256]{2,1,0:T(8,128)(2,1)S(1)}, u32[]{:S(2)}, u32[]{:S(2)}) async-start(bf16[16,8,256]{2,1,0:T(8,128)(2,1)} %fusion.3), calls=%async_computation.1 | async-start | bytes 131072 | tf_op jit(solution)/shard_map/all_to_all | solution.py:443
  58.8 6.9 %copy-start.9 = (bf16[2,32,128]{2,1,0:T(8,128)(2,1)S(1)}, bf16[2,32,128]{2,1,0:T(8,128)(2,1)}, u32[]{:S(2)}) copy-start(bf16[2,32,128]{2,1,0:T(8,128)(2,1)} %get-tuple-element.56) | copy-start | bytes 49156

commit v15 on v14

--- a/solution.py
+++ b/solution.py
@@ -311,14 +311,16 @@
 
 
 def picked_kernel(head_dim, packed, w_output, *refs):
-    parts, (picked, outgoing, prefix) = refs[:PLANE], refs[PLANE:]
+    parts, (picked, outgoing, earlier) = refs[:PLANE], refs[PLANE:]
     width = w_output.shape[0]
-    query, events, within = (packed[:, i * width : (i + 1) * width] for i in range(3))
+    events, within = (packed[:, i * width : (i + 1) * width] for i in (1, 2))
+    rank = lax.axis_index("seq") & (PLANE - 1)
     factor = packed[:, 3 * width : 3 * width + 1]
     selector = packed[:, 3 * width + head_dim :].astype(BF16)
-    put_prefix(prefix, parts, head_dim)
-    earlier = earlier_terms(query.astype(BF16), prefix, head_dim)
-    attended = ((within + earlier) * factor).astype(BF16)
+    for j, part in enumerate(parts):
+        cols = pl.ds(pl.multiple_of((j ^ rank) * (width // PLANE), width // PLANE), width // PLANE)
+        earlier[:, cols] = dot(packed[:, cols].astype(BF16), on_diagonal(part[...], head_dim))
+    attended = ((within + earlier[...]) * factor).astype(BF16)
     rows = (events + dot(attended, w_output[...])).astype(BF16)
     picked[...] = rows
     outgoing[...] = dot(selector, rows, ((0,), (0,))).astype(BF16)
@@ -329,13 +331,12 @@
     width = w_output.shape[0]
     head_dim = width // HEADS
     slots = packed.shape[1] - 3 * width - head_dim
-    pair = width // PLANE
     return near(
         functools.partial(picked_kernel, head_dim),
         [shaped((many, width), BF16), shaped((slots, width), BF16)],
         2 * many * width * width,
         2 * width * width,
-        [pltpu.VMEM((PLANE, pair, pair), BF16)],
+        [pltpu.VMEM((many, width), F32)],
     )(packed, w_output, *prefix)
 
 

time: 66.9 us -> 66.9 us (level)
  no operation moved by 1% of the time
where the time goes in v15:
time: 66.9 us; the launch traced here: 66.4 us
  Pallas kernels  30 us (45%)
  starting transfers between devices  26.3 us (39%)
  waiting for transfers between devices  4 us (6%)
  other arithmetic  3.09 us (5%)
  matrix products  2.16 us (3%)
  between operations  0.9 us (1%)
    all_to_all x2, starting transfers between devices, exchange(): return lax.all_to_all(x, 'seq', split_axis=0, concat_axis=0, tiled=True)  12.3 us
    pallas_call x1, Pallas kernels, queries_within(): call(functools.partial(within_kernel, head_dim, tile), (width // pair,),...  9.58 us
    ppermute x3, starting transfers between devices, later(): lax.ppermute(x, 'seq', [(i, i + s) for i in range(lax.axis_size('seq') -...  8.85 us
    pallas_call x1, Pallas kernels, key_value_state(): call(functools.partial(key_value_kernel, head_dim, tile), (PLANE // step,...  7.97 us
    pallas_call x1, Pallas kernels, hidden_rows(): call(functools.partial(hidden_kernel, head_dim, tile), (), [FAR] * (4 + P...  5.84 us
    ppermute x6, starting transfers between devices, flip(): return lax.ppermute(x, 'seq', [(i, i ^ j) for i in range(devices)])  5.11 us
    pallas_call x1, Pallas kernels, labelled_rows(): call(functools.partial(labelled_kernel, width // HEADS, devices // EXPERT...  5.04 us
    dot_general x3, matrix products, dot(): lax.dot_general(a, b, (contract, ((), ())), preferred_element_type=F32, *...  2.16 us
  transfers between devices with their start and end apart: 11, of which 4 were waited for; matrix products, arithmetic and copies ran while one was open for 5% of the time, Pallas kernels for 31%

profile of v15, /device:TPU:0, one launch (start us, length us, event | category | flops | bytes accessed | tf_op | source)
XLA Modules:
  0.0 66.4 jit_solution(5250555796967647418)
XLA Ops:
  0.6 8.0 %shard_map.122 = (bf16[2,4,768,256]{3,2,1,0:T(8,128)(2,1)}, bf16[2,1024,128]{2,1,0:T(8,128)(2,1)}, bf16[256,128]{1,0:T(8,128)(2,1)}, bf16[256,128]{1,0:T(8,128)(...) custom-call(bf16[768,1024]{1,0:T(8,128)(2,1)} %refs_0_.1, bf16[1024,1024]{1,0:T(8,128)(2,1)} %w_key.1, ...), custom_call_target="tpu_custom_call" | custom-call | flops 3221225472 | bytes 6291456 | tf_op jit(solution)/shard_map/pallas_call | solution.py:100
  8.6 0.5 collective-permute-start
  9.1 2.6 %collective-permute-start.1 = (bf16[256,128]{1,0:T(8,128)(2,1)}, bf16[256,128]{1,0:T(8,128)(2,1)S(1)}, u32[]{:S(2)}, u32[]{:S(2)}) collective-permute-start(bf16[256,128]{1,0:T(8,128)(2,1)} %get-tuple-element.32), channel_id=1, source_target_pairs={{0,2},{1,3},{2,0},{3,1},{4,6},{5,7},{6,4},{7,5},{8,10},{9,11},{10,... | collective-permute-start | bytes 196616 | tf_op jit(solution)/shard_map/ppermute | solution.py:276
  11.8 5.0 %shard_map.123 = (f32[32,3328]{1,0:T(8,128)}, bf16[2,32,128]{2,1,0:T(8,128)(2,1)}, f32[2,32,32]{2,1,0:T(8,128)}) custom-call(bf16[768,1024]{1,0:T(8,128)(2,1)} %refs_0_.1, bf16[1024,1024]{1,0:T(8,128)(2,1)} %w_query.1, bf16[2,4,768,256]{3,2,1,0:T(8,128)(2,1)} %get-tuple-element.48.keys_values_far.keys.values, s32[1,32]{1,0:T(1,128)} %bitcast.20, ...), custom_call_target="tpu_custom_call" | custom-call | flops 100663296 | bytes 6291456 | tf_op jit(solution)/shard_map/pallas_call | solution.py:169
  16.9 4.7 %collective-permute-start.5 = (bf16[256,128]{1,0:T(8,128)(2,1)S(1)}, bf16[256,128]{1,0:T(8,128)(2,1)S(1)}, u32[]{:S(2)}, u32[]{:S(2)}) collective-permute-start(bf16[256,128]{1,0:T(8,128)(2,1)S(1)} %fusion.22), channel_id=1, source_target_pairs={{0,8},{1,9},{2,10},{3,11},{4,12},{5,13},{6,14},{7,15},{16,24},{17,... | collective-permute-start | bytes 196616 | tf_op jit(solution)/shard_map/ppermute | solution.py:280
  21.7 2.3 %collective-permute-start.4 = (bf16[256,128]{1,0:T(8,128)(2,1)S(1)}, bf16[256,128]{1,0:T(8,128)(2,1)S(1)}, u32[]{:S(2)}, u32[]{:S(2)}) collective-permute-start(bf16[256,128]{1,0:T(8,128)(2,1)S(1)} %fusion.22), channel_id=1, source_target_pairs={{0,12},{1,13},{2,14},{3,15},{16,28},{17,29},{18,30},{19,31}} | collective-permute-start | bytes 196616 | tf_op jit(solution)/shard_map/ppermute | solution.py:280
  24.0 1.8 %collective-permute-start.3 = (bf16[256,128]{1,0:T(8,128)(2,1)S(1)}, bf16[256,128]{1,0:T(8,128)(2,1)S(1)}, u32[]{:S(2)}, u32[]{:S(2)}) collective-permute-start(bf16[256,128]{1,0:T(8,128)(2,1)S(1)} %fusion.22), channel_id=1, source_target_pairs={{0,4},{1,5},{2,6},{3,7},{4,8},{5,9},{6,10},{7,11},{8,12},{9,13},{1... | collective-permute-start | bytes 196616 | tf_op jit(solution)/shard_map/ppermute | solution.py:280
  25.9 1.8 %collective-permute-done.3 = bf16[256,128]{1,0:T(8,128)(2,1)S(1)} collective-permute-done((bf16[256,128]{1,0:T(8,128)(2,1)S(1)}, bf16[256,128]{1,0:T(8,128)(2,1)S(1)}, u32[]{:S(2)}, u32[]{:S(2)}) %collective-permute-start.3) | collective-permute-done | bytes 65568 | tf_op jit(solution)/shard_map/ppermute | solution.py:280
  27.7 0.2 fusion.17
  28.0 1.6 %collective-permute-start.7 = (bf16[256,128]{1,0:T(8,128)(2,1)S(1)}, bf16[256,128]{1,0:T(8,128)(2,1)S(1)}, u32[]{:S(2)}, u32[]{:S(2)}) collective-permute-start(bf16[256,128]{1,0:T(8,128)(2,1)S(1)} %get-tuple-element.44), channel_id=1, source_target_pairs={{0,2},{1,3},{2,0},{3,1},{4,6},{5,7},{6,4},{7,5},{8,10},{9,11},{10,... | collective-permute-start | bytes 196616 | tf_op jit(solution)/shard_map/ppermute | solution.py:276
  29.5 0.3 collective-permute-start.8
  29.8 1.0 %broadcast_multiply_fusion.1.packed = f32[32,3328]{1,0:T(8,128)S(1)} fusion(f32[32,3328]{1,0:T(8,128)} %get-tuple-element.36, f32[]{:T(128)S(6)} %convert_element_type.57), kind=kLoop, calls=%fused_computation.24 | loop fusion | flops 106496 | bytes 851972 | tf_op jit(solution)/shard_map/mul | solution.py:453
  30.9 1.7 %broadcast_multiply_fusion.w_output = bf16[1024,1024]{1,0:T(8,128)(2,1)S(1)} fusion(bf16[1024,1024]{1,0:T(8,128)(2,1)} %refs_3_.1, bf16[]{:T(256)} %constant.4.clone.1), kind=kLoop, calls=%fused_computation.7 | loop fusion | flops 1048576 | bytes 4194306 | tf_op jit(solution)/shard_map/mul | solution.py:453
  32.7 0.9 %collective-permute-done.8.refs_3_.refs_7_ = bf16[256,128]{1,0:T(8,128)(2,1)S(1)} collective-permute-done((bf16[256,128]{1,0:T(8,128)(2,1)S(1)}, bf16[256,128]{1,0:T(8,128)(2,1)S(1)}, u32[]{:S(2)}, u32[]{:S(2)}) %collective-permute-start.8) | collective-permute-done | bytes 65568 | tf_op jit(solution)/shard_map/ppermute | solution.py:276
  33.6 1.5 %shard_map.124 = (bf16[32,1024]{1,0:T(8,128)(2,1)S(1)}, bf16[128,1024]{1,0:T(8,128)(2,1)}) custom-call(f32[32,3328]{1,0:T(8,128)S(1)} %broadcast_multiply_fusion.1.packed, bf16[1024,1024]{1,0:T(8,128)(2,1)S(1)} %broadcast_multiply_fusion.w_output, bf16[256,128]{1,0:T(8,128)(2,1)S(1)} %get-tuple-element.42.refs_0_.refs_4_, ...), custom_call_target="tpu_custom_call" | custom-call | flops 67108864 | bytes 2097152 | tf_op jit(solution)/shard_map/pallas_call | solution.py:334
  35.1 6.4 %all-to-all-start = ((bf16[16,8,1024]{2,1,0:T(8,128)(2,1)}), bf16[16,8,1024]{2,1,0:T(8,128)(2,1)S(1)}, u32[]{:S(2)}, u32[]{:S(2)}) async-start(bf16[16,8,1024]{2,1,0:T(8,128)(2,1)} %bitcast.3), calls=%async_computation | async-start | bytes 524288 | tf_op jit(solution)/shard_map/all_to_all | solution.py:444
  41.6 0.1 fusion.25
  41.9 9.6 %shard_map.125 = (bf16[768,1024]{1,0:T(8,128)(2,1)}, bf16[768,1024]{1,0:T(8,128)(2,1)}) custom-call(bf16[768,1024]{1,0:T(8,128)(2,1)} %refs_0_.1, bf16[1024,1024]{1,0:T(8,128)(2,1)} %w_query.1, bf16[2,4,768,256]{3,2,1,0:T(8,128)(2,1)} %get-tuple-element.48.keys_values_far.keys.values, bf16[2,4,768,256]{3,2,1,0:T(8,128)(2,1)} %get-tuple-element.48.keys_values_far.keys.values, ...), custom_call_target="tpu_custom_call" | custom-call | flops 2415919104 | bytes 6291456 | tf_op jit(solution)/shard_map/pallas_call | solution.py:257
  51.5 0.2 all-to-all-done
  51.6 1.3 %fusion.3 = bf16[16,8,256]{2,1,0:T(8,128)(2,1)} fusion(bf16[1024,256]{1,0:T(8,128)(2,1)S(1)} %copy-done.5, bf16[128,1024]{1,0:T(8,128)(2,1)S(1)} %bitcast.18, bf16[1024,1024]{1,0:T(8,128)(2,1)S(1)} %copy-done), kind=kOutput, calls=%fused_computation.4 | convolution fusion | flops 335839232 | bytes 2949120 | tf_op jit(solution)/shard_map/dot_general | solution.py:20
  52.9 5.9 %all-to-all-start.1 = ((bf16[16,8,256]{2,1,0:T(8,128)(2,1)}), bf16[16,8,256]{2,1,0:T(8,128)(2,1)S(1)}, u32[]{:S(2)}, u32[]{:S(2)}) async-start(bf16[16,8,256]{2,1,0:T(8,128)(2,1)} %fusion.3), calls=%async_computation.1 | async-start | bytes 131072 | tf_op jit(solution)/shard_map/all_to_all | solution.py:444
  58.8 5.8 %shard_map.126 = bf16[768,1024]{1,0:T(8,128)(2,1)} custom-call(bf16[768,1024]{1,0:T(8,128)(2,1)} %refs_0_.1, bf16[768,1024]{1,0:T(8,128)(2,1)} %get-tuple-element.52.refs_1_, bf16[768,1024]{1,0:T(8,128)(2,1)} %get-tuple-element.53.refs_2_, bf16[1024,1024]{1,0:T(8,128)(2,1)} %refs_3_.1, bf16[256,128]{1,0:T(8,128)(2,1)} %copy-done.1, ...), custom_call_target="tpu_custom_call" | custom-call | flops 1610612736 | bytes 7864320 | tf_op jit(solution)/shard_map/pallas_call | solution.py:397
  64.6 1.0 %all-to-all-done.1 = bf16[16,8,256]{2,1,0:T(8,128)(2,1)S(1)} async-done(((bf16[16,8,256]{2,1,0:T(8,128)(2,1)}), bf16[16,8,256]{2,1,0:T(8,128)(2,1)S(1)}, u32[]{:S(2)}, u32[]{:S(2)}) %all-to-all-start.1) | async-done | bytes 65568 | tf_op jit(solution)/shard_map/all_to_all | solution.py:444
  65.7 0.8 %fusion.4 = f32[32,256]{1,0:T(8,128)} fusion(bf16[2,32,128]{2,1,0:T(8,128)(2,1)S(1)} %copy-done.9, bf16[16,8,256]{2,1,0:T(8,128)(2,1)S(1)} %all-to-all-done.1, f32[2,32]{1,0:T(2,128)S(1)} %add_divide_fusion), kind=kOutput, calls=%fused_computation.6 | convolution fusion | flops 4218880 | bytes 114944 | tf_op jit(solution)/shard_map/dot_general | solution.py:20
  (32 shorter events, 0.4 us)
Async XLA Ops:
  0.6 51.0 %copy-start = (bf16[1024,1024]{1,0:T(8,128)(2,1)S(1)}, bf16[1024,1024]{1,0:T(8,128)(2,1)}, u32[]{:S(2)}) copy-start(bf16[1024,1024]{1,0:T(8,128)(2,1)} %param.16) | copy-start | bytes 6291460
  8.6 8.2 %collective-permute-start = (bf16[256,128]{1,0:T(8,128)(2,1)}, bf16[256,128]{1,0:T(8,128)(2,1)S(1)}, u32[]{:S(2)}, u32[]{:S(2)}) collective-permute-start(bf16[256,128]{1,0:T(8,128)(2,1)} %get-tuple-element.31), channel_id=1, source_target_pairs={{0,1},{1,0},{2,3},{3,2},{4,5},{5,4},{6,7},{7,6},{8,9},{9,8},{10,11... | collective-permute-start | bytes 196616 | tf_op jit(solution)/shard_map/ppermute | solution.py:276
  9.1 7.7 %collective-permute-start.1 = (bf16[256,128]{1,0:T(8,128)(2,1)}, bf16[256,128]{1,0:T(8,128)(2,1)S(1)}, u32[]{:S(2)}, u32[]{:S(2)}) collective-permute-start(bf16[256,128]{1,0:T(8,128)(2,1)} %get-tuple-element.32), channel_id=1, source_target_pairs={{0,2},{1,3},{2,0},{3,1},{4,6},{5,7},{6,4},{7,5},{8,10},{9,11},{10,... | collective-permute-start | bytes 196616 | tf_op jit(solution)/shard_map/ppermute | solution.py:276
  11.7 5.1 %collective-permute-start.2 = (bf16[256,128]{1,0:T(8,128)(2,1)}, bf16[256,128]{1,0:T(8,128)(2,1)S(1)}, u32[]{:S(2)}, u32[]{:S(2)}) collective-permute-start(bf16[256,128]{1,0:T(8,128)(2,1)} %get-tuple-element.33), channel_id=1, source_target_pairs={{0,3},{1,2},{2,1},{3,0},{4,7},{5,6},{6,5},{7,4},{8,11},{9,10},{10,... | collective-permute-start | bytes 196616 | tf_op jit(solution)/shard_map/ppermute | solution.py:276
  11.8 5.1 %copy-start.6 = (bf16[256,128]{1,0:T(8,128)(2,1)S(1)}, bf16[256,128]{1,0:T(8,128)(2,1)}, u32[]{:S(2)}) copy-start(bf16[256,128]{1,0:T(8,128)(2,1)} %get-tuple-element.37) | copy-start | bytes 196612
  16.9 8.9 %collective-permute-start.5 = (bf16[256,128]{1,0:T(8,128)(2,1)S(1)}, bf16[256,128]{1,0:T(8,128)(2,1)S(1)}, u32[]{:S(2)}, u32[]{:S(2)}) collective-permute-start(bf16[256,128]{1,0:T(8,128)(2,1)S(1)} %fusion.22), channel_id=1, source_target_pairs={{0,8},{1,9},{2,10},{3,11},{4,12},{5,13},{6,14},{7,15},{16,24},{17,... | collective-permute-start | bytes 196616 | tf_op jit(solution)/shard_map/ppermute | solution.py:280
  21.7 4.2 %collective-permute-start.4 = (bf16[256,128]{1,0:T(8,128)(2,1)S(1)}, bf16[256,128]{1,0:T(8,128)(2,1)S(1)}, u32[]{:S(2)}, u32[]{:S(2)}) collective-permute-start(bf16[256,128]{1,0:T(8,128)(2,1)S(1)} %fusion.22), channel_id=1, source_target_pairs={{0,12},{1,13},{2,14},{3,15},{16,28},{17,29},{18,30},{19,31}} | collective-permute-start | bytes 196616 | tf_op jit(solution)/shard_map/ppermute | solution.py:280
  24.0 3.7 %collective-permute-start.3 = (bf16[256,128]{1,0:T(8,128)(2,1)S(1)}, bf16[256,128]{1,0:T(8,128)(2,1)S(1)}, u32[]{:S(2)}, u32[]{:S(2)}) collective-permute-start(bf16[256,128]{1,0:T(8,128)(2,1)S(1)} %fusion.22), channel_id=1, source_target_pairs={{0,4},{1,5},{2,6},{3,7},{4,8},{5,9},{6,10},{7,11},{8,12},{9,13},{1... | collective-permute-start | bytes 196616 | tf_op jit(solution)/shard_map/ppermute | solution.py:280
  27.9 5.7 %copy-start.1 = (bf16[256,128]{1,0:T(8,128)(2,1)}, bf16[256,128]{1,0:T(8,128)(2,1)S(1)}, u32[]{:S(2)}) copy-start(bf16[256,128]{1,0:T(8,128)(2,1)S(1)} %get-tuple-element.42.refs_0_.refs_4_) | copy-start | bytes 196612
  27.9 4.7 %collective-permute-start.6 = (bf16[256,128]{1,0:T(8,128)(2,1)S(1)}, bf16[256,128]{1,0:T(8,128)(2,1)S(1)}, u32[]{:S(2)}, u32[]{:S(2)}) collective-permute-start(bf16[256,128]{1,0:T(8,128)(2,1)S(1)} %get-tuple-element.43), channel_id=1, source_target_pairs={{0,1},{1,0},{2,3},{3,2},{4,5},{5,4},{6,7},{7,6},{8,9},{9,8},{10,11... | collective-permute-start | bytes 196616 | tf_op jit(solution)/shard_map/ppermute | solution.py:276
  28.0 4.7 %collective-permute-start.7 = (bf16[256,128]{1,0:T(8,128)(2,1)S(1)}, bf16[256,128]{1,0:T(8,128)(2,1)S(1)}, u32[]{:S(2)}, u32[]{:S(2)}) collective-permute-start(bf16[256,128]{1,0:T(8,128)(2,1)S(1)} %get-tuple-element.44), channel_id=1, source_target_pairs={{0,2},{1,3},{2,0},{3,1},{4,6},{5,7},{6,4},{7,5},{8,10},{9,11},{10,... | collective-permute-start | bytes 196616 | tf_op jit(solution)/shard_map/ppermute | solution.py:276
  29.5 4.0 %collective-permute-start.8 = (bf16[256,128]{1,0:T(8,128)(2,1)S(1)}, bf16[256,128]{1,0:T(8,128)(2,1)S(1)}, u32[]{:S(2)}, u32[]{:S(2)}) collective-permute-start(bf16[256,128]{1,0:T(8,128)(2,1)S(1)} %get-tuple-element.45), channel_id=1, source_target_pairs={{0,3},{1,2},{2,1},{3,0},{4,7},{5,6},{6,5},{7,4},{8,11},{9,10},{10,... | collective-permute-start | bytes 196616 | tf_op jit(solution)/shard_map/ppermute | solution.py:276
  32.6 9.0 %copy-start.7 = (bf16[1024,32]{0,1:T(8,128)(2,1)S(1)}, bf16[1024,32]{0,1:T(8,128)(2,1)}, u32[]{:S(2)}) copy-start(bf16[1024,32]{0,1:T(8,128)(2,1)} %param.18) | copy-start | bytes 196612
  32.6 9.1 %copy-start.8 = (f32[2,32,32]{2,1,0:T(8,128)S(1)}, f32[2,32,32]{2,1,0:T(8,128)}, u32[]{:S(2)}) copy-start(f32[2,32,32]{2,1,0:T(8,128)} %get-tuple-element.55) | copy-start | bytes 24580
  32.6 18.8 %copy-start.2 = (bf16[256,128]{1,0:T(8,128)(2,1)}, bf16[256,128]{1,0:T(8,128)(2,1)S(1)}, u32[]{:S(2)}) copy-start(bf16[256,128]{1,0:T(8,128)(2,1)S(1)} %collective-permute-done.6.refs_1_.refs_5_) | copy-start | bytes 196612
  32.7 18.8 %copy-start.3 = (bf16[256,128]{1,0:T(8,128)(2,1)}, bf16[256,128]{1,0:T(8,128)(2,1)S(1)}, u32[]{:S(2)}) copy-start(bf16[256,128]{1,0:T(8,128)(2,1)S(1)} %collective-permute-done.7.refs_2_.refs_6_) | copy-start | bytes 196612
  33.6 17.9 %copy-start.4 = (bf16[256,128]{1,0:T(8,128)(2,1)}, bf16[256,128]{1,0:T(8,128)(2,1)S(1)}, u32[]{:S(2)}) copy-start(bf16[256,128]{1,0:T(8,128)(2,1)S(1)} %collective-permute-done.8.refs_3_.refs_7_) | copy-start | bytes 196612
  35.1 16.5 %all-to-all-start = ((bf16[16,8,1024]{2,1,0:T(8,128)(2,1)}), bf16[16,8,1024]{2,1,0:T(8,128)(2,1)S(1)}, u32[]{:S(2)}, u32[]{:S(2)}) async-start(bf16[16,8,1024]{2,1,0:T(8,128)(2,1)} %bitcast.3), calls=%async_computation | async-start | bytes 524288 | tf_op jit(solution)/shard_map/all_to_all | solution.py:444
  41.9 9.8 %copy-start.5 = (bf16[1024,256]{1,0:T(8,128)(2,1)S(1)}, bf16[1024,256]{1,0:T(8,128)(2,1)}, u32[]{:S(2)}) copy-start(bf16[1024,256]{1,0:T(8,128)(2,1)} %param.17) | copy-start | bytes 1572868
  52.9 12.8 %all-to-all-start.1 = ((bf16[16,8,256]{2,1,0:T(8,128)(2,1)}), bf16[16,8,256]{2,1,0:T(8,128)(2,1)S(1)}, u32[]{:S(2)}, u32[]{:S(2)}) async-start(bf16[16,8,256]{2,1,0:T(8,128)(2,1)} %fusion.3), calls=%async_computation.1 | async-start | bytes 131072 | tf_op jit(solution)/shard_map/all_to_all | solution.py:444
  58.8 6.9 %copy-start.9 = (bf16[2,32,128]{2,1,0:T(8,128)(2,1)S(1)}, bf16[2,32,128]{2,1,0:T(8,128)(2,1)}, u32[]{:S(2)}) copy-start(bf16[2,32,128]{2,1,0:T(8,128)(2,1)} %get-tuple-element.56) | copy-start | bytes 49156
